TPU v7x, 32 devices: a whole 2x2x4 slice. The times are simulated.
32 devices in a mesh: dom: 32 (over z, y, x, core).
Axes of the slice: x: 2, y: 2, z: 4, core: 2. Of those that a mesh axis runs over, the one named last changes fastest.
Arguments:
- rhs_field: float32 [64, 4096], P(None, 'dom'), may hold values from -6 to 6
- initial_guess: float32 [64, 4096], P(None, 'dom'), may hold values from -6 to 6
- start_vector: float32 [64, 4096], P(None, 'dom'), may hold values from -90 to 90
- coefficient: float32 [4096], P('dom'), may hold values from 1 to 10
- refine_level: int32 [4096], P('dom'), may hold values from 0 to 2
- block_inverse: bfloat16 [64, 64, 4096], P(None, None, 'dom'), may hold values from -0.015 to 1, as said below
- side_elem: int32 [29760], P('dom'), may hold values from 0 to 127, as said below
- side_dir: int32 [29760], P('dom'), may hold values from 0 to 5, as said below
- side_case: int32 [29760], P('dom'), may hold values from 0 to 4, as said below
- side_kind: int32 [29760], P('dom'), may hold values from 0 to 1, as said below
- partner: int32 [29760], P('dom'), may hold values from 0 to 1625, as said below
- send_list: int32 [256, 96], P('dom'), may hold values from 0 to 930, as said below
Outputs:
- smoothed: float32 [64, 4096], P(None, 'dom')
- eigen_bound: float32 [], replicated
Inputs may be any that keep to these rules, and one draw needn't show every extreme that they name: `block_inverse`: each element's block is symmetric and positive definite. `side_elem`: an index among the 128 elements of the side's device. `side_dir`: 2 a is the face at the upper end of dimension a, 2 a + 1 the one at the lower end; partners lie on opposite faces of one dimension. `side_case`: 0 to 3 mark one quarter of a coarse face whose partner is the whole face of a finer element (case 4). `side_kind`: 1 marks a boundary side, whose partner entry is the side itself. `partner`: a device-local index; interior partners are mutual. `send_list`: row 8 d + p lists device d's sides for the device peer_offset[p] places higher; live entries are the first 96, 48, 24 or 24 of a row for offsets of size 1, 2, 3, 4; 930 marks an empty slot.
All inputs are finite; a program needn't handle non-finite values.
Results may differ from a plain program's by a relative error of at most 0.0003.
Values sent between devices are 32-bit elements; how exact they have to be, the bound alone decides.
No kernel may reach another device: no remote copies, remote signals or barrier semaphores. Data moves between devices by JAX's collectives and lax.ppermute only.
A program may use at most 64 MiB of HBM per device.

v0:
```python
import math

import jax
import jax.numpy as jnp
import numpy as np
from jax import lax
from jax.sharding import PartitionSpec as P

POWER = 4


penalty_factor = 32.0
highest = lax.Precision.HIGHEST
peer_offsets = (1, -1, 2, -2, 3, -3, 4, -4)


def passed_along(array, axis, by):
    size = lax.axis_size(axis)
    pairs = [(i, i + by) for i in range(size) if 0 <= i + by < size]
    return lax.ppermute(array, axis, pairs)


def lagrange_tables():
    root_five = 1.0 / math.sqrt(5.0)
    gll_nodes = np.array([0.0, 0.5 - 0.5 * root_five, 0.5 + 0.5 * root_five, 1.0])
    weights = np.array([1.0, 5.0, 5.0, 1.0]) / 12.0
    factor = np.array(
        [
            np.prod(
                [
                    gll_nodes[row_node] - gll_nodes[other_node]
                    for other_node in range(4)
                    if other_node != row_node
                ]
            )
            for row_node in range(4)
        ]
    )
    derivative = np.zeros((4, 4))
    for row_node in range(4):
        for col_node in range(4):
            if row_node != col_node:
                derivative[row_node, col_node] = factor[row_node] / (
                    factor[col_node] * (gll_nodes[row_node] - gll_nodes[col_node])
                )
        derivative[row_node, row_node] = -np.sum(derivative[row_node])
    halves = []
    for half_index in range(2):
        points = 0.5 * (gll_nodes + half_index)
        half_table = np.ones((4, 4))
        for col_node in range(4):
            for other_node in range(4):
                if other_node != col_node:
                    half_table[:, col_node] *= (points - gll_nodes[other_node]) / (
                        gll_nodes[col_node] - gll_nodes[other_node]
                    )
        halves.append(half_table)
    return (weights, derivative, halves)


def basis_tables():
    weights, derivative, halves = lagrange_tables()
    mass_matrix = np.eye(4) * weights[None, :]
    stiff_line = derivative.T @ mass_matrix @ derivative
    stiffness = (
        np.kron(np.kron(stiff_line, mass_matrix), mass_matrix)
        + np.kron(np.kron(mass_matrix, stiff_line), mass_matrix)
        + np.kron(np.kron(mass_matrix, mass_matrix), stiff_line)
    )
    trace_ops = np.zeros((32, 6, 64))
    for dimension in range(3):
        others = [other_dim for other_dim in range(3) if other_dim != dimension]
        for lower_end in range(2):
            face_index = 2 * dimension + lower_end
            fixed_node = 0 if lower_end else 3
            orientation = -1.0 if lower_end else 1.0
            for first_node in range(4):
                for second_node in range(4):
                    face_node = first_node * 4 + second_node
                    for along_node in range(4):
                        position = [0, 0, 0]
                        position[others[0]] = first_node
                        position[others[1]] = second_node
                        position[dimension] = along_node
                        nodal = position[0] * 16 + position[1] * 4 + position[2]
                        if along_node == fixed_node:
                            trace_ops[face_node, face_index, nodal] = 1.0
                        trace_ops[16 + face_node, face_index, nodal] = (
                            orientation * derivative[fixed_node, along_node]
                        )
    interp = np.zeros((5, 16, 16))
    for quarter in range(4):
        interp[quarter] = np.kron(halves[quarter // 2], halves[quarter % 2])
    interp[4] = np.eye(16)
    face_weight = np.kron(weights, weights)
    return (
        stiffness,
        trace_ops.reshape(192, 64),
        interp.reshape(80, 16),
        np.transpose(interp, (0, 2, 1)).reshape(80, 16),
        face_weight,
    )


def jnp_tables():
    return tuple((jnp.asarray(table_item, jnp.float32) for table_item in basis_tables()))


def element_scales(coefficient, refine_level):
    elem_size = jnp.power(jnp.float32(0.5), refine_level.astype(jnp.float32))
    return (elem_size, coefficient * elem_size, coefficient / elem_size)


def apply_case(values, side_case, stack):
    side_count = values.shape[1]
    paired = jnp.concatenate([values[:16], values[16:]], axis=1)
    quarters = jnp.dot(stack[:64], paired, precision=highest).reshape(4, 16, 2 * side_count)
    choose = (side_case[None, :] == jnp.arange(4, dtype=jnp.int32)[:, None]).astype(jnp.float32)
    choose = jnp.concatenate([choose, choose], axis=1)
    chosen = jnp.sum(quarters * choose[:, None, :], axis=0)
    hanging = side_case < 4
    hanging = jnp.concatenate([hanging, hanging], axis=0)[None, :]
    mixed = jnp.where(hanging, chosen, paired)
    return jnp.concatenate([mixed[:, :side_count], mixed[:, side_count:]], axis=0)


def mortar_traces(values_field, coefficient, refine_level, side_elem, side_dir, side_case, tables):
    stiffness, trace_ops, interp, interp_t, face_weight = tables
    elem_count = values_field.shape[1]
    elem_size, volume_scale, normal_scale = element_scales(coefficient, refine_level)
    face_values = jnp.dot(trace_ops, values_field, precision=highest)
    face_values = jnp.concatenate(
        [face_values[:96], face_values[96:] * normal_scale[None, :]], axis=0
    )
    face_values = face_values.reshape(32, 6 * elem_count)
    columns = side_dir * elem_count + side_elem
    picked = jnp.take(face_values, columns, axis=1)
    mortar = apply_case(picked, side_case, interp)
    side_size = jnp.take(elem_size, side_elem) * jnp.where(
        side_case < 4, jnp.float32(0.5), jnp.float32(1.0)
    )
    side_scalars = jnp.stack([jnp.take(coefficient, side_elem), side_size])
    return (mortar, side_scalars)


def apply_operator_local(
    values_field,
    coefficient,
    refine_level,
    mortar,
    side_scalars,
    outer_values,
    outer_scalars,
    side_elem,
    side_dir,
    side_case,
    side_kind,
    tables,
):
    stiffness, trace_ops, interp, interp_t, face_weight = tables
    elem_count = values_field.shape[1]
    elem_size, volume_scale, normal_scale = element_scales(coefficient, refine_level)
    boundary = (side_kind == 1).astype(jnp.float32)[None, :]
    trace_jump = mortar[:16] - (1.0 - boundary) * outer_values[:16]
    average = 0.5 * (mortar[16:] - outer_values[16:]) + boundary * 0.5 * (
        mortar[16:] + outer_values[16:]
    )
    mortar_size = jnp.minimum(side_scalars[1], outer_scalars[1])
    penalty = penalty_factor * (side_scalars[0] + outer_scalars[0]) / (2.0 * mortar_size)
    weighted = face_weight[:, None] * (mortar_size * mortar_size)[None, :]
    value_flux = weighted * (penalty[None, :] * trace_jump - average)
    slope_flux = -weighted * trace_jump * (0.5 + 0.5 * boundary)
    face_flux = apply_case(jnp.concatenate([value_flux, slope_flux], axis=0), side_case, interp_t)
    columns = side_dir * elem_count + side_elem
    gathered = jnp.zeros((32, 6 * elem_count), jnp.float32).at[:, columns].add(face_flux)
    gathered = gathered.reshape(192, elem_count)
    gathered = jnp.concatenate([gathered[:96], gathered[96:] * normal_scale[None, :]], axis=0)
    surface = jnp.dot(trace_ops.T, gathered, precision=highest)
    volume = jnp.dot(stiffness, values_field, precision=highest) * volume_scale[None, :]
    return volume + surface


def block_solve(inverse, residual):
    return jnp.sum(inverse.astype(jnp.float32) * residual[None, :, :], axis=1)


def local(
    rhs_field,
    initial_guess,
    start_vector,
    coefficient,
    refine_level,
    block_inverse,
    side_elem,
    side_dir,
    side_case,
    side_kind,
    partner,
    send_list,
):
    tables = jnp_tables()
    slot_width = send_list.shape[1]
    live_widths = [slot_width] * 8

    def operate(values_field):
        mortar, side_scalars = mortar_traces(
            values_field, coefficient, refine_level, side_elem, side_dir, side_case, tables
        )
        padded_values = jnp.concatenate([mortar, jnp.zeros((32, 1), jnp.float32)], axis=1)
        padded_scalars = jnp.concatenate([side_scalars, jnp.zeros((2, 1), jnp.float32)], axis=1)
        outgoing = []
        for peer_place in range(8):
            listed = send_list[peer_place, : live_widths[peer_place]]
            outgoing.append(
                (jnp.take(padded_values, listed, axis=1), jnp.take(padded_scalars, listed, axis=1))
            )
        arrived = []
        for peer_place in range(8):
            arrived.append(
                passed_along(
                    (outgoing[peer_place][0], outgoing[peer_place][1]),
                    "dom",
                    peer_offsets[peer_place],
                )
            )
        table_values = jnp.concatenate([mortar] + [received[0] for received in arrived], axis=1)
        table_scalars = jnp.concatenate(
            [side_scalars] + [received[1] for received in arrived], axis=1
        )
        outer_values = jnp.take(table_values, partner, axis=1)
        outer_scalars = jnp.take(table_scalars, partner, axis=1)
        return apply_operator_local(
            values_field,
            coefficient,
            refine_level,
            mortar,
            side_scalars,
            outer_values,
            outer_scalars,
            side_elem,
            side_dir,
            side_case,
            side_kind,
            tables,
        )

    def precondition(residual):
        return block_solve(block_inverse, residual)

    current = start_vector
    total = jnp.float32(1.0)
    for iteration in range(POWER):
        image = precondition(operate(current))
        total = lax.psum(jnp.sum(image * image), "dom")
        current = image / jnp.sqrt(total)
    eigen_bound = jnp.sqrt(total)
    upper_bound = 1.2 * eigen_bound
    lower_bound = upper_bound / 15.0
    center = 0.5 * (upper_bound + lower_bound)
    half_width = 0.5 * (upper_bound - lower_bound)
    spread_ratio = center / half_width
    damping = 1.0 / spread_ratio
    solution = initial_guess
    residual = precondition(rhs_field - operate(solution))
    update = residual / center
    solution = solution + update
    residual = precondition(rhs_field - operate(solution))
    damping_next = 1.0 / (2.0 * spread_ratio - damping)
    update = damping_next * damping * update + 2.0 * damping_next / half_width * residual
    solution = solution + update
    return (solution, eigen_bound)


def solution(mesh):
    placed = (
        P(None, "dom"),
        P(None, "dom"),
        P(None, "dom"),
        P("dom"),
        P("dom"),
        P(None, None, "dom"),
        P("dom"),
        P("dom"),
        P("dom"),
        P("dom"),
        P("dom"),
        P("dom", None),
    )
    return jax.shard_map(
        local, mesh=mesh, in_specs=placed, out_specs=(P(None, "dom"), P()), check_vma=False
    )
```

profile of v0, /device:TPU:8, one launch (start us, length us, event | category | flops | bytes accessed | tf_op | source)
XLA Modules:
  0.0 561.2 jit_solution(4375302517348391218)
XLA Ops:
  3.7 6.2 %gather_fusion.1 = f32[930]{0:T(1024)S(1)} fusion(f32[128]{0:T(128)S(1)} %copy-done.1, s32[1024]{0:T(1024)S(1)} %pad_clamp_fusion.10), kind=kCustom, calls=%fused_computation.6.clone | custom fusion | bytes 11160 | tf_op jit(solution)/shard_map/jit(_take)/gather | solution.py:142
  10.0 6.2 %gather_fusion = f32[930]{0:T(1024)S(1)} fusion(f32[128]{0:T(128)S(1)} %get-tuple-element.158, s32[1024]{0:T(1024)S(1)} %pad_clamp_fusion.10), kind=kCustom, calls=%fused_computation.clone | custom fusion | bytes 11160 | tf_op jit(solution)/shard_map/jit(_take)/gather | solution.py:139
  21.2 5.4 collective-permute-start.1
  31.2 5.7 %collective-permute-start.3 = (f32[2,96]{0,1:T(8,128)}, f32[2,96]{0,1:T(8,128)}, u32[]{:S(2)}, u32[]{:S(2)}) collective-permute-start(f32[2,96]{0,1:T(8,128)} %select_bitcast_fusion.17), channel_id=1, source_target_pairs={{2,0},{3,1},{4,2},{5,3},{6,4},{7,5},{8,6},{9,7},{10,8},{11,9},{12,... | collective-permute-start | bytes 2312 | tf_op jit(solution)/shard_map/ppermute | solution.py:20
  41.0 2.9 gather_fusion.21
  44.3 2.9 gather_fusion.11
  56.8 4.6 collective-permute-start.5
  63.3 4.8 collective-permute-start.7
  72.1 5.7 %collective-permute-start.19 = (f32[32,96]{1,0:T(8,128)S(1)}, f32[32,96]{1,0:T(8,128)S(1)}, u32[]{:S(2)}, u32[]{:S(2)}) collective-permute-start(f32[32,96]{1,0:T(8,128)S(1)} %select_bitcast_fusion.57), channel_id=1, source_target_pairs={{2,0},{3,1},{4,2},{5,3},{6,4},{7,5},{8,6},{9,7},{10,8},{11,9},{12,... | collective-permute-start | bytes 36872 | tf_op jit(solution)/shard_map/ppermute | solution.py:20
  79.8 4.5 collective-permute-start.21
  84.3 5.2 concatenate.193
  89.5 2.9 gather_fusion.10
  95.0 4.8 collective-permute-start.23
  99.8 2.2 collective-permute-start.16
  102.1 4.6 collective-permute-done.16
  107.1 2.9 gather_fusion.30
  111.4 6.3 %scatter_custom_fusion.1 = f32[32,768]{0,1:T(8,128)S(1)} fusion(s32[930]{0:T(1024)} %copy-done.39, f32[930,32]{1,0:T(8,128)S(1)} %copy.312, f32[]{:T(128)} %constant.66.clone.1), kind=kCustom, calls=%fused_computation.145 | custom fusion | flops 29760 | bytes 98816 | tf_op jit(solution)/shard_map/scatter-add | solution.py:175
  120.0 40.1 %psum.28 = f32[]{:T(128)} all-reduce(f32[]{:T(128)} %multiply_reduce_fusion.15), channel_id=1, replica_groups=mesh['dom'=32] {'dom'}, use_global_device_ids=true, to_apply=%region_9.16 | all-reduce | flops 1 | bytes 8 | tf_op jit(solution)/shard_map/psum | solution.py:254
  161.3 2.9 gather_fusion.31
  171.5 3.0 collective-permute-start.25
  174.6 3.1 collective-permute-start.26
  177.8 4.5 collective-permute-start.27
  184.4 4.5 collective-permute-start.29
  191.2 4.8 collective-permute-start.31
  198.2 4.7 collective-permute-done.24
  203.3 2.9 gather_fusion.40
  207.5 6.3 %scatter_custom_fusion.2 = f32[32,768]{0,1:T(8,128)S(1)} fusion(s32[930]{0:T(1024)} %copy-done.39, f32[930,32]{1,0:T(8,128)S(1)} %copy.335, f32[]{:T(128)} %constant.66.clone.1), kind=kCustom, calls=%fused_computation.143 | custom fusion | flops 29760 | bytes 98816 | tf_op jit(solution)/shard_map/scatter-add | solution.py:175
  215.7 39.5 %psum.29 = f32[]{:T(128)} all-reduce(f32[]{:T(128)} %multiply_reduce_fusion.14), channel_id=1, replica_groups=mesh['dom'=32] {'dom'}, use_global_device_ids=true, to_apply=%region_15.22 | all-reduce | flops 1 | bytes 8 | tf_op jit(solution)/shard_map/psum | solution.py:254
  256.4 2.9 gather_fusion.41
  266.5 3.1 collective-permute-start.33
  269.7 3.0 collective-permute-start.34
  272.8 4.6 collective-permute-start.35
  279.5 4.5 collective-permute-start.37
  286.3 4.8 collective-permute-start.39
  291.1 2.1 collective-permute-start.32
  293.4 4.5 collective-permute-done.32
  298.4 2.9 gather_fusion.50
  302.6 6.3 %scatter_custom_fusion.3 = f32[32,768]{0,1:T(8,128)S(1)} fusion(s32[930]{0:T(1024)} %copy-done.39, f32[930,32]{1,0:T(8,128)S(1)} %copy.358, f32[]{:T(128)} %constant.66.clone.1), kind=kCustom, calls=%fused_computation.141 | custom fusion | flops 29760 | bytes 98816 | tf_op jit(solution)/shard_map/scatter-add | solution.py:175
  311.4 39.4 %psum.30 = f32[]{:T(128)} all-reduce(f32[]{:T(128)} %multiply_reduce_fusion.13), channel_id=1, replica_groups=mesh['dom'=32] {'dom'}, use_global_device_ids=true, to_apply=%region_21.28 | all-reduce | flops 1 | bytes 8 | tf_op jit(solution)/shard_map/psum | solution.py:254
  352.0 2.9 gather_fusion.51
  371.6 4.4 collective-permute-start.47
  384.9 3.6 collective-permute-start.44
  390.0 6.1 %collective-permute-start.43 = (f32[32,96]{1,0:T(8,128)S(1)}, f32[32,96]{1,0:T(8,128)S(1)}, u32[]{:S(2)}, u32[]{:S(2)}) collective-permute-start(f32[32,96]{1,0:T(8,128)S(1)} %get-tuple-element.151), channel_id=1, source_target_pairs={{2,0},{3,1},{4,2},{5,3},{6,4},{7,5},{8,6},{9,7},{10,8},{11,9},{12,... | collective-permute-start | bytes 36872 | tf_op jit(solution)/shard_map/ppermute | solution.py:20
  403.0 3.3 collective-permute-start.41
  410.2 3.9 collective-permute-start.14
  414.1 5.0 collective-permute-start.13
  421.9 6.2 %collective-permute-start.11 = (f32[32,96]{1,0:T(8,128)}, f32[32,96]{1,0:T(8,128)}, u32[]{:S(2)}, u32[]{:S(2)}) collective-permute-start(f32[32,96]{1,0:T(8,128)} %get-tuple-element.150), channel_id=1, source_target_pairs={{2,0},{3,1},{4,2},{5,3},{6,4},{7,5},{8,6},{9,7},{10,8},{11,9},{12,... | collective-permute-start | bytes 36872 | tf_op jit(solution)/shard_map/ppermute | solution.py:20
  430.1 4.3 collective-permute-start.9
  434.4 2.1 collective-permute-start.8
  438.5 2.9 gather_fusion.60
  442.9 2.9 gather_fusion.20
  447.8 6.3 %scatter_custom_fusion = f32[32,768]{0,1:T(8,128)S(1)} fusion(s32[930]{0:T(1024)} %copy-done.39, f32[930,32]{1,0:T(8,128)S(1)} %copy.289, f32[]{:T(128)} %constant.66.clone.1), kind=kCustom, calls=%fused_computation.147 | custom fusion | flops 29760 | bytes 98816 | tf_op jit(solution)/shard_map/scatter-add | solution.py:175
  455.1 6.3 %scatter_custom_fusion.4 = f32[32,768]{0,1:T(8,128)S(1)} fusion(s32[930]{0:T(1024)} %copy-done.39, f32[930,32]{1,0:T(8,128)S(1)} %copy.381, f32[]{:T(128)} %constant.66.clone.1), kind=kCustom, calls=%fused_computation.139 | custom fusion | flops 29760 | bytes 98816 | tf_op jit(solution)/shard_map/scatter-add | solution.py:175
  463.9 39.3 %psum.31 = f32[]{:T(128)} all-reduce(f32[]{:T(128)} %multiply_reduce_fusion.12), channel_id=1, replica_groups=mesh['dom'=32] {'dom'}, use_global_device_ids=true, to_apply=%region_27.34 | all-reduce | flops 1 | bytes 8 | tf_op jit(solution)/shard_map/psum | solution.py:254
  504.4 2.9 gather_fusion.61
  514.6 3.5 collective-permute-start.49
  518.2 2.6 collective-permute-start.50
  520.9 5.0 collective-permute-start.51
  528.0 4.5 collective-permute-start.53
  532.9 2.2 collective-permute-start.54
  535.0 4.8 collective-permute-start.55
  542.2 4.5 collective-permute-done.48
  547.2 2.9 gather_fusion.70
  551.4 6.3 %scatter_custom_fusion.5 = f32[32,768]{0,1:T(8,128)S(1)} fusion(s32[930]{0:T(1024)} %copy-done.39, f32[930,32]{1,0:T(8,128)S(1)} %copy.404, f32[]{:T(128)} %constant.66.clone.1), kind=kCustom, calls=%fused_computation.137 | custom fusion | flops 29760 | bytes 98816 | tf_op jit(solution)/shard_map/scatter-add | solution.py:175
  (577 shorter events, 142.3 us)
Async XLA Ops:
  1.7 54.2 %copy-start.28 = (pred[96]{0:T(512)(128)(4,1)}, pred[96]{0:T(512)(128)(4,1)S(1)}, u32[]{:S(2)}) copy-start(pred[96]{0:T(512)(128)(4,1)S(1)} %get-tuple-element.120) | copy-start | bytes 292
  1.7 54.3 %copy-start.25 = (pred[96]{0:T(512)(128)(4,1)}, pred[96]{0:T(512)(128)(4,1)S(1)}, u32[]{:S(2)}) copy-start(pred[96]{0:T(512)(128)(4,1)S(1)} %get-tuple-element.118) | copy-start | bytes 292
  1.7 277.8 %copy-start.23 = (pred[96]{0:T(512)(128)(4,1)}, pred[96]{0:T(512)(128)(4,1)S(1)}, u32[]{:S(2)}) copy-start(pred[96]{0:T(512)(128)(4,1)S(1)} %get-tuple-element.116) | copy-start | bytes 292
  1.7 282.4 %copy-start.21 = (pred[96]{0:T(512)(128)(4,1)}, pred[96]{0:T(512)(128)(4,1)S(1)}, u32[]{:S(2)}) copy-start(pred[96]{0:T(512)(128)(4,1)S(1)} %get-tuple-element.128) | copy-start | bytes 292
  1.7 282.5 %copy-start.19 = (pred[96]{0:T(512)(128)(4,1)}, pred[96]{0:T(512)(128)(4,1)S(1)}, u32[]{:S(2)}) copy-start(pred[96]{0:T(512)(128)(4,1)S(1)} %get-tuple-element.20) | copy-start | bytes 292
  1.7 282.6 %copy-start.16 = (pred[96]{0:T(512)(128)(4,1)}, pred[96]{0:T(512)(128)(4,1)S(1)}, u32[]{:S(2)}) copy-start(pred[96]{0:T(512)(128)(4,1)S(1)} %get-tuple-element.126) | copy-start | bytes 292
  17.9 38.9 %collective-permute-start = (f32[2,96]{0,1:T(8,128)}, f32[2,96]{0,1:T(8,128)}, u32[]{:S(2)}, u32[]{:S(2)}) collective-permute-start(f32[2,96]{0,1:T(8,128)} %select_bitcast_fusion.20), channel_id=1, source_target_pairs={{0,1},{1,2},{2,3},{3,4},{4,5},{5,6},{6,7},{7,8},{8,9},{9,10},{10,1... | collective-permute-start | bytes 2312 | tf_op jit(solution)/shard_map/ppermute | solution.py:20
  21.2 40.2 %collective-permute-start.1 = (f32[2,96]{0,1:T(8,128)}, f32[2,96]{0,1:T(8,128)}, u32[]{:S(2)}, u32[]{:S(2)}) collective-permute-start(f32[2,96]{0,1:T(8,128)} %select_bitcast_fusion.19), channel_id=1, source_target_pairs={{1,0},{2,1},{3,2},{4,3},{5,4},{6,5},{7,6},{8,7},{9,8},{10,9},{11,1... | collective-permute-start | bytes 2312 | tf_op jit(solution)/shard_map/ppermute | solution.py:20
  28.0 35.4 %collective-permute-start.2 = (f32[2,96]{0,1:T(8,128)}, f32[2,96]{0,1:T(8,128)}, u32[]{:S(2)}, u32[]{:S(2)}) collective-permute-start(f32[2,96]{0,1:T(8,128)} %select_bitcast_fusion.18), channel_id=1, source_target_pairs={{0,2},{1,3},{2,4},{3,5},{4,6},{5,7},{6,8},{7,9},{8,10},{9,11},{10,... | collective-permute-start | bytes 2312 | tf_op jit(solution)/shard_map/ppermute | solution.py:20
  31.2 37.0 %collective-permute-start.3 = (f32[2,96]{0,1:T(8,128)}, f32[2,96]{0,1:T(8,128)}, u32[]{:S(2)}, u32[]{:S(2)}) collective-permute-start(f32[2,96]{0,1:T(8,128)} %select_bitcast_fusion.17), channel_id=1, source_target_pairs={{2,0},{3,1},{4,2},{5,3},{6,4},{7,5},{8,6},{9,7},{10,8},{11,9},{12,... | collective-permute-start | bytes 2312 | tf_op jit(solution)/shard_map/ppermute | solution.py:20
  38.3 31.8 %collective-permute-start.4 = (f32[2,96]{0,1:T(8,128)}, f32[2,96]{0,1:T(8,128)}, u32[]{:S(2)}, u32[]{:S(2)}) collective-permute-start(f32[2,96]{0,1:T(8,128)} %select_bitcast_fusion.16), channel_id=1, source_target_pairs={{0,3},{1,4},{2,5},{3,6},{4,7},{5,8},{6,9},{7,10},{8,11},{9,12},{10... | collective-permute-start | bytes 2312 | tf_op jit(solution)/shard_map/ppermute | solution.py:20
  41.0 314.0 %copy-start.13 = (pred[930]{0:T(1024)(128)(4,1)}, pred[930]{0:T(1024)(128)(4,1)S(1)}, u32[]{:S(2)}) copy-start(pred[930]{0:T(1024)(128)(4,1)S(1)} %get-tuple-element.18) | copy-start | bytes 2794
  56.8 244.6 %copy-start.11 = (pred[930]{0:T(1024)(128)(4,1)}, pred[930]{0:T(1024)(128)(4,1)S(1)}, u32[]{:S(2)}) copy-start(pred[930]{0:T(1024)(128)(4,1)S(1)} %compare_and_fusion.1) | copy-start | bytes 2794
  56.8 15.2 %collective-permute-start.5 = (f32[2,96]{0,1:T(8,128)S(1)}, f32[2,96]{0,1:T(8,128)S(1)}, u32[]{:S(2)}, u32[]{:S(2)}) collective-permute-start(f32[2,96]{0,1:T(8,128)S(1)} %select_bitcast_fusion.15), channel_id=1, source_target_pairs={{3,0},{4,1},{5,2},{6,3},{7,4},{8,5},{9,6},{10,7},{11,8},{12,9},{13... | collective-permute-start | bytes 2312 | tf_op jit(solution)/shard_map/ppermute | solution.py:20
  61.4 16.4 %collective-permute-start.6 = (f32[2,96]{0,1:T(8,128)S(1)}, f32[2,96]{0,1:T(8,128)S(1)}, u32[]{:S(2)}, u32[]{:S(2)}) collective-permute-start(f32[2,96]{0,1:T(8,128)S(1)} %select_bitcast_fusion.14), channel_id=1, source_target_pairs={{0,4},{1,5},{2,6},{3,7},{4,8},{5,9},{6,10},{7,11},{8,12},{9,13},{1... | collective-permute-start | bytes 2312 | tf_op jit(solution)/shard_map/ppermute | solution.py:20
  63.3 16.4 %collective-permute-start.7 = (f32[2,96]{0,1:T(8,128)S(1)}, f32[2,96]{0,1:T(8,128)S(1)}, u32[]{:S(2)}, u32[]{:S(2)}) collective-permute-start(f32[2,96]{0,1:T(8,128)S(1)} %select_bitcast_fusion.13), channel_id=1, source_target_pairs={{4,0},{5,1},{6,2},{7,3},{8,4},{9,5},{10,6},{11,7},{12,8},{13,9},{1... | collective-permute-start | bytes 2312 | tf_op jit(solution)/shard_map/ppermute | solution.py:20
  68.2 24.9 %collective-permute-start.17 = (f32[32,96]{1,0:T(8,128)S(1)}, f32[32,96]{1,0:T(8,128)S(1)}, u32[]{:S(2)}, u32[]{:S(2)}) collective-permute-start(f32[32,96]{1,0:T(8,128)S(1)} %select_bitcast_fusion.59), channel_id=1, source_target_pairs={{1,0},{2,1},{3,2},{4,3},{5,4},{6,5},{7,6},{8,7},{9,8},{10,9},{11,1... | collective-permute-start | bytes 36872 | tf_op jit(solution)/shard_map/ppermute | solution.py:20
  70.1 24.9 %collective-permute-start.18 = (f32[32,96]{1,0:T(8,128)S(1)}, f32[32,96]{1,0:T(8,128)S(1)}, u32[]{:S(2)}, u32[]{:S(2)}) collective-permute-start(f32[32,96]{1,0:T(8,128)S(1)} %select_bitcast_fusion.58), channel_id=1, source_target_pairs={{0,2},{1,3},{2,4},{3,5},{4,6},{5,7},{6,8},{7,9},{8,10},{9,11},{10,... | collective-permute-start | bytes 36872 | tf_op jit(solution)/shard_map/ppermute | solution.py:20
  72.1 27.8 %collective-permute-start.19 = (f32[32,96]{1,0:T(8,128)S(1)}, f32[32,96]{1,0:T(8,128)S(1)}, u32[]{:S(2)}, u32[]{:S(2)}) collective-permute-start(f32[32,96]{1,0:T(8,128)S(1)} %select_bitcast_fusion.57), channel_id=1, source_target_pairs={{2,0},{3,1},{4,2},{5,3},{6,4},{7,5},{8,6},{9,7},{10,8},{11,9},{12,... | collective-permute-start | bytes 36872 | tf_op jit(solution)/shard_map/ppermute | solution.py:20
  77.8 24.2 %collective-permute-start.20 = (f32[32,96]{1,0:T(8,128)S(1)}, f32[32,96]{1,0:T(8,128)S(1)}, u32[]{:S(2)}, u32[]{:S(2)}) collective-permute-start(f32[32,96]{1,0:T(8,128)S(1)} %select_bitcast_fusion.56), channel_id=1, source_target_pairs={{0,3},{1,4},{2,5},{3,6},{4,7},{5,8},{6,9},{7,10},{8,11},{9,12},{10... | collective-permute-start | bytes 36872 | tf_op jit(solution)/shard_map/ppermute | solution.py:20
  79.8 22.3 %collective-permute-start.21 = (f32[32,96]{1,0:T(8,128)S(1)}, f32[32,96]{1,0:T(8,128)S(1)}, u32[]{:S(2)}, u32[]{:S(2)}) collective-permute-start(f32[32,96]{1,0:T(8,128)S(1)} %select_bitcast_fusion.55), channel_id=1, source_target_pairs={{3,0},{4,1},{5,2},{6,3},{7,4},{8,5},{9,6},{10,7},{11,8},{12,9},{13... | collective-permute-start | bytes 36872 | tf_op jit(solution)/shard_map/ppermute | solution.py:20
  93.1 9.0 %collective-permute-start.22 = (f32[32,96]{1,0:T(8,128)S(1)}, f32[32,96]{1,0:T(8,128)S(1)}, u32[]{:S(2)}, u32[]{:S(2)}) collective-permute-start(f32[32,96]{1,0:T(8,128)S(1)} %select_bitcast_fusion.54), channel_id=1, source_target_pairs={{0,4},{1,5},{2,6},{3,7},{4,8},{5,9},{6,10},{7,11},{8,12},{9,13},{1... | collective-permute-start | bytes 36872 | tf_op jit(solution)/shard_map/ppermute | solution.py:20
  95.0 7.1 %collective-permute-start.23 = (f32[32,96]{1,0:T(8,128)S(1)}, f32[32,96]{1,0:T(8,128)S(1)}, u32[]{:S(2)}, u32[]{:S(2)}) collective-permute-start(f32[32,96]{1,0:T(8,128)S(1)} %select_bitcast_fusion.53), channel_id=1, source_target_pairs={{4,0},{5,1},{6,2},{7,3},{8,4},{9,5},{10,6},{11,7},{12,8},{13,9},{1... | collective-permute-start | bytes 36872 | tf_op jit(solution)/shard_map/ppermute | solution.py:20
  99.8 6.9 %collective-permute-start.16 = (f32[32,96]{1,0:T(8,128)S(1)}, f32[32,96]{1,0:T(8,128)S(1)}, u32[]{:S(2)}, u32[]{:S(2)}) collective-permute-start(f32[32,96]{1,0:T(8,128)S(1)} %select_bitcast_fusion.60), channel_id=1, source_target_pairs={{0,1},{1,2},{2,3},{3,4},{4,5},{5,6},{6,7},{7,8},{8,9},{9,10},{10,1... | collective-permute-start | bytes 36872 | tf_op jit(solution)/shard_map/ppermute | solution.py:20
  171.5 17.7 %collective-permute-start.25 = (f32[32,96]{1,0:T(8,128)S(1)}, f32[32,96]{1,0:T(8,128)S(1)}, u32[]{:S(2)}, u32[]{:S(2)}) collective-permute-start(f32[32,96]{1,0:T(8,128)S(1)} %select_bitcast_fusion.51), channel_id=1, source_target_pairs={{1,0},{2,1},{3,2},{4,3},{5,4},{6,5},{7,6},{8,7},{9,8},{10,9},{11,1... | collective-permute-start | bytes 36872 | tf_op jit(solution)/shard_map/ppermute | solution.py:20
  174.6 16.6 %collective-permute-start.26 = (f32[32,96]{1,0:T(8,128)S(1)}, f32[32,96]{1,0:T(8,128)S(1)}, u32[]{:S(2)}, u32[]{:S(2)}) collective-permute-start(f32[32,96]{1,0:T(8,128)S(1)} %select_bitcast_fusion.50), channel_id=1, source_target_pairs={{0,2},{1,3},{2,4},{3,5},{4,6},{5,7},{6,8},{7,9},{8,10},{9,11},{10,... | collective-permute-start | bytes 36872 | tf_op jit(solution)/shard_map/ppermute | solution.py:20
  177.8 18.2 %collective-permute-start.27 = (f32[32,96]{1,0:T(8,128)S(1)}, f32[32,96]{1,0:T(8,128)S(1)}, u32[]{:S(2)}, u32[]{:S(2)}) collective-permute-start(f32[32,96]{1,0:T(8,128)S(1)} %select_bitcast_fusion.49), channel_id=1, source_target_pairs={{2,0},{3,1},{4,2},{5,3},{6,4},{7,5},{8,6},{9,7},{10,8},{11,9},{12,... | collective-permute-start | bytes 36872 | tf_op jit(solution)/shard_map/ppermute | solution.py:20
  182.4 15.7 %collective-permute-start.28 = (f32[32,96]{1,0:T(8,128)S(1)}, f32[32,96]{1,0:T(8,128)S(1)}, u32[]{:S(2)}, u32[]{:S(2)}) collective-permute-start(f32[32,96]{1,0:T(8,128)S(1)} %select_bitcast_fusion.48), channel_id=1, source_target_pairs={{0,3},{1,4},{2,5},{3,6},{4,7},{5,8},{6,9},{7,10},{8,11},{9,12},{10... | collective-permute-start | bytes 36872 | tf_op jit(solution)/shard_map/ppermute | solution.py:20
  184.4 13.7 %collective-permute-start.29 = (f32[32,96]{1,0:T(8,128)S(1)}, f32[32,96]{1,0:T(8,128)S(1)}, u32[]{:S(2)}, u32[]{:S(2)}) collective-permute-start(f32[32,96]{1,0:T(8,128)S(1)} %select_bitcast_fusion.47), channel_id=1, source_target_pairs={{3,0},{4,1},{5,2},{6,3},{7,4},{8,5},{9,6},{10,7},{11,8},{12,9},{13... | collective-permute-start | bytes 36872 | tf_op jit(solution)/shard_map/ppermute | solution.py:20
  189.2 8.9 %collective-permute-start.30 = (f32[32,96]{1,0:T(8,128)S(1)}, f32[32,96]{1,0:T(8,128)S(1)}, u32[]{:S(2)}, u32[]{:S(2)}) collective-permute-start(f32[32,96]{1,0:T(8,128)S(1)} %select_bitcast_fusion.46), channel_id=1, source_target_pairs={{0,4},{1,5},{2,6},{3,7},{4,8},{5,9},{6,10},{7,11},{8,12},{9,13},{1... | collective-permute-start | bytes 36872 | tf_op jit(solution)/shard_map/ppermute | solution.py:20
  191.2 7.0 %collective-permute-start.31 = (f32[32,96]{1,0:T(8,128)S(1)}, f32[32,96]{1,0:T(8,128)S(1)}, u32[]{:S(2)}, u32[]{:S(2)}) collective-permute-start(f32[32,96]{1,0:T(8,128)S(1)} %select_bitcast_fusion.45), channel_id=1, source_target_pairs={{4,0},{5,1},{6,2},{7,3},{8,4},{9,5},{10,6},{11,7},{12,8},{13,9},{1... | collective-permute-start | bytes 36872 | tf_op jit(solution)/shard_map/ppermute | solution.py:20
  196.0 6.9 %collective-permute-start.24 = (f32[32,96]{1,0:T(8,128)S(1)}, f32[32,96]{1,0:T(8,128)S(1)}, u32[]{:S(2)}, u32[]{:S(2)}) collective-permute-start(f32[32,96]{1,0:T(8,128)S(1)} %select_bitcast_fusion.52), channel_id=1, source_target_pairs={{0,1},{1,2},{2,3},{3,4},{4,5},{5,6},{6,7},{7,8},{8,9},{9,10},{10,1... | collective-permute-start | bytes 36872 | tf_op jit(solution)/shard_map/ppermute | solution.py:20
  266.5 17.8 %collective-permute-start.33 = (f32[32,96]{1,0:T(8,128)S(1)}, f32[32,96]{1,0:T(8,128)S(1)}, u32[]{:S(2)}, u32[]{:S(2)}) collective-permute-start(f32[32,96]{1,0:T(8,128)S(1)} %select_bitcast_fusion.43), channel_id=1, source_target_pairs={{1,0},{2,1},{3,2},{4,3},{5,4},{6,5},{7,6},{8,7},{9,8},{10,9},{11,1... | collective-permute-start | bytes 36872 | tf_op jit(solution)/shard_map/ppermute | solution.py:20
  269.7 16.6 %collective-permute-start.34 = (f32[32,96]{1,0:T(8,128)S(1)}, f32[32,96]{1,0:T(8,128)S(1)}, u32[]{:S(2)}, u32[]{:S(2)}) collective-permute-start(f32[32,96]{1,0:T(8,128)S(1)} %select_bitcast_fusion.42), channel_id=1, source_target_pairs={{0,2},{1,3},{2,4},{3,5},{4,6},{5,7},{6,8},{7,9},{8,10},{9,11},{10,... | collective-permute-start | bytes 36872 | tf_op jit(solution)/shard_map/ppermute | solution.py:20
  272.8 18.3 %collective-permute-start.35 = (f32[32,96]{1,0:T(8,128)S(1)}, f32[32,96]{1,0:T(8,128)S(1)}, u32[]{:S(2)}, u32[]{:S(2)}) collective-permute-start(f32[32,96]{1,0:T(8,128)S(1)} %select_bitcast_fusion.41), channel_id=1, source_target_pairs={{2,0},{3,1},{4,2},{5,3},{6,4},{7,5},{8,6},{9,7},{10,8},{11,9},{12,... | collective-permute-start | bytes 36872 | tf_op jit(solution)/shard_map/ppermute | solution.py:20
  277.5 15.9 %collective-permute-start.36 = (f32[32,96]{1,0:T(8,128)S(1)}, f32[32,96]{1,0:T(8,128)S(1)}, u32[]{:S(2)}, u32[]{:S(2)}) collective-permute-start(f32[32,96]{1,0:T(8,128)S(1)} %select_bitcast_fusion.40), channel_id=1, source_target_pairs={{0,3},{1,4},{2,5},{3,6},{4,7},{5,8},{6,9},{7,10},{8,11},{9,12},{10... | collective-permute-start | bytes 36872 | tf_op jit(solution)/shard_map/ppermute | solution.py:20
  279.5 13.9 %collective-permute-start.37 = (f32[32,96]{1,0:T(8,128)S(1)}, f32[32,96]{1,0:T(8,128)S(1)}, u32[]{:S(2)}, u32[]{:S(2)}) collective-permute-start(f32[32,96]{1,0:T(8,128)S(1)} %select_bitcast_fusion.39), channel_id=1, source_target_pairs={{3,0},{4,1},{5,2},{6,3},{7,4},{8,5},{9,6},{10,7},{11,8},{12,9},{13... | collective-permute-start | bytes 36872 | tf_op jit(solution)/shard_map/ppermute | solution.py:20
  284.3 9.1 %collective-permute-start.38 = (f32[32,96]{1,0:T(8,128)S(1)}, f32[32,96]{1,0:T(8,128)S(1)}, u32[]{:S(2)}, u32[]{:S(2)}) collective-permute-start(f32[32,96]{1,0:T(8,128)S(1)} %select_bitcast_fusion.38), channel_id=1, source_target_pairs={{0,4},{1,5},{2,6},{3,7},{4,8},{5,9},{6,10},{7,11},{8,12},{9,13},{1... | collective-permute-start | bytes 36872 | tf_op jit(solution)/shard_map/ppermute | solution.py:20
  286.3 7.2 %collective-permute-start.39 = (f32[32,96]{1,0:T(8,128)S(1)}, f32[32,96]{1,0:T(8,128)S(1)}, u32[]{:S(2)}, u32[]{:S(2)}) collective-permute-start(f32[32,96]{1,0:T(8,128)S(1)} %select_bitcast_fusion.37), channel_id=1, source_target_pairs={{4,0},{5,1},{6,2},{7,3},{8,4},{9,5},{10,6},{11,7},{12,8},{13,9},{1... | collective-permute-start | bytes 36872 | tf_op jit(solution)/shard_map/ppermute | solution.py:20
  291.1 6.9 %collective-permute-start.32 = (f32[32,96]{1,0:T(8,128)S(1)}, f32[32,96]{1,0:T(8,128)S(1)}, u32[]{:S(2)}, u32[]{:S(2)}) collective-permute-start(f32[32,96]{1,0:T(8,128)S(1)} %select_bitcast_fusion.44), channel_id=1, source_target_pairs={{0,1},{1,2},{2,3},{3,4},{4,5},{5,6},{6,7},{7,8},{8,9},{9,10},{10,1... | collective-permute-start | bytes 36872 | tf_op jit(solution)/shard_map/ppermute | solution.py:20
  371.6 28.8 %collective-permute-start.47 = (f32[32,96]{1,0:T(8,128)}, f32[32,96]{1,0:T(8,128)}, u32[]{:S(2)}, u32[]{:S(2)}) collective-permute-start(f32[32,96]{1,0:T(8,128)} %get-tuple-element.143), channel_id=1, source_target_pairs={{4,0},{5,1},{6,2},{7,3},{8,4},{9,5},{10,6},{11,7},{12,8},{13,9},{1... | collective-permute-start | bytes 36872 | tf_op jit(solution)/shard_map/ppermute | solution.py:20
  378.2 24.8 %collective-permute-start.46 = (f32[32,96]{1,0:T(8,128)}, f32[32,96]{1,0:T(8,128)}, u32[]{:S(2)}, u32[]{:S(2)}) collective-permute-start(f32[32,96]{1,0:T(8,128)} %get-tuple-element.145), channel_id=1, source_target_pairs={{0,4},{1,5},{2,6},{3,7},{4,8},{5,9},{6,10},{7,11},{8,12},{9,13},{1... | collective-permute-start | bytes 36872 | tf_op jit(solution)/shard_map/ppermute | solution.py:20
  381.6 24.8 %collective-permute-start.45 = (f32[32,96]{1,0:T(8,128)S(1)}, f32[32,96]{1,0:T(8,128)S(1)}, u32[]{:S(2)}, u32[]{:S(2)}) collective-permute-start(f32[32,96]{1,0:T(8,128)S(1)} %get-tuple-element.147), channel_id=1, source_target_pairs={{3,0},{4,1},{5,2},{6,3},{7,4},{8,5},{9,6},{10,7},{11,8},{12,9},{13... | collective-permute-start | bytes 36872 | tf_op jit(solution)/shard_map/ppermute | solution.py:20
  384.9 23.3 %collective-permute-start.44 = (f32[32,96]{1,0:T(8,128)S(1)}, f32[32,96]{1,0:T(8,128)S(1)}, u32[]{:S(2)}, u32[]{:S(2)}) collective-permute-start(f32[32,96]{1,0:T(8,128)S(1)} %get-tuple-element.149), channel_id=1, source_target_pairs={{0,3},{1,4},{2,5},{3,6},{4,7},{5,8},{6,9},{7,10},{8,11},{9,12},{10... | collective-permute-start | bytes 36872 | tf_op jit(solution)/shard_map/ppermute | solution.py:20
  390.0 20.2 %collective-permute-start.43 = (f32[32,96]{1,0:T(8,128)S(1)}, f32[32,96]{1,0:T(8,128)S(1)}, u32[]{:S(2)}, u32[]{:S(2)}) collective-permute-start(f32[32,96]{1,0:T(8,128)S(1)} %get-tuple-element.151), channel_id=1, source_target_pairs={{2,0},{3,1},{4,2},{5,3},{6,4},{7,5},{8,6},{9,7},{10,8},{11,9},{12,... | collective-permute-start | bytes 36872 | tf_op jit(solution)/shard_map/ppermute | solution.py:20
  400.5 13.7 %collective-permute-start.42 = (f32[32,96]{1,0:T(8,128)S(1)}, f32[32,96]{1,0:T(8,128)S(1)}, u32[]{:S(2)}, u32[]{:S(2)}) collective-permute-start(f32[32,96]{1,0:T(8,128)S(1)} %get-tuple-element.153), channel_id=1, source_target_pairs={{0,2},{1,3},{2,4},{3,5},{4,6},{5,7},{6,8},{7,9},{8,10},{9,11},{10,... | collective-permute-start | bytes 36872 | tf_op jit(solution)/shard_map/ppermute | solution.py:20
  403.0 16.9 %collective-permute-start.41 = (f32[32,96]{1,0:T(8,128)S(1)}, f32[32,96]{1,0:T(8,128)S(1)}, u32[]{:S(2)}, u32[]{:S(2)}) collective-permute-start(f32[32,96]{1,0:T(8,128)S(1)} %get-tuple-element.155), channel_id=1, source_target_pairs={{1,0},{2,1},{3,2},{4,3},{5,4},{6,5},{7,6},{8,7},{9,8},{10,9},{11,1... | collective-permute-start | bytes 36872 | tf_op jit(solution)/shard_map/ppermute | solution.py:20
  406.3 15.6 %collective-permute-start.40 = (f32[32,96]{1,0:T(8,128)S(1)}, f32[32,96]{1,0:T(8,128)S(1)}, u32[]{:S(2)}, u32[]{:S(2)}) collective-permute-start(f32[32,96]{1,0:T(8,128)S(1)} %get-tuple-element.157), channel_id=1, source_target_pairs={{0,1},{1,2},{2,3},{3,4},{4,5},{5,6},{6,7},{7,8},{8,9},{9,10},{10,1... | collective-permute-start | bytes 36872 | tf_op jit(solution)/shard_map/ppermute | solution.py:20
  408.3 19.9 %collective-permute-start.15 = (f32[32,96]{1,0:T(8,128)}, f32[32,96]{1,0:T(8,128)S(1)}, u32[]{:S(2)}, u32[]{:S(2)}) collective-permute-start(f32[32,96]{1,0:T(8,128)} %get-tuple-element.142), channel_id=1, source_target_pairs={{4,0},{5,1},{6,2},{7,3},{8,4},{9,5},{10,6},{11,7},{12,8},{13,9},{1... | collective-permute-start | bytes 36872 | tf_op jit(solution)/shard_map/ppermute | solution.py:20
  410.2 19.9 %collective-permute-start.14 = (f32[32,96]{1,0:T(8,128)}, f32[32,96]{1,0:T(8,128)S(1)}, u32[]{:S(2)}, u32[]{:S(2)}) collective-permute-start(f32[32,96]{1,0:T(8,128)} %get-tuple-element.144), channel_id=1, source_target_pairs={{0,4},{1,5},{2,6},{3,7},{4,8},{5,9},{6,10},{7,11},{8,12},{9,13},{1... | collective-permute-start | bytes 36872 | tf_op jit(solution)/shard_map/ppermute | solution.py:20
  414.1 20.2 %collective-permute-start.13 = (f32[32,96]{1,0:T(8,128)}, f32[32,96]{1,0:T(8,128)S(1)}, u32[]{:S(2)}, u32[]{:S(2)}) collective-permute-start(f32[32,96]{1,0:T(8,128)} %get-tuple-element.146), channel_id=1, source_target_pairs={{3,0},{4,1},{5,2},{6,3},{7,4},{8,5},{9,6},{10,7},{11,8},{12,9},{13... | collective-permute-start | bytes 36872 | tf_op jit(solution)/shard_map/ppermute | solution.py:20
  420.0 21.6 %collective-permute-start.12 = (f32[32,96]{1,0:T(8,128)}, f32[32,96]{1,0:T(8,128)}, u32[]{:S(2)}, u32[]{:S(2)}) collective-permute-start(f32[32,96]{1,0:T(8,128)} %get-tuple-element.148), channel_id=1, source_target_pairs={{0,3},{1,4},{2,5},{3,6},{4,7},{5,8},{6,9},{7,10},{8,11},{9,12},{10... | collective-permute-start | bytes 36872 | tf_op jit(solution)/shard_map/ppermute | solution.py:20
  421.9 19.7 %collective-permute-start.11 = (f32[32,96]{1,0:T(8,128)}, f32[32,96]{1,0:T(8,128)}, u32[]{:S(2)}, u32[]{:S(2)}) collective-permute-start(f32[32,96]{1,0:T(8,128)} %get-tuple-element.150), channel_id=1, source_target_pairs={{2,0},{3,1},{4,2},{5,3},{6,4},{7,5},{8,6},{9,7},{10,8},{11,9},{12,... | collective-permute-start | bytes 36872 | tf_op jit(solution)/shard_map/ppermute | solution.py:20
  428.1 13.5 %collective-permute-start.10 = (f32[32,96]{1,0:T(8,128)}, f32[32,96]{1,0:T(8,128)}, u32[]{:S(2)}, u32[]{:S(2)}) collective-permute-start(f32[32,96]{1,0:T(8,128)} %get-tuple-element.152), channel_id=1, source_target_pairs={{0,2},{1,3},{2,4},{3,5},{4,6},{5,7},{6,8},{7,9},{8,10},{9,11},{10,... | collective-permute-start | bytes 36872 | tf_op jit(solution)/shard_map/ppermute | solution.py:20
  430.1 11.5 %collective-permute-start.9 = (f32[32,96]{1,0:T(8,128)}, f32[32,96]{1,0:T(8,128)}, u32[]{:S(2)}, u32[]{:S(2)}) collective-permute-start(f32[32,96]{1,0:T(8,128)} %get-tuple-element.154), channel_id=1, source_target_pairs={{1,0},{2,1},{3,2},{4,3},{5,4},{6,5},{7,6},{8,7},{9,8},{10,9},{11,1... | collective-permute-start | bytes 36872 | tf_op jit(solution)/shard_map/ppermute | solution.py:20
  434.4 7.2 %collective-permute-start.8 = (f32[32,96]{1,0:T(8,128)}, f32[32,96]{1,0:T(8,128)}, u32[]{:S(2)}, u32[]{:S(2)}) collective-permute-start(f32[32,96]{1,0:T(8,128)} %get-tuple-element.156), channel_id=1, source_target_pairs={{0,1},{1,2},{2,3},{3,4},{4,5},{5,6},{6,7},{7,8},{8,9},{9,10},{10,1... | collective-permute-start | bytes 36872 | tf_op jit(solution)/shard_map/ppermute | solution.py:20
  514.6 18.2 %collective-permute-start.49 = (f32[32,96]{1,0:T(8,128)S(1)}, f32[32,96]{1,0:T(8,128)S(1)}, u32[]{:S(2)}, u32[]{:S(2)}) collective-permute-start(f32[32,96]{1,0:T(8,128)S(1)} %select_bitcast_fusion.27), channel_id=1, source_target_pairs={{1,0},{2,1},{3,2},{4,3},{5,4},{6,5},{7,6},{8,7},{9,8},{10,9},{11,1... | collective-permute-start | bytes 36872 | tf_op jit(solution)/shard_map/ppermute | solution.py:20
  518.2 16.8 %collective-permute-start.50 = (f32[32,96]{1,0:T(8,128)S(1)}, f32[32,96]{1,0:T(8,128)S(1)}, u32[]{:S(2)}, u32[]{:S(2)}) collective-permute-start(f32[32,96]{1,0:T(8,128)S(1)} %select_bitcast_fusion.26), channel_id=1, source_target_pairs={{0,2},{1,3},{2,4},{3,5},{4,6},{5,7},{6,8},{7,9},{8,10},{9,11},{10,... | collective-permute-start | bytes 36872 | tf_op jit(solution)/shard_map/ppermute | solution.py:20
  520.9 19.0 %collective-permute-start.51 = (f32[32,96]{1,0:T(8,128)S(1)}, f32[32,96]{1,0:T(8,128)S(1)}, u32[]{:S(2)}, u32[]{:S(2)}) collective-permute-start(f32[32,96]{1,0:T(8,128)S(1)} %select_bitcast_fusion.25), channel_id=1, source_target_pairs={{2,0},{3,1},{4,2},{5,3},{6,4},{7,5},{8,6},{9,7},{10,8},{11,9},{12,... | collective-permute-start | bytes 36872 | tf_op jit(solution)/shard_map/ppermute | solution.py:20
  526.0 16.2 %collective-permute-start.52 = (f32[32,96]{1,0:T(8,128)S(1)}, f32[32,96]{1,0:T(8,128)S(1)}, u32[]{:S(2)}, u32[]{:S(2)}) collective-permute-start(f32[32,96]{1,0:T(8,128)S(1)} %select_bitcast_fusion.24), channel_id=1, source_target_pairs={{0,3},{1,4},{2,5},{3,6},{4,7},{5,8},{6,9},{7,10},{8,11},{9,12},{10... | collective-permute-start | bytes 36872 | tf_op jit(solution)/shard_map/ppermute | solution.py:20
  528.0 14.2 %collective-permute-start.53 = (f32[32,96]{1,0:T(8,128)S(1)}, f32[32,96]{1,0:T(8,128)S(1)}, u32[]{:S(2)}, u32[]{:S(2)}) collective-permute-start(f32[32,96]{1,0:T(8,128)S(1)} %select_bitcast_fusion.23), channel_id=1, source_target_pairs={{3,0},{4,1},{5,2},{6,3},{7,4},{8,5},{9,6},{10,7},{11,8},{12,9},{13... | collective-permute-start | bytes 36872 | tf_op jit(solution)/shard_map/ppermute | solution.py:20
  532.9 9.3 %collective-permute-start.54 = (f32[32,96]{1,0:T(8,128)S(1)}, f32[32,96]{1,0:T(8,128)S(1)}, u32[]{:S(2)}, u32[]{:S(2)}) collective-permute-start(f32[32,96]{1,0:T(8,128)S(1)} %select_bitcast_fusion.22), channel_id=1, source_target_pairs={{0,4},{1,5},{2,6},{3,7},{4,8},{5,9},{6,10},{7,11},{8,12},{9,13},{1... | collective-permute-start | bytes 36872 | tf_op jit(solution)/shard_map/ppermute | solution.py:20
  535.0 7.2 %collective-permute-start.55 = (f32[32,96]{1,0:T(8,128)S(1)}, f32[32,96]{1,0:T(8,128)S(1)}, u32[]{:S(2)}, u32[]{:S(2)}) collective-permute-start(f32[32,96]{1,0:T(8,128)S(1)} %select_bitcast_fusion.21), channel_id=1, source_target_pairs={{4,0},{5,1},{6,2},{7,3},{8,4},{9,5},{10,6},{11,7},{12,8},{13,9},{1... | collective-permute-start | bytes 36872 | tf_op jit(solution)/shard_map/ppermute | solution.py:20
  539.9 6.9 %collective-permute-start.48 = (f32[32,96]{1,0:T(8,128)S(1)}, f32[32,96]{1,0:T(8,128)S(1)}, u32[]{:S(2)}, u32[]{:S(2)}) collective-permute-start(f32[32,96]{1,0:T(8,128)S(1)} %select_bitcast_fusion.28), channel_id=1, source_target_pairs={{0,1},{1,2},{2,3},{3,4},{4,5},{5,6},{6,7},{7,8},{8,9},{9,10},{10,1... | collective-permute-start | bytes 36872 | tf_op jit(solution)/shard_map/ppermute | solution.py:20
  (50 other events, 750.0 us)
where the time goes:
time: 572 us; the launch traced here: 561 us
  starting transfers between devices  184 us (32%)
  blocking collectives  158 us (28%)
  local copies, waits for them, and re-layouts  117 us (20%)
  other arithmetic  62 us (11%)
  waiting for transfers between devices  18.5 us (3%)
  matrix products  13.8 us (2%)
  between operations  8.25 us (1%)
    ppermute x56, starting transfers between devices, passed_along(): return lax.ppermute(array, axis, pairs)  184 us
    psum x4, blocking collectives, local(): total = lax.psum(jnp.sum(image * image), 'dom')  158 us
    gather x96, local copies, waits for them, and re-layouts, operate(): jnp.take(padded_values, listed, axis=1)  41.8 us
    scatter-add x6, other arithmetic, apply_operator_local(): jnp.zeros((32, 6 * elem_count), jnp.float32).at[:, columns].add(face_flux)  37.5 us
    ppermute x56, waiting for transfers between devices, passed_along(): return lax.ppermute(array, axis, pairs)  18.5 us
    gather x12, local copies, waits for them, and re-layouts, mortar_traces(): picked = jnp.take(face_values, columns, axis=1)  18.2 us
    gather x12, local copies, waits for them, and re-layouts, operate(): outer_values = jnp.take(table_values, partner, axis=1)  18.2 us
  transfers between devices with their start and end apart: 56, of which 4 were waited for; matrix products, arithmetic and copies ran while one was open for 9% of the time, Pallas kernels for 0%

commit v1 on v0

v1 whole, which is shorter than its diff:
```python
import functools
import math

import jax
import jax.numpy as jnp
import numpy as np
from jax import lax
from jax.experimental import pallas as pl
from jax.experimental.pallas import tpu as pltpu
from jax.sharding import PartitionSpec as P

f32 = jnp.float32
bf16 = jnp.bfloat16
i32 = jnp.int32
peer_offsets = (1, -1, 2, -2, 3, -3, 4, -4)
live_width = {1: 96, 2: 48, 3: 24, 4: 24}
lanes = 128
side_pad = 1024


def lagrange_tables():
    root_five = 1.0 / math.sqrt(5.0)
    nodes = np.array([0.0, 0.5 - 0.5 * root_five, 0.5 + 0.5 * root_five, 1.0])
    weights = np.array([1.0, 5.0, 5.0, 1.0]) / 12.0
    factor = np.array(
        [np.prod([nodes[i] - nodes[j] for j in range(4) if j != i]) for i in range(4)]
    )
    derivative = np.zeros((4, 4))
    for i in range(4):
        for j in range(4):
            if i != j:
                derivative[i, j] = factor[i] / (factor[j] * (nodes[i] - nodes[j]))
        derivative[i, i] = -np.sum(derivative[i])
    halves = []
    for half in range(2):
        points = 0.5 * (nodes + half)
        table = np.ones((4, 4))
        for j in range(4):
            for other in range(4):
                if other != j:
                    table[:, j] *= (points - nodes[other]) / (nodes[j] - nodes[other])
        halves.append(table)
    return weights, derivative, halves


def basis_tables():
    weights, derivative, halves = lagrange_tables()
    mass = np.diag(weights)
    line = derivative.T @ mass @ derivative
    stiffness = (
        np.kron(np.kron(line, mass), mass)
        + np.kron(np.kron(mass, line), mass)
        + np.kron(np.kron(mass, mass), line)
    )
    trace = np.zeros((6, 32, 64))
    for dim in range(3):
        others = [d for d in range(3) if d != dim]
        for lower in range(2):
            face = 2 * dim + lower
            fixed = 0 if lower else 3
            sign = -1.0 if lower else 1.0
            for first in range(4):
                for second in range(4):
                    node = first * 4 + second
                    for along in range(4):
                        place = [0, 0, 0]
                        place[others[0]] = first
                        place[others[1]] = second
                        place[dim] = along
                        nodal = place[0] * 16 + place[1] * 4 + place[2]
                        if along == fixed:
                            trace[face, node, nodal] = 1.0
                        trace[face, 16 + node, nodal] = sign * derivative[fixed, along]
    quarter = [np.kron(halves[q // 2], halves[q % 2]) for q in range(4)]
    both = np.eye(2)
    interp = np.concatenate([np.kron(both, q) for q in quarter], axis=0)
    interp_t = np.concatenate([np.kron(both, q.T) for q in quarter], axis=0)
    face_weight = np.kron(weights, weights)
    return stiffness, trace.reshape(192, 64), interp, interp_t, face_weight


def stacked(table):
    table = np.asarray(table, np.float32)
    high = table.astype(jnp.bfloat16)
    low = (table - high.astype(np.float32)).astype(jnp.bfloat16)
    return np.concatenate([high, high, low], axis=1)


def const_tables():
    stiffness, trace, interp, interp_t, face_weight = basis_tables()
    lift = np.concatenate([stacked(trace.T), stacked(stiffness)], axis=1)
    weight = np.broadcast_to(np.concatenate([face_weight, face_weight])[:, None], (32, lanes))
    return (
        stacked(trace),
        stacked(interp),
        stacked(interp_t),
        lift,
        np.asarray(weight, np.float32),
    )


def two(x):
    high = x.astype(bf16)
    return high, (x - high.astype(f32)).astype(bf16)


def three(x):
    high = x.astype(bf16)
    rest = x - high.astype(f32)
    mid = rest.astype(bf16)
    return high, mid, (rest - mid.astype(f32)).astype(bf16)


def dot(a, b):
    return jnp.dot(a, b, preferred_element_type=f32)


def dot_t(a, b):
    return lax.dot_general(a, b, (((1,), (1,)), ((), ())), preferred_element_type=f32)


def cat(parts, axis):
    return parts[0] if len(parts) == 1 else jnp.concatenate(parts, axis=axis)


def table_dot(table, x):
    high, low = two(x)
    return dot(table, jnp.concatenate([high, low, high], axis=0))


def apply_case(table, x, case):
    quarters = table_dot(table, x)
    out = x
    for c in range(4):
        out = jnp.where(case == c, quarters[32 * c : 32 * c + 32], out)
    return out


def fields_case(table, x, case, nf):
    wide = cat([x[32 * k : 32 * k + 32] for k in range(nf)], 1)
    out = apply_case(table, wide, cat([case] * nf, 1))
    n = x.shape[1]
    return cat([out[:, n * k : n * k + n] for k in range(nf)], 0)


def one_hot(index_row, rows, first=0):
    place = lax.broadcasted_iota(i32, (rows, index_row.shape[1]), 0) + first
    return jnp.where(place == index_row, 1.0, 0.0).astype(bf16)


def element_rows(coef_ref, level_ref):
    coef = coef_ref[...]
    level = level_ref[...]
    size = jnp.where(level == 0, 1.0, jnp.where(level == 1, 0.5, 0.25)).astype(f32)
    inverse = jnp.where(level == 0, 1.0, jnp.where(level == 1, 2.0, 4.0)).astype(f32)
    return coef, size, coef * size, coef * inverse


def face_stack(trace_ref, u, normal_scale, nf):
    faces = table_dot(trace_ref[...], cat(u, 1))
    row = lax.broadcasted_iota(i32, (32, lanes), 0)
    scale = jnp.where(row < 16, 1.0, jnp.broadcast_to(normal_scale, (32, lanes)))
    fields = []
    for k in range(nf):
        part = faces[:, lanes * k : lanes * k + lanes]
        fields.append(
            jnp.concatenate([part[32 * f : 32 * f + 32] * scale for f in range(6)], axis=1)
        )
    high, low = two(cat(fields, 0))
    return jnp.concatenate([high, low], axis=0)


def gather_message(stack, hot, interp, case, nf):
    got = dot(stack, hot)
    h = 32 * nf
    out = fields_case(interp, got[:h] + got[h : 2 * h], case, nf)
    if stack.shape[0] == 2 * h:
        return out
    coef = got[2 * h : 2 * h + 1] + got[2 * h + 1 : 2 * h + 2] + got[2 * h + 2 : 2 * h + 3]
    size = got[2 * h + 3 : 2 * h + 4] * jnp.where((case >= 0) & (case < 4), 0.5, 1.0)
    row = lax.broadcasted_iota(i32, (8, out.shape[1]), 0)
    scalars = jnp.where(row == 0, coef, jnp.where(row == 1, size, 0.0))
    return jnp.concatenate([out, scalars], axis=0)


def where_am_i(chips):
    me = lax.axis_index("dom")
    chip = me // 2
    core = me - 2 * chip
    quad = lax.rem(chip, 4)
    odd = lax.rem(chip, 2)
    v_step = jnp.where(quad < 2, -1, 1)
    v_there = (chip + 2 * v_step >= 0) & (chip + 2 * v_step < chips)
    return chip, core, odd, -v_step, v_step, v_there


def row_of(offset):
    size = jnp.abs(offset)
    return 2 * (size - 1) + jnp.where(offset < 0, 1, 0)


def narrow(offset):
    return jnp.abs(offset) == 3


def send_setup_kernel(
    chips, start_ref, guess_ref, coef_ref, level_ref, side_ref, list_ref, trace_ref, interp_ref,
    hot_ref, case_ref, stack_ref, u_ref, v_ref, rolled_ref, slot_ref,
):
    chip, core, odd, u_step, v_step, v_there = where_am_i(chips)
    listed = jnp.concatenate([list_ref[...], jnp.full((8, 32), -1, i32)], axis=1)
    for place, shift in enumerate((0, 24, 48, 96)):
        rolled_ref[8 * place : 8 * place + 8] = (
            pltpu.roll(listed, shift, 1) if shift else listed
        )
    lane = lax.broadcasted_iota(i32, (1, lanes), 1)
    none = jnp.full((1, lanes), -1, i32)

    def part(place, row, low, high, valid):
        values = rolled_ref[pl.ds(8 * place + row, 1), :]
        keep = (lane >= low) & (lane < high) & valid
        return jnp.where(keep, values, none)

    always = core >= 0
    for tile, (step, there, place) in enumerate(((u_step, always, 0), (v_step, v_there, 1))):
        onward = there & (((odd == 1) & (step == 1)) | ((odd == 0) & (step == -1)))
        cross = 2 * step + 1 - 2 * core
        wide = part(1, row_of(cross), 24, 120, onward & (~narrow(cross)))
        slim = part(3, row_of(cross), 96, 120, onward & narrow(cross))
        slot_ref[0:1, 256 * tile : 256 * tile + 128] = jnp.maximum(wide, slim)
        over = there & (step == 2 * core - 1)
        direct = part(place, row_of(4 * step), 24 * place, 24 * place + 24, there)
        second = part(2, row_of(2 * step), 48, 96, onward)
        third = part(3, row_of(3 * step), 96, 120, over)
        slot_ref[0:1, 256 * tile + 128 : 256 * tile + 256] = jnp.maximum(
            jnp.maximum(direct, second), third
        )
    near = jnp.where(odd == 1, -1, 1)
    cross = 2 * near + 1 - 2 * core
    slot_ref[0:1, 512:640] = part(0, row_of(1 - 2 * core), 0, 96, always)
    slot_ref[0:1, 640:768] = part(0, row_of(2 * near), 0, 48, always)
    slot_ref[0:1, 768:896] = jnp.maximum(
        part(0, row_of(cross), 0, 96, ~narrow(cross)), part(0, row_of(cross), 0, 24, narrow(cross))
    )

    elem, direction, case = side_ref[0:1], side_ref[1:2], side_ref[2:3]
    live = lax.broadcasted_iota(i32, (1, side_pad), 1) < 930
    rows = [jnp.where(live, r, 0).astype(f32) for r in (elem, direction, case)]
    rows.append(jnp.where(live, 1.0, 0.0))
    row = lax.broadcasted_iota(i32, (16, side_pad), 0)
    attributes = jnp.zeros((16, side_pad), f32)
    for k, r in enumerate(rows):
        attributes = jnp.where(row == k, r, attributes)
    found = dot(attributes.astype(bf16), one_hot(slot_ref[0:1, :], side_pad))
    valid = found[3:4] > 0.5
    column = jnp.where(valid, (found[1:2] * 128.0 + found[0:1]).astype(i32), -1)
    slot_case = jnp.where(valid, found[2:3].astype(i32), -1)
    case_ref[0:1, :] = slot_case
    for f in range(6):
        hot_ref[lanes * f : lanes * f + lanes] = one_hot(column, lanes, lanes * f)

    coef, size, volume_scale, normal_scale = element_rows(coef_ref, level_ref)
    stack = face_stack(trace_ref, [start_ref[...], guess_ref[...]], normal_scale, 2)
    high, mid, low = (jnp.broadcast_to(x.astype(f32), (16, lanes)) for x in three(coef))
    row = lax.broadcasted_iota(i32, (16, lanes), 0)
    scalars = jnp.where(
        row == 0,
        high,
        jnp.where(row == 1, mid, jnp.where(row == 2, low, jnp.where(row == 3, size, 0.0))),
    ).astype(bf16)
    stack = jnp.concatenate([stack, jnp.concatenate([scalars] * 6, axis=1)], axis=0)
    stack_ref[...] = stack
    sent = gather_message(stack, hot_ref[:, 0:512], interp_ref[...], slot_case[:, 0:512], 2)
    u_ref[...] = sent[:, 0:256]
    v_ref[...] = sent[:, 256:512]


def own_kernel(nf, stack_ref, hot_ref, case_ref, interp_ref, own_ref):
    own_ref[...] = gather_message(
        stack_ref[...], hot_ref[:, 512:896], interp_ref[...], case_ref[0:1, 512:896], nf
    )


def relay_kernel(own_ref, u_ref, v_ref, one_ref, two_ref, three_ref):
    lane = lax.broadcasted_iota(i32, (1, lanes), 1)
    passed = u_ref[:, 128:256] + v_ref[:, 128:256]
    one_ref[...] = own_ref[:, 0:128] + jnp.where(lane >= 96, passed, 0.0)
    two_ref[...] = own_ref[:, 128:256] + jnp.where((lane >= 48) & (lane < 96), passed, 0.0)
    three_ref[...] = own_ref[:, 256:384] + (u_ref[:, 0:128] + v_ref[:, 0:128])


def setup_kernel(
    chips, coef_ref, level_ref, side_ref,
    own_hot_ref, partner_hot_ref, arrival_hot_ref, target_hot_ref, info_ref, arrived_case_ref,
):
    chip, core, odd, u_step, v_step, v_there = where_am_i(chips)
    elem, direction, case = side_ref[0:1], side_ref[1:2], side_ref[2:3]
    kind, partner = side_ref[3:4], side_ref[4:5]
    live = lax.broadcasted_iota(i32, (1, side_pad), 1) < 930
    column = jnp.where(live, direction * lanes + elem, -1)
    for f in range(6):
        own_hot_ref[lanes * f : lanes * f + lanes] = one_hot(column, lanes, lanes * f)

    coef, size, volume_scale, normal_scale = element_rows(coef_ref, level_ref)
    row = lax.broadcasted_iota(i32, (16, lanes), 0)
    scalars = jnp.zeros((16, lanes), f32)
    for k, r in enumerate([x.astype(f32) for x in three(coef)] + [size]):
        scalars = jnp.where(row == k, r, scalars)
    mine = dot(scalars.astype(bf16), one_hot(jnp.where(live, elem, -1), lanes))
    hanging = (case >= 0) & (case < 4)
    own_coef = mine[0:1] + mine[1:2] + mine[2:3]
    own_size = mine[3:4] * jnp.where(hanging, 0.5, 1.0)

    rows = [jnp.where(live, r, 0).astype(f32) for r in (elem, direction, case)]
    rows.append(jnp.where(live, 1.0, 0.0))
    rows += [mine[0:1], mine[1:2], mine[2:3], own_size]
    row = lax.broadcasted_iota(i32, (16, side_pad), 0)
    attributes = jnp.zeros((16, side_pad), f32)
    for k, r in enumerate(rows):
        attributes = jnp.where(row == k, r, attributes)
    attributes = attributes.astype(bf16)
    other = dot(attributes, one_hot(partner, side_pad))
    valid = other[3:4] > 0.5
    other_column = jnp.where(valid, (other[1:2] * 128.0 + other[0:1]).astype(i32), -1)
    for f in range(6):
        partner_hot_ref[lanes * f : lanes * f + lanes] = one_hot(other_column, lanes, lanes * f)
    boundary = jnp.where(kind == 1, 1.0, 0.0)
    info = [
        own_coef, own_size, other[4:5] + other[5:6] + other[6:7], other[7:8],
        case.astype(f32), other[2:3], boundary, boundary,
    ]
    row = lax.broadcasted_iota(i32, (8, side_pad), 0)
    table = jnp.zeros((8, side_pad), f32)
    for k, r in enumerate(info):
        table = jnp.where(row == k, r, table)
    info_ref[...] = table

    sought = jnp.where(live & (kind == 0), partner, -7)
    place = lax.broadcasted_iota(i32, (lanes, side_pad), 0)
    near = jnp.where(odd == 1, 1, -1)
    back = 1 - 2 * core
    own_cross = 2 * near - back
    far_cross = -2 * near - back
    split = jnp.where(narrow(own_cross), 24, 96)
    segments = (
        ((0, 96, row_of(-back)), (96, 120, row_of(3 * back))),
        ((0, 48, row_of(2 * near)), (48, 96, row_of(-2 * near))),
        ((0, split, row_of(own_cross)), (split, 120, row_of(far_cross))),
        ((0, 24, row_of(-4 * u_step)), (24, 48, row_of(-4 * v_step))),
    )
    for tile, parts in enumerate(segments):
        slot = jnp.full((lanes, side_pad), -5, i32)
        for low, high, peer in parts:
            slot = jnp.where((place >= low) & (place < high), 930 + 96 * peer + place - low, slot)
        arrival_hot_ref[lanes * tile : lanes * tile + lanes] = jnp.where(
            slot == sought, 1.0, 0.0
        ).astype(bf16)
    target = dot_t(attributes, arrival_hot_ref[...])
    valid = target[3:4] > 0.5
    target_column = jnp.where(valid, (target[1:2] * 128.0 + target[0:1]).astype(i32), -1)
    arrived_case_ref[0:1, :] = jnp.where(valid, target[2:3].astype(i32), -1)
    for f in range(6):
        target_hot_ref[lanes * f : lanes * f + lanes] = one_hot(target_column, lanes, lanes * f)


def sides_kernel(nf, stack_ref, own_hot_ref, partner_hot_ref, info_ref, interp_ref, own_ref, other_ref):
    h = 32 * nf
    stack = stack_ref[0 : 2 * h]
    table = interp_ref[...]
    got = dot(stack, own_hot_ref[...])
    own_ref[...] = fields_case(table, got[:h] + got[h:], info_ref[4:5].astype(i32), nf)
    got = dot(stack, partner_hot_ref[...])
    other_ref[...] = fields_case(table, got[:h] + got[h:], info_ref[5:6].astype(i32), nf)


def coef_kernel(one_ref, two_ref, three_ref, u_ref, v_ref, info_ref, arrival_hot_ref, side_coef_ref, arrived_coef_ref):
    scalars = jnp.concatenate(
        [one_ref[64:72], two_ref[64:72], three_ref[64:72], u_ref[64:72, 128:256] + v_ref[64:72, 128:256]],
        axis=1,
    )
    row = lax.broadcasted_iota(i32, (16, 512), 0)
    rows = jnp.zeros((16, 512), f32)
    for k, r in enumerate([x.astype(f32) for x in three(scalars[0:1])] + [scalars[1:2]]):
        rows = jnp.where(row == k, r, rows)
    hot = arrival_hot_ref[...]
    far = dot(rows.astype(bf16), hot)
    other_coef = info_ref[2:3] + far[0:1] + far[1:2] + far[2:3]
    other_size = info_ref[3:4] + far[3:4]
    edge = info_ref[6:7]
    least = jnp.minimum(info_ref[1:2], other_size)
    jump = 16.0 * (info_ref[0:1] + other_coef) * least
    area = least * least
    coefs = [jump, jump * (1.0 - edge), area * (0.5 + 0.5 * edge), area * (0.5 - 0.5 * edge)]
    row = lax.broadcasted_iota(i32, (8, side_pad), 0)
    table = jnp.zeros((8, side_pad), f32)
    for k, r in enumerate(coefs):
        table = jnp.where(row == k, r, table)
    side_coef_ref[...] = table
    row = lax.broadcasted_iota(i32, (16, side_pad), 0)
    rows = jnp.zeros((16, side_pad), f32)
    for k, r in enumerate([x.astype(f32) for x in three(coefs[1]) + three(coefs[3])]):
        rows = jnp.where(row == k, r, rows)
    got = dot_t(rows.astype(bf16), hot)
    row = lax.broadcasted_iota(i32, (8, 512), 0)
    arrived_coef_ref[...] = jnp.where(
        row == 0,
        got[0:1] + got[1:2] + got[2:3],
        jnp.where(row == 1, got[3:4] + got[4:5] + got[5:6], 0.0),
    )


def scatter(x, hot, nf):
    high, low = two(x)
    got = dot_t(jnp.concatenate([high, low], axis=0), hot)
    return got[: 32 * nf] + got[32 * nf :]


def flux_kernel(nf, own_ref, other_ref, coef_ref, info_ref, weight_ref, interp_ref, own_hot_ref, sum_ref):
    jump, jump_out, area, area_out = (coef_ref[k : k + 1] for k in range(4))
    weight = weight_ref[0:16, 0:1]
    flux = []
    for k in range(nf):
        value, slope = own_ref[32 * k : 32 * k + 16], own_ref[32 * k + 16 : 32 * k + 32]
        outer, outer_slope = other_ref[32 * k : 32 * k + 16], other_ref[32 * k + 16 : 32 * k + 32]
        flux.append(
            weight * (jump * value - jump_out * outer - area * slope + area_out * outer_slope)
        )
        flux.append(weight * (area_out * outer - area * value))
    flux = fields_case(interp_ref[...], jnp.concatenate(flux, axis=0), info_ref[4:5].astype(i32), nf)
    sum_ref[...] = scatter(flux, own_hot_ref[...], nf)


def halo_flux(nf, arrivals, coef_ref, case_ref, weight_ref, interp_ref, hot_ref):
    one_ref, two_ref, three_ref, u_ref, v_ref = arrivals
    h = 32 * nf
    got = jnp.concatenate(
        [one_ref[0:h], two_ref[0:h], three_ref[0:h], u_ref[0:h, 128:256] + v_ref[0:h, 128:256]], axis=1
    )
    jump, area = coef_ref[0:1], coef_ref[1:2]
    weight = weight_ref[0:16, 0:1]
    flux = []
    for k in range(nf):
        outer, outer_slope = got[32 * k : 32 * k + 16], got[32 * k + 16 : 32 * k + 32]
        flux.append(weight * (area * outer_slope - jump * outer))
        flux.append(weight * (area * outer))
    flux = fields_case(interp_ref[...], jnp.concatenate(flux, axis=0), case_ref[0:1], nf)
    return scatter(flux, hot_ref[...], nf)


def solve_blocks(inverse_ref, hold_ref, nf):
    sums = [jnp.zeros((64, lanes), f32) for _ in range(nf)]
    for col in range(64):
        block = inverse_ref[col].astype(f32)
        for k in range(nf):
            sums[k] = sums[k] + block * hold_ref[64 * k + col : 64 * k + col + 1, :]
    return sums


def update_kernel(
    nf, nf_next, residual,
    one_ref, two_ref, three_ref, u_in_ref, v_in_ref, local_ref, arrived_coef_ref, arrived_case_ref,
    target_hot_ref, weight_ref, interp_t_ref, lift_ref, field_ref, coef_ref, level_ref, inverse_ref,
    *rest,
):
    if residual:
        rhs_ref, *rest = rest
    if nf_next:
        trace_ref, interp_ref, hot_ref, case_ref, new_ref, stack_ref, u_ref, v_ref, hold_ref = rest
    else:
        new_ref, part_ref, hold_ref = rest
    arrivals = (one_ref, two_ref, three_ref, u_in_ref, v_in_ref)
    total = local_ref[...] + halo_flux(
        nf, arrivals, arrived_coef_ref, arrived_case_ref, weight_ref, interp_t_ref, target_hot_ref
    )
    coef, size, volume_scale, normal_scale = element_rows(coef_ref, level_ref)
    row = lax.broadcasted_iota(i32, (32, lanes), 0)
    scale = jnp.where(row < 16, 1.0, jnp.broadcast_to(normal_scale, (32, lanes)))
    operands = []
    for k in range(nf):
        mine = total[32 * k : 32 * k + 32]
        faces = jnp.concatenate(
            [mine[:, lanes * f : lanes * f + lanes] * scale for f in range(6)], axis=0
        )
        high, low = two(faces)
        field_high, field_low = two(field_ref[64 * k : 64 * k + 64] * volume_scale)
        operands.append(
            jnp.concatenate([high, low, high, field_high, field_low, field_high], axis=0)
        )
    image = dot(lift_ref[...], cat(operands, 1))
    for k in range(nf):
        part = image[:, lanes * k : lanes * k + lanes]
        if residual and k == 1:
            part = rhs_ref[...] - part
        hold_ref[64 * k : 64 * k + 64, :] = part
    new = solve_blocks(inverse_ref, hold_ref, nf)
    for k in range(nf):
        new_ref[64 * k : 64 * k + 64, :] = new[k]
    if nf_next:
        stack = face_stack(trace_ref, new[:nf_next], normal_scale, nf_next)
        stack_ref[...] = stack
        sent = gather_message(stack, hot_ref[:, 0:512], interp_ref[...], case_ref[0:1, 0:512], nf_next)
        u_ref[...] = sent[:, 0:256]
        v_ref[...] = sent[:, 256:512]
    else:
        before, after = field_ref[...], new[0]
        before = jnp.sum(jnp.sum(before * before, axis=1, keepdims=True), axis=0, keepdims=True)
        after = jnp.sum(jnp.sum(after * after, axis=1, keepdims=True), axis=0, keepdims=True)
        lane = lax.broadcasted_iota(i32, part_ref.shape, 1)
        part_ref[...] = jnp.where(lane == 0, before, jnp.where(lane == 1, after, 0.0))


def finish_kernel(part_ref, guess_ref, first_ref, second_ref, out_ref, bound_ref):
    total = jnp.sum(part_ref[...], axis=0, keepdims=True)
    bound = jnp.sqrt(total[:, 1:2] / total[:, 0:1])
    upper = 1.2 * bound
    lower = upper / 15.0
    center = 0.5 * (upper + lower)
    half = 0.5 * (upper - lower)
    ratio = center / half
    damping = 1.0 / ratio
    damping_next = 1.0 / (2.0 * ratio - damping)
    first = first_ref[64:128] / center
    second = first_ref[64:128] - second_ref[64:128] / center
    out_ref[...] = (
        guess_ref[...] + first + (damping_next * damping * first + 2.0 * damping_next / half * second)
    )
    bound_ref[...] = jnp.broadcast_to(bound, (1, lanes))


def in_vmem(x):
    return pltpu.with_memory_space_constraint(x, pltpu.VMEM)


def run(body, outs, ins, name, scratch=(), flops=1 << 24):
    spec = pl.BlockSpec(memory_space=pltpu.VMEM)
    return pl.pallas_call(
        body,
        out_shape=[pltpu.VMEM(shape, dtype) for shape, dtype in outs],
        in_specs=[spec] * len(ins),
        out_specs=[spec] * len(outs),
        scratch_shapes=list(scratch),
        compiler_params=pltpu.CompilerParams(vmem_limit_bytes=24 << 20),
        cost_estimate=pl.CostEstimate(flops=flops, bytes_accessed=1 << 20, transcendentals=0),
        name=name,
    )(*(in_vmem(x) for x in ins))


def local(
    rhs_field, initial_guess, start_vector, coefficient, refine_level, block_inverse,
    side_elem, side_dir, side_case, side_kind, partner, send_list,
):
    devices = lax.axis_size("dom")
    chips = devices // 2
    trace, interp, interp_t, lift, weight = (jnp.asarray(t) for t in const_tables())
    sides = jnp.stack([side_elem, side_dir, side_case, side_kind, partner])
    sides = jnp.pad(sides, ((0, 3), (0, side_pad - sides.shape[1])), constant_values=-1)
    coef = coefficient.reshape(1, lanes)
    level = refine_level.reshape(1, lanes)

    def swap(x, mask):
        return lax.ppermute(x, "dom", [(i, i ^ mask) for i in range(devices)])

    def swap_far(x):
        to = {}
        for c in range(chips):
            other = c + 2 if c % 4 >= 2 else c - 2
            to[c] = other if 0 <= other < chips else c ^ 1
        return lax.ppermute(
            x, "dom", [(2 * c + k, 2 * to[c] + k) for c in range(chips) for k in range(2)]
        )

    def exchange(u_out, v_out, stack, nf):
        rows = u_out.shape[0]
        u_in, v_in = swap(u_out, 4), swap_far(v_out)
        (own,) = run(
            functools.partial(own_kernel, nf), [((rows, 384), f32)], [stack, hot, case, interp], "own"
        )
        one, two_, three_ = run(
            relay_kernel, [((rows, lanes), f32)] * 3, [own, u_in, v_in], "relay"
        )
        return swap(one, 1), swap(two_, 2), swap(three_, 3), u_in, v_in

    hot, case, stack, u_out, v_out = run(
        functools.partial(send_setup_kernel, chips),
        [((768, 896), bf16), ((8, 896), i32), ((144, 768), bf16), ((72, 256), f32), ((72, 256), f32)],
        [start_vector, initial_guess, coef, level, sides, send_list, trace, interp],
        "send_setup",
        scratch=[pltpu.VMEM((32, lanes), i32), pltpu.VMEM((8, 896), i32)],
    )
    own_hot, partner_hot, arrival_hot, target_hot, info, arrived_case = run(
        functools.partial(setup_kernel, chips),
        [((768, side_pad), bf16), ((768, side_pad), bf16), ((512, side_pad), bf16), ((768, 512), bf16),
         ((8, side_pad), f32), ((8, 512), i32)],
        [coef, level, sides],
        "setup",
    )
    fields = jnp.concatenate([start_vector, initial_guess], axis=0)
    history = []
    side_coef = None
    for turn, nf in enumerate((2, 2, 1, 1)):
        arrivals = exchange(u_out, v_out, stack, nf)
        own_sides, other_sides = run(
            functools.partial(sides_kernel, nf),
            [((32 * nf, side_pad), f32)] * 2,
            [stack, own_hot, partner_hot, info, interp],
            "sides",
        )
        if turn == 0:
            side_coef, arrived_coef = run(
                coef_kernel,
                [((8, side_pad), f32), ((8, 512), f32)],
                [*arrivals, info, arrival_hot],
                "coef",
            )
        (sums,) = run(
            functools.partial(flux_kernel, nf),
            [((32 * nf, 768), f32)],
            [own_sides, other_sides, side_coef, info, weight, interp_t, own_hot],
            "flux",
        )
        ins = [
            *arrivals, sums, arrived_coef, arrived_case, target_hot, weight, interp_t, lift,
            fields, coef, level, block_inverse,
        ]
        if turn == 0:
            ins.append(rhs_field)
        nf_next = (2, 1, 1, 0)[turn]
        outs = [((64 * nf, lanes), f32)]
        if nf_next:
            ins += [trace, interp, hot, case]
            outs += [((64 * nf_next, 768), bf16)] + [((32 * nf_next, 256), f32)] * 2
        else:
            outs += [((devices, lanes), f32)]
        made = run(
            functools.partial(update_kernel, nf, nf_next, turn == 0),
            outs, ins, "update",
            scratch=[pltpu.VMEM((64 * nf, lanes), f32)],
        )
        if nf_next:
            fields, stack, u_out, v_out = made
            history.append(fields)
            if nf_next < nf:
                fields = fields[:64]
        else:
            fields, parts = made
    parts = lax.all_to_all(parts.reshape(devices, 1, lanes), "dom", 0, 0).reshape(devices, lanes)
    smoothed, bound = run(
        finish_kernel,
        [((64, lanes), f32), ((1, lanes), f32)],
        [parts, initial_guess, history[0], history[1]],
        "finish",
    )
    return smoothed, bound[0, 0]


def solution(mesh):
    placed = (
        P(None, "dom"), P(None, "dom"), P(None, "dom"), P("dom"), P("dom"), P(None, None, "dom"),
        P("dom"), P("dom"), P("dom"), P("dom"), P("dom"), P("dom", None),
    )
    return jax.shard_map(
        local, mesh=mesh, in_specs=placed, out_specs=(P(None, "dom"), P()), check_vma=False
    )
```

time: 572 us -> 73.2 us (0.13)
  the two profiles are of different devices: /device:TPU:8 before, /device:TPU:0 now
where the time goes in v1:
time: 73.2 us; the launch traced here: 72.7 us
  starting transfers between devices  20.7 us (28%)
  Pallas kernels  19.5 us (27%)
  blocking collectives  12.5 us (17%)
  waiting for transfers between devices  12.2 us (17%)
  local copies, waits for them, and re-layouts  6.67 us (9%)
  between operations  1.01 us (1%)
    pallas_call x24, Pallas kernels, run(): pl.pallas_call(body, out_shape=[pltpu.VMEM(shape, dtype) for shape, dtype...  19.5 us
    ppermute x16, starting transfers between devices, swap(): return lax.ppermute(x, 'dom', [(i, i ^ mask) for i in range(devices)])  15.9 us
    all_to_all x1, blocking collectives, local(): lax.all_to_all(parts.reshape(devices, 1, lanes), 'dom', 0, 0)  12.5 us
    ppermute x16, waiting for transfers between devices, swap(): return lax.ppermute(x, 'dom', [(i, i ^ mask) for i in range(devices)])  6.27 us
    ppermute x4, waiting for transfers between devices, swap_far(): lax.ppermute(x, 'dom', [(2 * c + k, 2 * to[c] + k) for c in range(chips)...  5.89 us
    unnamed x39, local copies, waits for them, and re-layouts  5.86 us
    ppermute x4, starting transfers between devices, swap_far(): lax.ppermute(x, 'dom', [(2 * c + k, 2 * to[c] + k) for c in range(chips)...  4.89 us
  transfers between devices with their start and end apart: 20, of which 15 were waited for; matrix products, arithmetic and copies ran while one was open for 0% of the time, Pallas kernels for 14%

profile of v1, /device:TPU:0, one launch (start us, length us, event | category | flops | bytes accessed | tf_op | source)
XLA Modules:
  0.0 72.7 jit_solution(10630236280971222477)
XLA Ops:
  0.7 0.8 %stack.23 = s32[5,930]{1,0:T(8,128)S(1)} concatenate(s32[1,930]{1,0:T(1,128)} %bitcast.28, s32[1,930]{1,0:T(1,128)} %bitcast.29, s32[1,930]{1,0:T(1,128)} %bitcast.30, s32[1,930]{1,0:T(1,128)} %bitcast.31, s32[1,930]{1,0:T(1,128)} %bitcast.32), dimensions={0} | concatenate | bytes 37200 | tf_op jit(solution)/shard_map/stack | solution.py:555
  1.5 0.7 %copy-done.1 = bf16[128,96]{1,0:T(8,128)(2,1)S(1)} copy-done((bf16[128,96]{1,0:T(8,128)(2,1)S(1)}, bf16[128,96]{1,0:T(8,128)(2,1)}, u32[]{:S(2)}) %copy-start.1) | copy-done | bytes 24600
  2.3 0.9 %copy-done.5 = bf16[192,192]{1,0:T(8,128)(2,1)S(1)} copy-done((bf16[192,192]{1,0:T(8,128)(2,1)S(1)}, bf16[192,192]{1,0:T(8,128)(2,1)}, u32[]{:S(2)}) %copy-start.5) | copy-done | bytes 73752
  3.2 0.8 %copy-done.8 = f32[64,128]{1,0:T(8,128)S(1)} copy-done((f32[64,128]{1,0:T(8,128)S(1)}, f32[64,128]{1,0:T(8,128)}, u32[]{:S(2)}) %copy-start.8) | copy-done | bytes 32792
  3.9 0.8 %copy-done.10 = f32[64,128]{1,0:T(8,128)S(1)} copy-done((f32[64,128]{1,0:T(8,128)S(1)}, f32[64,128]{1,0:T(8,128)}, u32[]{:S(2)}) %copy-start.10) | copy-done | bytes 32792
  4.7 0.7 copy-done.13
  5.3 0.7 copy-done.15
  6.0 0.7 copy-done.17
  6.7 1.1 %send_setup.1 = (bf16[768,896]{1,0:T(8,128)(2,1)S(1)}, s32[8,896]{1,0:T(8,128)S(1)}, bf16[144,768]{1,0:T(8,128)(2,1)S(1)}, f32[72,256]{1,0:T(8,128)S(1)}, f32[72,256]{1,0:T(8,128)S(1)}) custom-call(f32[64,128]{1,0:T(8,128)S(1)} %copy-done.10, f32[64,128]{1,0:T(8,128)S(1)} %copy-done.8, f32[1,128]{1,0:T(1,128)S(1)} %bitcast.15, s32[1,128]{1,0:T(1,128)S(1)} %bitcast.21, ...), custom_call_target="tpu_custom_call" | custom-call | flops 16777216 | bytes 1048576 | tf_op jit(solution)/shard_map/send_setup/pallas_call | solution.py:536
  7.8 3.0 %collective-permute-start = (f32[72,256]{1,0:T(8,128)S(1)}, f32[72,256]{1,0:T(8,128)S(1)}, u32[]{:S(2)}, u32[]{:S(2)}) collective-permute-start(f32[72,256]{1,0:T(8,128)S(1)} %get-tuple-element.53), channel_id=1, source_target_pairs={{0,4},{1,5},{2,6},{3,7},{4,0},{5,1},{6,2},{7,3},{8,12},{9,13},{10,... | collective-permute-start | bytes 221192 | tf_op jit(solution)/shard_map/ppermute | solution.py:561
  10.8 1.5 %collective-permute-start.1 = (f32[72,256]{1,0:T(8,128)S(1)}, f32[72,256]{1,0:T(8,128)S(1)}, u32[]{:S(2)}, u32[]{:S(2)}) collective-permute-start(f32[72,256]{1,0:T(8,128)S(1)} %get-tuple-element.54), channel_id=1, source_target_pairs={{0,2},{1,3},{2,0},{3,1},{4,8},{5,9},{6,10},{7,11},{8,4},{9,5},{10,... | collective-permute-start | bytes 221192 | tf_op jit(solution)/shard_map/ppermute | solution.py:568
  12.3 0.5 own.4.own_ref
  12.8 1.4 %collective-permute-done.u_ref.u_in_ref = f32[72,256]{1,0:T(8,128)S(1)} collective-permute-done((f32[72,256]{1,0:T(8,128)S(1)}, f32[72,256]{1,0:T(8,128)S(1)}, u32[]{:S(2)}, u32[]{:S(2)}) %collective-permute-start) | collective-permute-done | bytes 73760 | tf_op jit(solution)/shard_map/ppermute | solution.py:561
  14.2 1.0 %collective-permute-done.1.v_ref.v_in_ref = f32[72,256]{1,0:T(8,128)S(1)} collective-permute-done((f32[72,256]{1,0:T(8,128)S(1)}, f32[72,256]{1,0:T(8,128)S(1)}, u32[]{:S(2)}, u32[]{:S(2)}) %collective-permute-start.1) | collective-permute-done | bytes 73760 | tf_op jit(solution)/shard_map/ppermute | solution.py:568
  15.3 1.6 %collective-permute-start.3 = (f32[72,128]{1,0:T(8,128)S(1)}, f32[72,128]{1,0:T(8,128)S(1)}, u32[]{:S(2)}, u32[]{:S(2)}) collective-permute-start(f32[72,128]{1,0:T(8,128)S(1)} %get-tuple-element.56), channel_id=1, source_target_pairs={{0,2},{1,3},{2,0},{3,1},{4,6},{5,7},{6,4},{7,5},{8,10},{9,11},{10,... | collective-permute-start | bytes 110600 | tf_op jit(solution)/shard_map/ppermute | solution.py:561
  16.8 0.3 collective-permute-start.4
  17.2 1.8 %setup.1 = (bf16[768,1024]{1,0:T(8,128)(2,1)S(1)}, bf16[768,1024]{1,0:T(8,128)(2,1)S(1)}, bf16[512,1024]{1,0:T(8,128)(2,1)S(1)}, bf16[768,512]{1,0:T(8,128)(2,1)...) custom-call(f32[1,128]{1,0:T(1,128)S(1)} %bitcast.16, s32[1,128]{1,0:T(1,128)S(1)} %bitcast.22, s32[8,1024]{1,0:T(8,128)S(1)} %pad.4.side_ref), custom_call_target="tpu_custom_call" | custom-call | flops 16777216 | bytes 1048576 | tf_op jit(solution)/shard_map/setup/pallas_call | solution.py:536
  19.0 1.1 %sides.4 = (f32[64,1024]{1,0:T(8,128)S(1)}, f32[64,1024]{1,0:T(8,128)S(1)}) custom-call(bf16[144,768]{1,0:T(8,128)(2,1)S(1)} %get-tuple-element.50.stack_ref, bf16[768,1024]{1,0:T(8,128)(2,1)S(1)} %get-tuple-element.58.own_hot_ref, bf16[768,1024]{1,0:T(8,128)(2,1)S(1)} %get-tuple-element.59.partner_hot_ref, f32[8,1024]{1,0:T(8,128)S(1)} %get-tuple-element.60.info_ref, ...), custom_call_target="tpu_custom_call" | custom-call | flops 16777216 | bytes 1048576 | tf_op jit(solution)/shard_map/sides/pallas_call | solution.py:536
  20.1 0.1 collective-permute-done.4.three_ref
  20.3 0.6 coef.1
  20.9 0.8 %flux.4.local_ref = f32[64,768]{1,0:T(8,128)S(1)} custom-call(f32[64,1024]{1,0:T(8,128)S(1)} %get-tuple-element.61.own_ref, f32[64,1024]{1,0:T(8,128)S(1)} %get-tuple-element.62.other_ref, f32[8,1024]{1,0:T(8,128)S(1)} %get-tuple-element.64.coef_ref, f32[8,1024]{1,0:T(8,128)S(1)} %get-tuple-element.60.info_ref, f32[32,128]{1,0:T(8,128)S(1)} %copy-done.7, ...), custom_call_target="tpu_custom_call" | custom-call | flops 16777216 | bytes 1048576 | tf_op jit(solution)/shard_map/flux/pallas_call | solution.py:536
  21.8 1.9 %update.4 = (f32[128,128]{1,0:T(8,128)S(1)}, bf16[128,768]{1,0:T(8,128)(2,1)S(1)}, f32[64,256]{1,0:T(8,128)S(1)}, f32[64,256]{1,0:T(8,128)S(1)}) custom-call(f32[72,128]{1,0:T(8,128)S(1)} %collective-permute-done.2.one_ref, f32[72,128]{1,0:T(8,128)S(1)} %collective-permute-done.3.two_ref, f32[72,128]{1,0:T(8,128)S(1)} %collective-permute-done.4.three_ref, ...), custom_call_target="tpu_custom_call" | custom-call | flops 16777216 | bytes 1048576 | tf_op jit(solution)/shard_map/update/pallas_call | solution.py:536
  23.6 1.6 %collective-permute-start.5 = (f32[64,256]{1,0:T(8,128)S(1)}, f32[64,256]{1,0:T(8,128)S(1)}, u32[]{:S(2)}, u32[]{:S(2)}) collective-permute-start(f32[64,256]{1,0:T(8,128)S(1)} %get-tuple-element.69), channel_id=1, source_target_pairs={{0,4},{1,5},{2,6},{3,7},{4,0},{5,1},{6,2},{7,3},{8,12},{9,13},{10,... | collective-permute-start | bytes 196616 | tf_op jit(solution)/shard_map/ppermute | solution.py:561
  25.3 1.4 %collective-permute-start.6 = (f32[64,256]{1,0:T(8,128)S(1)}, f32[64,256]{1,0:T(8,128)S(1)}, u32[]{:S(2)}, u32[]{:S(2)}) collective-permute-start(f32[64,256]{1,0:T(8,128)S(1)} %get-tuple-element.70), channel_id=1, source_target_pairs={{0,2},{1,3},{2,0},{3,1},{4,8},{5,9},{6,10},{7,11},{8,4},{9,5},{10,... | collective-permute-start | bytes 196616 | tf_op jit(solution)/shard_map/ppermute | solution.py:568
  26.7 0.5 own.5.own_ref
  27.2 0.8 %collective-permute-done.5.u_ref.u_in_ref = f32[64,256]{1,0:T(8,128)S(1)} collective-permute-done((f32[64,256]{1,0:T(8,128)S(1)}, f32[64,256]{1,0:T(8,128)S(1)}, u32[]{:S(2)}, u32[]{:S(2)}) %collective-permute-start.5) | collective-permute-done | bytes 65568 | tf_op jit(solution)/shard_map/ppermute | solution.py:561
  28.0 1.6 %collective-permute-done.6.v_ref.v_in_ref = f32[64,256]{1,0:T(8,128)S(1)} collective-permute-done((f32[64,256]{1,0:T(8,128)S(1)}, f32[64,256]{1,0:T(8,128)S(1)}, u32[]{:S(2)}, u32[]{:S(2)}) %collective-permute-start.6) | collective-permute-done | bytes 65568 | tf_op jit(solution)/shard_map/ppermute | solution.py:568
  29.6 0.1 collective-permute-start.7
  29.6 1.5 %collective-permute-start.8 = (f32[64,128]{1,0:T(8,128)S(1)}, f32[64,128]{1,0:T(8,128)S(1)}, u32[]{:S(2)}, u32[]{:S(2)}) collective-permute-start(f32[64,128]{1,0:T(8,128)S(1)} %get-tuple-element.72), channel_id=1, source_target_pairs={{0,2},{1,3},{2,0},{3,1},{4,6},{5,7},{6,4},{7,5},{8,10},{9,11},{10,... | collective-permute-start | bytes 98312 | tf_op jit(solution)/shard_map/ppermute | solution.py:561
  31.1 0.4 collective-permute-start.9
  31.5 1.1 %sides.5 = (f32[64,1024]{1,0:T(8,128)S(1)}, f32[64,1024]{1,0:T(8,128)S(1)}) custom-call(bf16[128,768]{1,0:T(8,128)(2,1)S(1)} %get-tuple-element.68.stack_ref, bf16[768,1024]{1,0:T(8,128)(2,1)S(1)} %get-tuple-element.58.own_hot_ref, bf16[768,1024]{1,0:T(8,128)(2,1)S(1)} %get-tuple-element.59.partner_hot_ref, f32[8,1024]{1,0:T(8,128)S(1)} %get-tuple-element.60.info_ref, ...), custom_call_target="tpu_custom_call" | custom-call | flops 16777216 | bytes 1048576 | tf_op jit(solution)/shard_map/sides/pallas_call | solution.py:536
  32.6 0.8 %flux.5.local_ref = f32[64,768]{1,0:T(8,128)S(1)} custom-call(f32[64,1024]{1,0:T(8,128)S(1)} %get-tuple-element.74.own_ref, f32[64,1024]{1,0:T(8,128)S(1)} %get-tuple-element.75.other_ref, f32[8,1024]{1,0:T(8,128)S(1)} %get-tuple-element.64.coef_ref, f32[8,1024]{1,0:T(8,128)S(1)} %get-tuple-element.60.info_ref, f32[32,128]{1,0:T(8,128)S(1)} %copy-done.7, ...), custom_call_target="tpu_custom_call" | custom-call | flops 16777216 | bytes 1048576 | tf_op jit(solution)/shard_map/flux/pallas_call | solution.py:536
  33.4 0.2 collective-permute-done.8.two_ref
  33.6 0.8 %collective-permute-done.9.three_ref = f32[64,128]{1,0:T(8,128)S(1)} collective-permute-done((f32[64,128]{1,0:T(8,128)S(1)}, f32[64,128]{1,0:T(8,128)S(1)}, u32[]{:S(2)}, u32[]{:S(2)}) %collective-permute-start.9) | collective-permute-done | bytes 32800 | tf_op jit(solution)/shard_map/ppermute | solution.py:561
  34.5 1.8 %update.5 = (f32[128,128]{1,0:T(8,128)S(1)}, bf16[64,768]{1,0:T(8,128)(2,1)S(1)}, f32[32,256]{1,0:T(8,128)S(1)}, f32[32,256]{1,0:T(8,128)S(1)}) custom-call(f32[64,128]{1,0:T(8,128)S(1)} %collective-permute-done.7.one_ref, f32[64,128]{1,0:T(8,128)S(1)} %collective-permute-done.8.two_ref, f32[64,128]{1,0:T(8,128)S(1)} %collective-permute-done.9.three_ref, ...), custom_call_target="tpu_custom_call" | custom-call | flops 16777216 | bytes 1048576 | tf_op jit(solution)/shard_map/update/pallas_call | solution.py:536
  36.2 1.5 %collective-permute-start.10 = (f32[32,256]{1,0:T(8,128)S(1)}, f32[32,256]{1,0:T(8,128)S(1)}, u32[]{:S(2)}, u32[]{:S(2)}) collective-permute-start(f32[32,256]{1,0:T(8,128)S(1)} %get-tuple-element.78), channel_id=1, source_target_pairs={{0,4},{1,5},{2,6},{3,7},{4,0},{5,1},{6,2},{7,3},{8,12},{9,13},{10,... | collective-permute-start | bytes 98312 | tf_op jit(solution)/shard_map/ppermute | solution.py:561
  37.8 0.9 %collective-permute-start.11 = (f32[32,256]{1,0:T(8,128)S(1)}, f32[32,256]{1,0:T(8,128)S(1)}, u32[]{:S(2)}, u32[]{:S(2)}) collective-permute-start(f32[32,256]{1,0:T(8,128)S(1)} %get-tuple-element.79), channel_id=1, source_target_pairs={{0,2},{1,3},{2,0},{3,1},{4,8},{5,9},{6,10},{7,11},{8,4},{9,5},{10,... | collective-permute-start | bytes 98312 | tf_op jit(solution)/shard_map/ppermute | solution.py:568
  38.7 0.4 own.6.own_ref
  39.1 1.1 %collective-permute-done.10.u_ref.u_in_ref = f32[32,256]{1,0:T(8,128)S(1)} collective-permute-done((f32[32,256]{1,0:T(8,128)S(1)}, f32[32,256]{1,0:T(8,128)S(1)}, u32[]{:S(2)}, u32[]{:S(2)}) %collective-permute-start.10) | collective-permute-done | bytes 32800 | tf_op jit(solution)/shard_map/ppermute | solution.py:561
  40.2 1.5 %collective-permute-done.11.v_ref.v_in_ref = f32[32,256]{1,0:T(8,128)S(1)} collective-permute-done((f32[32,256]{1,0:T(8,128)S(1)}, f32[32,256]{1,0:T(8,128)S(1)}, u32[]{:S(2)}, u32[]{:S(2)}) %collective-permute-start.11) | collective-permute-done | bytes 32800 | tf_op jit(solution)/shard_map/ppermute | solution.py:568
  41.7 0.1 collective-permute-start.12
  41.8 1.0 %collective-permute-start.13 = (f32[32,128]{1,0:T(8,128)S(1)}, f32[32,128]{1,0:T(8,128)S(1)}, u32[]{:S(2)}, u32[]{:S(2)}) collective-permute-start(f32[32,128]{1,0:T(8,128)S(1)} %get-tuple-element.81), channel_id=1, source_target_pairs={{0,2},{1,3},{2,0},{3,1},{4,6},{5,7},{6,4},{7,5},{8,10},{9,11},{10,... | collective-permute-start | bytes 49160 | tf_op jit(solution)/shard_map/ppermute | solution.py:561
  42.7 0.9 %collective-permute-start.14 = (f32[32,128]{1,0:T(8,128)S(1)}, f32[32,128]{1,0:T(8,128)S(1)}, u32[]{:S(2)}, u32[]{:S(2)}) collective-permute-start(f32[32,128]{1,0:T(8,128)S(1)} %get-tuple-element.82), channel_id=1, source_target_pairs={{0,3},{1,2},{2,1},{3,0},{4,7},{5,6},{6,5},{7,4},{8,11},{9,10},{10,... | collective-permute-start | bytes 49160 | tf_op jit(solution)/shard_map/ppermute | solution.py:561
  43.7 1.0 %sides.6 = (f32[32,1024]{1,0:T(8,128)S(1)}, f32[32,1024]{1,0:T(8,128)S(1)}) custom-call(bf16[64,768]{1,0:T(8,128)(2,1)S(1)} %get-tuple-element.77.stack_ref, bf16[768,1024]{1,0:T(8,128)(2,1)S(1)} %get-tuple-element.58.own_hot_ref, bf16[768,1024]{1,0:T(8,128)(2,1)S(1)} %get-tuple-element.59.partner_hot_ref, f32[8,1024]{1,0:T(8,128)S(1)} %get-tuple-element.60.info_ref, ...), custom_call_target="tpu_custom_call" | custom-call | flops 16777216 | bytes 1048576 | tf_op jit(solution)/shard_map/sides/pallas_call | solution.py:536
  44.7 0.7 %flux.6.local_ref = f32[32,768]{1,0:T(8,128)S(1)} custom-call(f32[32,1024]{1,0:T(8,128)S(1)} %get-tuple-element.83.own_ref, f32[32,1024]{1,0:T(8,128)S(1)} %get-tuple-element.84.other_ref, f32[8,1024]{1,0:T(8,128)S(1)} %get-tuple-element.64.coef_ref, f32[8,1024]{1,0:T(8,128)S(1)} %get-tuple-element.60.info_ref, f32[32,128]{1,0:T(8,128)S(1)} %copy-done.7, ...), custom_call_target="tpu_custom_call" | custom-call | flops 16777216 | bytes 1048576 | tf_op jit(solution)/shard_map/flux/pallas_call | solution.py:536
  45.4 0.2 collective-permute-done.13.two_ref
  45.6 0.3 collective-permute-done.14.three_ref
  45.9 1.6 %update.6 = (f32[64,128]{1,0:T(8,128)S(1)}, bf16[64,768]{1,0:T(8,128)(2,1)S(1)}, f32[32,256]{1,0:T(8,128)S(1)}, f32[32,256]{1,0:T(8,128)S(1)}) custom-call(f32[32,128]{1,0:T(8,128)S(1)} %collective-permute-done.12.one_ref, f32[32,128]{1,0:T(8,128)S(1)} %collective-permute-done.13.two_ref, f32[32,128]{1,0:T(8,128)S(1)} %collective-permute-done.14.three_ref, ...), custom_call_target="tpu_custom_call" | custom-call | flops 16777216 | bytes 1048576 | tf_op jit(solution)/shard_map/update/pallas_call | solution.py:536
  47.5 1.9 %collective-permute-start.15 = (f32[32,256]{1,0:T(8,128)S(1)}, f32[32,256]{1,0:T(8,128)S(1)}, u32[]{:S(2)}, u32[]{:S(2)}) collective-permute-start(f32[32,256]{1,0:T(8,128)S(1)} %get-tuple-element.87), channel_id=1, source_target_pairs={{0,4},{1,5},{2,6},{3,7},{4,0},{5,1},{6,2},{7,3},{8,12},{9,13},{10,... | collective-permute-start | bytes 98312 | tf_op jit(solution)/shard_map/ppermute | solution.py:561
  49.4 1.1 %collective-permute-start.16 = (f32[32,256]{1,0:T(8,128)S(1)}, f32[32,256]{1,0:T(8,128)S(1)}, u32[]{:S(2)}, u32[]{:S(2)}) collective-permute-start(f32[32,256]{1,0:T(8,128)S(1)} %get-tuple-element.88), channel_id=1, source_target_pairs={{0,2},{1,3},{2,0},{3,1},{4,8},{5,9},{6,10},{7,11},{8,4},{9,5},{10,... | collective-permute-start | bytes 98312 | tf_op jit(solution)/shard_map/ppermute | solution.py:568
  50.5 0.4 own.7.own_ref
  50.9 0.6 collective-permute-done.15.u_ref.u_in_ref
  51.5 1.9 %collective-permute-done.16.v_ref.v_in_ref = f32[32,256]{1,0:T(8,128)S(1)} collective-permute-done((f32[32,256]{1,0:T(8,128)S(1)}, f32[32,256]{1,0:T(8,128)S(1)}, u32[]{:S(2)}, u32[]{:S(2)}) %collective-permute-start.16) | collective-permute-done | bytes 32800 | tf_op jit(solution)/shard_map/ppermute | solution.py:568
  53.3 0.1 collective-permute-start.17
  53.4 1.2 %collective-permute-start.18 = (f32[32,128]{1,0:T(8,128)S(1)}, f32[32,128]{1,0:T(8,128)S(1)}, u32[]{:S(2)}, u32[]{:S(2)}) collective-permute-start(f32[32,128]{1,0:T(8,128)S(1)} %get-tuple-element.90), channel_id=1, source_target_pairs={{0,2},{1,3},{2,0},{3,1},{4,6},{5,7},{6,4},{7,5},{8,10},{9,11},{10,... | collective-permute-start | bytes 49160 | tf_op jit(solution)/shard_map/ppermute | solution.py:561
  54.6 0.7 collective-permute-start.19
  55.3 1.0 %sides.7 = (f32[32,1024]{1,0:T(8,128)S(1)}, f32[32,1024]{1,0:T(8,128)S(1)}) custom-call(bf16[64,768]{1,0:T(8,128)(2,1)S(1)} %get-tuple-element.86.stack_ref, bf16[768,1024]{1,0:T(8,128)(2,1)S(1)} %get-tuple-element.58.own_hot_ref, bf16[768,1024]{1,0:T(8,128)(2,1)S(1)} %get-tuple-element.59.partner_hot_ref, f32[8,1024]{1,0:T(8,128)S(1)} %get-tuple-element.60.info_ref, ...), custom_call_target="tpu_custom_call" | custom-call | flops 16777216 | bytes 1048576 | tf_op jit(solution)/shard_map/sides/pallas_call | solution.py:536
  56.3 0.7 %flux.7.local_ref = f32[32,768]{1,0:T(8,128)S(1)} custom-call(f32[32,1024]{1,0:T(8,128)S(1)} %get-tuple-element.92.own_ref, f32[32,1024]{1,0:T(8,128)S(1)} %get-tuple-element.93.other_ref, f32[8,1024]{1,0:T(8,128)S(1)} %get-tuple-element.64.coef_ref, f32[8,1024]{1,0:T(8,128)S(1)} %get-tuple-element.60.info_ref, f32[32,128]{1,0:T(8,128)S(1)} %copy-done.7, ...), custom_call_target="tpu_custom_call" | custom-call | flops 16777216 | bytes 1048576 | tf_op jit(solution)/shard_map/flux/pallas_call | solution.py:536
  57.0 0.2 collective-permute-done.18.two_ref
  57.2 0.5 collective-permute-done.19.three_ref
  57.7 1.6 %update.7 = (f32[64,128]{1,0:T(8,128)}, f32[32,128]{1,0:T(8,128)S(1)}) custom-call(f32[32,128]{1,0:T(8,128)S(1)} %collective-permute-done.17.one_ref, f32[32,128]{1,0:T(8,128)S(1)} %collective-permute-done.18.two_ref, f32[32,128]{1,0:T(8,128)S(1)} %collective-permute-done.19.three_ref, f32[32,256]{1,0:T(8,128)S(1)} %collective-permute-done.15.u_ref.u_in_ref, ...), custom_call_target="tpu_custom_call" | custom-call | flops 16777216 | bytes 1048576 | tf_op jit(solution)/shard_map/update/pallas_call | solution.py:536
  59.3 12.5 %all_to_all.5 = f32[32,1,128]{2,1,0:T(1,128)S(1)} all-to-all(f32[32,1,128]{2,1,0:T(1,128)S(1)} %bitcast.14), channel_id=1, replica_groups=mesh['dom'=32] {'dom'}, dimensions={0} | all-to-all | bytes 32768 | tf_op jit(solution)/shard_map/all_to_all | solution.py:646
  71.8 0.2 finish.1
  72.0 0.6 copy.20
  (44 shorter events, 0.3 us)
Async XLA Ops:
  0.6 18.3 %copy-start.2 = (bf16[128,96]{1,0:T(8,128)(2,1)S(1)}, bf16[128,96]{1,0:T(8,128)(2,1)}, u32[]{:S(2)}) copy-start(bf16[128,96]{1,0:T(8,128)(2,1)} %constant.13.clone.interp_ref.rest_2_.rest_1_) | copy-start | bytes 73732
  0.6 16.5 %copy-start.14 = (f32[128]{0:T(128)S(1)}, f32[128]{0:T(128)}, u32[]{:S(2)}) copy-start(f32[128]{0:T(128)} %param.20) | copy-start | bytes 1540
  0.7 16.5 %copy-start.16 = (s32[128]{0:T(128)S(1)}, s32[128]{0:T(128)}, u32[]{:S(2)}) copy-start(s32[128]{0:T(128)} %param.21) | copy-start | bytes 1540
  0.7 16.5 %copy-start.9 = (f32[64,128]{1,0:T(8,128)S(1)}, f32[64,128]{1,0:T(8,128)}, u32[]{:S(2)}) copy-start(f32[64,128]{1,0:T(8,128)} %guess_ref.3) | copy-start | bytes 98308
  0.7 16.4 %copy-start.11 = (f32[64,128]{1,0:T(8,128)S(1)}, f32[64,128]{1,0:T(8,128)}, u32[]{:S(2)}) copy-start(f32[64,128]{1,0:T(8,128)} %start_ref.1) | copy-start | bytes 98308
  1.5 0.8 %copy-start.1 = (bf16[128,96]{1,0:T(8,128)(2,1)S(1)}, bf16[128,96]{1,0:T(8,128)(2,1)}, u32[]{:S(2)}) copy-start(bf16[128,96]{1,0:T(8,128)(2,1)} %constant.13.clone.interp_ref.rest_2_.rest_1_) | copy-start | bytes 73732
  2.3 0.9 %copy-start.5 = (bf16[192,192]{1,0:T(8,128)(2,1)S(1)}, bf16[192,192]{1,0:T(8,128)(2,1)}, u32[]{:S(2)}) copy-start(bf16[192,192]{1,0:T(8,128)(2,1)} %constant.12.clone.trace_ref.rest_1_.rest_0_) | copy-start | bytes 221188
  3.2 0.8 %copy-start.8 = (f32[64,128]{1,0:T(8,128)S(1)}, f32[64,128]{1,0:T(8,128)}, u32[]{:S(2)}) copy-start(f32[64,128]{1,0:T(8,128)} %guess_ref.3) | copy-start | bytes 98308
  3.9 0.8 %copy-start.10 = (f32[64,128]{1,0:T(8,128)S(1)}, f32[64,128]{1,0:T(8,128)}, u32[]{:S(2)}) copy-start(f32[64,128]{1,0:T(8,128)} %start_ref.1) | copy-start | bytes 98308
  4.7 0.7 copy-start.13
  5.3 0.7 copy-start.15
  6.0 0.7 copy-start.17
  7.8 6.4 %collective-permute-start = (f32[72,256]{1,0:T(8,128)S(1)}, f32[72,256]{1,0:T(8,128)S(1)}, u32[]{:S(2)}, u32[]{:S(2)}) collective-permute-start(f32[72,256]{1,0:T(8,128)S(1)} %get-tuple-element.53), channel_id=1, source_target_pairs={{0,4},{1,5},{2,6},{3,7},{4,0},{5,1},{6,2},{7,3},{8,12},{9,13},{10,... | collective-permute-start | bytes 221192 | tf_op jit(solution)/shard_map/ppermute | solution.py:561
  10.8 4.4 %collective-permute-start.1 = (f32[72,256]{1,0:T(8,128)S(1)}, f32[72,256]{1,0:T(8,128)S(1)}, u32[]{:S(2)}, u32[]{:S(2)}) collective-permute-start(f32[72,256]{1,0:T(8,128)S(1)} %get-tuple-element.54), channel_id=1, source_target_pairs={{0,2},{1,3},{2,0},{3,1},{4,8},{5,9},{6,10},{7,11},{8,4},{9,5},{10,... | collective-permute-start | bytes 221192 | tf_op jit(solution)/shard_map/ppermute | solution.py:568
  15.2 4.9 %collective-permute-start.2 = (f32[72,128]{1,0:T(8,128)S(1)}, f32[72,128]{1,0:T(8,128)S(1)}, u32[]{:S(2)}, u32[]{:S(2)}) collective-permute-start(f32[72,128]{1,0:T(8,128)S(1)} %get-tuple-element.55), channel_id=1, source_target_pairs={{0,1},{1,0},{2,3},{3,2},{4,5},{5,4},{6,7},{7,6},{8,9},{9,8},{10,11... | collective-permute-start | bytes 110600 | tf_op jit(solution)/shard_map/ppermute | solution.py:561
  15.3 4.8 %collective-permute-start.3 = (f32[72,128]{1,0:T(8,128)S(1)}, f32[72,128]{1,0:T(8,128)S(1)}, u32[]{:S(2)}, u32[]{:S(2)}) collective-permute-start(f32[72,128]{1,0:T(8,128)S(1)} %get-tuple-element.56), channel_id=1, source_target_pairs={{0,2},{1,3},{2,0},{3,1},{4,6},{5,7},{6,4},{7,5},{8,10},{9,11},{10,... | collective-permute-start | bytes 110600 | tf_op jit(solution)/shard_map/ppermute | solution.py:561
  16.8 3.4 %collective-permute-start.4 = (f32[72,128]{1,0:T(8,128)S(1)}, f32[72,128]{1,0:T(8,128)S(1)}, u32[]{:S(2)}, u32[]{:S(2)}) collective-permute-start(f32[72,128]{1,0:T(8,128)S(1)} %get-tuple-element.57), channel_id=1, source_target_pairs={{0,3},{1,2},{2,1},{3,0},{4,7},{5,6},{6,5},{7,4},{8,11},{9,10},{10,... | collective-permute-start | bytes 110600 | tf_op jit(solution)/shard_map/ppermute | solution.py:561
  19.0 1.9 %copy-start.3 = (bf16[128,96]{1,0:T(8,128)(2,1)S(1)}, bf16[128,96]{1,0:T(8,128)(2,1)}, u32[]{:S(2)}) copy-start(bf16[128,96]{1,0:T(8,128)(2,1)} %constant.14.clone.interp_ref.interp_t_ref) | copy-start | bytes 73732
  19.0 1.9 %copy-start.7 = (f32[32,128]{1,0:T(8,128)S(1)}, f32[32,128]{1,0:T(8,128)}, u32[]{:S(2)}) copy-start(f32[32,128]{1,0:T(8,128)} %constant.16.clone.weight_ref) | copy-start | bytes 49156
  20.2 1.5 %copy-start = (bf16[64,64,128]{2,1,0:T(8,128)(2,1)S(1)}, bf16[64,64,128]{2,1,0:T(8,128)(2,1)}, u32[]{:S(2)}) copy-start(bf16[64,64,128]{2,1,0:T(8,128)(2,1)} %inverse_ref.7) | copy-start | bytes 3145732
  20.2 1.5 %copy-start.4 = (bf16[64,768]{1,0:T(8,128)(2,1)S(1)}, bf16[64,768]{1,0:T(8,128)(2,1)}, u32[]{:S(2)}) copy-start(bf16[64,768]{1,0:T(8,128)(2,1)} %constant.15.clone.lift_ref) | copy-start | bytes 294916
  20.3 1.5 %copy-start.6 = (bf16[192,192]{1,0:T(8,128)(2,1)S(1)}, bf16[192,192]{1,0:T(8,128)(2,1)}, u32[]{:S(2)}) copy-start(bf16[192,192]{1,0:T(8,128)(2,1)} %constant.12.clone.trace_ref.rest_1_.rest_0_) | copy-start | bytes 221188
  20.3 1.5 %copy-start.12 = (f32[64,128]{1,0:T(8,128)S(1)}, f32[64,128]{1,0:T(8,128)}, u32[]{:S(2)}) copy-start(f32[64,128]{1,0:T(8,128)} %rest_0_.3) | copy-start | bytes 98308
  23.6 4.3 %collective-permute-start.5 = (f32[64,256]{1,0:T(8,128)S(1)}, f32[64,256]{1,0:T(8,128)S(1)}, u32[]{:S(2)}, u32[]{:S(2)}) collective-permute-start(f32[64,256]{1,0:T(8,128)S(1)} %get-tuple-element.69), channel_id=1, source_target_pairs={{0,4},{1,5},{2,6},{3,7},{4,0},{5,1},{6,2},{7,3},{8,12},{9,13},{10,... | collective-permute-start | bytes 196616 | tf_op jit(solution)/shard_map/ppermute | solution.py:561
  25.3 4.3 %collective-permute-start.6 = (f32[64,256]{1,0:T(8,128)S(1)}, f32[64,256]{1,0:T(8,128)S(1)}, u32[]{:S(2)}, u32[]{:S(2)}) collective-permute-start(f32[64,256]{1,0:T(8,128)S(1)} %get-tuple-element.70), channel_id=1, source_target_pairs={{0,2},{1,3},{2,0},{3,1},{4,8},{5,9},{6,10},{7,11},{8,4},{9,5},{10,... | collective-permute-start | bytes 196616 | tf_op jit(solution)/shard_map/ppermute | solution.py:568
  29.6 3.9 %collective-permute-start.7 = (f32[64,128]{1,0:T(8,128)S(1)}, f32[64,128]{1,0:T(8,128)S(1)}, u32[]{:S(2)}, u32[]{:S(2)}) collective-permute-start(f32[64,128]{1,0:T(8,128)S(1)} %get-tuple-element.71), channel_id=1, source_target_pairs={{0,1},{1,0},{2,3},{3,2},{4,5},{5,4},{6,7},{7,6},{8,9},{9,8},{10,11... | collective-permute-start | bytes 98312 | tf_op jit(solution)/shard_map/ppermute | solution.py:561
  29.6 4.0 %collective-permute-start.8 = (f32[64,128]{1,0:T(8,128)S(1)}, f32[64,128]{1,0:T(8,128)S(1)}, u32[]{:S(2)}, u32[]{:S(2)}) collective-permute-start(f32[64,128]{1,0:T(8,128)S(1)} %get-tuple-element.72), channel_id=1, source_target_pairs={{0,2},{1,3},{2,0},{3,1},{4,6},{5,7},{6,4},{7,5},{8,10},{9,11},{10,... | collective-permute-start | bytes 98312 | tf_op jit(solution)/shard_map/ppermute | solution.py:561
  31.1 3.3 %collective-permute-start.9 = (f32[64,128]{1,0:T(8,128)S(1)}, f32[64,128]{1,0:T(8,128)S(1)}, u32[]{:S(2)}, u32[]{:S(2)}) collective-permute-start(f32[64,128]{1,0:T(8,128)S(1)} %get-tuple-element.73), channel_id=1, source_target_pairs={{0,3},{1,2},{2,1},{3,0},{4,7},{5,6},{6,5},{7,4},{8,11},{9,10},{10,... | collective-permute-start | bytes 98312 | tf_op jit(solution)/shard_map/ppermute | solution.py:561
  36.2 4.0 %collective-permute-start.10 = (f32[32,256]{1,0:T(8,128)S(1)}, f32[32,256]{1,0:T(8,128)S(1)}, u32[]{:S(2)}, u32[]{:S(2)}) collective-permute-start(f32[32,256]{1,0:T(8,128)S(1)} %get-tuple-element.78), channel_id=1, source_target_pairs={{0,4},{1,5},{2,6},{3,7},{4,0},{5,1},{6,2},{7,3},{8,12},{9,13},{10,... | collective-permute-start | bytes 98312 | tf_op jit(solution)/shard_map/ppermute | solution.py:561
  37.8 3.9 %collective-permute-start.11 = (f32[32,256]{1,0:T(8,128)S(1)}, f32[32,256]{1,0:T(8,128)S(1)}, u32[]{:S(2)}, u32[]{:S(2)}) collective-permute-start(f32[32,256]{1,0:T(8,128)S(1)} %get-tuple-element.79), channel_id=1, source_target_pairs={{0,2},{1,3},{2,0},{3,1},{4,8},{5,9},{6,10},{7,11},{8,4},{9,5},{10,... | collective-permute-start | bytes 98312 | tf_op jit(solution)/shard_map/ppermute | solution.py:568
  41.7 3.7 %collective-permute-start.12 = (f32[32,128]{1,0:T(8,128)S(1)}, f32[32,128]{1,0:T(8,128)S(1)}, u32[]{:S(2)}, u32[]{:S(2)}) collective-permute-start(f32[32,128]{1,0:T(8,128)S(1)} %get-tuple-element.80), channel_id=1, source_target_pairs={{0,1},{1,0},{2,3},{3,2},{4,5},{5,4},{6,7},{7,6},{8,9},{9,8},{10,11... | collective-permute-start | bytes 49160 | tf_op jit(solution)/shard_map/ppermute | solution.py:561
  41.8 3.8 %collective-permute-start.13 = (f32[32,128]{1,0:T(8,128)S(1)}, f32[32,128]{1,0:T(8,128)S(1)}, u32[]{:S(2)}, u32[]{:S(2)}) collective-permute-start(f32[32,128]{1,0:T(8,128)S(1)} %get-tuple-element.81), channel_id=1, source_target_pairs={{0,2},{1,3},{2,0},{3,1},{4,6},{5,7},{6,4},{7,5},{8,10},{9,11},{10,... | collective-permute-start | bytes 49160 | tf_op jit(solution)/shard_map/ppermute | solution.py:561
  42.7 3.2 %collective-permute-start.14 = (f32[32,128]{1,0:T(8,128)S(1)}, f32[32,128]{1,0:T(8,128)S(1)}, u32[]{:S(2)}, u32[]{:S(2)}) collective-permute-start(f32[32,128]{1,0:T(8,128)S(1)} %get-tuple-element.82), channel_id=1, source_target_pairs={{0,3},{1,2},{2,1},{3,0},{4,7},{5,6},{6,5},{7,4},{8,11},{9,10},{10,... | collective-permute-start | bytes 49160 | tf_op jit(solution)/shard_map/ppermute | solution.py:561
  47.5 4.0 %collective-permute-start.15 = (f32[32,256]{1,0:T(8,128)S(1)}, f32[32,256]{1,0:T(8,128)S(1)}, u32[]{:S(2)}, u32[]{:S(2)}) collective-permute-start(f32[32,256]{1,0:T(8,128)S(1)} %get-tuple-element.87), channel_id=1, source_target_pairs={{0,4},{1,5},{2,6},{3,7},{4,0},{5,1},{6,2},{7,3},{8,12},{9,13},{10,... | collective-permute-start | bytes 98312 | tf_op jit(solution)/shard_map/ppermute | solution.py:561
  49.4 3.9 %collective-permute-start.16 = (f32[32,256]{1,0:T(8,128)S(1)}, f32[32,256]{1,0:T(8,128)S(1)}, u32[]{:S(2)}, u32[]{:S(2)}) collective-permute-start(f32[32,256]{1,0:T(8,128)S(1)} %get-tuple-element.88), channel_id=1, source_target_pairs={{0,2},{1,3},{2,0},{3,1},{4,8},{5,9},{6,10},{7,11},{8,4},{9,5},{10,... | collective-permute-start | bytes 98312 | tf_op jit(solution)/shard_map/ppermute | solution.py:568
  53.3 3.7 %collective-permute-start.17 = (f32[32,128]{1,0:T(8,128)S(1)}, f32[32,128]{1,0:T(8,128)S(1)}, u32[]{:S(2)}, u32[]{:S(2)}) collective-permute-start(f32[32,128]{1,0:T(8,128)S(1)} %get-tuple-element.89), channel_id=1, source_target_pairs={{0,1},{1,0},{2,3},{3,2},{4,5},{5,4},{6,7},{7,6},{8,9},{9,8},{10,11... | collective-permute-start | bytes 49160 | tf_op jit(solution)/shard_map/ppermute | solution.py:561
  53.4 3.8 %collective-permute-start.18 = (f32[32,128]{1,0:T(8,128)S(1)}, f32[32,128]{1,0:T(8,128)S(1)}, u32[]{:S(2)}, u32[]{:S(2)}) collective-permute-start(f32[32,128]{1,0:T(8,128)S(1)} %get-tuple-element.90), channel_id=1, source_target_pairs={{0,2},{1,3},{2,0},{3,1},{4,6},{5,7},{6,4},{7,5},{8,10},{9,11},{10,... | collective-permute-start | bytes 49160 | tf_op jit(solution)/shard_map/ppermute | solution.py:561
  54.6 3.2 %collective-permute-start.19 = (f32[32,128]{1,0:T(8,128)S(1)}, f32[32,128]{1,0:T(8,128)S(1)}, u32[]{:S(2)}, u32[]{:S(2)}) collective-permute-start(f32[32,128]{1,0:T(8,128)S(1)} %get-tuple-element.91), channel_id=1, source_target_pairs={{0,3},{1,2},{2,1},{3,0},{4,7},{5,6},{6,5},{7,4},{8,11},{9,10},{10,... | collective-permute-start | bytes 49160 | tf_op jit(solution)/shard_map/ppermute | solution.py:561
  72.0 0.6 copy-start.18

commit v2 on v1

v2 whole, which is shorter than its diff:
```python
import functools
import math

import jax
import jax.numpy as jnp
import numpy as np
from jax import lax
from jax.experimental import pallas as pl
from jax.experimental.pallas import tpu as pltpu
from jax.sharding import PartitionSpec as P

f32 = jnp.float32
bf16 = jnp.bfloat16
i32 = jnp.int32
peer_offsets = (1, -1, 2, -2, 3, -3, 4, -4)
live_width = {1: 96, 2: 48, 3: 24, 4: 24}
lanes = 128
side_pad = 1024


def lagrange_tables():
    root_five = 1.0 / math.sqrt(5.0)
    nodes = np.array([0.0, 0.5 - 0.5 * root_five, 0.5 + 0.5 * root_five, 1.0])
    weights = np.array([1.0, 5.0, 5.0, 1.0]) / 12.0
    factor = np.array(
        [np.prod([nodes[i] - nodes[j] for j in range(4) if j != i]) for i in range(4)]
    )
    derivative = np.zeros((4, 4))
    for i in range(4):
        for j in range(4):
            if i != j:
                derivative[i, j] = factor[i] / (factor[j] * (nodes[i] - nodes[j]))
        derivative[i, i] = -np.sum(derivative[i])
    halves = []
    for half in range(2):
        points = 0.5 * (nodes + half)
        table = np.ones((4, 4))
        for j in range(4):
            for other in range(4):
                if other != j:
                    table[:, j] *= (points - nodes[other]) / (nodes[j] - nodes[other])
        halves.append(table)
    return weights, derivative, halves


def basis_tables():
    weights, derivative, halves = lagrange_tables()
    mass = np.diag(weights)
    line = derivative.T @ mass @ derivative
    stiffness = (
        np.kron(np.kron(line, mass), mass)
        + np.kron(np.kron(mass, line), mass)
        + np.kron(np.kron(mass, mass), line)
    )
    trace = np.zeros((6, 32, 64))
    for dim in range(3):
        others = [d for d in range(3) if d != dim]
        for lower in range(2):
            face = 2 * dim + lower
            fixed = 0 if lower else 3
            sign = -1.0 if lower else 1.0
            for first in range(4):
                for second in range(4):
                    node = first * 4 + second
                    for along in range(4):
                        place = [0, 0, 0]
                        place[others[0]] = first
                        place[others[1]] = second
                        place[dim] = along
                        nodal = place[0] * 16 + place[1] * 4 + place[2]
                        if along == fixed:
                            trace[face, node, nodal] = 1.0
                        trace[face, 16 + node, nodal] = sign * derivative[fixed, along]
    quarter = [np.kron(halves[q // 2], halves[q % 2]) for q in range(4)]
    both = np.eye(2)
    interp = np.concatenate([np.kron(both, q) for q in quarter], axis=0)
    interp_t = np.concatenate([np.kron(both, q.T) for q in quarter], axis=0)
    face_weight = np.kron(weights, weights)
    return stiffness, trace.reshape(192, 64), interp, interp_t, face_weight


def stacked(table):
    table = np.asarray(table, np.float32)
    high = table.astype(jnp.bfloat16)
    low = (table - high.astype(np.float32)).astype(jnp.bfloat16)
    return np.concatenate([high, high, low], axis=1)


def const_tables():
    stiffness, trace, interp, interp_t, face_weight = basis_tables()
    lift = np.concatenate([stacked(trace.T), stacked(stiffness)], axis=1)
    weight = np.broadcast_to(np.concatenate([face_weight, face_weight])[:, None], (32, lanes))
    return (
        stacked(trace),
        stacked(interp),
        stacked(interp_t),
        lift,
        np.asarray(weight, np.float32),
    )


def two(x):
    high = x.astype(bf16)
    return high, (x - high.astype(f32)).astype(bf16)


def three(x):
    high = x.astype(bf16)
    rest = x - high.astype(f32)
    mid = rest.astype(bf16)
    return high, mid, (rest - mid.astype(f32)).astype(bf16)


def dot(a, b):
    return jnp.dot(a, b, preferred_element_type=f32)


def dot_t(a, b):
    return lax.dot_general(a, b, (((1,), (1,)), ((), ())), preferred_element_type=f32)


def cat(parts, axis):
    return parts[0] if len(parts) == 1 else jnp.concatenate(parts, axis=axis)


def table_dot(table, x):
    high, low = two(x)
    return dot(table, jnp.concatenate([high, low, high], axis=0))


def apply_case(table, x, case):
    quarters = table_dot(table, x)
    out = x
    for c in range(4):
        out = jnp.where(case == c, quarters[32 * c : 32 * c + 32], out)
    return out


def fields_case(table, x, case, nf):
    wide = cat([x[32 * k : 32 * k + 32] for k in range(nf)], 1)
    out = apply_case(table, wide, cat([case] * nf, 1))
    n = x.shape[1]
    return cat([out[:, n * k : n * k + n] for k in range(nf)], 0)


def rows_of(rows, count, width):
    place = lax.broadcasted_iota(i32, (count, width), 0)
    table = jnp.zeros((count, width), f32)
    for k, r in enumerate(rows):
        table = jnp.where(place == k, r, table)
    return table


def one_hot(index_row, rows, first=0):
    place = lax.broadcasted_iota(i32, (rows, index_row.shape[1]), 0) + first
    return jnp.where(place == index_row, 1.0, 0.0).astype(bf16)


def element_rows(coef_ref, level_ref):
    coef = coef_ref[...]
    level = level_ref[...]
    size = jnp.where(level == 0, 1.0, jnp.where(level == 1, 0.5, 0.25)).astype(f32)
    inverse = jnp.where(level == 0, 1.0, jnp.where(level == 1, 2.0, 4.0)).astype(f32)
    return coef, size, coef * size, coef * inverse


def face_stack(trace_ref, u, normal_scale, nf):
    faces = table_dot(trace_ref[...], cat(u, 1))
    row = lax.broadcasted_iota(i32, (32, lanes), 0)
    scale = jnp.where(row < 16, 1.0, jnp.broadcast_to(normal_scale, (32, lanes)))
    fields = []
    for k in range(nf):
        part = faces[:, lanes * k : lanes * k + lanes]
        fields.append(
            jnp.concatenate([part[32 * f : 32 * f + 32] * scale for f in range(6)], axis=1)
        )
    high, low = two(cat(fields, 0))
    return jnp.concatenate([high, low], axis=0)


def gather_message(stack, hot, interp, case, nf):
    got = dot(stack, hot)
    h = 32 * nf
    out = fields_case(interp, got[:h] + got[h : 2 * h], case, nf)
    if stack.shape[0] == 2 * h:
        return out
    coef = got[2 * h : 2 * h + 1] + got[2 * h + 1 : 2 * h + 2] + got[2 * h + 2 : 2 * h + 3]
    size = got[2 * h + 3 : 2 * h + 4] * jnp.where((case >= 0) & (case < 4), 0.5, 1.0)
    row = lax.broadcasted_iota(i32, (8, out.shape[1]), 0)
    scalars = jnp.where(row == 0, coef, jnp.where(row == 1, size, 0.0))
    return jnp.concatenate([out, scalars], axis=0)


def where_am_i(chips):
    me = lax.axis_index("dom")
    chip = me // 2
    core = me - 2 * chip
    near = jnp.where(lax.rem(chip, 2) == 1, -1, 1)
    u_step = jnp.where(lax.rem(chip, 4) < 2, 2, -2)
    w_there = (chip - near >= 0) & (chip - near < chips)
    v_there = (chip - u_step >= 0) & (chip - u_step < chips)
    return core, near, u_step, w_there, v_there


def mixed_lanes():
    lane = lax.broadcasted_iota(i32, (1, lanes), 1)
    u_lanes = (lane < 24) | ((lane >= 48) & (lane < 72))
    v_lanes = ((lane >= 24) & (lane < 48)) | ((lane >= 72) & (lane < 96))
    return lane, u_lanes, v_lanes


def fill_messages(sent, nf, w_ref, v_ref, u_ref, x_ref):
    lane, u_lanes, v_lanes = mixed_lanes()
    h = 32 * nf
    x_ref[0:h] = sent[0:h, 0:128]
    w_ref[0:h] = sent[0:h, 128:256]
    for k in range(nf):
        mixed = sent[32 * k : 32 * k + 32, 256:384]
        top, bottom = mixed[0:16], mixed[16:32]
        u_ref[16 * k : 16 * k + 16] = jnp.where(u_lanes, top, pltpu.roll(bottom, 24, 1))
        v_ref[16 * k : 16 * k + 16] = jnp.where(v_lanes, top, pltpu.roll(bottom, 104, 1))
        extra = mixed[0:8]
        for g in range(1, 4):
            moved = pltpu.roll(mixed[8 * g : 8 * g + 8], 128 - 32 * g, 1)
            extra = jnp.where((lane >= 96 - 32 * g) & (lane < 128 - 32 * g), moved, extra)
        x_ref[h + 8 * k : h + 8 * k + 8] = extra
        w_ref[h + 8 * k : h + 8 * k + 8] = extra
    if sent.shape[0] > h:
        third = [sent[h : h + 1, 256:384], sent[h + 1 : h + 2, 256:384]]
        for ref, low in ((x_ref, 0), (w_ref, 128)):
            main = [sent[h : h + 1, low : low + 128], sent[h + 1 : h + 2, low : low + 128]]
            ref[40 * nf : 40 * nf + 8] = rows_of(main + third, 8, lanes)
        for ref in (u_ref, v_ref):
            ref[16 * nf : 16 * nf + 8] = rows_of(third + third, 8, lanes)


def received(nf, w_ref, v_ref, u_ref, x_ref):
    lane, u_lanes, v_lanes = mixed_lanes()
    h = 32 * nf
    mixed = []
    for k in range(nf):
        u, v = u_ref[16 * k : 16 * k + 16], v_ref[16 * k : 16 * k + 16]
        x, w = x_ref[h + 8 * k : h + 8 * k + 8], w_ref[h + 8 * k : h + 8 * k + 8]
        far = jnp.concatenate(
            [jnp.where(u_lanes, u, v), jnp.where(u_lanes, pltpu.roll(u, 104, 1), pltpu.roll(v, 24, 1))],
            axis=0,
        )
        extra = jnp.where(lane < 112, x, w)
        rolled = [extra]
        for g in range(1, 4):
            rolled.append(
                jnp.where(lane < 112, pltpu.roll(x, 32 * g, 1), pltpu.roll(w, 32 * g, 1))
            )
        mixed.append(jnp.where(lane < 96, far, jnp.concatenate(rolled, axis=0)))
    main, after = x_ref[0:h], w_ref[0:h]
    if x_ref.shape[0] > 40 * nf:
        low = 40 * nf
        third = []
        for row in (2, 3):
            far = jnp.where(
                u_lanes, u_ref[16 * nf + row : 16 * nf + row + 1], v_ref[16 * nf + row : 16 * nf + row + 1]
            )
            extra = jnp.where(
                lane < 112, x_ref[low + row : low + row + 1], w_ref[low + row : low + row + 1]
            )
            third.append(jnp.where(lane < 96, far, extra))
        mixed.append(rows_of(third, 8, lanes))
        main = jnp.concatenate([main, x_ref[low : low + 8]], axis=0)
        after = jnp.concatenate([after, w_ref[low : low + 8]], axis=0)
    return main, after, cat(mixed, 0)


def row_of(offset):
    size = jnp.abs(offset)
    return 2 * (size - 1) + jnp.where(offset < 0, 1, 0)


def narrow(offset):
    return jnp.abs(offset) == 3


def slot_attributes(side_ref, slots):
    live = lax.broadcasted_iota(i32, (1, side_pad), 1) < 930
    rows = [jnp.where(live, side_ref[k : k + 1], 0).astype(f32) for k in range(3)]
    rows.append(jnp.where(live, 1.0, 0.0))
    found = dot(rows_of(rows, 16, side_pad).astype(bf16), one_hot(slots, side_pad))
    valid = found[3:4] > 0.5
    column = jnp.where(valid, (found[1:2] * 128.0 + found[0:1]).astype(i32), -1)
    return column, jnp.where(valid, found[2:3].astype(i32), -1)


def fill_one_hot(hot_ref, column):
    for f in range(6):
        hot_ref[lanes * f : lanes * f + lanes] = one_hot(column, lanes, lanes * f)


def listed_part(rolled_ref, place, offset, low, high, valid):
    lane = lax.broadcasted_iota(i32, (1, lanes), 1)
    values = rolled_ref[pl.ds(8 * place + jnp.minimum(row_of(offset), 7), 1), :]
    return jnp.where((lane >= low) & (lane < high) & valid, values, -1)


def send_setup_kernel(chips, *refs):
    sources, refs = refs[:12], refs[12:]
    hot_ref, case_ref, stack_ref, side_ref, rolled_ref = refs[:5]
    messages, landed = refs[5:9], (*refs[14:22], *refs[9:13])
    slot_ref, arrived = refs[13], refs[22]
    copies = [
        pltpu.make_async_copy(source, target, arrived.at[k])
        for k, (source, target) in enumerate(zip(sources, landed))
    ]
    for copy in copies:
        copy.start()
    elem_ref, dir_ref, sidecase_ref, kind_ref, partner_ref, list_ref = landed[:6]
    start_ref, guess_ref, coef_ref, level_ref, trace_ref, interp_ref = landed[6:]
    for copy in copies:
        copy.wait()
    side_ref[...] = jnp.full((8, side_pad), -1, i32)
    sides = elem_ref.shape[1]
    for k, ref in enumerate((elem_ref, dir_ref, sidecase_ref, kind_ref, partner_ref)):
        side_ref[k : k + 1, 0:sides] = ref[...]
    core, near, u_step, w_there, v_there = where_am_i(chips)
    listed = jnp.concatenate([list_ref[...], jnp.full((8, 32), -1, i32)], axis=1)
    shifts = (0, 24, 48, 72, 96, 64, 80)
    for place, shift in enumerate(shifts):
        rolled_ref[8 * place : 8 * place + 8] = (
            pltpu.roll(listed, shift, 1) if shift else listed
        )

    def part(shift, offset, low, high, valid):
        return listed_part(rolled_ref, shifts.index(shift), offset, low, high, valid)

    always = core >= 0
    flip = 1 - 2 * core
    mixed = []
    for tile, (step, there, extra) in enumerate(((near, always, 64), (-near, w_there, 80))):
        cross = 2 * step + flip
        direct = part(0, cross, 0, jnp.where(narrow(cross), 24, 96), there)
        passed = part(96, 2 * step, 96, 128, there)
        slot_ref[0:1, 128 * tile : 128 * tile + 128] = jnp.maximum(direct, passed)
        mixed.append(part(extra, 2 * step, extra + 32, extra + 48, there))
    for step, there, low in ((u_step, always, 0), (-u_step, v_there, 24)):
        cross = 2 * step + flip
        mixed.append(part(low, cross, low, low + 24, there & narrow(cross)))
        mixed.append(part(low + 48, 2 * step, low + 48, low + 72, there))
    slot_ref[0:1, 256:384] = functools.reduce(jnp.maximum, mixed)
    column, slot_case = slot_attributes(side_ref, slot_ref[0:1, :])
    case_ref[0:1, :] = slot_case
    fill_one_hot(hot_ref, column)

    coef, size, volume_scale, normal_scale = element_rows(coef_ref, level_ref)
    stack = face_stack(trace_ref, [start_ref[...], guess_ref[...]], normal_scale, 2)
    scalars = rows_of([x.astype(f32) for x in three(coef)] + [size], 16, lanes).astype(bf16)
    stack = jnp.concatenate([stack, jnp.concatenate([scalars] * 6, axis=1)], axis=0)
    stack_ref[...] = stack
    sent = gather_message(stack, hot_ref[...], interp_ref[...], slot_case, 2)
    fill_messages(sent, 2, *messages)


def own_setup_kernel(chips, side_ref, rolled_ref, hot_ref, case_ref):
    core = where_am_i(chips)[0]
    slots = listed_part(rolled_ref, 0, 1 - 2 * core, 0, 96, core >= 0)
    column, slot_case = slot_attributes(side_ref, slots)
    case_ref[0:1, :] = slot_case
    fill_one_hot(hot_ref, column)


def own_kernel(nf, stack_ref, hot_ref, case_ref, interp_ref, own_ref):
    own_ref[...] = gather_message(
        stack_ref[...], hot_ref[...], interp_ref[...], case_ref[0:1], nf
    )


def own_sides_kernel(
    nf, stack_ref, hot_ref, case_ref, interp_ref, own_hot_ref, partner_hot_ref, far_hot_ref, info_ref,
    arrival_ref, own_ref, mine_ref, other_ref, target_ref,
):
    own_kernel(nf, stack_ref, hot_ref, case_ref, interp_ref, own_ref)
    sides_kernel(
        nf, stack_ref, interp_ref, own_hot_ref, partner_hot_ref, far_hot_ref, info_ref, arrival_ref,
        mine_ref, other_ref, target_ref,
    )


def relay_kernel(nf, w_ref, v_ref, u_ref, x_ref, own_ref, *rest):
    out_ref = rest[-1]
    lane = lax.broadcasted_iota(i32, (1, lanes), 1)
    main, after, mixed = received(nf, w_ref, v_ref, u_ref, x_ref)
    out_ref[:, 0:128] = jnp.where(lane < 96, own_ref[...], main)
    out_ref[:, 128:256] = jnp.where(lane < 32, pltpu.roll(after, 32, 1), mixed)


def setup_kernel(
    chips, coef_ref, level_ref, side_ref,
    info_ref, own_hot_ref, partner_hot_ref, far_hot_ref, arrival_ref, arrival_hot_ref,
):
    core, near, u_step, w_there, v_there = where_am_i(chips)
    elem, direction, case = side_ref[0:1], side_ref[1:2], side_ref[2:3]
    kind, partner = side_ref[3:4], side_ref[4:5]
    live = lax.broadcasted_iota(i32, (1, side_pad), 1) < 930
    own_column = jnp.where(live, direction * lanes + elem, -1)

    coef, size, volume_scale, normal_scale = element_rows(coef_ref, level_ref)
    scalars = rows_of([x.astype(f32) for x in three(coef)] + [size], 16, lanes)
    mine = dot(scalars.astype(bf16), one_hot(jnp.where(live, elem, -1), lanes))
    hanging = (case >= 0) & (case < 4)
    own_coef = mine[0:1] + mine[1:2] + mine[2:3]
    own_size = mine[3:4] * jnp.where(hanging, 0.5, 1.0)

    rows = [jnp.where(live, r, 0).astype(f32) for r in (elem, direction, case)]
    rows.append(jnp.where(live, 1.0, 0.0))
    rows += [mine[0:1], mine[1:2], mine[2:3], own_size]
    attributes = rows_of(rows, 16, side_pad).astype(bf16)
    other = dot(attributes, one_hot(jnp.where(partner < 930, partner, -1), side_pad))
    valid = other[3:4] > 0.5
    fill_one_hot(
        partner_hot_ref, jnp.where(valid, (other[1:2] * 128.0 + other[0:1]).astype(i32), -1)
    )
    edge = jnp.where(kind == 1, 1.0, 0.0)
    least = jnp.where(valid, jnp.minimum(own_size, other[7:8]), 0.0)
    jump = 16.0 * (own_coef + other[4:5] + other[5:6] + other[6:7]) * least
    area = least * least
    info_ref[:, 0:side_pad] = rows_of(
        [jump, jump * (1.0 - edge), area * (0.5 + 0.5 * edge), area * (0.5 - 0.5 * edge),
         case.astype(f32), other[2:3]],
        8, side_pad,
    )

    sought = jnp.where(live & (kind == 0), partner, -7)
    place = lax.broadcasted_iota(i32, (lanes, side_pad), 0)
    flip = 1 - 2 * core
    pair, after = 2 * near + flip, flip - 2 * near
    segments = (
        ((0, jnp.where(narrow(pair), 24, 96), -pair, 0), (96, 120, -(2 * u_step + flip), 0)),
        ((0, jnp.where(narrow(after), 24, 96), -after, 0), (96, 120, -(flip - 2 * u_step), 0)),
        ((0, 96, -flip, 0), (96, 128, -2 * near, 0)),
        ((0, 32, 2 * near, 0), (48, 72, -2 * u_step, 0), (72, 96, 2 * u_step, 0),
         (96, 112, -2 * near, 32), (112, 128, 2 * near, 32)),
    )
    for tile, parts in enumerate(segments):
        slot = jnp.full((lanes, side_pad), -5, i32)
        for low, high, offset, begin in parts:
            entry = 930 + 96 * row_of(offset) + begin - low
            slot = jnp.where((place >= low) & (place < high), entry + place, slot)
        arrival_hot_ref[lanes * tile : lanes * tile + lanes] = jnp.where(
            slot == sought, 1.0, 0.0
        ).astype(bf16)
    target = dot_t(attributes, arrival_hot_ref[...])
    valid = target[3:4] > 0.5
    target_column = jnp.where(valid, (target[1:2] * 128.0 + target[0:1]).astype(i32), -1)
    fill_one_hot(own_hot_ref, jnp.concatenate([own_column, target_column[:, 0:256]], axis=1))
    fill_one_hot(far_hot_ref, target_column[:, 256:512])
    info_ref[:, side_pad:] = rows_of(
        [jnp.zeros((1, 256), f32)] * 4 + [jnp.where(valid, target[2:3], -1.0)[:, 0:256]], 8, 256
    )
    arrival_ref[...] = rows_of(
        [jnp.where(valid, target[2:3], -1.0), target[4:5] + target[5:6] + target[6:7], target[7:8]],
        8, 512,
    )


def sides_kernel(
    nf, stack_ref, interp_ref, own_hot_ref, partner_hot_ref, far_hot_ref, info_ref, arrival_ref,
    mine_ref, other_ref, target_ref,
):
    h = 32 * nf
    stack = stack_ref[0 : 2 * h]
    table = interp_ref[...]
    for hot_ref, case, out_ref in (
        (own_hot_ref, info_ref[4:5], mine_ref),
        (partner_hot_ref, info_ref[5:6, 0:side_pad], other_ref),
        (far_hot_ref, arrival_ref[0:1, 256:512], target_ref),
    ):
        got = dot(stack, hot_ref[...])
        out_ref[...] = fields_case(table, got[:h] + got[h:], case.astype(i32), nf)


def scatter(x, hot, nf):
    high, low = two(x)
    got = dot_t(jnp.concatenate([high, low], axis=0), hot)
    return got[: 32 * nf] + got[32 * nf :]


def side_flux(nf, mine, outer, coefs, case, weight_ref, interp_ref, hot):
    jump, jump_out, area, area_out = coefs
    weight = weight_ref[0:16, 0:1]
    flux = []
    for k in range(nf):
        value, slope = mine[32 * k : 32 * k + 16], mine[32 * k + 16 : 32 * k + 32]
        other, other_slope = outer[32 * k : 32 * k + 16], outer[32 * k + 16 : 32 * k + 32]
        flux.append(
            weight * (jump * value - jump_out * other - area * slope + area_out * other_slope)
        )
        flux.append(weight * (area_out * other - area * value))
    flux = fields_case(interp_ref[...], jnp.concatenate(flux, axis=0), case.astype(i32), nf)
    high, low = two(flux)
    got = dot_t(jnp.concatenate([high, low], axis=0), hot)
    return got[: 32 * nf] + got[32 * nf :]


def halo_coefs(coef, size, other_coef, other_size):
    least = jnp.minimum(size, other_size)
    return 16.0 * (coef + other_coef) * least, 0.5 * least * least


def flux_kernel(
    nf, w_ref, v_ref, u_ref, x_ref, mine_ref, other_ref, info_ref, arrival_ref, weight_ref, interp_ref,
    own_hot_ref, *rest,
):
    h = 32 * nf
    lane = lax.broadcasted_iota(i32, (1, lanes), 1)
    main, after, mixed = received(nf, w_ref, v_ref, u_ref, x_ref)
    got = jnp.concatenate(
        [
            jnp.where(lane < 96, main, pltpu.roll(mixed, 96, 1)),
            jnp.where(lane < 96, after, pltpu.roll(mixed, 72, 1)),
        ],
        axis=1,
    )
    if got.shape[0] > h:
        sum_ref, halo_ref = rest
        halo = halo_coefs(
            arrival_ref[1:2, 0:256], arrival_ref[2:3, 0:256], got[h : h + 1], got[h + 1 : h + 2]
        )
        halo_ref[...] = rows_of(halo, 8, 256)
    else:
        halo_ref, sum_ref = rest
        halo = halo_ref[0:1], halo_ref[1:2]
    coefs = [
        jnp.concatenate([info_ref[k : k + 1, 0:side_pad], halo[k // 2]], axis=1) for k in range(4)
    ]
    outer = jnp.concatenate([other_ref[...], got[0:h]], axis=1)
    sum_ref[...] = side_flux(
        nf, mine_ref, outer, coefs, info_ref[4:5], weight_ref, interp_ref, own_hot_ref[...]
    )


def solve_blocks(inverse_ref, hold_ref, nf):
    sums = [jnp.zeros((64, lanes), f32) for _ in range(nf)]
    for col in range(64):
        block = inverse_ref[col].astype(f32)
        for k in range(nf):
            sums[k] = sums[k] + block * hold_ref[64 * k + col : 64 * k + col + 1, :]
    return sums


def update_kernel(
    nf, nf_next, residual,
    one_ref, local_ref, target_ref, arrival_ref, far_hot_ref, weight_ref, interp_t_ref, lift_ref,
    field_ref, coef_ref, level_ref, inverse_ref, *rest,
):
    if residual:
        rhs_ref, *rest = rest
    else:
        halo_ref, *rest = rest
    if nf_next:
        trace_ref, interp_ref, hot_ref, case_ref, new_ref, stack_ref, *rest = rest
        messages, rest = rest[:4], rest[4:]
    else:
        new_ref, part_ref, *rest = rest
    hold_ref = rest[-1]
    h = 32 * nf
    if residual:
        halo = halo_coefs(
            arrival_ref[1:2, 256:512], arrival_ref[2:3, 256:512],
            one_ref[h : h + 1], one_ref[h + 1 : h + 2],
        )
        rest[0][...] = rows_of(halo, 8, 256)
    else:
        halo = (halo_ref[0:1], halo_ref[1:2])
    total = local_ref[...] + side_flux(
        nf, target_ref, one_ref, (halo[0], halo[0], halo[1], halo[1]), arrival_ref[0:1, 256:512],
        weight_ref, interp_t_ref, far_hot_ref[...],
    )
    coef, size, volume_scale, normal_scale = element_rows(coef_ref, level_ref)
    row = lax.broadcasted_iota(i32, (32, lanes), 0)
    scale = jnp.where(row < 16, 1.0, jnp.broadcast_to(normal_scale, (32, lanes)))
    operands = []
    for k in range(nf):
        mine = total[32 * k : 32 * k + 32]
        faces = jnp.concatenate(
            [mine[:, lanes * f : lanes * f + lanes] * scale for f in range(6)], axis=0
        )
        high, low = two(faces)
        field_high, field_low = two(field_ref[64 * k : 64 * k + 64] * volume_scale)
        operands.append(
            jnp.concatenate([high, low, high, field_high, field_low, field_high], axis=0)
        )
    image = dot(lift_ref[...], cat(operands, 1))
    for k in range(nf):
        part = image[:, lanes * k : lanes * k + lanes]
        if residual and k == 1:
            part = rhs_ref[...] - part
        hold_ref[64 * k : 64 * k + 64, :] = part
    new = solve_blocks(inverse_ref, hold_ref, nf)
    for k in range(nf):
        new_ref[64 * k : 64 * k + 64, :] = new[k]
    if nf_next:
        stack = face_stack(trace_ref, new[:nf_next], normal_scale, nf_next)
        stack_ref[...] = stack
        sent = gather_message(stack, hot_ref[...], interp_ref[...], case_ref[0:1], nf_next)
        fill_messages(sent, nf_next, *messages)
    else:
        before, after = field_ref[...], new[0]
        before = jnp.sum(jnp.sum(before * before, axis=1, keepdims=True), axis=0, keepdims=True)
        after = jnp.sum(jnp.sum(after * after, axis=1, keepdims=True), axis=0, keepdims=True)
        lane = lax.broadcasted_iota(i32, part_ref.shape, 1)
        part_ref[...] = jnp.where(lane == 0, before, jnp.where(lane == 1, after, 0.0))


def finish_kernel(part_ref, guess_ref, first_ref, second_ref, out_ref, bound_ref):
    total = jnp.sum(part_ref[...], axis=0, keepdims=True)
    bound = jnp.sqrt(total[:, 1:2] / total[:, 0:1])
    upper = 1.2 * bound
    lower = upper / 15.0
    center = 0.5 * (upper + lower)
    half = 0.5 * (upper - lower)
    ratio = center / half
    damping = 1.0 / ratio
    damping_next = 1.0 / (2.0 * ratio - damping)
    first = first_ref[64:128] / center
    second = first_ref[64:128] - second_ref[64:128] / center
    out_ref[...] = (
        guess_ref[...] + first + (damping_next * damping * first + 2.0 * damping_next / half * second)
    )
    bound_ref[...] = jnp.broadcast_to(bound, (1, lanes))


def in_vmem(x):
    return pltpu.with_memory_space_constraint(x, pltpu.VMEM)


def in_hbm(x):
    return pltpu.with_memory_space_constraint(x, pltpu.HBM)


def run(body, outs, ins, name, scratch=(), flops=1 << 24, placed=True, kept=True):
    spec = pl.BlockSpec(memory_space=pltpu.VMEM)
    return pl.pallas_call(
        body,
        out_shape=[(pltpu.VMEM if kept else jax.ShapeDtypeStruct)(shape, dtype) for shape, dtype in outs],
        in_specs=[spec if placed else pl.BlockSpec(memory_space=pltpu.HBM)] * len(ins),
        out_specs=[spec] * len(outs),
        scratch_shapes=list(scratch),
        compiler_params=pltpu.CompilerParams(vmem_limit_bytes=24 << 20),
        cost_estimate=pl.CostEstimate(flops=flops, bytes_accessed=1 << 20, transcendentals=0),
        name=name,
    )(*(in_vmem(x) if placed else in_hbm(x) for x in ins))


def local(
    rhs_field, initial_guess, start_vector, coefficient, refine_level, block_inverse,
    side_elem, side_dir, side_case, side_kind, partner, send_list,
):
    devices = lax.axis_size("dom")
    chips = devices // 2
    trace, interp, interp_t, lift, weight = (jnp.asarray(t) for t in const_tables())
    coef = coefficient.reshape(1, lanes)
    level = refine_level.reshape(1, lanes)

    def swap(x, mask):
        return lax.ppermute(x, "dom", [(i, i ^ mask) for i in range(devices)])

    def swap_chips(x, to):
        return lax.ppermute(
            x, "dom",
            [(2 * c + k, 2 * to.get(c, c) + 1 - k) for c in range(chips) for k in range(2)],
        )

    after_pair = {c: c + 1 if c % 2 else c - 1 for c in range(1, chips - 1)}
    two_away = {c: c + 2 if c % 4 >= 2 else c - 2 for c in range(2, chips - 2)}
    two_away.update({c: c ^ 1 for c in (0, 1, chips - 2, chips - 1)})

    def exchange(messages, nf, work):
        w, v, u, x = messages
        first = (swap_chips(w, after_pair), swap_chips(v, two_away), swap(u, 5), swap(x, 3))
        own, *rest = work()
        (one,) = run(
            functools.partial(relay_kernel, nf), [((own.shape[0], 256), f32)],
            [*first, own, *rest[:1]], "relay",
        )
        return first, swap(one, 1), rest

    def message_shapes(nf, extra=0):
        return [((rows * nf + extra, lanes), f32) for rows in (40, 16, 16, 40)]

    sides = [x.reshape(1, -1) for x in (side_elem, side_dir, side_case, side_kind, partner)]
    first = [*sides, send_list, start_vector, initial_guess, coef, level, trace, interp]
    hot, case, stack, sides, rolled, *rest = run(
        functools.partial(send_setup_kernel, chips),
        [((768, 384), bf16), ((8, 384), i32), ((144, 768), bf16), ((8, side_pad), i32), ((56, lanes), i32),
         *message_shapes(2, 8), *((x.shape, x.dtype) for x in first[8:])],
        first,
        "send_setup",
        scratch=[
            pltpu.VMEM((8, 384), i32),
            *(pltpu.VMEM(x.shape, x.dtype) for x in first[:8]), pltpu.SemaphoreType.DMA((len(first),)),
        ],
        placed=False,
    )
    messages, (coef, level, trace, interp) = rest[:4], rest[4:]
    fields = jnp.concatenate([start_vector, initial_guess], axis=0)
    history = []
    for turn, nf in enumerate((2, 2, 1, 1)):
        h = 32 * nf
        sides_out = [((h, side_pad + 256), f32), ((h, side_pad), f32), ((h, 256), f32)]
        own_out = [((h if turn else h + 8, lanes), f32)]

        def first_work():
            own_slots = run(
                functools.partial(own_setup_kernel, chips),
                [((768, lanes), bf16), ((8, lanes), i32)],
                [sides, rolled],
                "own_setup",
            )
            made = run(
                functools.partial(setup_kernel, chips),
                [((8, side_pad + 256), f32), ((768, side_pad + 256), bf16), ((768, side_pad), bf16),
                 ((768, 256), bf16), ((8, 512), f32)],
                [coef, level, sides],
                "setup",
                scratch=[pltpu.VMEM((512, side_pad), bf16)],
            )
            (own,) = run(
                functools.partial(own_kernel, nf), own_out, [stack, *own_slots, interp], "own"
            )
            return [own, *made, *own_slots]

        def later_work():
            return run(
                functools.partial(own_sides_kernel, nf),
                own_out + sides_out,
                [stack, *own_slots, interp, own_hot, partner_hot, far_hot, info, arrival],
                "own_sides",
            )

        arrivals, one, rest = exchange(messages, nf, later_work if turn else first_work)
        if turn == 0:
            info, own_hot, partner_hot, far_hot, arrival, *own_slots = rest
            mine, others, targets = run(
                functools.partial(sides_kernel, nf),
                sides_out,
                [stack, interp, own_hot, partner_hot, far_hot, info, arrival],
                "sides",
            )
        else:
            mine, others, targets = rest
        halo_out = [((8, 256), f32)] if turn == 0 else []
        sums, *made = run(
            functools.partial(flux_kernel, nf),
            [((h, 768), f32)] + halo_out,
            [*arrivals, mine, others, info, arrival, weight, interp_t, own_hot]
            + ([near_halo] if turn else []),
            "flux",
        )
        if turn == 0:
            near_halo = made[0]
        nf_next = (2, 1, 1, 0)[turn]
        ins = [
            one, sums, targets, arrival, far_hot, weight, interp_t, lift,
            fields, coef, level, block_inverse, far_halo if turn else rhs_field,
        ]
        outs = [((64 * nf, lanes), f32)]
        if nf_next:
            ins += [trace, interp, hot, case]
            outs += [((64 * nf_next, 768), bf16)] + message_shapes(nf_next)
        else:
            outs += [((devices, lanes), f32)]
        made = run(
            functools.partial(update_kernel, nf, nf_next, turn == 0),
            outs + halo_out, ins, "update",
            scratch=[pltpu.VMEM((64 * nf, lanes), f32)],
        )
        if turn == 0:
            far_halo = made[-1]
        if nf_next:
            fields, stack, *messages = made[:6]
            history.append(fields)
            if nf_next < nf:
                fields = fields[:64]
        else:
            fields, parts = made
    parts = lax.all_to_all(parts.reshape(devices, 1, lanes), "dom", 0, 0).reshape(devices, lanes)
    smoothed, bound = run(
        finish_kernel,
        [((64, lanes), f32), ((1, lanes), f32)],
        [parts, initial_guess, history[0], history[1]],
        "finish",
        kept=False,
    )
    return smoothed, bound[0, 0]


def solution(mesh):
    placed = (
        P(None, "dom"), P(None, "dom"), P(None, "dom"), P("dom"), P("dom"), P(None, None, "dom"),
        P("dom"), P("dom"), P("dom"), P("dom"), P("dom"), P("dom", None),
    )
    return jax.shard_map(
        local, mesh=mesh, in_specs=placed, out_specs=(P(None, "dom"), P()), check_vma=False
    )
```

time: 73.2 us -> 58.6 us (0.80)
  waiting for transfers between devices: 12.2 us -> 0.4 us
  local copies, waits for them, and re-layouts: 6.67 us -> 0.05 us
  starting transfers between devices: 20.7 us -> 24.5 us
  Pallas kernels: 19.5 us -> 21.4 us
  blocking collectives: 12.5 us -> 11 us
    ppermute x16 -> x12, starting transfers between devices: 15.9 us -> 22.3 us  [swap(): return lax.ppermute(x, 'dom', [(i, i ^ mask) for i in range(devices)])]
    ppermute x16 -> x12, waiting for transfers between devices: 6.27 us -> 0.37 us  [swap(): return lax.ppermute(x, 'dom', [(i, i ^ mask) for i in range(devices)])]
    ppermute x4 -> x8, waiting for transfers between devices: 5.89 us -> 0.02 us  [swap_chips(): lax.ppermute(x, 'dom', [(2 * c + k, 2 * to.get(c, c) + 1 - k) for c in ra...]
    unnamed x39 -> x14, local copies, waits for them, and re-layouts: 5.86 us -> 0.05 us
    ppermute x4 -> x8, starting transfers between devices: 4.89 us -> 2.25 us  [swap_chips(): lax.ppermute(x, 'dom', [(2 * c + k, 2 * to.get(c, c) + 1 - k) for c in ra...]
    pallas_call x24 -> x21, Pallas kernels: 19.5 us -> 21.4 us  [run(): pl.pallas_call(body, out_shape=[(pltpu.VMEM if kept else jax.ShapeDtypeSt...]
    all_to_all x1, blocking collectives: 12.5 us -> 11 us  [local(): lax.all_to_all(parts.reshape(devices, 1, lanes), 'dom', 0, 0)]
    another operation x1 -> x0, local copies, waits for them, and re-layouts: 0.81 us -> none  [local(): sides = jnp.stack([side_elem, side_dir, side_case, side_kind, partner])]
  transfers between devices with their start and end apart: 20 -> 20, of which waited for: 15 -> 2; matrix products, arithmetic and copies ran while one was open for 0% -> 0% of each run, Pallas kernels for 14% -> 20%
where the time goes in v2:
time: 58.6 us; the launch traced here: 58.4 us
  starting transfers between devices  24.5 us (42%)
  Pallas kernels  21.4 us (37%)
  blocking collectives  11 us (19%)
  between operations  0.95 us (2%)
    ppermute x12, starting transfers between devices, swap(): return lax.ppermute(x, 'dom', [(i, i ^ mask) for i in range(devices)])  22.3 us
    pallas_call x21, Pallas kernels, run(): pl.pallas_call(body, out_shape=[(pltpu.VMEM if kept else jax.ShapeDtypeSt...  21.4 us
    all_to_all x1, blocking collectives, local(): lax.all_to_all(parts.reshape(devices, 1, lanes), 'dom', 0, 0)  11 us
    ppermute x8, starting transfers between devices, swap_chips(): lax.ppermute(x, 'dom', [(2 * c + k, 2 * to.get(c, c) + 1 - k) for c in ra...  2.25 us
  transfers between devices with their start and end apart: 20, of which 2 were waited for; matrix products, arithmetic and copies ran while one was open for 0% of the time, Pallas kernels for 20%

profile of v2, /device:TPU:0, one launch (start us, length us, event | category | flops | bytes accessed | tf_op | source)
XLA Modules:
  0.0 58.4 jit_solution(3561848782327953956)
XLA Ops:
  0.6 2.1 %send_setup.1 = (bf16[768,384]{1,0:T(8,128)(2,1)S(1)}, s32[8,384]{1,0:T(8,128)S(1)}, bf16[144,768]{1,0:T(8,128)(2,1)S(1)}, s32[8,1024]{1,0:T(8,128)S(1)}, s32[56...) custom-call(s32[1,930]{1,0:T(1,128)} %bitcast.15, ...), custom_call_target="tpu_custom_call" | custom-call | flops 16777216 | bytes 1048576 | tf_op jit(solution)/shard_map/send_setup/pallas_call | solution.py:639
  2.7 0.5 collective-permute-start
  3.2 3.7 %collective-permute-start.3 = (f32[88,128]{1,0:T(8,128)S(1)}, f32[88,128]{1,0:T(8,128)S(1)}, u32[]{:S(2)}, u32[]{:S(2)}) collective-permute-start(f32[88,128]{1,0:T(8,128)S(1)} %get-tuple-element.64), channel_id=1, source_target_pairs={{0,3},{1,2},{2,1},{3,0},{4,7},{5,6},{6,5},{7,4},{8,11},{9,10},{10,... | collective-permute-start | bytes 135176 | tf_op jit(solution)/shard_map/ppermute | solution.py:662
  6.9 0.0 collective-permute-start.1
  7.0 2.7 %collective-permute-start.2 = (f32[40,128]{1,0:T(8,128)S(1)}, f32[40,128]{1,0:T(8,128)S(1)}, u32[]{:S(2)}, u32[]{:S(2)}) collective-permute-start(f32[40,128]{1,0:T(8,128)S(1)} %get-tuple-element.63), channel_id=1, source_target_pairs={{0,5},{1,4},{2,7},{3,6},{4,1},{5,0},{6,3},{7,2},{8,13},{9,12},{10,... | collective-permute-start | bytes 61448 | tf_op jit(solution)/shard_map/ppermute | solution.py:662
  9.7 0.2 own_setup.1
  9.9 1.8 %setup.1 = (f32[8,1280]{1,0:T(8,128)S(1)}, bf16[768,1280]{1,0:T(8,128)(2,1)S(1)}, bf16[768,1024]{1,0:T(8,128)(2,1)S(1)}, bf16[768,256]{1,0:T(8,128)(2,1)S(1)}, f32[8,512]{1,0:T(8,128)S(1)}) custom-call(f32[1,128]{1,0:T(1,128)S(1)} %get-tuple-element.71.coef_ref, s32[1,128]{1,0:T(1,128)S(1)} %get-tuple-element.72.level_ref, ...), custom_call_target="tpu_custom_call" | custom-call | flops 16777216 | bytes 1048576 | tf_op jit(solution)/shard_map/setup/pallas_call | solution.py:639
  11.7 0.4 own.1.own_ref
  12.1 0.0 copy-start.4
  12.1 0.0 copy-start.6
  12.1 0.0 copy-start.1
  12.1 0.0 copy-start.3
  12.1 1.4 %sides.1 = (f32[64,1280]{1,0:T(8,128)S(1)}, f32[64,1024]{1,0:T(8,128)S(1)}, f32[64,256]{1,0:T(8,128)S(1)}) custom-call(bf16[144,768]{1,0:T(8,128)(2,1)S(1)} %get-tuple-element.65.stack_ref, bf16[128,96]{1,0:T(8,128)(2,1)S(1)} %get-tuple-element.70.interp_ref.rest_2_, bf16[768,1280]{1,0:T(8,128)(2,1)S(1)} %get-tuple-element.74.own_hot_ref, ...), custom_call_target="tpu_custom_call" | custom-call | flops 16777216 | bytes 1048576 | tf_op jit(solution)/shard_map/sides/pallas_call | solution.py:639
  13.6 0.0 copy-start
  13.6 0.0 copy-start.2
  13.6 0.0 copy-start.5
  13.6 0.0 collective-permute-done.1.v_ref
  13.6 0.0 collective-permute-done.2.u_ref
  13.6 0.0 collective-permute-done.w_ref
  13.6 0.0 collective-permute-done.3.x_ref
  13.7 0.1 relay.4
  13.8 0.1 collective-permute-start.4
  13.9 1.0 %flux.4 = (f32[64,768]{1,0:T(8,128)S(1)}, f32[8,256]{1,0:T(8,128)S(1)}) custom-call(f32[88,128]{1,0:T(8,128)S(1)} %collective-permute-done.w_ref, f32[40,128]{1,0:T(8,128)S(1)} %collective-permute-done.1.v_ref, f32[40,128]{1,0:T(8,128)S(1)} %collective-permute-done.2.u_ref, f32[88,128]{1,0:T(8,128)S(1)} %collective-permute-done.3.x_ref, ...), custom_call_target="tpu_custom_call" | custom-call | flops 16777216 | bytes 1048576 | tf_op jit(solution)/shard_map/flux/pallas_call | solution.py:639
  14.9 0.1 collective-permute-done.4.one_ref
  15.1 1.8 %update.4 = (f32[128,128]{1,0:T(8,128)S(1)}, bf16[128,768]{1,0:T(8,128)(2,1)S(1)}, f32[80,128]{1,0:T(8,128)S(1)}, f32[32,128]{1,0:T(8,128)S(1)}, f32[32,128]{1,0...) custom-call(f32[72,256]{1,0:T(8,128)S(1)} %collective-permute-done.4.one_ref, ...), custom_call_target="tpu_custom_call" | custom-call | flops 16777216 | bytes 1048576 | tf_op jit(solution)/shard_map/update/pallas_call | solution.py:639
  16.9 0.4 collective-permute-start.5
  17.3 1.1 %collective-permute-start.8 = (f32[80,128]{1,0:T(8,128)S(1)}, f32[80,128]{1,0:T(8,128)S(1)}, u32[]{:S(2)}, u32[]{:S(2)}) collective-permute-start(f32[80,128]{1,0:T(8,128)S(1)} %get-tuple-element.88), channel_id=1, source_target_pairs={{0,3},{1,2},{2,1},{3,0},{4,7},{5,6},{6,5},{7,4},{8,11},{9,10},{10,... | collective-permute-start | bytes 122888 | tf_op jit(solution)/shard_map/ppermute | solution.py:662
  18.4 0.7 %collective-permute-start.6 = (f32[32,128]{1,0:T(8,128)S(1)}, f32[32,128]{1,0:T(8,128)S(1)}, u32[]{:S(2)}, u32[]{:S(2)}) collective-permute-start(f32[32,128]{1,0:T(8,128)S(1)} %get-tuple-element.86), channel_id=1, source_target_pairs={{0,3},{1,2},{2,1},{3,0},{4,9},{5,8},{6,11},{7,10},{8,5},{9,4},{10,... | collective-permute-start | bytes 49160 | tf_op jit(solution)/shard_map/ppermute | solution.py:665
  19.1 2.2 %collective-permute-start.7 = (f32[32,128]{1,0:T(8,128)S(1)}, f32[32,128]{1,0:T(8,128)S(1)}, u32[]{:S(2)}, u32[]{:S(2)}) collective-permute-start(f32[32,128]{1,0:T(8,128)S(1)} %get-tuple-element.87), channel_id=1, source_target_pairs={{0,5},{1,4},{2,7},{3,6},{4,1},{5,0},{6,3},{7,2},{8,13},{9,12},{10,... | collective-permute-start | bytes 49160 | tf_op jit(solution)/shard_map/ppermute | solution.py:662
  21.3 1.5 %own_sides.3 = (f32[64,128]{1,0:T(8,128)S(1)}, f32[64,1280]{1,0:T(8,128)S(1)}, f32[64,1024]{1,0:T(8,128)S(1)}, f32[64,256]{1,0:T(8,128)S(1)}) custom-call(bf16[128,768]{1,0:T(8,128)(2,1)S(1)} %get-tuple-element.89.stack_ref, bf16[768,128]{1,0:T(8,128)(2,1)S(1)} %get-tuple-element.68.hot_ref, s32[8,128]{1,0:T(8,128)S(1)} %get-tuple-element.69.case_ref, ...), custom_call_target="tpu_custom_call" | custom-call | flops 16777216 | bytes 1048576 | tf_op jit(solution)/shard_map/own_sides/pallas_call | solution.py:639
  22.8 0.0 collective-permute-done.6.v_ref
  22.8 0.0 collective-permute-done.7.u_ref
  22.9 0.0 collective-permute-done.5.w_ref
  22.9 0.0 collective-permute-done.8.x_ref
  22.9 0.1 relay.5
  23.0 0.4 collective-permute-start.9
  23.4 1.0 %flux.5.local_ref = f32[64,768]{1,0:T(8,128)S(1)} custom-call(f32[80,128]{1,0:T(8,128)S(1)} %collective-permute-done.5.w_ref, f32[32,128]{1,0:T(8,128)S(1)} %collective-permute-done.6.v_ref, f32[32,128]{1,0:T(8,128)S(1)} %collective-permute-done.7.u_ref, f32[80,128]{1,0:T(8,128)S(1)} %collective-permute-done.8.x_ref, ...), custom_call_target="tpu_custom_call" | custom-call | flops 16777216 | bytes 1048576 | tf_op jit(solution)/shard_map/flux/pallas_call | solution.py:639
  24.5 1.6 %update.5 = (f32[128,128]{1,0:T(8,128)S(1)}, bf16[64,768]{1,0:T(8,128)(2,1)S(1)}, f32[40,128]{1,0:T(8,128)S(1)}, f32[16,128]{1,0:T(8,128)S(1)}, f32[16,128]{1,0:T(8,128)S(1)}, /*index=5*/f32[40,128]{1,0:T(8,128)S(1)}) custom-call(f32[64,256]{1,0:T(8,128)S(1)} %collective-permute-done.9.one_ref, f32[64,768]{1,0:T(8,128)S(1)} %flux.5.local_ref, ...), custom_call_target="tpu_custom_call" | custom-call | flops 16777216 | bytes 1048576 | tf_op jit(solution)/shard_map/update/pallas_call | solution.py:639
  26.1 0.2 collective-permute-start.10
  26.3 3.4 %collective-permute-start.13 = (f32[40,128]{1,0:T(8,128)S(1)}, f32[40,128]{1,0:T(8,128)S(1)}, u32[]{:S(2)}, u32[]{:S(2)}) collective-permute-start(f32[40,128]{1,0:T(8,128)S(1)} %get-tuple-element.100), channel_id=1, source_target_pairs={{0,3},{1,2},{2,1},{3,0},{4,7},{5,6},{6,5},{7,4},{8,11},{9,10},{10,... | collective-permute-start | bytes 61448 | tf_op jit(solution)/shard_map/ppermute | solution.py:662
  29.7 0.0 collective-permute-start.11
  29.7 2.7 %collective-permute-start.12 = (f32[16,128]{1,0:T(8,128)S(1)}, f32[16,128]{1,0:T(8,128)S(1)}, u32[]{:S(2)}, u32[]{:S(2)}) collective-permute-start(f32[16,128]{1,0:T(8,128)S(1)} %get-tuple-element.99), channel_id=1, source_target_pairs={{0,5},{1,4},{2,7},{3,6},{4,1},{5,0},{6,3},{7,2},{8,13},{9,12},{10,... | collective-permute-start | bytes 24584 | tf_op jit(solution)/shard_map/ppermute | solution.py:662
  32.5 1.3 %own_sides.4 = (f32[32,128]{1,0:T(8,128)S(1)}, f32[32,1280]{1,0:T(8,128)S(1)}, f32[32,1024]{1,0:T(8,128)S(1)}, f32[32,256]{1,0:T(8,128)S(1)}) custom-call(bf16[64,768]{1,0:T(8,128)(2,1)S(1)} %get-tuple-element.101.stack_ref, bf16[768,128]{1,0:T(8,128)(2,1)S(1)} %get-tuple-element.68.hot_ref, s32[8,128]{1,0:T(8,128)S(1)} %get-tuple-element.69.case_ref, ...), custom_call_target="tpu_custom_call" | custom-call | flops 16777216 | bytes 1048576 | tf_op jit(solution)/shard_map/own_sides/pallas_call | solution.py:639
  33.8 0.0 collective-permute-done.12.u_ref
  33.8 0.1 relay.6
  33.9 0.2 collective-permute-start.14
  34.2 0.9 %flux.6.local_ref = f32[32,768]{1,0:T(8,128)S(1)} custom-call(f32[40,128]{1,0:T(8,128)S(1)} %collective-permute-done.10.w_ref, f32[16,128]{1,0:T(8,128)S(1)} %collective-permute-done.11.v_ref, f32[16,128]{1,0:T(8,128)S(1)} %collective-permute-done.12.u_ref, f32[40,128]{1,0:T(8,128)S(1)} %collective-permute-done.13.x_ref, ...), custom_call_target="tpu_custom_call" | custom-call | flops 16777216 | bytes 1048576 | tf_op jit(solution)/shard_map/flux/pallas_call | solution.py:639
  35.1 0.1 collective-permute-done.14.one_ref
  35.2 1.4 %update.6 = (f32[64,128]{1,0:T(8,128)S(1)}, bf16[64,768]{1,0:T(8,128)(2,1)S(1)}, f32[40,128]{1,0:T(8,128)S(1)}, f32[16,128]{1,0:T(8,128)S(1)}, f32[16,128]{1,0:T(8,128)S(1)}, /*index=5*/f32[40,128]{1,0:T(8,128)S(1)}) custom-call(f32[32,256]{1,0:T(8,128)S(1)} %collective-permute-done.14.one_ref, f32[32,768]{1,0:T(8,128)S(1)} %flux.6.local_ref, ...), custom_call_target="tpu_custom_call" | custom-call | flops 16777216 | bytes 1048576 | tf_op jit(solution)/shard_map/update/pallas_call | solution.py:639
  36.6 0.3 collective-permute-start.15
  36.9 2.8 %collective-permute-start.18 = (f32[40,128]{1,0:T(8,128)S(1)}, f32[40,128]{1,0:T(8,128)S(1)}, u32[]{:S(2)}, u32[]{:S(2)}) collective-permute-start(f32[40,128]{1,0:T(8,128)S(1)} %get-tuple-element.110), channel_id=1, source_target_pairs={{0,3},{1,2},{2,1},{3,0},{4,7},{5,6},{6,5},{7,4},{8,11},{9,10},{10,... | collective-permute-start | bytes 61448 | tf_op jit(solution)/shard_map/ppermute | solution.py:662
  39.6 0.0 collective-permute-start.16
  39.7 2.6 %collective-permute-start.17 = (f32[16,128]{1,0:T(8,128)S(1)}, f32[16,128]{1,0:T(8,128)S(1)}, u32[]{:S(2)}, u32[]{:S(2)}) collective-permute-start(f32[16,128]{1,0:T(8,128)S(1)} %get-tuple-element.109), channel_id=1, source_target_pairs={{0,5},{1,4},{2,7},{3,6},{4,1},{5,0},{6,3},{7,2},{8,13},{9,12},{10,... | collective-permute-start | bytes 24584 | tf_op jit(solution)/shard_map/ppermute | solution.py:662
  42.3 1.3 %own_sides.5 = (f32[32,128]{1,0:T(8,128)S(1)}, f32[32,1280]{1,0:T(8,128)S(1)}, f32[32,1024]{1,0:T(8,128)S(1)}, f32[32,256]{1,0:T(8,128)S(1)}) custom-call(bf16[64,768]{1,0:T(8,128)(2,1)S(1)} %get-tuple-element.111.stack_ref, bf16[768,128]{1,0:T(8,128)(2,1)S(1)} %get-tuple-element.68.hot_ref, s32[8,128]{1,0:T(8,128)S(1)} %get-tuple-element.69.case_ref, ...), custom_call_target="tpu_custom_call" | custom-call | flops 16777216 | bytes 1048576 | tf_op jit(solution)/shard_map/own_sides/pallas_call | solution.py:639
  43.6 0.0 collective-permute-done.17.u_ref
  43.7 0.0 collective-permute-done.15.w_ref
  43.7 0.0 collective-permute-done.18.x_ref
  43.7 0.1 relay.7
  43.7 0.3 collective-permute-start.19
  44.1 0.9 %flux.7.local_ref = f32[32,768]{1,0:T(8,128)S(1)} custom-call(f32[40,128]{1,0:T(8,128)S(1)} %collective-permute-done.15.w_ref, f32[16,128]{1,0:T(8,128)S(1)} %collective-permute-done.16.v_ref, f32[16,128]{1,0:T(8,128)S(1)} %collective-permute-done.17.u_ref, f32[40,128]{1,0:T(8,128)S(1)} %collective-permute-done.18.x_ref, ...), custom_call_target="tpu_custom_call" | custom-call | flops 16777216 | bytes 1048576 | tf_op jit(solution)/shard_map/flux/pallas_call | solution.py:639
  45.0 0.0 collective-permute-done.19.one_ref
  45.0 1.5 %update.7 = (f32[64,128]{1,0:T(8,128)}, f32[32,128]{1,0:T(8,128)S(1)}) custom-call(f32[32,256]{1,0:T(8,128)S(1)} %collective-permute-done.19.one_ref, f32[32,768]{1,0:T(8,128)S(1)} %flux.7.local_ref, f32[32,256]{1,0:T(8,128)S(1)} %get-tuple-element.115.target_ref, f32[8,512]{1,0:T(8,128)S(1)} %get-tuple-element.77.arrival_ref, ...), custom_call_target="tpu_custom_call" | custom-call | flops 16777216 | bytes 1048576 | tf_op jit(solution)/shard_map/update/pallas_call | solution.py:639
  46.5 11.0 %all_to_all.5 = f32[32,1,128]{2,1,0:T(1,128)S(1)} all-to-all(f32[32,1,128]{2,1,0:T(1,128)S(1)} %bitcast.14), channel_id=1, replica_groups=mesh['dom'=32] {'dom'}, dimensions={0} | all-to-all | bytes 32768 | tf_op jit(solution)/shard_map/all_to_all | solution.py:783
  57.5 0.8 %finish.1 = (f32[64,128]{1,0:T(8,128)}, f32[1,128]{1,0:T(1,128)}) custom-call(f32[32,128]{1,0:T(8,128)S(1)} %bitcast.13, f32[64,128]{1,0:T(8,128)S(1)} %copy-done.4, f32[128,128]{1,0:T(8,128)S(1)} %get-tuple-element.95.field_ref.first_ref, f32[128,128]{1,0:T(8,128)S(1)} %get-tuple-element.106.second_ref), custom_call_target="tpu_custom_call" | custom-call | flops 16777216 | bytes 1048576 | tf_op jit(solution)/shard_map/finish/pallas_call | solution.py:639
  (14 shorter events, 0.0 us)
Async XLA Ops:
  2.7 10.9 %collective-permute-start = (f32[88,128]{1,0:T(8,128)S(1)}, f32[88,128]{1,0:T(8,128)S(1)}, u32[]{:S(2)}, u32[]{:S(2)}) collective-permute-start(f32[88,128]{1,0:T(8,128)S(1)} %get-tuple-element.61), channel_id=1, source_target_pairs={{0,1},{1,0},{2,5},{3,4},{4,3},{5,2},{6,9},{7,8},{8,7},{9,6},{10,13... | collective-permute-start | bytes 135176 | tf_op jit(solution)/shard_map/ppermute | solution.py:665
  3.2 10.4 %collective-permute-start.3 = (f32[88,128]{1,0:T(8,128)S(1)}, f32[88,128]{1,0:T(8,128)S(1)}, u32[]{:S(2)}, u32[]{:S(2)}) collective-permute-start(f32[88,128]{1,0:T(8,128)S(1)} %get-tuple-element.64), channel_id=1, source_target_pairs={{0,3},{1,2},{2,1},{3,0},{4,7},{5,6},{6,5},{7,4},{8,11},{9,10},{10,... | collective-permute-start | bytes 135176 | tf_op jit(solution)/shard_map/ppermute | solution.py:662
  6.9 6.7 %collective-permute-start.1 = (f32[40,128]{1,0:T(8,128)S(1)}, f32[40,128]{1,0:T(8,128)S(1)}, u32[]{:S(2)}, u32[]{:S(2)}) collective-permute-start(f32[40,128]{1,0:T(8,128)S(1)} %get-tuple-element.62), channel_id=1, source_target_pairs={{0,3},{1,2},{2,1},{3,0},{4,9},{5,8},{6,11},{7,10},{8,5},{9,4},{10,... | collective-permute-start | bytes 61448 | tf_op jit(solution)/shard_map/ppermute | solution.py:665
  7.0 6.7 %collective-permute-start.2 = (f32[40,128]{1,0:T(8,128)S(1)}, f32[40,128]{1,0:T(8,128)S(1)}, u32[]{:S(2)}, u32[]{:S(2)}) collective-permute-start(f32[40,128]{1,0:T(8,128)S(1)} %get-tuple-element.63), channel_id=1, source_target_pairs={{0,5},{1,4},{2,7},{3,6},{4,1},{5,0},{6,3},{7,2},{8,13},{9,12},{10,... | collective-permute-start | bytes 61448 | tf_op jit(solution)/shard_map/ppermute | solution.py:662
  12.1 1.8 %copy-start.4 = (f32[64,128]{1,0:T(8,128)S(1)}, f32[64,128]{1,0:T(8,128)}, u32[]{:S(2)}) copy-start(f32[64,128]{1,0:T(8,128)} %guess_ref.1) | copy-start | bytes 98308
  12.1 1.8 %copy-start.6 = (f32[64,128]{1,0:T(8,128)S(1)}, f32[64,128]{1,0:T(8,128)}, u32[]{:S(2)}) copy-start(f32[64,128]{1,0:T(8,128)} %refs_6_.1) | copy-start | bytes 98308
  12.1 1.8 %copy-start.1 = (bf16[128,96]{1,0:T(8,128)(2,1)S(1)}, bf16[128,96]{1,0:T(8,128)(2,1)}, u32[]{:S(2)}) copy-start(bf16[128,96]{1,0:T(8,128)(2,1)} %constant.12.clone.interp_ref.interp_t_ref) | copy-start | bytes 73732
  12.1 1.8 %copy-start.3 = (f32[32,128]{1,0:T(8,128)S(1)}, f32[32,128]{1,0:T(8,128)}, u32[]{:S(2)}) copy-start(f32[32,128]{1,0:T(8,128)} %constant.14.clone.weight_ref) | copy-start | bytes 49156
  13.6 1.5 %copy-start = (bf16[64,64,128]{2,1,0:T(8,128)(2,1)S(1)}, bf16[64,64,128]{2,1,0:T(8,128)(2,1)}, u32[]{:S(2)}) copy-start(bf16[64,64,128]{2,1,0:T(8,128)(2,1)} %inverse_ref.7) | copy-start | bytes 3145732
  13.6 1.5 %copy-start.2 = (bf16[64,768]{1,0:T(8,128)(2,1)S(1)}, bf16[64,768]{1,0:T(8,128)(2,1)}, u32[]{:S(2)}) copy-start(bf16[64,768]{1,0:T(8,128)(2,1)} %constant.13.clone.lift_ref) | copy-start | bytes 294916
  13.6 1.5 %copy-start.5 = (f32[64,128]{1,0:T(8,128)S(1)}, f32[64,128]{1,0:T(8,128)}, u32[]{:S(2)}) copy-start(f32[64,128]{1,0:T(8,128)} %rest_0_.1) | copy-start | bytes 98308
  13.8 1.3 %collective-permute-start.4 = (f32[72,256]{1,0:T(8,128)S(1)}, f32[72,256]{1,0:T(8,128)S(1)}, u32[]{:S(2)}, u32[]{:S(2)}) collective-permute-start(f32[72,256]{1,0:T(8,128)S(1)} %relay.4), channel_id=1, source_target_pairs={{0,1},{1,0},{2,3},{3,2},{4,5},{5,4},{6,7},{7,6},{8,9},{9,8},{10,11... | collective-permute-start | bytes 221192 | tf_op jit(solution)/shard_map/ppermute | solution.py:662
  16.9 6.0 %collective-permute-start.5 = (f32[80,128]{1,0:T(8,128)S(1)}, f32[80,128]{1,0:T(8,128)S(1)}, u32[]{:S(2)}, u32[]{:S(2)}) collective-permute-start(f32[80,128]{1,0:T(8,128)S(1)} %get-tuple-element.85), channel_id=1, source_target_pairs={{0,1},{1,0},{2,5},{3,4},{4,3},{5,2},{6,9},{7,8},{8,7},{9,6},{10,13... | collective-permute-start | bytes 122888 | tf_op jit(solution)/shard_map/ppermute | solution.py:665
  17.3 5.6 %collective-permute-start.8 = (f32[80,128]{1,0:T(8,128)S(1)}, f32[80,128]{1,0:T(8,128)S(1)}, u32[]{:S(2)}, u32[]{:S(2)}) collective-permute-start(f32[80,128]{1,0:T(8,128)S(1)} %get-tuple-element.88), channel_id=1, source_target_pairs={{0,3},{1,2},{2,1},{3,0},{4,7},{5,6},{6,5},{7,4},{8,11},{9,10},{10,... | collective-permute-start | bytes 122888 | tf_op jit(solution)/shard_map/ppermute | solution.py:662
  18.4 4.5 %collective-permute-start.6 = (f32[32,128]{1,0:T(8,128)S(1)}, f32[32,128]{1,0:T(8,128)S(1)}, u32[]{:S(2)}, u32[]{:S(2)}) collective-permute-start(f32[32,128]{1,0:T(8,128)S(1)} %get-tuple-element.86), channel_id=1, source_target_pairs={{0,3},{1,2},{2,1},{3,0},{4,9},{5,8},{6,11},{7,10},{8,5},{9,4},{10,... | collective-permute-start | bytes 49160 | tf_op jit(solution)/shard_map/ppermute | solution.py:665
  19.1 3.8 %collective-permute-start.7 = (f32[32,128]{1,0:T(8,128)S(1)}, f32[32,128]{1,0:T(8,128)S(1)}, u32[]{:S(2)}, u32[]{:S(2)}) collective-permute-start(f32[32,128]{1,0:T(8,128)S(1)} %get-tuple-element.87), channel_id=1, source_target_pairs={{0,5},{1,4},{2,7},{3,6},{4,1},{5,0},{6,3},{7,2},{8,13},{9,12},{10,... | collective-permute-start | bytes 49160 | tf_op jit(solution)/shard_map/ppermute | solution.py:662
  23.0 1.5 %collective-permute-start.9 = (f32[64,256]{1,0:T(8,128)S(1)}, f32[64,256]{1,0:T(8,128)S(1)}, u32[]{:S(2)}, u32[]{:S(2)}) collective-permute-start(f32[64,256]{1,0:T(8,128)S(1)} %relay.5), channel_id=1, source_target_pairs={{0,1},{1,0},{2,3},{3,2},{4,5},{5,4},{6,7},{7,6},{8,9},{9,8},{10,11... | collective-permute-start | bytes 196616 | tf_op jit(solution)/shard_map/ppermute | solution.py:662
  26.1 7.7 %collective-permute-start.10 = (f32[40,128]{1,0:T(8,128)S(1)}, f32[40,128]{1,0:T(8,128)S(1)}, u32[]{:S(2)}, u32[]{:S(2)}) collective-permute-start(f32[40,128]{1,0:T(8,128)S(1)} %get-tuple-element.97), channel_id=1, source_target_pairs={{0,1},{1,0},{2,5},{3,4},{4,3},{5,2},{6,9},{7,8},{8,7},{9,6},{10,13... | collective-permute-start | bytes 61448 | tf_op jit(solution)/shard_map/ppermute | solution.py:665
  26.3 7.5 %collective-permute-start.13 = (f32[40,128]{1,0:T(8,128)S(1)}, f32[40,128]{1,0:T(8,128)S(1)}, u32[]{:S(2)}, u32[]{:S(2)}) collective-permute-start(f32[40,128]{1,0:T(8,128)S(1)} %get-tuple-element.100), channel_id=1, source_target_pairs={{0,3},{1,2},{2,1},{3,0},{4,7},{5,6},{6,5},{7,4},{8,11},{9,10},{10,... | collective-permute-start | bytes 61448 | tf_op jit(solution)/shard_map/ppermute | solution.py:662
  29.7 4.1 %collective-permute-start.11 = (f32[16,128]{1,0:T(8,128)S(1)}, f32[16,128]{1,0:T(8,128)S(1)}, u32[]{:S(2)}, u32[]{:S(2)}) collective-permute-start(f32[16,128]{1,0:T(8,128)S(1)} %get-tuple-element.98), channel_id=1, source_target_pairs={{0,3},{1,2},{2,1},{3,0},{4,9},{5,8},{6,11},{7,10},{8,5},{9,4},{10,... | collective-permute-start | bytes 24584 | tf_op jit(solution)/shard_map/ppermute | solution.py:665
  29.7 4.1 %collective-permute-start.12 = (f32[16,128]{1,0:T(8,128)S(1)}, f32[16,128]{1,0:T(8,128)S(1)}, u32[]{:S(2)}, u32[]{:S(2)}) collective-permute-start(f32[16,128]{1,0:T(8,128)S(1)} %get-tuple-element.99), channel_id=1, source_target_pairs={{0,5},{1,4},{2,7},{3,6},{4,1},{5,0},{6,3},{7,2},{8,13},{9,12},{10,... | collective-permute-start | bytes 24584 | tf_op jit(solution)/shard_map/ppermute | solution.py:662
  33.9 1.3 %collective-permute-start.14 = (f32[32,256]{1,0:T(8,128)S(1)}, f32[32,256]{1,0:T(8,128)S(1)}, u32[]{:S(2)}, u32[]{:S(2)}) collective-permute-start(f32[32,256]{1,0:T(8,128)S(1)} %relay.6), channel_id=1, source_target_pairs={{0,1},{1,0},{2,3},{3,2},{4,5},{5,4},{6,7},{7,6},{8,9},{9,8},{10,11... | collective-permute-start | bytes 98312 | tf_op jit(solution)/shard_map/ppermute | solution.py:662
  36.6 7.1 %collective-permute-start.15 = (f32[40,128]{1,0:T(8,128)S(1)}, f32[40,128]{1,0:T(8,128)S(1)}, u32[]{:S(2)}, u32[]{:S(2)}) collective-permute-start(f32[40,128]{1,0:T(8,128)S(1)} %get-tuple-element.107), channel_id=1, source_target_pairs={{0,1},{1,0},{2,5},{3,4},{4,3},{5,2},{6,9},{7,8},{8,7},{9,6},{10,13... | collective-permute-start | bytes 61448 | tf_op jit(solution)/shard_map/ppermute | solution.py:665
  36.9 6.8 %collective-permute-start.18 = (f32[40,128]{1,0:T(8,128)S(1)}, f32[40,128]{1,0:T(8,128)S(1)}, u32[]{:S(2)}, u32[]{:S(2)}) collective-permute-start(f32[40,128]{1,0:T(8,128)S(1)} %get-tuple-element.110), channel_id=1, source_target_pairs={{0,3},{1,2},{2,1},{3,0},{4,7},{5,6},{6,5},{7,4},{8,11},{9,10},{10,... | collective-permute-start | bytes 61448 | tf_op jit(solution)/shard_map/ppermute | solution.py:662
  39.6 4.0 %collective-permute-start.16 = (f32[16,128]{1,0:T(8,128)S(1)}, f32[16,128]{1,0:T(8,128)S(1)}, u32[]{:S(2)}, u32[]{:S(2)}) collective-permute-start(f32[16,128]{1,0:T(8,128)S(1)} %get-tuple-element.108), channel_id=1, source_target_pairs={{0,3},{1,2},{2,1},{3,0},{4,9},{5,8},{6,11},{7,10},{8,5},{9,4},{10,... | collective-permute-start | bytes 24584 | tf_op jit(solution)/shard_map/ppermute | solution.py:665
  39.7 4.0 %collective-permute-start.17 = (f32[16,128]{1,0:T(8,128)S(1)}, f32[16,128]{1,0:T(8,128)S(1)}, u32[]{:S(2)}, u32[]{:S(2)}) collective-permute-start(f32[16,128]{1,0:T(8,128)S(1)} %get-tuple-element.109), channel_id=1, source_target_pairs={{0,5},{1,4},{2,7},{3,6},{4,1},{5,0},{6,3},{7,2},{8,13},{9,12},{10,... | collective-permute-start | bytes 24584 | tf_op jit(solution)/shard_map/ppermute | solution.py:662
  43.7 1.3 %collective-permute-start.19 = (f32[32,256]{1,0:T(8,128)S(1)}, f32[32,256]{1,0:T(8,128)S(1)}, u32[]{:S(2)}, u32[]{:S(2)}) collective-permute-start(f32[32,256]{1,0:T(8,128)S(1)} %relay.7), channel_id=1, source_target_pairs={{0,1},{1,0},{2,3},{3,2},{4,5},{5,4},{6,7},{7,6},{8,9},{9,8},{10,11... | collective-permute-start | bytes 98312 | tf_op jit(solution)/shard_map/ppermute | solution.py:662

commit v3 on v2

--- a/solution.py
+++ b/solution.py
@@ -15,6 +15,7 @@
 peer_offsets = (1, -1, 2, -2, 3, -3, 4, -4)
 live_width = {1: 96, 2: 48, 3: 24, 4: 24}
 lanes = 128
+shifts = (0, 24, 48, 96)
 side_pad = 1024
 
 
@@ -196,78 +197,18 @@
     chip = me // 2
     core = me - 2 * chip
     near = jnp.where(lax.rem(chip, 2) == 1, -1, 1)
-    u_step = jnp.where(lax.rem(chip, 4) < 2, 2, -2)
-    w_there = (chip - near >= 0) & (chip - near < chips)
-    v_there = (chip - u_step >= 0) & (chip - u_step < chips)
-    return core, near, u_step, w_there, v_there
-
-
-def mixed_lanes():
-    lane = lax.broadcasted_iota(i32, (1, lanes), 1)
-    u_lanes = (lane < 24) | ((lane >= 48) & (lane < 72))
-    v_lanes = ((lane >= 24) & (lane < 48)) | ((lane >= 72) & (lane < 96))
-    return lane, u_lanes, v_lanes
-
-
-def fill_messages(sent, nf, w_ref, v_ref, u_ref, x_ref):
-    lane, u_lanes, v_lanes = mixed_lanes()
-    h = 32 * nf
-    x_ref[0:h] = sent[0:h, 0:128]
-    w_ref[0:h] = sent[0:h, 128:256]
-    for k in range(nf):
-        mixed = sent[32 * k : 32 * k + 32, 256:384]
-        top, bottom = mixed[0:16], mixed[16:32]
-        u_ref[16 * k : 16 * k + 16] = jnp.where(u_lanes, top, pltpu.roll(bottom, 24, 1))
-        v_ref[16 * k : 16 * k + 16] = jnp.where(v_lanes, top, pltpu.roll(bottom, 104, 1))
-        extra = mixed[0:8]
-        for g in range(1, 4):
-            moved = pltpu.roll(mixed[8 * g : 8 * g + 8], 128 - 32 * g, 1)
-            extra = jnp.where((lane >= 96 - 32 * g) & (lane < 128 - 32 * g), moved, extra)
-        x_ref[h + 8 * k : h + 8 * k + 8] = extra
-        w_ref[h + 8 * k : h + 8 * k + 8] = extra
-    if sent.shape[0] > h:
-        third = [sent[h : h + 1, 256:384], sent[h + 1 : h + 2, 256:384]]
-        for ref, low in ((x_ref, 0), (w_ref, 128)):
-            main = [sent[h : h + 1, low : low + 128], sent[h + 1 : h + 2, low : low + 128]]
-            ref[40 * nf : 40 * nf + 8] = rows_of(main + third, 8, lanes)
-        for ref in (u_ref, v_ref):
-            ref[16 * nf : 16 * nf + 8] = rows_of(third + third, 8, lanes)
-
-
-def received(nf, w_ref, v_ref, u_ref, x_ref):
-    lane, u_lanes, v_lanes = mixed_lanes()
-    h = 32 * nf
-    mixed = []
-    for k in range(nf):
-        u, v = u_ref[16 * k : 16 * k + 16], v_ref[16 * k : 16 * k + 16]
-        x, w = x_ref[h + 8 * k : h + 8 * k + 8], w_ref[h + 8 * k : h + 8 * k + 8]
-        far = jnp.concatenate(
-            [jnp.where(u_lanes, u, v), jnp.where(u_lanes, pltpu.roll(u, 104, 1), pltpu.roll(v, 24, 1))],
-            axis=0,
-        )
-        extra = jnp.where(lane < 112, x, w)
-        rolled = [extra]
-        for g in range(1, 4):
-            rolled.append(
-                jnp.where(lane < 112, pltpu.roll(x, 32 * g, 1), pltpu.roll(w, 32 * g, 1))
-            )
-        mixed.append(jnp.where(lane < 96, far, jnp.concatenate(rolled, axis=0)))
-    main, after = x_ref[0:h], w_ref[0:h]
-    if x_ref.shape[0] > 40 * nf:
-        low = 40 * nf
-        third = []
-        for row in (2, 3):
-            far = jnp.where(
-                u_lanes, u_ref[16 * nf + row : 16 * nf + row + 1], v_ref[16 * nf + row : 16 * nf + row + 1]
-            )
-            extra = jnp.where(
-                lane < 112, x_ref[low + row : low + row + 1], w_ref[low + row : low + row + 1]
-            )
-            third.append(jnp.where(lane < 96, far, extra))
-        mixed.append(rows_of(third, 8, lanes))
-        main = jnp.concatenate([main, x_ref[low : low + 8]], axis=0)
-        after = jnp.concatenate([after, w_ref[low : low + 8]], axis=0)
-    return main, after, cat(mixed, 0)
+    far = jnp.where(lax.rem(chip, 4) < 2, 1, -1)
+    end = (chip == 0) | (chip == chips - 1)
+    far_there = (chip - 2 * far >= 0) & (chip - 2 * far < chips)
+    return core, near, far, end, ~end, far_there
+
+
+def carried(core, near, far, near_there, far_there):
+    first = core == 0
+    return (
+        jnp.where(first, near, -near), jnp.where(first, far, -far),
+        first | near_there, first | far_there,
+    )
 
 
 def row_of(offset):
@@ -294,7 +235,8 @@
         hot_ref[lanes * f : lanes * f + lanes] = one_hot(column, lanes, lanes * f)
 
 
-def listed_part(rolled_ref, place, offset, low, high, valid):
+def listed_part(rolled_ref, shift, offset, low, high, valid):
+    place = shifts.index(shift)
     lane = lax.broadcasted_iota(i32, (1, lanes), 1)
     values = rolled_ref[pl.ds(8 * place + jnp.minimum(row_of(offset), 7), 1), :]
     return jnp.where((lane >= low) & (lane < high) & valid, values, -1)
@@ -303,8 +245,8 @@
 def send_setup_kernel(chips, *refs):
     sources, refs = refs[:12], refs[12:]
     hot_ref, case_ref, stack_ref, side_ref, rolled_ref = refs[:5]
-    messages, landed = refs[5:9], (*refs[14:22], *refs[9:13])
-    slot_ref, arrived = refs[13], refs[22]
+    sent_ref, landed = refs[5], (*refs[11:19], *refs[6:10])
+    slot_ref, arrived = refs[10], refs[19]
     copies = [
         pltpu.make_async_copy(source, target, arrived.at[k])
         for k, (source, target) in enumerate(zip(sources, landed))
@@ -319,31 +261,24 @@
     sides = elem_ref.shape[1]
     for k, ref in enumerate((elem_ref, dir_ref, sidecase_ref, kind_ref, partner_ref)):
         side_ref[k : k + 1, 0:sides] = ref[...]
-    core, near, u_step, w_there, v_there = where_am_i(chips)
+    core, near, far, end, near_there, far_there = where_am_i(chips)
     listed = jnp.concatenate([list_ref[...], jnp.full((8, 32), -1, i32)], axis=1)
-    shifts = (0, 24, 48, 72, 96, 64, 80)
     for place, shift in enumerate(shifts):
         rolled_ref[8 * place : 8 * place + 8] = (
             pltpu.roll(listed, shift, 1) if shift else listed
         )
-
-    def part(shift, offset, low, high, valid):
-        return listed_part(rolled_ref, shifts.index(shift), offset, low, high, valid)
-
-    always = core >= 0
-    flip = 1 - 2 * core
-    mixed = []
-    for tile, (step, there, extra) in enumerate(((near, always, 64), (-near, w_there, 80))):
-        cross = 2 * step + flip
-        direct = part(0, cross, 0, jnp.where(narrow(cross), 24, 96), there)
-        passed = part(96, 2 * step, 96, 128, there)
-        slot_ref[0:1, 128 * tile : 128 * tile + 128] = jnp.maximum(direct, passed)
-        mixed.append(part(extra, 2 * step, extra + 32, extra + 48, there))
-    for step, there, low in ((u_step, always, 0), (-u_step, v_there, 24)):
-        cross = 2 * step + flip
-        mixed.append(part(low, cross, low, low + 24, there & narrow(cross)))
-        mixed.append(part(low + 48, 2 * step, low + 48, low + 72, there))
-    slot_ref[0:1, 256:384] = functools.reduce(jnp.maximum, mixed)
+    part = functools.partial(listed_part, rolled_ref)
+    other = 1 - core
+    step, step_two, there, there_two = carried(other, near, far, near_there, far_there)
+    cross, cross_two = 2 * step + other - core, 4 * step_two + other - core
+    first = (
+        part(0, cross_two, 0, 24, there_two & narrow(cross_two)),
+        part(24, 4 * step_two, 24, 48, there_two),
+        part(48, 2 * step, 48, 96, there),
+        part(96, cross, 96, 120, there & narrow(cross)),
+    )
+    slot_ref[0:1, 0:128] = functools.reduce(jnp.maximum, first)
+    slot_ref[0:1, 128:256] = part(0, cross, 0, 96, there & ~narrow(cross))
     column, slot_case = slot_attributes(side_ref, slot_ref[0:1, :])
     case_ref[0:1, :] = slot_case
     fill_one_hot(hot_ref, column)
@@ -354,13 +289,25 @@
     stack = jnp.concatenate([stack, jnp.concatenate([scalars] * 6, axis=1)], axis=0)
     stack_ref[...] = stack
     sent = gather_message(stack, hot_ref[...], interp_ref[...], slot_case, 2)
-    fill_messages(sent, 2, *messages)
-
-
-def own_setup_kernel(chips, side_ref, rolled_ref, hot_ref, case_ref):
-    core = where_am_i(chips)[0]
-    slots = listed_part(rolled_ref, 0, 1 - 2 * core, 0, 96, core >= 0)
-    column, slot_case = slot_attributes(side_ref, slots)
+    sent_ref[...] = sent
+
+
+def own_setup_kernel(chips, side_ref, rolled_ref, hot_ref, case_ref, slot_ref):
+    core, near, far, end, near_there, far_there = where_am_i(chips)
+    part = functools.partial(listed_part, rolled_ref)
+    flip = 1 - 2 * core
+    step, step_two, there, there_two = carried(core, near, far, near_there, far_there)
+    cross, cross_two = 2 * step + flip, 4 * step_two + flip
+    slot_ref[0:1, 0:128] = jnp.maximum(
+        part(0, 4 * step_two, 0, 24, there_two),
+        part(24, cross_two, 24, 48, there_two & narrow(cross_two)),
+    )
+    slot_ref[0:1, 128:256] = jnp.maximum(
+        part(0, 2 * step, 0, 48, there), part(96, cross, 96, 120, there & narrow(cross))
+    )
+    slot_ref[0:1, 256:384] = part(0, cross, 0, 96, there & ~narrow(cross))
+    slot_ref[0:1, 384:512] = part(0, flip, 0, 96, core >= 0)
+    column, slot_case = slot_attributes(side_ref, slot_ref[0:1, :])
     case_ref[0:1, :] = slot_case
     fill_one_hot(hot_ref, column)
 
@@ -371,30 +318,31 @@
     )
 
 
-def own_sides_kernel(
-    nf, stack_ref, hot_ref, case_ref, interp_ref, own_hot_ref, partner_hot_ref, far_hot_ref, info_ref,
-    arrival_ref, own_ref, mine_ref, other_ref, target_ref,
-):
-    own_kernel(nf, stack_ref, hot_ref, case_ref, interp_ref, own_ref)
-    sides_kernel(
-        nf, stack_ref, interp_ref, own_hot_ref, partner_hot_ref, far_hot_ref, info_ref, arrival_ref,
-        mine_ref, other_ref, target_ref,
-    )
-
-
-def relay_kernel(nf, w_ref, v_ref, u_ref, x_ref, own_ref, *rest):
+def carry_kernel(sent_ref, own_ref, two_ref, one_ref):
+    lane = lax.broadcasted_iota(i32, (1, lanes), 1)
+    sent = sent_ref[:, 0:128]
+    handed = jnp.where((lane >= 48) & (lane < 96), pltpu.roll(sent, 48, 1), 0.0)
+    two_ref[...] = own_ref[:, 0:128] + handed
+    one_ref[:, 0:128] = own_ref[:, 128:256] + jnp.where(lane >= 48, sent, 0.0)
+    one_ref[:, 128:256] = own_ref[:, 256:384] + sent_ref[:, 128:256]
+
+
+def relay_kernel(chips, one_ref, two_ref, own_ref, *rest):
     out_ref = rest[-1]
+    core, near, far, end, near_there, far_there = where_am_i(chips)
     lane = lax.broadcasted_iota(i32, (1, lanes), 1)
-    main, after, mixed = received(nf, w_ref, v_ref, u_ref, x_ref)
-    out_ref[:, 0:128] = jnp.where(lane < 96, own_ref[...], main)
-    out_ref[:, 128:256] = jnp.where(lane < 32, pltpu.roll(after, 32, 1), mixed)
+    one, two_away = one_ref[:, 0:128], two_ref[...]
+    out_ref[:, 0:128] = own_ref[:, 384:512]
+    passed = jnp.where(lane < 24, pltpu.roll(two_away, 56, 1), two_away)
+    out_ref[:, 128:256] = jnp.where((lane < 48) & ~(end & (core == 1)), passed, one)
+    out_ref[:, 256:384] = one_ref[:, 128:256]
 
 
 def setup_kernel(
     chips, coef_ref, level_ref, side_ref,
     info_ref, own_hot_ref, partner_hot_ref, far_hot_ref, arrival_ref, arrival_hot_ref,
 ):
-    core, near, u_step, w_there, v_there = where_am_i(chips)
+    core, near, far, end, near_there, far_there = where_am_i(chips)
     elem, direction, case = side_ref[0:1], side_ref[1:2], side_ref[2:3]
     kind, partner = side_ref[3:4], side_ref[4:5]
     live = lax.broadcasted_iota(i32, (1, side_pad), 1) < 930
@@ -428,19 +376,40 @@
 
     sought = jnp.where(live & (kind == 0), partner, -7)
     place = lax.broadcasted_iota(i32, (lanes, side_pad), 0)
-    flip = 1 - 2 * core
-    pair, after = 2 * near + flip, flip - 2 * near
-    segments = (
-        ((0, jnp.where(narrow(pair), 24, 96), -pair, 0), (96, 120, -(2 * u_step + flip), 0)),
-        ((0, jnp.where(narrow(after), 24, 96), -after, 0), (96, 120, -(flip - 2 * u_step), 0)),
-        ((0, 96, -flip, 0), (96, 128, -2 * near, 0)),
-        ((0, 32, 2 * near, 0), (48, 72, -2 * u_step, 0), (72, 96, 2 * u_step, 0),
-         (96, 112, -2 * near, 32), (112, 128, 2 * near, 32)),
-    )
+    def arrives(carrier):
+        last = end & (carrier == 1)
+        back = jnp.where((carrier == 0) | end, -near, near)
+        back_two = jnp.where(carrier == 0, -far, far)
+        turn = 2 * core - 1
+        return (
+            2 * back, 2 * back + turn, 4 * back_two, 4 * back_two + turn,
+            ~(end & (carrier == 0)), ~last, last,
+        )
+
+    def span(low, high, valid):
+        return low, jnp.where(valid, high, low)
+
+    segments = []
+    for mine, carrier in ((True, core), (False, 1 - core)):
+        straight, cross, straight_two, cross_two, there, there_two, last = arrives(carrier)
+        slim, wide = there & narrow(cross), there & ~narrow(cross)
+        at_first = (last & (core != 1)) | (~last & (carrier == core))
+        if mine:
+            two_parts = ((*span(48, 72, there_two & narrow(cross_two)), cross_two),
+                         (*span(72, 96, there_two), straight_two))
+        else:
+            segments.append(((0, 96, 2 * core - 1),))
+            two_parts = ((*span(0, 24, there_two), straight_two),
+                         (*span(24, 48, there_two & narrow(cross_two)), cross_two))
+        segments.append((
+            (*span(0, 48, there & at_first), straight), (*span(48, 96, there & ~at_first), straight),
+            (*span(96, 120, slim), cross), *two_parts,
+        ))
+        segments.append(((*span(0, 96, wide), cross),))
     for tile, parts in enumerate(segments):
         slot = jnp.full((lanes, side_pad), -5, i32)
-        for low, high, offset, begin in parts:
-            entry = 930 + 96 * row_of(offset) + begin - low
+        for low, high, offset in parts:
+            entry = 930 + 96 * row_of(offset) - low
             slot = jnp.where((place >= low) & (place < high), entry + place, slot)
         arrival_hot_ref[lanes * tile : lanes * tile + lanes] = jnp.where(
             slot == sought, 1.0, 0.0
@@ -449,13 +418,13 @@
     valid = target[3:4] > 0.5
     target_column = jnp.where(valid, (target[1:2] * 128.0 + target[0:1]).astype(i32), -1)
     fill_one_hot(own_hot_ref, jnp.concatenate([own_column, target_column[:, 0:256]], axis=1))
-    fill_one_hot(far_hot_ref, target_column[:, 256:512])
+    fill_one_hot(far_hot_ref, target_column[:, 256:640])
     info_ref[:, side_pad:] = rows_of(
         [jnp.zeros((1, 256), f32)] * 4 + [jnp.where(valid, target[2:3], -1.0)[:, 0:256]], 8, 256
     )
     arrival_ref[...] = rows_of(
         [jnp.where(valid, target[2:3], -1.0), target[4:5] + target[5:6] + target[6:7], target[7:8]],
-        8, 512,
+        8, 640,
     )
 
 
@@ -469,7 +438,7 @@
     for hot_ref, case, out_ref in (
         (own_hot_ref, info_ref[4:5], mine_ref),
         (partner_hot_ref, info_ref[5:6, 0:side_pad], other_ref),
-        (far_hot_ref, arrival_ref[0:1, 256:512], target_ref),
+        (far_hot_ref, arrival_ref[0:1, 256:640], target_ref),
     ):
         got = dot(stack, hot_ref[...])
         out_ref[...] = fields_case(table, got[:h] + got[h:], case.astype(i32), nf)
@@ -504,18 +473,17 @@
 
 
 def flux_kernel(
-    nf, w_ref, v_ref, u_ref, x_ref, mine_ref, other_ref, info_ref, arrival_ref, weight_ref, interp_ref,
+    nf, chips, one_ref, two_ref, mine_ref, other_ref, info_ref, arrival_ref, weight_ref, interp_ref,
     own_hot_ref, *rest,
 ):
     h = 32 * nf
+    core, near, far, end, near_there, far_there = where_am_i(chips)
     lane = lax.broadcasted_iota(i32, (1, lanes), 1)
-    main, after, mixed = received(nf, w_ref, v_ref, u_ref, x_ref)
+    two_away = two_ref[...]
+    kept = jnp.where(lane < 72, two_away, pltpu.roll(two_away, 72, 1))
+    inside = (lane >= 48) & (lane < 96) & ~(end & (core == 1))
     got = jnp.concatenate(
-        [
-            jnp.where(lane < 96, main, pltpu.roll(mixed, 96, 1)),
-            jnp.where(lane < 96, after, pltpu.roll(mixed, 72, 1)),
-        ],
-        axis=1,
+        [jnp.where(inside, kept, one_ref[:, 0:128]), one_ref[:, 128:256]], axis=1
     )
     if got.shape[0] > h:
         sum_ref, halo_ref = rest
@@ -554,22 +522,21 @@
     else:
         halo_ref, *rest = rest
     if nf_next:
-        trace_ref, interp_ref, hot_ref, case_ref, new_ref, stack_ref, *rest = rest
-        messages, rest = rest[:4], rest[4:]
+        trace_ref, interp_ref, hot_ref, case_ref, new_ref, stack_ref, sent_ref, *rest = rest
     else:
         new_ref, part_ref, *rest = rest
     hold_ref = rest[-1]
     h = 32 * nf
     if residual:
         halo = halo_coefs(
-            arrival_ref[1:2, 256:512], arrival_ref[2:3, 256:512],
+            arrival_ref[1:2, 256:640], arrival_ref[2:3, 256:640],
             one_ref[h : h + 1], one_ref[h + 1 : h + 2],
         )
-        rest[0][...] = rows_of(halo, 8, 256)
+        rest[0][...] = rows_of(halo, 8, 384)
     else:
         halo = (halo_ref[0:1], halo_ref[1:2])
     total = local_ref[...] + side_flux(
-        nf, target_ref, one_ref, (halo[0], halo[0], halo[1], halo[1]), arrival_ref[0:1, 256:512],
+        nf, target_ref, one_ref, (halo[0], halo[0], halo[1], halo[1]), arrival_ref[0:1, 256:640],
         weight_ref, interp_t_ref, far_hot_ref[...],
     )
     coef, size, volume_scale, normal_scale = element_rows(coef_ref, level_ref)
@@ -599,7 +566,7 @@
         stack = face_stack(trace_ref, new[:nf_next], normal_scale, nf_next)
         stack_ref[...] = stack
         sent = gather_message(stack, hot_ref[...], interp_ref[...], case_ref[0:1], nf_next)
-        fill_messages(sent, nf_next, *messages)
+        sent_ref[...] = sent
     else:
         before, after = field_ref[...], new[0]
         before = jnp.sum(jnp.sum(before * before, axis=1, keepdims=True), axis=0, keepdims=True)
@@ -658,97 +625,96 @@
     coef = coefficient.reshape(1, lanes)
     level = refine_level.reshape(1, lanes)
 
-    def swap(x, mask):
-        return lax.ppermute(x, "dom", [(i, i ^ mask) for i in range(devices)])
-
-    def swap_chips(x, to):
-        return lax.ppermute(
-            x, "dom",
-            [(2 * c + k, 2 * to.get(c, c) + 1 - k) for c in range(chips) for k in range(2)],
-        )
-
-    after_pair = {c: c + 1 if c % 2 else c - 1 for c in range(1, chips - 1)}
-    two_away = {c: c + 2 if c % 4 >= 2 else c - 2 for c in range(2, chips - 2)}
-    two_away.update({c: c ^ 1 for c in (0, 1, chips - 2, chips - 1)})
-
-    def exchange(messages, nf, work):
-        w, v, u, x = messages
-        first = (swap_chips(w, after_pair), swap_chips(v, two_away), swap(u, 5), swap(x, 3))
-        own, *rest = work()
-        (one,) = run(
-            functools.partial(relay_kernel, nf), [((own.shape[0], 256), f32)],
-            [*first, own, *rest[:1]], "relay",
-        )
-        return first, swap(one, 1), rest
-
-    def message_shapes(nf, extra=0):
-        return [((rows * nf + extra, lanes), f32) for rows in (40, 16, 16, 40)]
+    def permute(x, to):
+        return lax.ppermute(x, "dom", sorted(to.items()))
+
+    swapped = {i: i ^ 1 for i in range(devices)}
+    two_away, one_away = {}, {}
+    for c in range(chips):
+        two_away[2 * c] = 2 * (c ^ 2)
+        one_away[2 * c] = 2 * (c ^ 1)
+        over = c + 2 if c % 4 >= 2 else c - 2
+        two_away[2 * c + 1] = 2 * (over if 0 <= over < chips else c ^ 1) + 1
+        if 0 < c < chips - 1:
+            one_away[2 * c + 1] = 2 * (c + 1 if c % 2 else c - 1) + 1
+    for c in (0, chips - 1):
+        one_away[2 * (c ^ 1)] = 2 * c + 1
+        one_away[2 * c + 1] = 2 * c
+
+    def exchange(sent, nf, own_work, work):
+        rows = sent.shape[0]
+        (own,) = own_work()
+        two_out, one_out = run(
+            carry_kernel, [((rows, lanes), f32), ((rows, 256), f32)], [permute(sent, swapped), own],
+            "carry",
+        )
+        arrivals = permute(one_out, one_away), permute(two_out, two_away)
+        made = work()
+        (last,) = run(
+            functools.partial(relay_kernel, chips), [((rows, 384), f32)],
+            [*arrivals, own, *made[:1]], "relay",
+        )
+        return arrivals, permute(last, swapped), made
 
     sides = [x.reshape(1, -1) for x in (side_elem, side_dir, side_case, side_kind, partner)]
     first = [*sides, send_list, start_vector, initial_guess, coef, level, trace, interp]
-    hot, case, stack, sides, rolled, *rest = run(
+    hot, case, stack, sides, rolled, sent, coef, level, trace, interp = run(
         functools.partial(send_setup_kernel, chips),
-        [((768, 384), bf16), ((8, 384), i32), ((144, 768), bf16), ((8, side_pad), i32), ((56, lanes), i32),
-         *message_shapes(2, 8), *((x.shape, x.dtype) for x in first[8:])],
+        [((768, 256), bf16), ((8, 256), i32), ((144, 768), bf16), ((8, side_pad), i32), ((32, lanes), i32),
+         ((72, 256), f32), *((x.shape, x.dtype) for x in first[8:])],
         first,
         "send_setup",
         scratch=[
-            pltpu.VMEM((8, 384), i32),
+            pltpu.VMEM((8, 256), i32),
             *(pltpu.VMEM(x.shape, x.dtype) for x in first[:8]), pltpu.SemaphoreType.DMA((len(first),)),
         ],
         placed=False,
     )
-    messages, (coef, level, trace, interp) = rest[:4], rest[4:]
+    own_slots = run(
+        functools.partial(own_setup_kernel, chips),
+        [((768, 512), bf16), ((8, 512), i32)],
+        [sides, rolled],
+        "own_setup",
+        scratch=[pltpu.VMEM((8, 512), i32)],
+    )
     fields = jnp.concatenate([start_vector, initial_guess], axis=0)
     history = []
     for turn, nf in enumerate((2, 2, 1, 1)):
         h = 32 * nf
-        sides_out = [((h, side_pad + 256), f32), ((h, side_pad), f32), ((h, 256), f32)]
-        own_out = [((h if turn else h + 8, lanes), f32)]
-
-        def first_work():
-            own_slots = run(
-                functools.partial(own_setup_kernel, chips),
-                [((768, lanes), bf16), ((8, lanes), i32)],
-                [sides, rolled],
-                "own_setup",
+        def own_work():
+            return run(
+                functools.partial(own_kernel, nf),
+                [((sent.shape[0], 512), f32)],
+                [stack, *own_slots, interp],
+                "own",
             )
-            made = run(
-                functools.partial(setup_kernel, chips),
-                [((8, side_pad + 256), f32), ((768, side_pad + 256), bf16), ((768, side_pad), bf16),
-                 ((768, 256), bf16), ((8, 512), f32)],
-                [coef, level, sides],
-                "setup",
-                scratch=[pltpu.VMEM((512, side_pad), bf16)],
-            )
-            (own,) = run(
-                functools.partial(own_kernel, nf), own_out, [stack, *own_slots, interp], "own"
-            )
-            return [own, *made, *own_slots]
-
-        def later_work():
+
+        def side_work():
             return run(
-                functools.partial(own_sides_kernel, nf),
-                own_out + sides_out,
-                [stack, *own_slots, interp, own_hot, partner_hot, far_hot, info, arrival],
-                "own_sides",
-            )
-
-        arrivals, one, rest = exchange(messages, nf, later_work if turn else first_work)
-        if turn == 0:
-            info, own_hot, partner_hot, far_hot, arrival, *own_slots = rest
-            mine, others, targets = run(
                 functools.partial(sides_kernel, nf),
-                sides_out,
+                [((h, side_pad + 256), f32), ((h, side_pad), f32), ((h, 384), f32)],
                 [stack, interp, own_hot, partner_hot, far_hot, info, arrival],
                 "sides",
             )
-        else:
-            mine, others, targets = rest
-        halo_out = [((8, 256), f32)] if turn == 0 else []
+
+        def first_work():
+            return run(
+                functools.partial(setup_kernel, chips),
+                [((8, side_pad + 256), f32), ((768, side_pad + 256), bf16), ((768, side_pad), bf16),
+                 ((768, 384), bf16), ((8, 640), f32)],
+                [coef, level, sides],
+                "setup",
+                scratch=[pltpu.VMEM((640, side_pad), bf16)],
+            )
+
+        arrivals, last, made = exchange(sent, nf, own_work, side_work if turn else first_work)
+        if turn == 0:
+            info, own_hot, partner_hot, far_hot, arrival = made
+            made = side_work()
+        mine, others, targets = made
         sums, *made = run(
-            functools.partial(flux_kernel, nf),
-            [((h, 768), f32)] + halo_out,
+            functools.partial(flux_kernel, nf, chips),
+            [((h, 768), f32)] + ([] if turn else [((8, 256), f32)]),
             [*arrivals, mine, others, info, arrival, weight, interp_t, own_hot]
             + ([near_halo] if turn else []),
             "flux",
@@ -757,24 +723,24 @@
             near_halo = made[0]
         nf_next = (2, 1, 1, 0)[turn]
         ins = [
-            one, sums, targets, arrival, far_hot, weight, interp_t, lift,
+            last, sums, targets, arrival, far_hot, weight, interp_t, lift,
             fields, coef, level, block_inverse, far_halo if turn else rhs_field,
         ]
         outs = [((64 * nf, lanes), f32)]
         if nf_next:
             ins += [trace, interp, hot, case]
-            outs += [((64 * nf_next, 768), bf16)] + message_shapes(nf_next)
+            outs += [((64 * nf_next, 768), bf16), ((32 * nf_next, 256), f32)]
         else:
             outs += [((devices, lanes), f32)]
         made = run(
             functools.partial(update_kernel, nf, nf_next, turn == 0),
-            outs + halo_out, ins, "update",
+            outs + ([] if turn else [((8, 384), f32)]), ins, "update",
             scratch=[pltpu.VMEM((64 * nf, lanes), f32)],
         )
         if turn == 0:
             far_halo = made[-1]
         if nf_next:
-            fields, stack, *messages = made[:6]
+            fields, stack, sent = made[:3]
             history.append(fields)
             if nf_next < nf:
                 fields = fields[:64]

time: 58.6 us -> 56.8 us (0.969)
  starting transfers between devices: 24.5 us -> 15.9 us
  waiting for transfers between devices: 0.4 us -> 3.76 us
  Pallas kernels: 21.4 us -> 23.4 us
  blocking collectives: 11 us -> 12.5 us
    ppermute x20 -> x16, starting transfers between devices: 24.5 us -> 15.9 us  [permute(): return lax.ppermute(x, 'dom', sorted(to.items()))]
    ppermute x20 -> x16, waiting for transfers between devices: 0.4 us -> 3.76 us  [permute(): return lax.ppermute(x, 'dom', sorted(to.items()))]
    pallas_call x21 -> x28, Pallas kernels: 21.4 us -> 23.4 us  [run(): pl.pallas_call(body, out_shape=[(pltpu.VMEM if kept else jax.ShapeDtypeSt...]
    all_to_all x1, blocking collectives: 11 us -> 12.5 us  [local(): lax.all_to_all(parts.reshape(devices, 1, lanes), 'dom', 0, 0)]
  transfers between devices with their start and end apart: 20 -> 16, of which waited for: 2 -> 9; matrix products, arithmetic and copies ran while one was open for 0% -> 0% of each run, Pallas kernels for 20% -> 24%
where the time goes in v3:
time: 56.8 us; the launch traced here: 56.6 us
  Pallas kernels  23.4 us (41%)
  starting transfers between devices  15.9 us (28%)
  blocking collectives  12.5 us (22%)
  waiting for transfers between devices  3.76 us (7%)
  between operations  0.89 us (2%)
    pallas_call x28, Pallas kernels, run(): pl.pallas_call(body, out_shape=[(pltpu.VMEM if kept else jax.ShapeDtypeSt...  23.4 us
    ppermute x16, starting transfers between devices, permute(): return lax.ppermute(x, 'dom', sorted(to.items()))  15.9 us
    all_to_all x1, blocking collectives, local(): lax.all_to_all(parts.reshape(devices, 1, lanes), 'dom', 0, 0)  12.5 us
    ppermute x16, waiting for transfers between devices, permute(): return lax.ppermute(x, 'dom', sorted(to.items()))  3.76 us
  transfers between devices with their start and end apart: 16, of which 9 were waited for; matrix products, arithmetic and copies ran while one was open for 0% of the time, Pallas kernels for 24%

profile of v3, /device:TPU:0, one launch (start us, length us, event | category | flops | bytes accessed | tf_op | source)
XLA Modules:
  0.0 56.6 jit_solution(10238991600638859362)
XLA Ops:
  0.6 2.0 %send_setup.1 = (bf16[768,256]{1,0:T(8,128)(2,1)S(1)}, s32[8,256]{1,0:T(8,128)S(1)}, bf16[144,768]{1,0:T(8,128)(2,1)S(1)}, s32[8,1024]{1,0:T(8,128)S(1)}, s32[32...) custom-call(s32[1,930]{1,0:T(1,128)} %bitcast.15, ...), custom_call_target="tpu_custom_call" | custom-call | flops 16777216 | bytes 1048576 | tf_op jit(solution)/shard_map/send_setup/pallas_call | solution.py:606
  2.6 0.5 collective-permute-start
  3.1 0.5 own_setup.1
  3.6 0.5 own.4.own_ref
  4.1 0.1 carry.4
  4.2 2.8 %collective-permute-start.1 = (f32[72,256]{1,0:T(8,128)S(1)}, f32[72,256]{1,0:T(8,128)S(1)}, u32[]{:S(2)}, u32[]{:S(2)}) collective-permute-start(f32[72,256]{1,0:T(8,128)S(1)} %get-tuple-element.61), channel_id=1, source_target_pairs={{0,2},{1,0},{2,1},{3,5},{4,6},{5,3},{6,4},{7,9},{8,10},{9,7},{10,8... | collective-permute-start | bytes 221192 | tf_op jit(solution)/shard_map/ppermute | solution.py:629
  7.0 1.5 %collective-permute-start.2 = (f32[72,128]{1,0:T(8,128)S(1)}, f32[72,128]{1,0:T(8,128)S(1)}, u32[]{:S(2)}, u32[]{:S(2)}) collective-permute-start(f32[72,128]{1,0:T(8,128)S(1)} %get-tuple-element.62), channel_id=1, source_target_pairs={{0,4},{1,3},{2,6},{3,1},{4,0},{5,9},{6,2},{7,11},{8,12},{9,5},{10,... | collective-permute-start | bytes 110600 | tf_op jit(solution)/shard_map/ppermute | solution.py:629
  8.5 1.9 %setup.1 = (f32[8,1280]{1,0:T(8,128)S(1)}, bf16[768,1280]{1,0:T(8,128)(2,1)S(1)}, bf16[768,1024]{1,0:T(8,128)(2,1)S(1)}, bf16[768,384]{1,0:T(8,128)(2,1)S(1)}, f32[8,640]{1,0:T(8,128)S(1)}) custom-call(f32[1,128]{1,0:T(1,128)S(1)} %get-tuple-element.63.coef_ref, s32[1,128]{1,0:T(1,128)S(1)} %get-tuple-element.64.level_ref, ...), custom_call_target="tpu_custom_call" | custom-call | flops 16777216 | bytes 1048576 | tf_op jit(solution)/shard_map/setup/pallas_call | solution.py:606
  10.4 0.0 copy-start.4
  10.4 0.0 copy-start.6
  10.4 0.0 copy-start.1
  10.4 0.0 copy-start.3
  10.4 1.5 %sides.4 = (f32[64,1280]{1,0:T(8,128)S(1)}, f32[64,1024]{1,0:T(8,128)S(1)}, f32[64,384]{1,0:T(8,128)S(1)}) custom-call(bf16[144,768]{1,0:T(8,128)(2,1)S(1)} %get-tuple-element.55.stack_ref, bf16[128,96]{1,0:T(8,128)(2,1)S(1)} %get-tuple-element.60.interp_ref.rest_2_, bf16[768,1280]{1,0:T(8,128)(2,1)S(1)} %get-tuple-element.66.own_hot_ref, ...), custom_call_target="tpu_custom_call" | custom-call | flops 16777216 | bytes 1048576 | tf_op jit(solution)/shard_map/sides/pallas_call | solution.py:606
  11.9 0.0 copy-start
  11.9 0.0 copy-start.2
  12.0 0.0 copy-start.5
  12.0 0.0 collective-permute-done.1.one_ref
  12.0 0.1 relay.4
  12.1 0.1 collective-permute-start.3
  12.2 1.0 %flux.4 = (f32[64,768]{1,0:T(8,128)S(1)}, f32[8,256]{1,0:T(8,128)S(1)}) custom-call(f32[72,256]{1,0:T(8,128)S(1)} %collective-permute-done.1.one_ref, f32[72,128]{1,0:T(8,128)S(1)} %collective-permute-done.2.two_ref, f32[64,1280]{1,0:T(8,128)S(1)} %get-tuple-element.70.mine_ref, f32[64,1024]{1,0:T(8,128)S(1)} %get-tuple-element.71.other_ref, ...), custom_call_target="tpu_custom_call" | custom-call | flops 16777216 | bytes 1048576 | tf_op jit(solution)/shard_map/flux/pallas_call | solution.py:606
  13.3 0.2 collective-permute-done.3.one_ref
  13.5 1.8 %update.4 = (f32[128,128]{1,0:T(8,128)S(1)}, bf16[128,768]{1,0:T(8,128)(2,1)S(1)}, f32[64,256]{1,0:T(8,128)S(1)}, f32[8,384]{1,0:T(8,128)S(1)}) custom-call(f32[72,384]{1,0:T(8,128)S(1)} %collective-permute-done.3.one_ref, f32[64,768]{1,0:T(8,128)S(1)} %get-tuple-element.72.local_ref, f32[64,384]{1,0:T(8,128)S(1)} %get-tuple-element.73.target_ref, ...), custom_call_target="tpu_custom_call" | custom-call | flops 16777216 | bytes 1048576 | tf_op jit(solution)/shard_map/update/pallas_call | solution.py:606
  15.2 0.4 collective-permute-start.4
  15.6 0.5 own.5.own_ref
  16.1 0.5 collective-permute-done.4.sent_ref
  16.6 0.1 carry.5
  16.6 0.6 %collective-permute-start.5 = (f32[64,256]{1,0:T(8,128)S(1)}, f32[64,256]{1,0:T(8,128)S(1)}, u32[]{:S(2)}, u32[]{:S(2)}) collective-permute-start(f32[64,256]{1,0:T(8,128)S(1)} %get-tuple-element.79), channel_id=1, source_target_pairs={{0,2},{1,0},{2,1},{3,5},{4,6},{5,3},{6,4},{7,9},{8,10},{9,7},{10,8... | collective-permute-start | bytes 196616 | tf_op jit(solution)/shard_map/ppermute | solution.py:629
  17.2 1.9 %collective-permute-start.6 = (f32[64,128]{1,0:T(8,128)S(1)}, f32[64,128]{1,0:T(8,128)S(1)}, u32[]{:S(2)}, u32[]{:S(2)}) collective-permute-start(f32[64,128]{1,0:T(8,128)S(1)} %get-tuple-element.80), channel_id=1, source_target_pairs={{0,4},{1,3},{2,6},{3,1},{4,0},{5,9},{6,2},{7,11},{8,12},{9,5},{10,... | collective-permute-start | bytes 98312 | tf_op jit(solution)/shard_map/ppermute | solution.py:629
  19.2 1.5 %sides.5 = (f32[64,1280]{1,0:T(8,128)S(1)}, f32[64,1024]{1,0:T(8,128)S(1)}, f32[64,384]{1,0:T(8,128)S(1)}) custom-call(bf16[128,768]{1,0:T(8,128)(2,1)S(1)} %get-tuple-element.78.stack_ref, bf16[128,96]{1,0:T(8,128)(2,1)S(1)} %get-tuple-element.60.interp_ref.rest_2_, bf16[768,1280]{1,0:T(8,128)(2,1)S(1)} %get-tuple-element.66.own_hot_ref, ...), custom_call_target="tpu_custom_call" | custom-call | flops 16777216 | bytes 1048576 | tf_op jit(solution)/shard_map/sides/pallas_call | solution.py:606
  20.6 0.7 %collective-permute-done.6.two_ref = f32[64,128]{1,0:T(8,128)S(1)} collective-permute-done((f32[64,128]{1,0:T(8,128)S(1)}, f32[64,128]{1,0:T(8,128)S(1)}, u32[]{:S(2)}, u32[]{:S(2)}) %collective-permute-start.6) | collective-permute-done | bytes 32800 | tf_op jit(solution)/shard_map/ppermute | solution.py:629
  21.3 0.0 collective-permute-done.5.one_ref
  21.3 0.1 relay.5
  21.4 0.5 collective-permute-start.7
  21.9 1.1 %flux.5.local_ref = f32[64,768]{1,0:T(8,128)S(1)} custom-call(f32[64,256]{1,0:T(8,128)S(1)} %collective-permute-done.5.one_ref, f32[64,128]{1,0:T(8,128)S(1)} %collective-permute-done.6.two_ref, f32[64,1280]{1,0:T(8,128)S(1)} %get-tuple-element.81.rest_0_.mine_ref, f32[64,1024]{1,0:T(8,128)S(1)} %get-tuple-element.82.other_ref, ...), custom_call_target="tpu_custom_call" | custom-call | flops 16777216 | bytes 1048576 | tf_op jit(solution)/shard_map/flux/pallas_call | solution.py:606
  22.9 1.7 %update.5 = (f32[128,128]{1,0:T(8,128)S(1)}, bf16[64,768]{1,0:T(8,128)(2,1)S(1)}, f32[32,256]{1,0:T(8,128)S(1)}) custom-call(f32[64,384]{1,0:T(8,128)S(1)} %collective-permute-done.7.one_ref, f32[64,768]{1,0:T(8,128)S(1)} %flux.5.local_ref, f32[64,384]{1,0:T(8,128)S(1)} %get-tuple-element.84.target_ref, f32[8,640]{1,0:T(8,128)S(1)} %get-tuple-element.69.arrival_ref, ...), custom_call_target="tpu_custom_call" | custom-call | flops 16777216 | bytes 1048576 | tf_op jit(solution)/shard_map/update/pallas_call | solution.py:606
  24.6 0.3 collective-permute-start.8
  24.9 0.4 own.6.own_ref
  25.3 0.6 collective-permute-done.8.sent_ref
  25.9 0.1 carry.6
  26.0 1.6 %collective-permute-start.9 = (f32[32,256]{1,0:T(8,128)S(1)}, f32[32,256]{1,0:T(8,128)S(1)}, u32[]{:S(2)}, u32[]{:S(2)}) collective-permute-start(f32[32,256]{1,0:T(8,128)S(1)} %get-tuple-element.89), channel_id=1, source_target_pairs={{0,2},{1,0},{2,1},{3,5},{4,6},{5,3},{6,4},{7,9},{8,10},{9,7},{10,8... | collective-permute-start | bytes 98312 | tf_op jit(solution)/shard_map/ppermute | solution.py:629
  27.5 2.2 %collective-permute-start.10 = (f32[32,128]{1,0:T(8,128)S(1)}, f32[32,128]{1,0:T(8,128)S(1)}, u32[]{:S(2)}, u32[]{:S(2)}) collective-permute-start(f32[32,128]{1,0:T(8,128)S(1)} %get-tuple-element.90), channel_id=1, source_target_pairs={{0,4},{1,3},{2,6},{3,1},{4,0},{5,9},{6,2},{7,11},{8,12},{9,5},{10,... | collective-permute-start | bytes 49160 | tf_op jit(solution)/shard_map/ppermute | solution.py:629
  29.8 1.3 %sides.6 = (f32[32,1280]{1,0:T(8,128)S(1)}, f32[32,1024]{1,0:T(8,128)S(1)}, f32[32,384]{1,0:T(8,128)S(1)}) custom-call(bf16[64,768]{1,0:T(8,128)(2,1)S(1)} %get-tuple-element.88.stack_ref, bf16[128,96]{1,0:T(8,128)(2,1)S(1)} %get-tuple-element.60.interp_ref.rest_2_, bf16[768,1280]{1,0:T(8,128)(2,1)S(1)} %get-tuple-element.66.own_hot_ref, ...), custom_call_target="tpu_custom_call" | custom-call | flops 16777216 | bytes 1048576 | tf_op jit(solution)/shard_map/sides/pallas_call | solution.py:606
  31.1 0.4 collective-permute-done.10.two_ref
  31.5 0.0 collective-permute-done.9.one_ref
  31.5 0.1 relay.6
  31.6 0.0 collective-permute-start.11
  31.6 0.9 %flux.6.local_ref = f32[32,768]{1,0:T(8,128)S(1)} custom-call(f32[32,256]{1,0:T(8,128)S(1)} %collective-permute-done.9.one_ref, f32[32,128]{1,0:T(8,128)S(1)} %collective-permute-done.10.two_ref, f32[32,1280]{1,0:T(8,128)S(1)} %get-tuple-element.91.rest_0_.mine_ref, f32[32,1024]{1,0:T(8,128)S(1)} %get-tuple-element.92.other_ref, ...), custom_call_target="tpu_custom_call" | custom-call | flops 16777216 | bytes 1048576 | tf_op jit(solution)/shard_map/flux/pallas_call | solution.py:606
  32.5 0.3 collective-permute-done.11.one_ref
  32.8 1.5 %update.6 = (f32[64,128]{1,0:T(8,128)S(1)}, bf16[64,768]{1,0:T(8,128)(2,1)S(1)}, f32[32,256]{1,0:T(8,128)S(1)}) custom-call(f32[32,384]{1,0:T(8,128)S(1)} %collective-permute-done.11.one_ref, f32[32,768]{1,0:T(8,128)S(1)} %flux.6.local_ref, f32[32,384]{1,0:T(8,128)S(1)} %get-tuple-element.93.target_ref, f32[8,640]{1,0:T(8,128)S(1)} %get-tuple-element.69.arrival_ref, ...), custom_call_target="tpu_custom_call" | custom-call | flops 16777216 | bytes 1048576 | tf_op jit(solution)/shard_map/update/pallas_call | solution.py:606
  34.3 0.3 collective-permute-start.12
  34.6 0.4 own.7.own_ref
  35.0 0.6 collective-permute-done.12.sent_ref
  35.5 0.1 carry.7
  35.6 0.6 %collective-permute-start.13 = (f32[32,256]{1,0:T(8,128)S(1)}, f32[32,256]{1,0:T(8,128)S(1)}, u32[]{:S(2)}, u32[]{:S(2)}) collective-permute-start(f32[32,256]{1,0:T(8,128)S(1)} %get-tuple-element.97), channel_id=1, source_target_pairs={{0,2},{1,0},{2,1},{3,5},{4,6},{5,3},{6,4},{7,9},{8,10},{9,7},{10,8... | collective-permute-start | bytes 98312 | tf_op jit(solution)/shard_map/ppermute | solution.py:629
  36.3 2.4 %collective-permute-start.14 = (f32[32,128]{1,0:T(8,128)S(1)}, f32[32,128]{1,0:T(8,128)S(1)}, u32[]{:S(2)}, u32[]{:S(2)}) collective-permute-start(f32[32,128]{1,0:T(8,128)S(1)} %get-tuple-element.98), channel_id=1, source_target_pairs={{0,4},{1,3},{2,6},{3,1},{4,0},{5,9},{6,2},{7,11},{8,12},{9,5},{10,... | collective-permute-start | bytes 49160 | tf_op jit(solution)/shard_map/ppermute | solution.py:629
  38.6 1.3 %sides.7 = (f32[32,1280]{1,0:T(8,128)S(1)}, f32[32,1024]{1,0:T(8,128)S(1)}, f32[32,384]{1,0:T(8,128)S(1)}) custom-call(bf16[64,768]{1,0:T(8,128)(2,1)S(1)} %get-tuple-element.96.stack_ref, bf16[128,96]{1,0:T(8,128)(2,1)S(1)} %get-tuple-element.60.interp_ref.rest_2_, bf16[768,1280]{1,0:T(8,128)(2,1)S(1)} %get-tuple-element.66.own_hot_ref, ...), custom_call_target="tpu_custom_call" | custom-call | flops 16777216 | bytes 1048576 | tf_op jit(solution)/shard_map/sides/pallas_call | solution.py:606
  40.0 0.4 collective-permute-done.14.two_ref
  40.4 0.1 relay.7
  40.4 0.1 collective-permute-start.15
  40.6 0.9 %flux.7.local_ref = f32[32,768]{1,0:T(8,128)S(1)} custom-call(f32[32,256]{1,0:T(8,128)S(1)} %collective-permute-done.13.one_ref, f32[32,128]{1,0:T(8,128)S(1)} %collective-permute-done.14.two_ref, f32[32,1280]{1,0:T(8,128)S(1)} %get-tuple-element.99.rest_0_.mine_ref, f32[32,1024]{1,0:T(8,128)S(1)} %get-tuple-element.100.other_ref, ...), custom_call_target="tpu_custom_call" | custom-call | flops 16777216 | bytes 1048576 | tf_op jit(solution)/shard_map/flux/pallas_call | solution.py:606
  41.5 0.2 collective-permute-done.15.one_ref
  41.7 1.5 %update.7 = (f32[64,128]{1,0:T(8,128)}, f32[32,128]{1,0:T(8,128)S(1)}) custom-call(f32[32,384]{1,0:T(8,128)S(1)} %collective-permute-done.15.one_ref, f32[32,768]{1,0:T(8,128)S(1)} %flux.7.local_ref, f32[32,384]{1,0:T(8,128)S(1)} %get-tuple-element.101.target_ref, f32[8,640]{1,0:T(8,128)S(1)} %get-tuple-element.69.arrival_ref, ...), custom_call_target="tpu_custom_call" | custom-call | flops 16777216 | bytes 1048576 | tf_op jit(solution)/shard_map/update/pallas_call | solution.py:606
  43.2 12.5 %all_to_all.5 = f32[32,1,128]{2,1,0:T(1,128)S(1)} all-to-all(f32[32,1,128]{2,1,0:T(1,128)S(1)} %bitcast.14), channel_id=1, replica_groups=mesh['dom'=32] {'dom'}, dimensions={0} | all-to-all | bytes 32768 | tf_op jit(solution)/shard_map/all_to_all | solution.py:749
  55.7 0.8 %finish.1 = (f32[64,128]{1,0:T(8,128)}, f32[1,128]{1,0:T(1,128)}) custom-call(f32[32,128]{1,0:T(8,128)S(1)} %bitcast.13, f32[64,128]{1,0:T(8,128)S(1)} %copy-done.4, f32[128,128]{1,0:T(8,128)S(1)} %get-tuple-element.85.field_ref.first_ref, f32[128,128]{1,0:T(8,128)S(1)} %get-tuple-element.94.second_ref), custom_call_target="tpu_custom_call" | custom-call | flops 16777216 | bytes 1048576 | tf_op jit(solution)/shard_map/finish/pallas_call | solution.py:606
  (13 shorter events, 0.0 us)
Async XLA Ops:
  2.6 1.5 %collective-permute-start = (f32[72,256]{1,0:T(8,128)S(1)}, f32[72,256]{1,0:T(8,128)S(1)}, u32[]{:S(2)}, u32[]{:S(2)}) collective-permute-start(f32[72,256]{1,0:T(8,128)S(1)} %get-tuple-element.54), channel_id=1, source_target_pairs={{0,1},{1,0},{2,3},{3,2},{4,5},{5,4},{6,7},{7,6},{8,9},{9,8},{10,11... | collective-permute-start | bytes 221192 | tf_op jit(solution)/shard_map/ppermute | solution.py:629
  4.2 7.8 %collective-permute-start.1 = (f32[72,256]{1,0:T(8,128)S(1)}, f32[72,256]{1,0:T(8,128)S(1)}, u32[]{:S(2)}, u32[]{:S(2)}) collective-permute-start(f32[72,256]{1,0:T(8,128)S(1)} %get-tuple-element.61), channel_id=1, source_target_pairs={{0,2},{1,0},{2,1},{3,5},{4,6},{5,3},{6,4},{7,9},{8,10},{9,7},{10,8... | collective-permute-start | bytes 221192 | tf_op jit(solution)/shard_map/ppermute | solution.py:629
  7.0 5.0 %collective-permute-start.2 = (f32[72,128]{1,0:T(8,128)S(1)}, f32[72,128]{1,0:T(8,128)S(1)}, u32[]{:S(2)}, u32[]{:S(2)}) collective-permute-start(f32[72,128]{1,0:T(8,128)S(1)} %get-tuple-element.62), channel_id=1, source_target_pairs={{0,4},{1,3},{2,6},{3,1},{4,0},{5,9},{6,2},{7,11},{8,12},{9,5},{10,... | collective-permute-start | bytes 110600 | tf_op jit(solution)/shard_map/ppermute | solution.py:629
  10.4 1.8 %copy-start.4 = (f32[64,128]{1,0:T(8,128)S(1)}, f32[64,128]{1,0:T(8,128)}, u32[]{:S(2)}) copy-start(f32[64,128]{1,0:T(8,128)} %guess_ref.1) | copy-start | bytes 98308
  10.4 1.8 %copy-start.6 = (f32[64,128]{1,0:T(8,128)S(1)}, f32[64,128]{1,0:T(8,128)}, u32[]{:S(2)}) copy-start(f32[64,128]{1,0:T(8,128)} %refs_6_.1) | copy-start | bytes 98308
  10.4 1.8 %copy-start.1 = (bf16[128,96]{1,0:T(8,128)(2,1)S(1)}, bf16[128,96]{1,0:T(8,128)(2,1)}, u32[]{:S(2)}) copy-start(bf16[128,96]{1,0:T(8,128)(2,1)} %constant.12.clone.interp_ref.interp_t_ref) | copy-start | bytes 73732
  10.4 1.8 %copy-start.3 = (f32[32,128]{1,0:T(8,128)S(1)}, f32[32,128]{1,0:T(8,128)}, u32[]{:S(2)}) copy-start(f32[32,128]{1,0:T(8,128)} %constant.14.clone.weight_ref) | copy-start | bytes 49156
  11.9 1.5 %copy-start = (bf16[64,64,128]{2,1,0:T(8,128)(2,1)S(1)}, bf16[64,64,128]{2,1,0:T(8,128)(2,1)}, u32[]{:S(2)}) copy-start(bf16[64,64,128]{2,1,0:T(8,128)(2,1)} %inverse_ref.7) | copy-start | bytes 3145732
  11.9 1.5 %copy-start.2 = (bf16[64,768]{1,0:T(8,128)(2,1)S(1)}, bf16[64,768]{1,0:T(8,128)(2,1)}, u32[]{:S(2)}) copy-start(bf16[64,768]{1,0:T(8,128)(2,1)} %constant.13.clone.lift_ref) | copy-start | bytes 294916
  12.0 1.5 %copy-start.5 = (f32[64,128]{1,0:T(8,128)S(1)}, f32[64,128]{1,0:T(8,128)}, u32[]{:S(2)}) copy-start(f32[64,128]{1,0:T(8,128)} %rest_0_.1) | copy-start | bytes 98308
  12.1 1.4 %collective-permute-start.3 = (f32[72,384]{1,0:T(8,128)S(1)}, f32[72,384]{1,0:T(8,128)S(1)}, u32[]{:S(2)}, u32[]{:S(2)}) collective-permute-start(f32[72,384]{1,0:T(8,128)S(1)} %relay.4), channel_id=1, source_target_pairs={{0,1},{1,0},{2,3},{3,2},{4,5},{5,4},{6,7},{7,6},{8,9},{9,8},{10,11... | collective-permute-start | bytes 331784 | tf_op jit(solution)/shard_map/ppermute | solution.py:629
  15.2 1.3 %collective-permute-start.4 = (f32[64,256]{1,0:T(8,128)S(1)}, f32[64,256]{1,0:T(8,128)S(1)}, u32[]{:S(2)}, u32[]{:S(2)}) collective-permute-start(f32[64,256]{1,0:T(8,128)S(1)} %get-tuple-element.77), channel_id=1, source_target_pairs={{0,1},{1,0},{2,3},{3,2},{4,5},{5,4},{6,7},{7,6},{8,9},{9,8},{10,11... | collective-permute-start | bytes 196616 | tf_op jit(solution)/shard_map/ppermute | solution.py:629
  16.6 4.6 %collective-permute-start.5 = (f32[64,256]{1,0:T(8,128)S(1)}, f32[64,256]{1,0:T(8,128)S(1)}, u32[]{:S(2)}, u32[]{:S(2)}) collective-permute-start(f32[64,256]{1,0:T(8,128)S(1)} %get-tuple-element.79), channel_id=1, source_target_pairs={{0,2},{1,0},{2,1},{3,5},{4,6},{5,3},{6,4},{7,9},{8,10},{9,7},{10,8... | collective-permute-start | bytes 196616 | tf_op jit(solution)/shard_map/ppermute | solution.py:629
  17.2 4.1 %collective-permute-start.6 = (f32[64,128]{1,0:T(8,128)S(1)}, f32[64,128]{1,0:T(8,128)S(1)}, u32[]{:S(2)}, u32[]{:S(2)}) collective-permute-start(f32[64,128]{1,0:T(8,128)S(1)} %get-tuple-element.80), channel_id=1, source_target_pairs={{0,4},{1,3},{2,6},{3,1},{4,0},{5,9},{6,2},{7,11},{8,12},{9,5},{10,... | collective-permute-start | bytes 98312 | tf_op jit(solution)/shard_map/ppermute | solution.py:629
  21.4 1.6 %collective-permute-start.7 = (f32[64,384]{1,0:T(8,128)S(1)}, f32[64,384]{1,0:T(8,128)S(1)}, u32[]{:S(2)}, u32[]{:S(2)}) collective-permute-start(f32[64,384]{1,0:T(8,128)S(1)} %relay.5), channel_id=1, source_target_pairs={{0,1},{1,0},{2,3},{3,2},{4,5},{5,4},{6,7},{7,6},{8,9},{9,8},{10,11... | collective-permute-start | bytes 294920 | tf_op jit(solution)/shard_map/ppermute | solution.py:629
  24.6 1.3 %collective-permute-start.8 = (f32[32,256]{1,0:T(8,128)S(1)}, f32[32,256]{1,0:T(8,128)S(1)}, u32[]{:S(2)}, u32[]{:S(2)}) collective-permute-start(f32[32,256]{1,0:T(8,128)S(1)} %get-tuple-element.87), channel_id=1, source_target_pairs={{0,1},{1,0},{2,3},{3,2},{4,5},{5,4},{6,7},{7,6},{8,9},{9,8},{10,11... | collective-permute-start | bytes 98312 | tf_op jit(solution)/shard_map/ppermute | solution.py:629
  26.0 5.5 %collective-permute-start.9 = (f32[32,256]{1,0:T(8,128)S(1)}, f32[32,256]{1,0:T(8,128)S(1)}, u32[]{:S(2)}, u32[]{:S(2)}) collective-permute-start(f32[32,256]{1,0:T(8,128)S(1)} %get-tuple-element.89), channel_id=1, source_target_pairs={{0,2},{1,0},{2,1},{3,5},{4,6},{5,3},{6,4},{7,9},{8,10},{9,7},{10,8... | collective-permute-start | bytes 98312 | tf_op jit(solution)/shard_map/ppermute | solution.py:629
  27.5 3.9 %collective-permute-start.10 = (f32[32,128]{1,0:T(8,128)S(1)}, f32[32,128]{1,0:T(8,128)S(1)}, u32[]{:S(2)}, u32[]{:S(2)}) collective-permute-start(f32[32,128]{1,0:T(8,128)S(1)} %get-tuple-element.90), channel_id=1, source_target_pairs={{0,4},{1,3},{2,6},{3,1},{4,0},{5,9},{6,2},{7,11},{8,12},{9,5},{10,... | collective-permute-start | bytes 49160 | tf_op jit(solution)/shard_map/ppermute | solution.py:629
  31.6 1.2 %collective-permute-start.11 = (f32[32,384]{1,0:T(8,128)S(1)}, f32[32,384]{1,0:T(8,128)S(1)}, u32[]{:S(2)}, u32[]{:S(2)}) collective-permute-start(f32[32,384]{1,0:T(8,128)S(1)} %relay.6), channel_id=1, source_target_pairs={{0,1},{1,0},{2,3},{3,2},{4,5},{5,4},{6,7},{7,6},{8,9},{9,8},{10,11... | collective-permute-start | bytes 147464 | tf_op jit(solution)/shard_map/ppermute | solution.py:629
  34.3 1.3 %collective-permute-start.12 = (f32[32,256]{1,0:T(8,128)S(1)}, f32[32,256]{1,0:T(8,128)S(1)}, u32[]{:S(2)}, u32[]{:S(2)}) collective-permute-start(f32[32,256]{1,0:T(8,128)S(1)} %get-tuple-element.95), channel_id=1, source_target_pairs={{0,1},{1,0},{2,3},{3,2},{4,5},{5,4},{6,7},{7,6},{8,9},{9,8},{10,11... | collective-permute-start | bytes 98312 | tf_op jit(solution)/shard_map/ppermute | solution.py:629
  35.6 4.8 %collective-permute-start.13 = (f32[32,256]{1,0:T(8,128)S(1)}, f32[32,256]{1,0:T(8,128)S(1)}, u32[]{:S(2)}, u32[]{:S(2)}) collective-permute-start(f32[32,256]{1,0:T(8,128)S(1)} %get-tuple-element.97), channel_id=1, source_target_pairs={{0,2},{1,0},{2,1},{3,5},{4,6},{5,3},{6,4},{7,9},{8,10},{9,7},{10,8... | collective-permute-start | bytes 98312 | tf_op jit(solution)/shard_map/ppermute | solution.py:629
  36.3 4.1 %collective-permute-start.14 = (f32[32,128]{1,0:T(8,128)S(1)}, f32[32,128]{1,0:T(8,128)S(1)}, u32[]{:S(2)}, u32[]{:S(2)}) collective-permute-start(f32[32,128]{1,0:T(8,128)S(1)} %get-tuple-element.98), channel_id=1, source_target_pairs={{0,4},{1,3},{2,6},{3,1},{4,0},{5,9},{6,2},{7,11},{8,12},{9,5},{10,... | collective-permute-start | bytes 49160 | tf_op jit(solution)/shard_map/ppermute | solution.py:629
  40.4 1.2 %collective-permute-start.15 = (f32[32,384]{1,0:T(8,128)S(1)}, f32[32,384]{1,0:T(8,128)S(1)}, u32[]{:S(2)}, u32[]{:S(2)}) collective-permute-start(f32[32,384]{1,0:T(8,128)S(1)} %relay.7), channel_id=1, source_target_pairs={{0,1},{1,0},{2,3},{3,2},{4,5},{5,4},{6,7},{7,6},{8,9},{9,8},{10,11... | collective-permute-start | bytes 147464 | tf_op jit(solution)/shard_map/ppermute | solution.py:629

commit v4 on v3

--- a/solution.py
+++ b/solution.py
@@ -157,6 +157,35 @@
     return jnp.where(place == index_row, 1.0, 0.0).astype(bf16)
 
 
+def gather_columns(stack, hot, face, nf):
+    h = 32 * nf
+    if hot.shape[0] == 768:
+        got = dot(stack, hot)
+        return got[:h] + got[h:]
+    parts = [stack[:, lanes * f : lanes * f + lanes] for f in range(6)]
+    got = dot(jnp.concatenate(parts, axis=0), hot)
+    out = got[:h] + got[h : 2 * h]
+    for f in range(1, 6):
+        low = 2 * h * f
+        out = jnp.where(face == f, got[low : low + h] + got[low + h : low + 2 * h], out)
+    return out
+
+
+def scatter_columns(x, hot, face, nf):
+    h = 32 * nf
+    high, low = two(x)
+    both = jnp.concatenate([high, low], axis=0)
+    if hot.shape[1] == 768:
+        got = dot(both, hot)
+        return got[:h] + got[h:]
+    parts = [both * jnp.where(face == f, 1.0, 0.0).astype(bf16) for f in range(6)]
+    got = dot_t(jnp.concatenate(parts, axis=0), hot)
+    return jnp.concatenate(
+        [got[2 * h * f : 2 * h * f + h] + got[2 * h * f + h : 2 * h * f + 2 * h] for f in range(6)],
+        axis=1,
+    )
+
+
 def element_rows(coef_ref, level_ref):
     coef = coef_ref[...]
     level = level_ref[...]
@@ -220,19 +249,34 @@
     return jnp.abs(offset) == 3
 
 
-def slot_attributes(side_ref, slots):
+def side_attributes(side_ref, more=()):
     live = lax.broadcasted_iota(i32, (1, side_pad), 1) < 930
     rows = [jnp.where(live, side_ref[k : k + 1], 0).astype(f32) for k in range(3)]
     rows.append(jnp.where(live, 1.0, 0.0))
-    found = dot(rows_of(rows, 16, side_pad).astype(bf16), one_hot(slots, side_pad))
+    return rows_of(rows + list(more), 16, side_pad).astype(bf16)
+
+
+def look_up(attributes, index):
+    blocks = jnp.concatenate(
+        [attributes[:, lanes * k : lanes * k + lanes] for k in range(side_pad // lanes)], axis=0
+    )
+    found = dot(blocks, one_hot(index & 127, lanes))
+    block = index >> 7
+    out = jnp.zeros((8, index.shape[1]), f32)
+    for k in range(side_pad // lanes):
+        out = jnp.where(block == k, found[16 * k : 16 * k + 8], out)
+    return out
+
+
+def place_of(found):
     valid = found[3:4] > 0.5
-    column = jnp.where(valid, (found[1:2] * 128.0 + found[0:1]).astype(i32), -1)
-    return column, jnp.where(valid, found[2:3].astype(i32), -1)
-
-
-def fill_one_hot(hot_ref, column):
+    return tuple(jnp.where(valid, found[k : k + 1], -1.0).astype(i32) for k in range(3))
+
+
+def fill_one_hot(hot_ref, elem, face):
+    hot = one_hot(elem, lanes)
     for f in range(6):
-        hot_ref[lanes * f : lanes * f + lanes] = one_hot(column, lanes, lanes * f)
+        hot_ref[lanes * f : lanes * f + lanes] = hot * jnp.where(face == f, 1.0, 0.0).astype(bf16)
 
 
 def listed_part(rolled_ref, shift, offset, low, high, valid):
@@ -245,8 +289,8 @@
 def send_setup_kernel(chips, *refs):
     sources, refs = refs[:12], refs[12:]
     hot_ref, case_ref, stack_ref, side_ref, rolled_ref = refs[:5]
-    sent_ref, landed = refs[5], (*refs[11:19], *refs[6:10])
-    slot_ref, arrived = refs[10], refs[19]
+    sent_ref, landed = refs[5], (*refs[12:19], *refs[6:11])
+    slot_ref, arrived = refs[11], refs[19]
     copies = [
         pltpu.make_async_copy(source, target, arrived.at[k])
         for k, (source, target) in enumerate(zip(sources, landed))
@@ -254,7 +298,7 @@
     for copy in copies:
         copy.start()
     elem_ref, dir_ref, sidecase_ref, kind_ref, partner_ref, list_ref = landed[:6]
-    start_ref, guess_ref, coef_ref, level_ref, trace_ref, interp_ref = landed[6:]
+    start_ref, coef_ref, level_ref, trace_ref, interp_ref = landed[6:11]
     for copy in copies:
         copy.wait()
     side_ref[...] = jnp.full((8, side_pad), -1, i32)
@@ -279,16 +323,16 @@
     )
     slot_ref[0:1, 0:128] = functools.reduce(jnp.maximum, first)
     slot_ref[0:1, 128:256] = part(0, cross, 0, 96, there & ~narrow(cross))
-    column, slot_case = slot_attributes(side_ref, slot_ref[0:1, :])
+    elem, face, slot_case = place_of(look_up(side_attributes(side_ref), slot_ref[0:1, :]))
     case_ref[0:1, :] = slot_case
-    fill_one_hot(hot_ref, column)
+    fill_one_hot(hot_ref, elem, face)
 
     coef, size, volume_scale, normal_scale = element_rows(coef_ref, level_ref)
-    stack = face_stack(trace_ref, [start_ref[...], guess_ref[...]], normal_scale, 2)
+    stack = face_stack(trace_ref, [start_ref[...]], normal_scale, 1)
     scalars = rows_of([x.astype(f32) for x in three(coef)] + [size], 16, lanes).astype(bf16)
     stack = jnp.concatenate([stack, jnp.concatenate([scalars] * 6, axis=1)], axis=0)
     stack_ref[...] = stack
-    sent = gather_message(stack, hot_ref[...], interp_ref[...], slot_case, 2)
+    sent = gather_message(stack, hot_ref[...], interp_ref[...], slot_case, 1)
     sent_ref[...] = sent
 
 
@@ -307,9 +351,9 @@
     )
     slot_ref[0:1, 256:384] = part(0, cross, 0, 96, there & ~narrow(cross))
     slot_ref[0:1, 384:512] = part(0, flip, 0, 96, core >= 0)
-    column, slot_case = slot_attributes(side_ref, slot_ref[0:1, :])
+    elem, face, slot_case = place_of(look_up(side_attributes(side_ref), slot_ref[0:1, :]))
     case_ref[0:1, :] = slot_case
-    fill_one_hot(hot_ref, column)
+    fill_one_hot(hot_ref, elem, face)
 
 
 def own_kernel(nf, stack_ref, hot_ref, case_ref, interp_ref, own_ref):
@@ -318,7 +362,8 @@
     )
 
 
-def carry_kernel(sent_ref, own_ref, two_ref, one_ref):
+def carry_kernel(sent_ref, own_ref, *rest):
+    two_ref, one_ref = rest[-2:]
     lane = lax.broadcasted_iota(i32, (1, lanes), 1)
     sent = sent_ref[:, 0:128]
     handed = jnp.where((lane >= 48) & (lane < 96), pltpu.roll(sent, 48, 1), 0.0)
@@ -340,30 +385,26 @@
 
 def setup_kernel(
     chips, coef_ref, level_ref, side_ref,
-    info_ref, own_hot_ref, partner_hot_ref, far_hot_ref, arrival_ref, arrival_hot_ref,
+    own_hot_ref, partner_hot_ref, far_hot_ref, place_ref, info_ref, arrival_ref,
 ):
     core, near, far, end, near_there, far_there = where_am_i(chips)
     elem, direction, case = side_ref[0:1], side_ref[1:2], side_ref[2:3]
     kind, partner = side_ref[3:4], side_ref[4:5]
     live = lax.broadcasted_iota(i32, (1, side_pad), 1) < 930
-    own_column = jnp.where(live, direction * lanes + elem, -1)
 
     coef, size, volume_scale, normal_scale = element_rows(coef_ref, level_ref)
     scalars = rows_of([x.astype(f32) for x in three(coef)] + [size], 16, lanes)
-    mine = dot(scalars.astype(bf16), one_hot(jnp.where(live, elem, -1), lanes))
+    mine = dot(scalars.astype(bf16), one_hot(elem, lanes))
     hanging = (case >= 0) & (case < 4)
     own_coef = mine[0:1] + mine[1:2] + mine[2:3]
     own_size = mine[3:4] * jnp.where(hanging, 0.5, 1.0)
 
-    rows = [jnp.where(live, r, 0).astype(f32) for r in (elem, direction, case)]
-    rows.append(jnp.where(live, 1.0, 0.0))
-    rows += [mine[0:1], mine[1:2], mine[2:3], own_size]
-    attributes = rows_of(rows, 16, side_pad).astype(bf16)
-    other = dot(attributes, one_hot(jnp.where(partner < 930, partner, -1), side_pad))
+    attributes = side_attributes(side_ref, (mine[0:1], mine[1:2], mine[2:3], own_size))
+    here = live & (partner < 930)
+    other = look_up(attributes, jnp.where(here, partner, -1))
+    other_elem, other_face = place_of(other)[:2]
+    partner_hot_ref[...] = one_hot(other_elem, lanes)
     valid = other[3:4] > 0.5
-    fill_one_hot(
-        partner_hot_ref, jnp.where(valid, (other[1:2] * 128.0 + other[0:1]).astype(i32), -1)
-    )
     edge = jnp.where(kind == 1, 1.0, 0.0)
     least = jnp.where(valid, jnp.minimum(own_size, other[7:8]), 0.0)
     jump = 16.0 * (own_coef + other[4:5] + other[5:6] + other[6:7]) * least
@@ -374,8 +415,6 @@
         8, side_pad,
     )
 
-    sought = jnp.where(live & (kind == 0), partner, -7)
-    place = lax.broadcasted_iota(i32, (lanes, side_pad), 0)
     def arrives(carrier):
         last = end & (carrier == 1)
         back = jnp.where((carrier == 0) | end, -near, near)
@@ -406,51 +445,84 @@
             (*span(96, 120, slim), cross), *two_parts,
         ))
         segments.append(((*span(0, 96, wide), cross),))
+    entry = partner - 930
+    peer = (entry * 683) >> 16
+    entry = entry - 96 * peer
+    sought = live & (partner >= 930) & (kind == 0)
+    column = jnp.full((1, side_pad), -1, i32)
     for tile, parts in enumerate(segments):
-        slot = jnp.full((lanes, side_pad), -5, i32)
         for low, high, offset in parts:
-            entry = 930 + 96 * row_of(offset) - low
-            slot = jnp.where((place >= low) & (place < high), entry + place, slot)
-        arrival_hot_ref[lanes * tile : lanes * tile + lanes] = jnp.where(
-            slot == sought, 1.0, 0.0
-        ).astype(bf16)
-    target = dot_t(attributes, arrival_hot_ref[...])
-    valid = target[3:4] > 0.5
-    target_column = jnp.where(valid, (target[1:2] * 128.0 + target[0:1]).astype(i32), -1)
-    fill_one_hot(own_hot_ref, jnp.concatenate([own_column, target_column[:, 0:256]], axis=1))
-    fill_one_hot(far_hot_ref, target_column[:, 256:640])
+            match = sought & (peer == row_of(offset)) & (entry < high - low)
+            column = jnp.where(match, lanes * tile + low + entry, column)
+    block = column >> 7
+    split = [
+        attributes * jnp.where(block == tile, 1.0, 0.0).astype(bf16) for tile in range(len(segments))
+    ]
+    target = dot_t(jnp.concatenate(split, axis=0), one_hot(column & 127, lanes))
+    target = jnp.concatenate(
+        [target[16 * tile : 16 * tile + 8] for tile in range(len(segments))], axis=1
+    )
+    target_elem, target_face, target_case = place_of(target)
+    elems = jnp.concatenate([elem, target_elem], axis=1)
+    faces = jnp.concatenate([direction, target_face], axis=1)
+    near = side_pad + 256
+    own_hot_ref[...] = one_hot(elems[:, :near], lanes)
+    far_hot_ref[...] = one_hot(elems[:, near:], lanes)
+    other_face = jnp.concatenate([other_face, jnp.full((1, 640), -1, i32)], axis=1)
+    place_ref[...] = rows_of(
+        [elems.astype(f32), faces.astype(f32), other_face.astype(f32)], 16, elems.shape[1]
+    )
     info_ref[:, side_pad:] = rows_of(
-        [jnp.zeros((1, 256), f32)] * 4 + [jnp.where(valid, target[2:3], -1.0)[:, 0:256]], 8, 256
+        [jnp.zeros((1, 256), f32)] * 4 + [target_case[:, 0:256].astype(f32)], 8, 256
     )
     arrival_ref[...] = rows_of(
-        [jnp.where(valid, target[2:3], -1.0), target[4:5] + target[5:6] + target[6:7], target[7:8]],
+        [target_case.astype(f32), target[4:5] + target[5:6] + target[6:7], target[7:8]],
         8, 640,
     )
 
 
+def whole_kernel(own_elem_ref, partner_elem_ref, far_elem_ref, place_ref, own_ref, partner_ref, far_ref):
+    near = side_pad + 256
+    for source, row, low, high, target in (
+        (own_elem_ref, 1, 0, near, own_ref),
+        (partner_elem_ref, 2, 0, side_pad, partner_ref),
+        (far_elem_ref, 1, near, near + 384, far_ref),
+    ):
+        hot, face = source[...], place_ref[row : row + 1, low:high]
+        for f in range(6):
+            target[lanes * f : lanes * f + lanes] = hot * jnp.where(face == f, 1.0, 0.0).astype(bf16)
+
+
+def turn_kernel(place_ref, own_ref, far_ref):
+    row = lax.broadcasted_iota(i32, (16, lanes), 0)
+    weight = jnp.where(row == 0, 1.0, jnp.where(row == 1, 128.0, 0.0)).astype(bf16)
+    column = lax.dot_general(
+        place_ref[...].astype(bf16), weight, (((0,), (0,)), ((), ())), preferred_element_type=f32
+    )
+    lane = lax.broadcasted_iota(i32, (1, lanes), 1).astype(f32)
+    split = own_ref.shape[0]
+    for f in range(6):
+        part = jnp.where(column == lane + 128.0 * f, 1.0, 0.0).astype(bf16)
+        own_ref[:, lanes * f : lanes * f + lanes] = part[:split]
+        far_ref[:, lanes * f : lanes * f + lanes] = part[split:]
+
+
 def sides_kernel(
-    nf, stack_ref, interp_ref, own_hot_ref, partner_hot_ref, far_hot_ref, info_ref, arrival_ref,
-    mine_ref, other_ref, target_ref,
+    nf, stack_ref, interp_ref, own_hot_ref, partner_hot_ref, far_hot_ref, place_ref, info_ref,
+    arrival_ref, mine_ref, other_ref, target_ref,
 ):
-    h = 32 * nf
-    stack = stack_ref[0 : 2 * h]
-    table = interp_ref[...]
-    for hot_ref, case, out_ref in (
-        (own_hot_ref, info_ref[4:5], mine_ref),
-        (partner_hot_ref, info_ref[5:6, 0:side_pad], other_ref),
-        (far_hot_ref, arrival_ref[0:1, 256:640], target_ref),
+    stack = stack_ref[0 : 64 * nf]
+    near = side_pad + 256
+    for hot_ref, face, case, out_ref in (
+        (own_hot_ref, place_ref[1:2, 0:near], info_ref[4:5], mine_ref),
+        (partner_hot_ref, place_ref[2:3, 0:side_pad], info_ref[5:6, 0:side_pad], other_ref),
+        (far_hot_ref, place_ref[1:2, near:], arrival_ref[0:1, 256:640], target_ref),
     ):
-        got = dot(stack, hot_ref[...])
-        out_ref[...] = fields_case(table, got[:h] + got[h:], case.astype(i32), nf)
-
-
-def scatter(x, hot, nf):
-    high, low = two(x)
-    got = dot_t(jnp.concatenate([high, low], axis=0), hot)
-    return got[: 32 * nf] + got[32 * nf :]
-
-
-def side_flux(nf, mine, outer, coefs, case, weight_ref, interp_ref, hot):
+        got = gather_columns(stack, hot_ref[...], face, nf)
+        out_ref[...] = fields_case(interp_ref[...], got, case.astype(i32), nf)
+
+
+def side_flux(nf, mine, outer, coefs, case, face, weight_ref, interp_ref, hot):
     jump, jump_out, area, area_out = coefs
     weight = weight_ref[0:16, 0:1]
     flux = []
@@ -462,9 +534,7 @@
         )
         flux.append(weight * (area_out * other - area * value))
     flux = fields_case(interp_ref[...], jnp.concatenate(flux, axis=0), case.astype(i32), nf)
-    high, low = two(flux)
-    got = dot_t(jnp.concatenate([high, low], axis=0), hot)
-    return got[: 32 * nf] + got[32 * nf :]
+    return scatter_columns(flux, hot, face, nf)
 
 
 def halo_coefs(coef, size, other_coef, other_size):
@@ -473,7 +543,7 @@
 
 
 def flux_kernel(
-    nf, chips, one_ref, two_ref, mine_ref, other_ref, info_ref, arrival_ref, weight_ref, interp_ref,
+    nf, chips, one_ref, two_ref, mine_ref, other_ref, place_ref, info_ref, arrival_ref, weight_ref, interp_ref,
     own_hot_ref, *rest,
 ):
     h = 32 * nf
@@ -499,7 +569,8 @@
     ]
     outer = jnp.concatenate([other_ref[...], got[0:h]], axis=1)
     sum_ref[...] = side_flux(
-        nf, mine_ref, outer, coefs, info_ref[4:5], weight_ref, interp_ref, own_hot_ref[...]
+        nf, mine_ref, outer, coefs, info_ref[4:5], place_ref[1:2, 0 : side_pad + 256], weight_ref,
+        interp_ref, own_hot_ref[...],
     )
 
 
@@ -513,21 +584,23 @@
 
 
 def update_kernel(
-    nf, nf_next, residual,
-    one_ref, local_ref, target_ref, arrival_ref, far_hot_ref, weight_ref, interp_t_ref, lift_ref,
+    turn, nf, nf_next,
+    one_ref, local_ref, target_ref, place_ref, arrival_ref, far_hot_ref, weight_ref, interp_t_ref, lift_ref,
     field_ref, coef_ref, level_ref, inverse_ref, *rest,
 ):
-    if residual:
-        rhs_ref, *rest = rest
+    if turn == 0:
+        guess_ref, *rest = rest
     else:
         halo_ref, *rest = rest
+    if turn == 1:
+        rhs_ref, *rest = rest
     if nf_next:
         trace_ref, interp_ref, hot_ref, case_ref, new_ref, stack_ref, sent_ref, *rest = rest
     else:
-        new_ref, part_ref, *rest = rest
+        part_ref, *rest = rest
     hold_ref = rest[-1]
     h = 32 * nf
-    if residual:
+    if turn == 0:
         halo = halo_coefs(
             arrival_ref[1:2, 256:640], arrival_ref[2:3, 256:640],
             one_ref[h : h + 1], one_ref[h + 1 : h + 2],
@@ -537,7 +610,7 @@
         halo = (halo_ref[0:1], halo_ref[1:2])
     total = local_ref[...] + side_flux(
         nf, target_ref, one_ref, (halo[0], halo[0], halo[1], halo[1]), arrival_ref[0:1, 256:640],
-        weight_ref, interp_t_ref, far_hot_ref[...],
+        place_ref[1:2, side_pad + 256 :], weight_ref, interp_t_ref, far_hot_ref[...],
     )
     coef, size, volume_scale, normal_scale = element_rows(coef_ref, level_ref)
     row = lax.broadcasted_iota(i32, (32, lanes), 0)
@@ -556,28 +629,34 @@
     image = dot(lift_ref[...], cat(operands, 1))
     for k in range(nf):
         part = image[:, lanes * k : lanes * k + lanes]
-        if residual and k == 1:
+        if turn == 1 and k == 1:
             part = rhs_ref[...] - part
         hold_ref[64 * k : 64 * k + 64, :] = part
     new = solve_blocks(inverse_ref, hold_ref, nf)
-    for k in range(nf):
-        new_ref[64 * k : 64 * k + 64, :] = new[k]
+    if turn == 0:
+        new.append(guess_ref[...])
     if nf_next:
+        for k, x in enumerate(new):
+            new_ref[64 * k : 64 * k + 64, :] = x
         stack = face_stack(trace_ref, new[:nf_next], normal_scale, nf_next)
         stack_ref[...] = stack
         sent = gather_message(stack, hot_ref[...], interp_ref[...], case_ref[0:1], nf_next)
         sent_ref[...] = sent
     else:
-        before, after = field_ref[...], new[0]
-        before = jnp.sum(jnp.sum(before * before, axis=1, keepdims=True), axis=0, keepdims=True)
-        after = jnp.sum(jnp.sum(after * after, axis=1, keepdims=True), axis=0, keepdims=True)
-        lane = lax.broadcasted_iota(i32, part_ref.shape, 1)
-        part_ref[...] = jnp.where(lane == 0, before, jnp.where(lane == 1, after, 0.0))
+        lane = lax.broadcasted_iota(i32, (1, lanes), 1)
+        sums = []
+        for x in (field_ref[...], new[0]):
+            total = jnp.sum(x * x, axis=0, keepdims=True)
+            sums.append(total + pltpu.roll(total, 64, 1))
+        part_ref[...] = jnp.broadcast_to(jnp.where(lane < 64, sums[0], sums[1]), part_ref.shape)
 
 
 def finish_kernel(part_ref, guess_ref, first_ref, second_ref, out_ref, bound_ref):
     total = jnp.sum(part_ref[...], axis=0, keepdims=True)
-    bound = jnp.sqrt(total[:, 1:2] / total[:, 0:1])
+    lane = lax.broadcasted_iota(i32, (1, lanes), 1)
+    before = jnp.sum(jnp.where(lane < 64, total, 0.0), axis=1, keepdims=True)
+    after = jnp.sum(jnp.where(lane < 64, 0.0, total), axis=1, keepdims=True)
+    bound = jnp.sqrt(after / before)
     upper = 1.2 * bound
     lower = upper / 15.0
     center = 0.5 * (upper + lower)
@@ -641,32 +720,32 @@
         one_away[2 * (c ^ 1)] = 2 * c + 1
         one_away[2 * c + 1] = 2 * c
 
-    def exchange(sent, nf, own_work, work):
+    def exchange(sent, nf, own_work, work, *beside):
         rows = sent.shape[0]
         (own,) = own_work()
         two_out, one_out = run(
-            carry_kernel, [((rows, lanes), f32), ((rows, 256), f32)], [permute(sent, swapped), own],
-            "carry",
+            carry_kernel, [((rows, lanes), f32), ((rows, 256), f32)],
+            [permute(sent, swapped), own, *beside[:1]], "carry",
         )
         arrivals = permute(one_out, one_away), permute(two_out, two_away)
         made = work()
         (last,) = run(
             functools.partial(relay_kernel, chips), [((rows, 384), f32)],
-            [*arrivals, own, *made[:1]], "relay",
+            [*arrivals, own, made[2], *beside[1:]], "relay",
         )
         return arrivals, permute(last, swapped), made
 
     sides = [x.reshape(1, -1) for x in (side_elem, side_dir, side_case, side_kind, partner)]
-    first = [*sides, send_list, start_vector, initial_guess, coef, level, trace, interp]
-    hot, case, stack, sides, rolled, sent, coef, level, trace, interp = run(
+    first = [*sides, send_list, start_vector, coef, level, trace, interp, initial_guess]
+    hot, case, stack, sides, rolled, sent, coef, level, trace, interp, guess = run(
         functools.partial(send_setup_kernel, chips),
-        [((768, 256), bf16), ((8, 256), i32), ((144, 768), bf16), ((8, side_pad), i32), ((32, lanes), i32),
-         ((72, 256), f32), *((x.shape, x.dtype) for x in first[8:])],
+        [((768, 256), bf16), ((8, 256), i32), ((80, 768), bf16), ((8, side_pad), i32), ((32, lanes), i32),
+         ((40, 256), f32), *((x.shape, x.dtype) for x in first[7:])],
         first,
         "send_setup",
         scratch=[
             pltpu.VMEM((8, 256), i32),
-            *(pltpu.VMEM(x.shape, x.dtype) for x in first[:8]), pltpu.SemaphoreType.DMA((len(first),)),
+            *(pltpu.VMEM(x.shape, x.dtype) for x in first[:7]), pltpu.SemaphoreType.DMA((len(first),)),
         ],
         placed=False,
     )
@@ -677,9 +756,9 @@
         "own_setup",
         scratch=[pltpu.VMEM((8, 512), i32)],
     )
-    fields = jnp.concatenate([start_vector, initial_guess], axis=0)
+    fields = start_vector
     history = []
-    for turn, nf in enumerate((2, 2, 1, 1)):
+    for turn, (nf, nf_next) in enumerate(((1, 2), (2, 2), (2, 1), (1, 0))):
         h = 32 * nf
         def own_work():
             return run(
@@ -689,51 +768,66 @@
                 "own",
             )
 
-        def side_work():
+        def side_work(hots):
             return run(
                 functools.partial(sides_kernel, nf),
                 [((h, side_pad + 256), f32), ((h, side_pad), f32), ((h, 384), f32)],
-                [stack, interp, own_hot, partner_hot, far_hot, info, arrival],
+                [stack, interp, *hots, *places],
                 "sides",
             )
 
-        def first_work():
-            return run(
+        if turn == 0:
+            *hots, place, info, arrival = run(
                 functools.partial(setup_kernel, chips),
-                [((8, side_pad + 256), f32), ((768, side_pad + 256), bf16), ((768, side_pad), bf16),
-                 ((768, 384), bf16), ((8, 640), f32)],
+                [((lanes, side_pad + 256), bf16), ((lanes, side_pad), bf16), ((lanes, 384), bf16),
+                 ((16, side_pad + 640), f32), ((8, side_pad + 256), f32), ((8, 640), f32)],
                 [coef, level, sides],
                 "setup",
-                scratch=[pltpu.VMEM((640, side_pad), bf16)],
             )
-
-        arrivals, last, made = exchange(sent, nf, own_work, side_work if turn else first_work)
-        if turn == 0:
-            info, own_hot, partner_hot, far_hot, arrival = made
-            made = side_work()
+            places = [place, info, arrival]
+            own_scatter, _, far_scatter = hots
+        elif turn == 1:
+            hots = run(
+                whole_kernel,
+                [((768, side_pad + 256), bf16), ((768, side_pad), bf16), ((768, 384), bf16)],
+                [*hots, place],
+                "whole",
+            )
+            own_scatter, far_scatter = run(
+                turn_kernel,
+                [((side_pad + 256, 768), bf16), ((384, 768), bf16)],
+                [place],
+                "turn",
+            )
+        arrivals, last, made = exchange(
+            sent, nf, own_work, functools.partial(side_work, hots),
+            *((hots[0], own_scatter) if turn == 1 else ()),
+        )
         mine, others, targets = made
         sums, *made = run(
             functools.partial(flux_kernel, nf, chips),
             [((h, 768), f32)] + ([] if turn else [((8, 256), f32)]),
-            [*arrivals, mine, others, info, arrival, weight, interp_t, own_hot]
+            [*arrivals, mine, others, *places, weight, interp_t, own_scatter]
             + ([near_halo] if turn else []),
             "flux",
         )
         if turn == 0:
             near_halo = made[0]
-        nf_next = (2, 1, 1, 0)[turn]
         ins = [
-            last, sums, targets, arrival, far_hot, weight, interp_t, lift,
-            fields, coef, level, block_inverse, far_halo if turn else rhs_field,
+            last, sums, targets, place, arrival, far_scatter, weight, interp_t, lift,
+            fields, coef, level, block_inverse,
         ]
-        outs = [((64 * nf, lanes), f32)]
+        ins += [far_halo] if turn else [guess]
+        ins += [rhs_field] if turn == 1 else []
         if nf_next:
             ins += [trace, interp, hot, case]
-            outs += [((64 * nf_next, 768), bf16), ((32 * nf_next, 256), f32)]
+            outs = [
+                ((64 * max(nf, nf_next), lanes), f32), ((64 * nf_next, 768), bf16), ((32 * nf_next, 256), f32)
+            ]
         else:
-            outs += [((devices, lanes), f32)]
+            outs = [((devices, lanes), f32)]
         made = run(
-            functools.partial(update_kernel, nf, nf_next, turn == 0),
+            functools.partial(update_kernel, turn, nf, nf_next),
             outs + ([] if turn else [((8, 384), f32)]), ins, "update",
             scratch=[pltpu.VMEM((64 * nf, lanes), f32)],
         )
@@ -745,12 +839,12 @@
             if nf_next < nf:
                 fields = fields[:64]
         else:
-            fields, parts = made
+            (parts,) = made
     parts = lax.all_to_all(parts.reshape(devices, 1, lanes), "dom", 0, 0).reshape(devices, lanes)
     smoothed, bound = run(
         finish_kernel,
         [((64, lanes), f32), ((1, lanes), f32)],
-        [parts, initial_guess, history[0], history[1]],
+        [parts, guess, history[1], history[2]],
         "finish",
         kept=False,
     )

time: 56.8 us -> 54.7 us (0.963)
  Pallas kernels: 23.4 us -> 21.5 us
    pallas_call x28 -> x30, Pallas kernels: 23.4 us -> 21.5 us  [run(): pl.pallas_call(body, out_shape=[(pltpu.VMEM if kept else jax.ShapeDtypeSt...]
  transfers between devices with their start and end apart: 16 -> 16, of which waited for: 9 -> 11; matrix products, arithmetic and copies ran while one was open for 0% -> 0% of each run, Pallas kernels for 24% -> 23%
where the time goes in v4:
time: 54.7 us; the launch traced here: 54.5 us
  Pallas kernels  21.5 us (39%)
  starting transfers between devices  16 us (29%)
  blocking collectives  12.1 us (22%)
  waiting for transfers between devices  3.93 us (7%)
  between operations  0.88 us (2%)
    pallas_call x30, Pallas kernels, run(): pl.pallas_call(body, out_shape=[(pltpu.VMEM if kept else jax.ShapeDtypeSt...  21.5 us
    ppermute x16, starting transfers between devices, permute(): return lax.ppermute(x, 'dom', sorted(to.items()))  16 us
    all_to_all x1, blocking collectives, local(): lax.all_to_all(parts.reshape(devices, 1, lanes), 'dom', 0, 0)  12.1 us
    ppermute x16, waiting for transfers between devices, permute(): return lax.ppermute(x, 'dom', sorted(to.items()))  3.93 us
  transfers between devices with their start and end apart: 16, of which 11 were waited for; matrix products, arithmetic and copies ran while one was open for 0% of the time, Pallas kernels for 23%

profile of v4, /device:TPU:0, one launch (start us, length us, event | category | flops | bytes accessed | tf_op | source)
XLA Modules:
  0.0 54.5 jit_solution(9519766644049364616)
XLA Ops:
  0.6 0.0 copy-start.3
  0.6 0.0 copy-start.1
  0.7 0.0 copy-start.2
  0.7 1.9 %send_setup.1 = (bf16[768,256]{1,0:T(8,128)(2,1)S(1)}, s32[8,256]{1,0:T(8,128)S(1)}, bf16[80,768]{1,0:T(8,128)(2,1)S(1)}, s32[8,1024]{1,0:T(8,128)S(1)}, s32[32,...) custom-call(s32[1,930]{1,0:T(1,128)} %bitcast.15, ...), custom_call_target="tpu_custom_call" | custom-call | flops 16777216 | bytes 1048576 | tf_op jit(solution)/shard_map/send_setup/pallas_call | solution.py:685
  2.6 0.5 collective-permute-start
  3.1 0.3 own_setup.1
  3.4 0.4 own.4.own_ref
  3.8 0.1 collective-permute-done.sent_ref
  4.0 0.1 carry.4
  4.0 2.8 %collective-permute-start.1 = (f32[40,256]{1,0:T(8,128)S(1)}, f32[40,256]{1,0:T(8,128)S(1)}, u32[]{:S(2)}, u32[]{:S(2)}) collective-permute-start(f32[40,256]{1,0:T(8,128)S(1)} %get-tuple-element.67), channel_id=1, source_target_pairs={{0,2},{1,0},{2,1},{3,5},{4,6},{5,3},{6,4},{7,9},{8,10},{9,7},{10,8... | collective-permute-start | bytes 122888 | tf_op jit(solution)/shard_map/ppermute | solution.py:708
  6.9 1.5 %collective-permute-start.2 = (f32[40,128]{1,0:T(8,128)S(1)}, f32[40,128]{1,0:T(8,128)S(1)}, u32[]{:S(2)}, u32[]{:S(2)}) collective-permute-start(f32[40,128]{1,0:T(8,128)S(1)} %get-tuple-element.68), channel_id=1, source_target_pairs={{0,4},{1,3},{2,6},{3,1},{4,0},{5,9},{6,2},{7,11},{8,12},{9,5},{10,... | collective-permute-start | bytes 61448 | tf_op jit(solution)/shard_map/ppermute | solution.py:708
  8.4 0.7 %setup.1 = (bf16[128,1280]{1,0:T(8,128)(2,1)S(1)}, bf16[128,1024]{1,0:T(8,128)(2,1)S(1)}, bf16[128,384]{1,0:T(8,128)(2,1)S(1)}, f32[16,1664]{1,0:T(8,128)S(1)}, ...) custom-call(f32[1,128]{1,0:T(1,128)S(1)} %get-tuple-element.69.coef_ref, s32[1,128]{1,0:T(1,128)S(1)} %get-tuple-element.70.level_ref, ...), custom_call_target="tpu_custom_call" | custom-call | flops 16777216 | bytes 1048576 | tf_op jit(solution)/shard_map/setup/pallas_call | solution.py:685
  9.1 1.2 %sides.4 = (f32[32,1280]{1,0:T(8,128)S(1)}, f32[32,1024]{1,0:T(8,128)S(1)}, f32[32,384]{1,0:T(8,128)S(1)}) custom-call(bf16[80,768]{1,0:T(8,128)(2,1)S(1)} %get-tuple-element.61.stack_ref, bf16[128,96]{1,0:T(8,128)(2,1)S(1)} %get-tuple-element.66.interp_ref.rest_2_.rest_3_, bf16[128,1280]{1,0:T(8,128)(2,1)S(1)} %get-tuple-element.71.own_hot_ref.own_elem_ref, ...), custom_call_target="tpu_custom_call" | custom-call | flops 16777216 | bytes 1048576 | tf_op jit(solution)/shard_map/sides/pallas_call | solution.py:685
  10.3 0.3 collective-permute-done.2.two_ref
  10.7 0.0 collective-permute-done.1.one_ref
  10.7 0.1 relay.4
  10.7 0.0 collective-permute-start.3
  10.8 0.7 %flux.4 = (f32[32,768]{1,0:T(8,128)S(1)}, f32[8,256]{1,0:T(8,128)S(1)}) custom-call(f32[40,256]{1,0:T(8,128)S(1)} %collective-permute-done.1.one_ref, f32[40,128]{1,0:T(8,128)S(1)} %collective-permute-done.2.two_ref, f32[32,1280]{1,0:T(8,128)S(1)} %get-tuple-element.78.mine_ref, f32[32,1024]{1,0:T(8,128)S(1)} %get-tuple-element.79.other_ref, ...), custom_call_target="tpu_custom_call" | custom-call | flops 16777216 | bytes 1048576 | tf_op jit(solution)/shard_map/flux/pallas_call | solution.py:685
  11.5 0.5 collective-permute-done.3.one_ref
  12.0 1.4 %update.4 = (f32[128,128]{1,0:T(8,128)S(1)}, bf16[128,768]{1,0:T(8,128)(2,1)S(1)}, f32[64,256]{1,0:T(8,128)S(1)}, f32[8,384]{1,0:T(8,128)S(1)}) custom-call(f32[40,384]{1,0:T(8,128)S(1)} %collective-permute-done.3.one_ref, f32[32,768]{1,0:T(8,128)S(1)} %get-tuple-element.80.local_ref, f32[32,384]{1,0:T(8,128)S(1)} %get-tuple-element.77.rest_0_.target_ref, ...), custom_call_target="tpu_custom_call" | custom-call | flops 16777216 | bytes 1048576 | tf_op jit(solution)/shard_map/update/pallas_call | solution.py:685
  13.4 0.2 collective-permute-start.4
  13.6 0.4 whole.1
  14.0 0.5 own.5.own_ref
  14.5 0.3 collective-permute-done.4.sent_ref
  14.8 0.1 carry.5
  14.8 0.6 %collective-permute-start.5 = (f32[64,256]{1,0:T(8,128)S(1)}, f32[64,256]{1,0:T(8,128)S(1)}, u32[]{:S(2)}, u32[]{:S(2)}) collective-permute-start(f32[64,256]{1,0:T(8,128)S(1)} %get-tuple-element.88), channel_id=1, source_target_pairs={{0,2},{1,0},{2,1},{3,5},{4,6},{5,3},{6,4},{7,9},{8,10},{9,7},{10,8... | collective-permute-start | bytes 196616 | tf_op jit(solution)/shard_map/ppermute | solution.py:708
  15.4 1.9 %collective-permute-start.6 = (f32[64,128]{1,0:T(8,128)S(1)}, f32[64,128]{1,0:T(8,128)S(1)}, u32[]{:S(2)}, u32[]{:S(2)}) collective-permute-start(f32[64,128]{1,0:T(8,128)S(1)} %get-tuple-element.89), channel_id=1, source_target_pairs={{0,4},{1,3},{2,6},{3,1},{4,0},{5,9},{6,2},{7,11},{8,12},{9,5},{10,... | collective-permute-start | bytes 98312 | tf_op jit(solution)/shard_map/ppermute | solution.py:708
  17.3 0.7 %turn.1 = (bf16[1280,768]{1,0:T(8,128)(2,1)S(1)}, bf16[384,768]{1,0:T(8,128)(2,1)S(1)}) custom-call(f32[16,1664]{1,0:T(8,128)S(1)} %get-tuple-element.74.place_ref), custom_call_target="tpu_custom_call" | custom-call | flops 16777216 | bytes 1048576 | tf_op jit(solution)/shard_map/turn/pallas_call | solution.py:685
  18.0 1.5 %sides.5 = (f32[64,1280]{1,0:T(8,128)S(1)}, f32[64,1024]{1,0:T(8,128)S(1)}, f32[64,384]{1,0:T(8,128)S(1)}) custom-call(bf16[128,768]{1,0:T(8,128)(2,1)S(1)} %get-tuple-element.86.stack_ref, bf16[128,96]{1,0:T(8,128)(2,1)S(1)} %get-tuple-element.66.interp_ref.rest_2_.rest_3_, bf16[768,1280]{1,0:T(8,128)(2,1)S(1)} %get-tuple-element.87.rest_0_.own_hot_ref, ...), custom_call_target="tpu_custom_call" | custom-call | flops 16777216 | bytes 1048576 | tf_op jit(solution)/shard_map/sides/pallas_call | solution.py:685
  19.5 0.0 collective-permute-done.5.one_ref
  19.5 0.1 relay.5
  19.6 0.4 collective-permute-start.7
  20.0 0.9 %flux.5.local_ref = f32[64,768]{1,0:T(8,128)S(1)} custom-call(f32[64,256]{1,0:T(8,128)S(1)} %collective-permute-done.5.one_ref, f32[64,128]{1,0:T(8,128)S(1)} %collective-permute-done.6.two_ref, f32[64,1280]{1,0:T(8,128)S(1)} %get-tuple-element.94.mine_ref, f32[64,1024]{1,0:T(8,128)S(1)} %get-tuple-element.95.other_ref, ...), custom_call_target="tpu_custom_call" | custom-call | flops 16777216 | bytes 1048576 | tf_op jit(solution)/shard_map/flux/pallas_call | solution.py:685
  20.9 0.1 collective-permute-done.7.one_ref
  21.0 1.7 %update.5 = (f32[128,128]{1,0:T(8,128)S(1)}, bf16[128,768]{1,0:T(8,128)(2,1)S(1)}, f32[64,256]{1,0:T(8,128)S(1)}) custom-call(f32[64,384]{1,0:T(8,128)S(1)} %collective-permute-done.7.one_ref, f32[64,768]{1,0:T(8,128)S(1)} %flux.5.local_ref, f32[64,384]{1,0:T(8,128)S(1)} %get-tuple-element.92.rest_0_.target_ref, f32[16,1664]{1,0:T(8,128)S(1)} %get-tuple-element.74.place_ref, ...), custom_call_target="tpu_custom_call" | custom-call | flops 16777216 | bytes 1048576 | tf_op jit(solution)/shard_map/update/pallas_call | solution.py:685
  22.7 0.4 collective-permute-start.8
  23.1 0.5 own.6.own_ref
  23.6 0.4 collective-permute-done.8.sent_ref
  24.0 0.1 carry.6
  24.1 1.6 %collective-permute-start.9 = (f32[64,256]{1,0:T(8,128)S(1)}, f32[64,256]{1,0:T(8,128)S(1)}, u32[]{:S(2)}, u32[]{:S(2)}) collective-permute-start(f32[64,256]{1,0:T(8,128)S(1)} %get-tuple-element.102), channel_id=1, source_target_pairs={{0,2},{1,0},{2,1},{3,5},{4,6},{5,3},{6,4},{7,9},{8,10},{9,7},{10,8... | collective-permute-start | bytes 196616 | tf_op jit(solution)/shard_map/ppermute | solution.py:708
  25.7 2.5 %collective-permute-start.10 = (f32[64,128]{1,0:T(8,128)S(1)}, f32[64,128]{1,0:T(8,128)S(1)}, u32[]{:S(2)}, u32[]{:S(2)}) collective-permute-start(f32[64,128]{1,0:T(8,128)S(1)} %get-tuple-element.103), channel_id=1, source_target_pairs={{0,4},{1,3},{2,6},{3,1},{4,0},{5,9},{6,2},{7,11},{8,12},{9,5},{10,... | collective-permute-start | bytes 98312 | tf_op jit(solution)/shard_map/ppermute | solution.py:708
  28.2 1.5 %sides.6 = (f32[64,1280]{1,0:T(8,128)S(1)}, f32[64,1024]{1,0:T(8,128)S(1)}, f32[64,384]{1,0:T(8,128)S(1)}) custom-call(bf16[128,768]{1,0:T(8,128)(2,1)S(1)} %get-tuple-element.101.stack_ref, bf16[128,96]{1,0:T(8,128)(2,1)S(1)} %get-tuple-element.66.interp_ref.rest_2_.rest_3_, bf16[768,1280]{1,0:T(8,128)(2,1)S(1)} %get-tuple-element.87.rest_0_.own_hot_ref, ...), custom_call_target="tpu_custom_call" | custom-call | flops 16777216 | bytes 1048576 | tf_op jit(solution)/shard_map/sides/pallas_call | solution.py:685
  29.7 0.4 collective-permute-done.10.two_ref
  30.1 0.1 relay.6
  30.2 0.1 collective-permute-start.11
  30.2 0.9 %flux.6.local_ref = f32[64,768]{1,0:T(8,128)S(1)} custom-call(f32[64,256]{1,0:T(8,128)S(1)} %collective-permute-done.9.one_ref, f32[64,128]{1,0:T(8,128)S(1)} %collective-permute-done.10.two_ref, f32[64,1280]{1,0:T(8,128)S(1)} %get-tuple-element.105.mine_ref, f32[64,1024]{1,0:T(8,128)S(1)} %get-tuple-element.106.other_ref, ...), custom_call_target="tpu_custom_call" | custom-call | flops 16777216 | bytes 1048576 | tf_op jit(solution)/shard_map/flux/pallas_call | solution.py:685
  31.1 0.4 collective-permute-done.11.one_ref
  31.5 1.6 %update.6 = (f32[128,128]{1,0:T(8,128)S(1)}, bf16[64,768]{1,0:T(8,128)(2,1)S(1)}, f32[32,256]{1,0:T(8,128)S(1)}) custom-call(f32[64,384]{1,0:T(8,128)S(1)} %collective-permute-done.11.one_ref, f32[64,768]{1,0:T(8,128)S(1)} %flux.6.local_ref, f32[64,384]{1,0:T(8,128)S(1)} %get-tuple-element.104.rest_0_.target_ref, ...), custom_call_target="tpu_custom_call" | custom-call | flops 16777216 | bytes 1048576 | tf_op jit(solution)/shard_map/update/pallas_call | solution.py:685
  33.1 0.2 collective-permute-start.12
  33.3 0.4 own.7.own_ref
  33.8 0.6 %collective-permute-done.12.sent_ref = f32[32,256]{1,0:T(8,128)S(1)} collective-permute-done((f32[32,256]{1,0:T(8,128)S(1)}, f32[32,256]{1,0:T(8,128)S(1)}, u32[]{:S(2)}, u32[]{:S(2)}) %collective-permute-start.12) | collective-permute-done | bytes 32800 | tf_op jit(solution)/shard_map/ppermute | solution.py:708
  34.4 0.1 carry.7
  34.5 0.5 collective-permute-start.13
  35.0 2.7 %collective-permute-start.14 = (f32[32,128]{1,0:T(8,128)S(1)}, f32[32,128]{1,0:T(8,128)S(1)}, u32[]{:S(2)}, u32[]{:S(2)}) collective-permute-start(f32[32,128]{1,0:T(8,128)S(1)} %get-tuple-element.111), channel_id=1, source_target_pairs={{0,4},{1,3},{2,6},{3,1},{4,0},{5,9},{6,2},{7,11},{8,12},{9,5},{10,... | collective-permute-start | bytes 49160 | tf_op jit(solution)/shard_map/ppermute | solution.py:708
  37.7 1.3 %sides.7 = (f32[32,1280]{1,0:T(8,128)S(1)}, f32[32,1024]{1,0:T(8,128)S(1)}, f32[32,384]{1,0:T(8,128)S(1)}) custom-call(bf16[64,768]{1,0:T(8,128)(2,1)S(1)} %get-tuple-element.109.stack_ref, bf16[128,96]{1,0:T(8,128)(2,1)S(1)} %get-tuple-element.66.interp_ref.rest_2_.rest_3_, bf16[768,1280]{1,0:T(8,128)(2,1)S(1)} %get-tuple-element.87.rest_0_.own_hot_ref, ...), custom_call_target="tpu_custom_call" | custom-call | flops 16777216 | bytes 1048576 | tf_op jit(solution)/shard_map/sides/pallas_call | solution.py:685
  39.0 0.4 collective-permute-done.14.two_ref
  39.4 0.0 collective-permute-done.13.one_ref
  39.4 0.1 relay.7
  39.5 0.1 collective-permute-start.15
  39.6 0.7 %flux.7.local_ref = f32[32,768]{1,0:T(8,128)S(1)} custom-call(f32[32,256]{1,0:T(8,128)S(1)} %collective-permute-done.13.one_ref, f32[32,128]{1,0:T(8,128)S(1)} %collective-permute-done.14.two_ref, f32[32,1280]{1,0:T(8,128)S(1)} %get-tuple-element.113.mine_ref, f32[32,1024]{1,0:T(8,128)S(1)} %get-tuple-element.114.other_ref, ...), custom_call_target="tpu_custom_call" | custom-call | flops 16777216 | bytes 1048576 | tf_op jit(solution)/shard_map/flux/pallas_call | solution.py:685
  40.3 0.4 collective-permute-done.15.one_ref
  40.7 0.9 %update.7 = f32[32,128]{1,0:T(8,128)S(1)} custom-call(f32[32,384]{1,0:T(8,128)S(1)} %collective-permute-done.15.one_ref, f32[32,768]{1,0:T(8,128)S(1)} %flux.7.local_ref, f32[32,384]{1,0:T(8,128)S(1)} %get-tuple-element.112.rest_0_.target_ref, f32[16,1664]{1,0:T(8,128)S(1)} %get-tuple-element.74.place_ref, f32[8,640]{1,0:T(8,128)S(1)} %get-tuple-element.76.arrival_ref, ...), custom_call_target="tpu_custom_call" | custom-call | flops 16777216 | bytes 1048576 | tf_op jit(solution)/shard_map/update/pallas_call | solution.py:685
  41.6 12.1 %all_to_all.5 = f32[32,1,128]{2,1,0:T(1,128)S(1)} all-to-all(f32[32,1,128]{2,1,0:T(1,128)S(1)} %bitcast.13), channel_id=1, replica_groups=mesh['dom'=32] {'dom'}, dimensions={0} | all-to-all | bytes 32768 | tf_op jit(solution)/shard_map/all_to_all | solution.py:843
  53.8 0.7 %finish.1 = (f32[64,128]{1,0:T(8,128)}, f32[1,128]{1,0:T(1,128)}) custom-call(f32[32,128]{1,0:T(8,128)S(1)} %bitcast.14, f32[64,128]{1,0:T(8,128)S(1)} %get-tuple-element.81.rest_0_.guess_ref, f32[128,128]{1,0:T(8,128)S(1)} %get-tuple-element.107.field_ref.first_ref, f32[128,128]{1,0:T(8,128)S(1)} %get-tuple-element.115.second_ref), custom_call_target="tpu_custom_call" | custom-call | flops 16777216 | bytes 1048576 | tf_op jit(solution)/shard_map/finish/pallas_call | solution.py:685
  (12 shorter events, 0.0 us)
Async XLA Ops:
  0.6 10.1 %copy-start.3 = (f32[32,128]{1,0:T(8,128)S(1)}, f32[32,128]{1,0:T(8,128)}, u32[]{:S(2)}) copy-start(f32[32,128]{1,0:T(8,128)} %constant.14.clone.weight_ref) | copy-start | bytes 49156
  0.6 10.1 %copy-start.1 = (bf16[128,96]{1,0:T(8,128)(2,1)S(1)}, bf16[128,96]{1,0:T(8,128)(2,1)}, u32[]{:S(2)}) copy-start(bf16[128,96]{1,0:T(8,128)(2,1)} %constant.12.clone.interp_ref.interp_t_ref) | copy-start | bytes 73732
  0.7 11.3 %copy-start.2 = (bf16[64,768]{1,0:T(8,128)(2,1)S(1)}, bf16[64,768]{1,0:T(8,128)(2,1)}, u32[]{:S(2)}) copy-start(bf16[64,768]{1,0:T(8,128)(2,1)} %constant.13.clone.lift_ref) | copy-start | bytes 294916
  0.7 11.3 %copy-start.4 = (f32[64,128]{1,0:T(8,128)S(1)}, f32[64,128]{1,0:T(8,128)}, u32[]{:S(2)}) copy-start(f32[64,128]{1,0:T(8,128)} %field_ref.1) | copy-start | bytes 98308
  0.7 11.3 %copy-start = (bf16[64,64,128]{2,1,0:T(8,128)(2,1)S(1)}, bf16[64,64,128]{2,1,0:T(8,128)(2,1)}, u32[]{:S(2)}) copy-start(bf16[64,64,128]{2,1,0:T(8,128)(2,1)} %inverse_ref.7) | copy-start | bytes 3145732
  2.6 1.4 %collective-permute-start = (f32[40,256]{1,0:T(8,128)S(1)}, f32[40,256]{1,0:T(8,128)S(1)}, u32[]{:S(2)}, u32[]{:S(2)}) collective-permute-start(f32[40,256]{1,0:T(8,128)S(1)} %get-tuple-element.60), channel_id=1, source_target_pairs={{0,1},{1,0},{2,3},{3,2},{4,5},{5,4},{6,7},{7,6},{8,9},{9,8},{10,11... | collective-permute-start | bytes 122888 | tf_op jit(solution)/shard_map/ppermute | solution.py:708
  4.0 6.6 %collective-permute-start.1 = (f32[40,256]{1,0:T(8,128)S(1)}, f32[40,256]{1,0:T(8,128)S(1)}, u32[]{:S(2)}, u32[]{:S(2)}) collective-permute-start(f32[40,256]{1,0:T(8,128)S(1)} %get-tuple-element.67), channel_id=1, source_target_pairs={{0,2},{1,0},{2,1},{3,5},{4,6},{5,3},{6,4},{7,9},{8,10},{9,7},{10,8... | collective-permute-start | bytes 122888 | tf_op jit(solution)/shard_map/ppermute | solution.py:708
  6.9 3.8 %collective-permute-start.2 = (f32[40,128]{1,0:T(8,128)S(1)}, f32[40,128]{1,0:T(8,128)S(1)}, u32[]{:S(2)}, u32[]{:S(2)}) collective-permute-start(f32[40,128]{1,0:T(8,128)S(1)} %get-tuple-element.68), channel_id=1, source_target_pairs={{0,4},{1,3},{2,6},{3,1},{4,0},{5,9},{6,2},{7,11},{8,12},{9,5},{10,... | collective-permute-start | bytes 61448 | tf_op jit(solution)/shard_map/ppermute | solution.py:708
  10.7 1.3 %collective-permute-start.3 = (f32[40,384]{1,0:T(8,128)S(1)}, f32[40,384]{1,0:T(8,128)S(1)}, u32[]{:S(2)}, u32[]{:S(2)}) collective-permute-start(f32[40,384]{1,0:T(8,128)S(1)} %relay.4), channel_id=1, source_target_pairs={{0,1},{1,0},{2,3},{3,2},{4,5},{5,4},{6,7},{7,6},{8,9},{9,8},{10,11... | collective-permute-start | bytes 184328 | tf_op jit(solution)/shard_map/ppermute | solution.py:708
  13.4 1.3 %collective-permute-start.4 = (f32[64,256]{1,0:T(8,128)S(1)}, f32[64,256]{1,0:T(8,128)S(1)}, u32[]{:S(2)}, u32[]{:S(2)}) collective-permute-start(f32[64,256]{1,0:T(8,128)S(1)} %get-tuple-element.85), channel_id=1, source_target_pairs={{0,1},{1,0},{2,3},{3,2},{4,5},{5,4},{6,7},{7,6},{8,9},{9,8},{10,11... | collective-permute-start | bytes 196616 | tf_op jit(solution)/shard_map/ppermute | solution.py:708
  14.8 4.7 %collective-permute-start.5 = (f32[64,256]{1,0:T(8,128)S(1)}, f32[64,256]{1,0:T(8,128)S(1)}, u32[]{:S(2)}, u32[]{:S(2)}) collective-permute-start(f32[64,256]{1,0:T(8,128)S(1)} %get-tuple-element.88), channel_id=1, source_target_pairs={{0,2},{1,0},{2,1},{3,5},{4,6},{5,3},{6,4},{7,9},{8,10},{9,7},{10,8... | collective-permute-start | bytes 196616 | tf_op jit(solution)/shard_map/ppermute | solution.py:708
  15.4 4.1 %collective-permute-start.6 = (f32[64,128]{1,0:T(8,128)S(1)}, f32[64,128]{1,0:T(8,128)S(1)}, u32[]{:S(2)}, u32[]{:S(2)}) collective-permute-start(f32[64,128]{1,0:T(8,128)S(1)} %get-tuple-element.89), channel_id=1, source_target_pairs={{0,4},{1,3},{2,6},{3,1},{4,0},{5,9},{6,2},{7,11},{8,12},{9,5},{10,... | collective-permute-start | bytes 98312 | tf_op jit(solution)/shard_map/ppermute | solution.py:708
  19.6 1.4 %copy-start.5 = (f32[64,128]{1,0:T(8,128)S(1)}, f32[64,128]{1,0:T(8,128)}, u32[]{:S(2)}) copy-start(f32[64,128]{1,0:T(8,128)} %rest_1_.1) | copy-start | bytes 98308
  19.6 1.4 %collective-permute-start.7 = (f32[64,384]{1,0:T(8,128)S(1)}, f32[64,384]{1,0:T(8,128)S(1)}, u32[]{:S(2)}, u32[]{:S(2)}) collective-permute-start(f32[64,384]{1,0:T(8,128)S(1)} %relay.5), channel_id=1, source_target_pairs={{0,1},{1,0},{2,3},{3,2},{4,5},{5,4},{6,7},{7,6},{8,9},{9,8},{10,11... | collective-permute-start | bytes 294920 | tf_op jit(solution)/shard_map/ppermute | solution.py:708
  22.7 1.3 %collective-permute-start.8 = (f32[64,256]{1,0:T(8,128)S(1)}, f32[64,256]{1,0:T(8,128)S(1)}, u32[]{:S(2)}, u32[]{:S(2)}) collective-permute-start(f32[64,256]{1,0:T(8,128)S(1)} %get-tuple-element.100), channel_id=1, source_target_pairs={{0,1},{1,0},{2,3},{3,2},{4,5},{5,4},{6,7},{7,6},{8,9},{9,8},{10,11... | collective-permute-start | bytes 196616 | tf_op jit(solution)/shard_map/ppermute | solution.py:708
  24.1 6.0 %collective-permute-start.9 = (f32[64,256]{1,0:T(8,128)S(1)}, f32[64,256]{1,0:T(8,128)S(1)}, u32[]{:S(2)}, u32[]{:S(2)}) collective-permute-start(f32[64,256]{1,0:T(8,128)S(1)} %get-tuple-element.102), channel_id=1, source_target_pairs={{0,2},{1,0},{2,1},{3,5},{4,6},{5,3},{6,4},{7,9},{8,10},{9,7},{10,8... | collective-permute-start | bytes 196616 | tf_op jit(solution)/shard_map/ppermute | solution.py:708
  25.7 4.4 %collective-permute-start.10 = (f32[64,128]{1,0:T(8,128)S(1)}, f32[64,128]{1,0:T(8,128)S(1)}, u32[]{:S(2)}, u32[]{:S(2)}) collective-permute-start(f32[64,128]{1,0:T(8,128)S(1)} %get-tuple-element.103), channel_id=1, source_target_pairs={{0,4},{1,3},{2,6},{3,1},{4,0},{5,9},{6,2},{7,11},{8,12},{9,5},{10,... | collective-permute-start | bytes 98312 | tf_op jit(solution)/shard_map/ppermute | solution.py:708
  30.2 1.3 %collective-permute-start.11 = (f32[64,384]{1,0:T(8,128)S(1)}, f32[64,384]{1,0:T(8,128)S(1)}, u32[]{:S(2)}, u32[]{:S(2)}) collective-permute-start(f32[64,384]{1,0:T(8,128)S(1)} %relay.6), channel_id=1, source_target_pairs={{0,1},{1,0},{2,3},{3,2},{4,5},{5,4},{6,7},{7,6},{8,9},{9,8},{10,11... | collective-permute-start | bytes 294920 | tf_op jit(solution)/shard_map/ppermute | solution.py:708
  33.1 1.3 %collective-permute-start.12 = (f32[32,256]{1,0:T(8,128)S(1)}, f32[32,256]{1,0:T(8,128)S(1)}, u32[]{:S(2)}, u32[]{:S(2)}) collective-permute-start(f32[32,256]{1,0:T(8,128)S(1)} %get-tuple-element.108), channel_id=1, source_target_pairs={{0,1},{1,0},{2,3},{3,2},{4,5},{5,4},{6,7},{7,6},{8,9},{9,8},{10,11... | collective-permute-start | bytes 98312 | tf_op jit(solution)/shard_map/ppermute | solution.py:708
  34.5 4.9 %collective-permute-start.13 = (f32[32,256]{1,0:T(8,128)S(1)}, f32[32,256]{1,0:T(8,128)S(1)}, u32[]{:S(2)}, u32[]{:S(2)}) collective-permute-start(f32[32,256]{1,0:T(8,128)S(1)} %get-tuple-element.110), channel_id=1, source_target_pairs={{0,2},{1,0},{2,1},{3,5},{4,6},{5,3},{6,4},{7,9},{8,10},{9,7},{10,8... | collective-permute-start | bytes 98312 | tf_op jit(solution)/shard_map/ppermute | solution.py:708
  35.0 4.4 %collective-permute-start.14 = (f32[32,128]{1,0:T(8,128)S(1)}, f32[32,128]{1,0:T(8,128)S(1)}, u32[]{:S(2)}, u32[]{:S(2)}) collective-permute-start(f32[32,128]{1,0:T(8,128)S(1)} %get-tuple-element.111), channel_id=1, source_target_pairs={{0,4},{1,3},{2,6},{3,1},{4,0},{5,9},{6,2},{7,11},{8,12},{9,5},{10,... | collective-permute-start | bytes 49160 | tf_op jit(solution)/shard_map/ppermute | solution.py:708
  39.5 1.2 %collective-permute-start.15 = (f32[32,384]{1,0:T(8,128)S(1)}, f32[32,384]{1,0:T(8,128)S(1)}, u32[]{:S(2)}, u32[]{:S(2)}) collective-permute-start(f32[32,384]{1,0:T(8,128)S(1)} %relay.7), channel_id=1, source_target_pairs={{0,1},{1,0},{2,3},{3,2},{4,5},{5,4},{6,7},{7,6},{8,9},{9,8},{10,11... | collective-permute-start | bytes 147464 | tf_op jit(solution)/shard_map/ppermute | solution.py:708

commit v5 on v4

--- a/solution.py
+++ b/solution.py
@@ -72,12 +72,10 @@
                         if along == fixed:
                             trace[face, node, nodal] = 1.0
                         trace[face, 16 + node, nodal] = sign * derivative[fixed, along]
-    quarter = [np.kron(halves[q // 2], halves[q % 2]) for q in range(4)]
-    both = np.eye(2)
-    interp = np.concatenate([np.kron(both, q) for q in quarter], axis=0)
-    interp_t = np.concatenate([np.kron(both, q.T) for q in quarter], axis=0)
     face_weight = np.kron(weights, weights)
-    return stiffness, trace.reshape(192, 64), interp, interp_t, face_weight
+    order = [16 * part + 4 * first + second for first in range(4) for part in range(2) for second in range(4)]
+    weight = np.concatenate([face_weight, face_weight])[order]
+    return stiffness, trace[:, order].reshape(192, 64), weight
 
 
 def stacked(table):
@@ -88,16 +86,10 @@
 
 
 def const_tables():
-    stiffness, trace, interp, interp_t, face_weight = basis_tables()
+    stiffness, trace, face_weight = basis_tables()
     lift = np.concatenate([stacked(trace.T), stacked(stiffness)], axis=1)
-    weight = np.broadcast_to(np.concatenate([face_weight, face_weight])[:, None], (32, lanes))
-    return (
-        stacked(trace),
-        stacked(interp),
-        stacked(interp_t),
-        lift,
-        np.asarray(weight, np.float32),
-    )
+    weight = np.broadcast_to(face_weight[:, None], (32, lanes))
+    return stacked(trace), lift, np.asarray(weight, np.float32)
 
 
 def two(x):
@@ -129,19 +121,54 @@
     return dot(table, jnp.concatenate([high, low, high], axis=0))
 
 
-def apply_case(table, x, case):
-    quarters = table_dot(table, x)
-    out = x
-    for c in range(4):
-        out = jnp.where(case == c, quarters[32 * c : 32 * c + 32], out)
-    return out
-
-
-def fields_case(table, x, case, nf):
-    wide = cat([x[32 * k : 32 * k + 32] for k in range(nf)], 1)
-    out = apply_case(table, wide, cat([case] * nf, 1))
+def interpolate(x, case, nf, transposed=False):
+    halves = [h.T if transposed else h for h in lagrange_tables()[2]]
     n = x.shape[1]
-    return cat([out[:, n * k : n * k + n] for k in range(nf)], 0)
+    case = jnp.broadcast_to(case, (8, n))
+    hanging = (case >= 0) & (case < 4)
+    place = lax.broadcasted_iota(i32, (8, n), 0) & 3
+
+    def pick(second, low, high, whole):
+        return jnp.where(hanging, jnp.where(second, high, low), whole)
+
+    def along(half, step):
+        tile = jnp.zeros((8, n), f32)
+        for j in range(4):
+            if 0 <= j + step < 4:
+                tile = jnp.where(place == j, float(half[j, j + step]), tile)
+        return tile
+
+    first, second = case >= 2, (case & 1) == 1
+    across = [
+        [pick(first, float(halves[0][i, j]), float(halves[1][i, j]), float(i == j)) for j in range(4)]
+        for i in range(4)
+    ]
+    within = {
+        step: pick(second, along(halves[0], step), along(halves[1], step), float(step == 0))
+        for step in range(-3, 4)
+    }
+    out = []
+    for k in range(nf):
+        part = [x[32 * k + 8 * i : 32 * k + 8 * i + 8] for i in range(4)]
+        for i in range(4):
+            mixed = sum(across[i][j] * part[j] for j in range(4))
+            out.append(
+                sum(
+                    within[step] * (pltpu.roll(mixed, -step % 8, 0) if step else mixed)
+                    for step in range(-3, 4)
+                )
+            )
+    return jnp.concatenate(out, axis=0)
+
+
+def other_part(x):
+    return jnp.concatenate(
+        [pltpu.roll(x[8 * g : 8 * g + 8], 4, 0) for g in range(x.shape[0] // 8)], axis=0
+    )
+
+
+def slope_rows(shape):
+    return (lax.broadcasted_iota(i32, shape, 0) & 4) == 4
 
 
 def rows_of(rows, count, width):
@@ -196,8 +223,7 @@
 
 def face_stack(trace_ref, u, normal_scale, nf):
     faces = table_dot(trace_ref[...], cat(u, 1))
-    row = lax.broadcasted_iota(i32, (32, lanes), 0)
-    scale = jnp.where(row < 16, 1.0, jnp.broadcast_to(normal_scale, (32, lanes)))
+    scale = jnp.where(slope_rows((32, lanes)), jnp.broadcast_to(normal_scale, (32, lanes)), 1.0)
     fields = []
     for k in range(nf):
         part = faces[:, lanes * k : lanes * k + lanes]
@@ -208,10 +234,10 @@
     return jnp.concatenate([high, low], axis=0)
 
 
-def gather_message(stack, hot, interp, case, nf):
+def gather_message(stack, hot, case, nf):
     got = dot(stack, hot)
     h = 32 * nf
-    out = fields_case(interp, got[:h] + got[h : 2 * h], case, nf)
+    out = interpolate(got[:h] + got[h : 2 * h], case, nf)
     if stack.shape[0] == 2 * h:
         return out
     coef = got[2 * h : 2 * h + 1] + got[2 * h + 1 : 2 * h + 2] + got[2 * h + 2 : 2 * h + 3]
@@ -287,10 +313,10 @@
 
 
 def send_setup_kernel(chips, *refs):
-    sources, refs = refs[:12], refs[12:]
+    sources, refs = refs[:11], refs[11:]
     hot_ref, case_ref, stack_ref, side_ref, rolled_ref = refs[:5]
-    sent_ref, landed = refs[5], (*refs[12:19], *refs[6:11])
-    slot_ref, arrived = refs[11], refs[19]
+    sent_ref, landed = refs[5], (*refs[11:18], *refs[6:10])
+    slot_ref, arrived = refs[10], refs[18]
     copies = [
         pltpu.make_async_copy(source, target, arrived.at[k])
         for k, (source, target) in enumerate(zip(sources, landed))
@@ -298,7 +324,7 @@
     for copy in copies:
         copy.start()
     elem_ref, dir_ref, sidecase_ref, kind_ref, partner_ref, list_ref = landed[:6]
-    start_ref, coef_ref, level_ref, trace_ref, interp_ref = landed[6:11]
+    start_ref, coef_ref, level_ref, trace_ref = landed[6:10]
     for copy in copies:
         copy.wait()
     side_ref[...] = jnp.full((8, side_pad), -1, i32)
@@ -332,7 +358,7 @@
     scalars = rows_of([x.astype(f32) for x in three(coef)] + [size], 16, lanes).astype(bf16)
     stack = jnp.concatenate([stack, jnp.concatenate([scalars] * 6, axis=1)], axis=0)
     stack_ref[...] = stack
-    sent = gather_message(stack, hot_ref[...], interp_ref[...], slot_case, 1)
+    sent = gather_message(stack, hot_ref[...], slot_case, 1)
     sent_ref[...] = sent
 
 
@@ -356,9 +382,9 @@
     fill_one_hot(hot_ref, elem, face)
 
 
-def own_kernel(nf, stack_ref, hot_ref, case_ref, interp_ref, own_ref):
+def own_kernel(nf, stack_ref, hot_ref, case_ref, own_ref):
     own_ref[...] = gather_message(
-        stack_ref[...], hot_ref[...], interp_ref[...], case_ref[0:1], nf
+        stack_ref[...], hot_ref[...], case_ref[0:1], nf
     )
 
 
@@ -508,7 +534,7 @@
 
 
 def sides_kernel(
-    nf, stack_ref, interp_ref, own_hot_ref, partner_hot_ref, far_hot_ref, place_ref, info_ref,
+    nf, stack_ref, own_hot_ref, partner_hot_ref, far_hot_ref, place_ref, info_ref,
     arrival_ref, mine_ref, other_ref, target_ref,
 ):
     stack = stack_ref[0 : 64 * nf]
@@ -519,21 +545,18 @@
         (far_hot_ref, place_ref[1:2, near:], arrival_ref[0:1, 256:640], target_ref),
     ):
         got = gather_columns(stack, hot_ref[...], face, nf)
-        out_ref[...] = fields_case(interp_ref[...], got, case.astype(i32), nf)
-
-
-def side_flux(nf, mine, outer, coefs, case, face, weight_ref, interp_ref, hot):
+        out_ref[...] = interpolate(got, case.astype(i32), nf)
+
+
+def side_flux(nf, mine, outer, coefs, case, face, weight_ref, hot):
     jump, jump_out, area, area_out = coefs
-    weight = weight_ref[0:16, 0:1]
+    weight = weight_ref[:, 0:1]
     flux = []
     for k in range(nf):
-        value, slope = mine[32 * k : 32 * k + 16], mine[32 * k + 16 : 32 * k + 32]
-        other, other_slope = outer[32 * k : 32 * k + 16], outer[32 * k + 16 : 32 * k + 32]
-        flux.append(
-            weight * (jump * value - jump_out * other - area * slope + area_out * other_slope)
-        )
-        flux.append(weight * (area_out * other - area * value))
-    flux = fields_case(interp_ref[...], jnp.concatenate(flux, axis=0), case.astype(i32), nf)
+        inner, other = mine[32 * k : 32 * k + 32], outer[32 * k : 32 * k + 32]
+        jumps = jnp.where(slope_rows(inner.shape), 0.0, jump * inner - jump_out * other)
+        flux.append(weight * (jumps - other_part(area * inner - area_out * other)))
+    flux = interpolate(cat(flux, 0), case.astype(i32), nf, transposed=True)
     return scatter_columns(flux, hot, face, nf)
 
 
@@ -543,7 +566,7 @@
 
 
 def flux_kernel(
-    nf, chips, one_ref, two_ref, mine_ref, other_ref, place_ref, info_ref, arrival_ref, weight_ref, interp_ref,
+    nf, chips, one_ref, two_ref, mine_ref, other_ref, place_ref, info_ref, arrival_ref, weight_ref,
     own_hot_ref, *rest,
 ):
     h = 32 * nf
@@ -570,7 +593,7 @@
     outer = jnp.concatenate([other_ref[...], got[0:h]], axis=1)
     sum_ref[...] = side_flux(
         nf, mine_ref, outer, coefs, info_ref[4:5], place_ref[1:2, 0 : side_pad + 256], weight_ref,
-        interp_ref, own_hot_ref[...],
+        own_hot_ref[...],
     )
 
 
@@ -585,7 +608,7 @@
 
 def update_kernel(
     turn, nf, nf_next,
-    one_ref, local_ref, target_ref, place_ref, arrival_ref, far_hot_ref, weight_ref, interp_t_ref, lift_ref,
+    one_ref, local_ref, target_ref, place_ref, arrival_ref, far_hot_ref, weight_ref, lift_ref,
     field_ref, coef_ref, level_ref, inverse_ref, *rest,
 ):
     if turn == 0:
@@ -595,7 +618,7 @@
     if turn == 1:
         rhs_ref, *rest = rest
     if nf_next:
-        trace_ref, interp_ref, hot_ref, case_ref, new_ref, stack_ref, sent_ref, *rest = rest
+        trace_ref, hot_ref, case_ref, new_ref, stack_ref, sent_ref, *rest = rest
     else:
         part_ref, *rest = rest
     hold_ref = rest[-1]
@@ -610,11 +633,10 @@
         halo = (halo_ref[0:1], halo_ref[1:2])
     total = local_ref[...] + side_flux(
         nf, target_ref, one_ref, (halo[0], halo[0], halo[1], halo[1]), arrival_ref[0:1, 256:640],
-        place_ref[1:2, side_pad + 256 :], weight_ref, interp_t_ref, far_hot_ref[...],
+        place_ref[1:2, side_pad + 256 :], weight_ref, far_hot_ref[...],
     )
     coef, size, volume_scale, normal_scale = element_rows(coef_ref, level_ref)
-    row = lax.broadcasted_iota(i32, (32, lanes), 0)
-    scale = jnp.where(row < 16, 1.0, jnp.broadcast_to(normal_scale, (32, lanes)))
+    scale = jnp.where(slope_rows((32, lanes)), jnp.broadcast_to(normal_scale, (32, lanes)), 1.0)
     operands = []
     for k in range(nf):
         mine = total[32 * k : 32 * k + 32]
@@ -640,7 +662,7 @@
             new_ref[64 * k : 64 * k + 64, :] = x
         stack = face_stack(trace_ref, new[:nf_next], normal_scale, nf_next)
         stack_ref[...] = stack
-        sent = gather_message(stack, hot_ref[...], interp_ref[...], case_ref[0:1], nf_next)
+        sent = gather_message(stack, hot_ref[...], case_ref[0:1], nf_next)
         sent_ref[...] = sent
     else:
         lane = lax.broadcasted_iota(i32, (1, lanes), 1)
@@ -700,7 +722,7 @@
 ):
     devices = lax.axis_size("dom")
     chips = devices // 2
-    trace, interp, interp_t, lift, weight = (jnp.asarray(t) for t in const_tables())
+    trace, lift, weight = (jnp.asarray(t) for t in const_tables())
     coef = coefficient.reshape(1, lanes)
     level = refine_level.reshape(1, lanes)
 
@@ -736,8 +758,8 @@
         return arrivals, permute(last, swapped), made
 
     sides = [x.reshape(1, -1) for x in (side_elem, side_dir, side_case, side_kind, partner)]
-    first = [*sides, send_list, start_vector, coef, level, trace, interp, initial_guess]
-    hot, case, stack, sides, rolled, sent, coef, level, trace, interp, guess = run(
+    first = [*sides, send_list, start_vector, coef, level, trace, initial_guess]
+    hot, case, stack, sides, rolled, sent, coef, level, trace, guess = run(
         functools.partial(send_setup_kernel, chips),
         [((768, 256), bf16), ((8, 256), i32), ((80, 768), bf16), ((8, side_pad), i32), ((32, lanes), i32),
          ((40, 256), f32), *((x.shape, x.dtype) for x in first[7:])],
@@ -764,7 +786,7 @@
             return run(
                 functools.partial(own_kernel, nf),
                 [((sent.shape[0], 512), f32)],
-                [stack, *own_slots, interp],
+                [stack, *own_slots],
                 "own",
             )
 
@@ -772,7 +794,7 @@
             return run(
                 functools.partial(sides_kernel, nf),
                 [((h, side_pad + 256), f32), ((h, side_pad), f32), ((h, 384), f32)],
-                [stack, interp, *hots, *places],
+                [stack, *hots, *places],
                 "sides",
             )
 
@@ -807,20 +829,20 @@
         sums, *made = run(
             functools.partial(flux_kernel, nf, chips),
             [((h, 768), f32)] + ([] if turn else [((8, 256), f32)]),
-            [*arrivals, mine, others, *places, weight, interp_t, own_scatter]
+            [*arrivals, mine, others, *places, weight, own_scatter]
             + ([near_halo] if turn else []),
             "flux",
         )
         if turn == 0:
             near_halo = made[0]
         ins = [
-            last, sums, targets, place, arrival, far_scatter, weight, interp_t, lift,
+            last, sums, targets, place, arrival, far_scatter, weight, lift,
             fields, coef, level, block_inverse,
         ]
         ins += [far_halo] if turn else [guess]
         ins += [rhs_field] if turn == 1 else []
         if nf_next:
-            ins += [trace, interp, hot, case]
+            ins += [trace, hot, case]
             outs = [
                 ((64 * max(nf, nf_next), lanes), f32), ((64 * nf_next, 768), bf16), ((32 * nf_next, 256), f32)
             ]

time: 54.7 us -> 53.9 us (0.985)
  Pallas kernels: 21.5 us -> 18.6 us
  waiting for transfers between devices: 3.93 us -> 5.63 us
    pallas_call x30, Pallas kernels: 21.5 us -> 18.6 us  [run(): pl.pallas_call(body, out_shape=[(pltpu.VMEM if kept else jax.ShapeDtypeSt...]
    ppermute x16, waiting for transfers between devices: 3.93 us -> 5.63 us  [permute(): return lax.ppermute(x, 'dom', sorted(to.items()))]
  transfers between devices with their start and end apart: 16 -> 16, of which waited for: 11 -> 12; matrix products, arithmetic and copies ran while one was open for 0% -> 0% of each run, Pallas kernels for 23% -> 20%
where the time goes in v5:
time: 53.9 us; the launch traced here: 53.7 us
  Pallas kernels  18.6 us (35%)
  starting transfers between devices  16.5 us (31%)
  blocking collectives  12.1 us (22%)
  waiting for transfers between devices  5.63 us (10%)
  between operations  0.86 us (2%)
    pallas_call x30, Pallas kernels, run(): pl.pallas_call(body, out_shape=[(pltpu.VMEM if kept else jax.ShapeDtypeSt...  18.6 us
    ppermute x16, starting transfers between devices, permute(): return lax.ppermute(x, 'dom', sorted(to.items()))  16.5 us
    all_to_all x1, blocking collectives, local(): lax.all_to_all(parts.reshape(devices, 1, lanes), 'dom', 0, 0)  12.1 us
    ppermute x16, waiting for transfers between devices, permute(): return lax.ppermute(x, 'dom', sorted(to.items()))  5.63 us
  transfers between devices with their start and end apart: 16, of which 12 were waited for; matrix products, arithmetic and copies ran while one was open for 0% of the time, Pallas kernels for 20%

profile of v5, /device:TPU:0, one launch (start us, length us, event | category | flops | bytes accessed | tf_op | source)
XLA Modules:
  0.0 53.7 jit_solution(10129345222602818162)
XLA Ops:
  0.6 0.0 copy-start.2
  0.6 0.0 copy-start.1
  0.7 1.7 %send_setup.1 = (bf16[768,256]{1,0:T(8,128)(2,1)S(1)}, s32[8,256]{1,0:T(8,128)S(1)}, bf16[80,768]{1,0:T(8,128)(2,1)S(1)}, s32[8,1024]{1,0:T(8,128)S(1)}, s32[32,...) custom-call(s32[1,930]{1,0:T(1,128)} %bitcast.15, ...), custom_call_target="tpu_custom_call" | custom-call | flops 16777216 | bytes 1048576 | tf_op jit(solution)/shard_map/send_setup/pallas_call | solution.py:707
  2.4 0.5 collective-permute-start
  2.9 0.3 own_setup.1
  3.3 0.3 own.4.own_ref
  3.6 0.2 collective-permute-done.sent_ref
  3.8 0.1 carry.4
  3.9 2.8 %collective-permute-start.1 = (f32[40,256]{1,0:T(8,128)S(1)}, f32[40,256]{1,0:T(8,128)S(1)}, u32[]{:S(2)}, u32[]{:S(2)}) collective-permute-start(f32[40,256]{1,0:T(8,128)S(1)} %get-tuple-element.65), channel_id=1, source_target_pairs={{0,2},{1,0},{2,1},{3,5},{4,6},{5,3},{6,4},{7,9},{8,10},{9,7},{10,8... | collective-permute-start | bytes 122888 | tf_op jit(solution)/shard_map/ppermute | solution.py:730
  6.7 1.5 %collective-permute-start.2 = (f32[40,128]{1,0:T(8,128)S(1)}, f32[40,128]{1,0:T(8,128)S(1)}, u32[]{:S(2)}, u32[]{:S(2)}) collective-permute-start(f32[40,128]{1,0:T(8,128)S(1)} %get-tuple-element.66), channel_id=1, source_target_pairs={{0,4},{1,3},{2,6},{3,1},{4,0},{5,9},{6,2},{7,11},{8,12},{9,5},{10,... | collective-permute-start | bytes 61448 | tf_op jit(solution)/shard_map/ppermute | solution.py:730
  8.2 0.7 %setup.1 = (bf16[128,1280]{1,0:T(8,128)(2,1)S(1)}, bf16[128,1024]{1,0:T(8,128)(2,1)S(1)}, bf16[128,384]{1,0:T(8,128)(2,1)S(1)}, f32[16,1664]{1,0:T(8,128)S(1)}, ...) custom-call(f32[1,128]{1,0:T(1,128)S(1)} %get-tuple-element.67.coef_ref, s32[1,128]{1,0:T(1,128)S(1)} %get-tuple-element.68.level_ref, ...), custom_call_target="tpu_custom_call" | custom-call | flops 16777216 | bytes 1048576 | tf_op jit(solution)/shard_map/setup/pallas_call | solution.py:707
  8.9 0.8 %sides.4 = (f32[32,1280]{1,0:T(8,128)S(1)}, f32[32,1024]{1,0:T(8,128)S(1)}, f32[32,384]{1,0:T(8,128)S(1)}) custom-call(bf16[80,768]{1,0:T(8,128)(2,1)S(1)} %get-tuple-element.60.stack_ref, bf16[128,1280]{1,0:T(8,128)(2,1)S(1)} %get-tuple-element.69.own_hot_ref.own_elem_ref, bf16[128,1024]{1,0:T(8,128)(2,1)S(1)} %get-tuple-element.70.partner_hot_ref.partner_elem_ref, ...), custom_call_target="tpu_custom_call" | custom-call | flops 16777216 | bytes 1048576 | tf_op jit(solution)/shard_map/sides/pallas_call | solution.py:707
  9.7 0.8 %collective-permute-done.2.two_ref = f32[40,128]{1,0:T(8,128)S(1)} collective-permute-done((f32[40,128]{1,0:T(8,128)S(1)}, f32[40,128]{1,0:T(8,128)S(1)}, u32[]{:S(2)}, u32[]{:S(2)}) %collective-permute-start.2) | collective-permute-done | bytes 20512 | tf_op jit(solution)/shard_map/ppermute | solution.py:730
  10.5 0.1 relay.4
  10.6 0.0 collective-permute-start.3
  10.6 0.6 %flux.4 = (f32[32,768]{1,0:T(8,128)S(1)}, f32[8,256]{1,0:T(8,128)S(1)}) custom-call(f32[40,256]{1,0:T(8,128)S(1)} %collective-permute-done.1.one_ref, f32[40,128]{1,0:T(8,128)S(1)} %collective-permute-done.2.two_ref, f32[32,1280]{1,0:T(8,128)S(1)} %get-tuple-element.76.mine_ref, f32[32,1024]{1,0:T(8,128)S(1)} %get-tuple-element.77.other_ref, ...), custom_call_target="tpu_custom_call" | custom-call | flops 16777216 | bytes 1048576 | tf_op jit(solution)/shard_map/flux/pallas_call | solution.py:707
  11.3 0.6 %collective-permute-done.3.one_ref = f32[40,384]{1,0:T(8,128)S(1)} collective-permute-done((f32[40,384]{1,0:T(8,128)S(1)}, f32[40,384]{1,0:T(8,128)S(1)}, u32[]{:S(2)}, u32[]{:S(2)}) %collective-permute-start.3) | collective-permute-done | bytes 61472 | tf_op jit(solution)/shard_map/ppermute | solution.py:730
  11.8 1.2 %update.4 = (f32[128,128]{1,0:T(8,128)S(1)}, bf16[128,768]{1,0:T(8,128)(2,1)S(1)}, f32[64,256]{1,0:T(8,128)S(1)}, f32[8,384]{1,0:T(8,128)S(1)}) custom-call(f32[40,384]{1,0:T(8,128)S(1)} %collective-permute-done.3.one_ref, f32[32,768]{1,0:T(8,128)S(1)} %get-tuple-element.78.local_ref, f32[32,384]{1,0:T(8,128)S(1)} %get-tuple-element.75.rest_0_.target_ref, ...), custom_call_target="tpu_custom_call" | custom-call | flops 16777216 | bytes 1048576 | tf_op jit(solution)/shard_map/update/pallas_call | solution.py:707
  13.0 0.2 collective-permute-start.4
  13.3 0.4 whole.1
  13.6 0.4 own.5.own_ref
  14.0 0.4 collective-permute-done.4.sent_ref
  14.4 0.1 carry.5
  14.4 0.6 %collective-permute-start.5 = (f32[64,256]{1,0:T(8,128)S(1)}, f32[64,256]{1,0:T(8,128)S(1)}, u32[]{:S(2)}, u32[]{:S(2)}) collective-permute-start(f32[64,256]{1,0:T(8,128)S(1)} %get-tuple-element.86), channel_id=1, source_target_pairs={{0,2},{1,0},{2,1},{3,5},{4,6},{5,3},{6,4},{7,9},{8,10},{9,7},{10,8... | collective-permute-start | bytes 196616 | tf_op jit(solution)/shard_map/ppermute | solution.py:730
  15.0 1.9 %collective-permute-start.6 = (f32[64,128]{1,0:T(8,128)S(1)}, f32[64,128]{1,0:T(8,128)S(1)}, u32[]{:S(2)}, u32[]{:S(2)}) collective-permute-start(f32[64,128]{1,0:T(8,128)S(1)} %get-tuple-element.87), channel_id=1, source_target_pairs={{0,4},{1,3},{2,6},{3,1},{4,0},{5,9},{6,2},{7,11},{8,12},{9,5},{10,... | collective-permute-start | bytes 98312 | tf_op jit(solution)/shard_map/ppermute | solution.py:730
  16.9 0.7 %turn.1 = (bf16[1280,768]{1,0:T(8,128)(2,1)S(1)}, bf16[384,768]{1,0:T(8,128)(2,1)S(1)}) custom-call(f32[16,1664]{1,0:T(8,128)S(1)} %get-tuple-element.72.place_ref), custom_call_target="tpu_custom_call" | custom-call | flops 16777216 | bytes 1048576 | tf_op jit(solution)/shard_map/turn/pallas_call | solution.py:707
  17.6 1.2 %sides.5 = (f32[64,1280]{1,0:T(8,128)S(1)}, f32[64,1024]{1,0:T(8,128)S(1)}, f32[64,384]{1,0:T(8,128)S(1)}) custom-call(bf16[128,768]{1,0:T(8,128)(2,1)S(1)} %get-tuple-element.84.stack_ref, bf16[768,1280]{1,0:T(8,128)(2,1)S(1)} %get-tuple-element.85.rest_0_.own_hot_ref, bf16[768,1024]{1,0:T(8,128)(2,1)S(1)} %get-tuple-element.88.partner_hot_ref, ...), custom_call_target="tpu_custom_call" | custom-call | flops 16777216 | bytes 1048576 | tf_op jit(solution)/shard_map/sides/pallas_call | solution.py:707
  18.8 0.1 collective-permute-done.6.two_ref
  18.9 0.0 collective-permute-done.5.one_ref
  18.9 0.1 relay.5
  19.0 0.5 %collective-permute-start.7 = (f32[64,384]{1,0:T(8,128)S(1)}, f32[64,384]{1,0:T(8,128)S(1)}, u32[]{:S(2)}, u32[]{:S(2)}) collective-permute-start(f32[64,384]{1,0:T(8,128)S(1)} %relay.5), channel_id=1, source_target_pairs={{0,1},{1,0},{2,3},{3,2},{4,5},{5,4},{6,7},{7,6},{8,9},{9,8},{10,11... | collective-permute-start | bytes 294920 | tf_op jit(solution)/shard_map/ppermute | solution.py:730
  19.6 0.9 %flux.5.local_ref = f32[64,768]{1,0:T(8,128)S(1)} custom-call(f32[64,256]{1,0:T(8,128)S(1)} %collective-permute-done.5.one_ref, f32[64,128]{1,0:T(8,128)S(1)} %collective-permute-done.6.two_ref, f32[64,1280]{1,0:T(8,128)S(1)} %get-tuple-element.92.mine_ref, f32[64,1024]{1,0:T(8,128)S(1)} %get-tuple-element.93.other_ref, ...), custom_call_target="tpu_custom_call" | custom-call | flops 16777216 | bytes 1048576 | tf_op jit(solution)/shard_map/flux/pallas_call | solution.py:707
  20.4 0.1 collective-permute-done.7.one_ref
  20.5 1.5 %update.5 = (f32[128,128]{1,0:T(8,128)S(1)}, bf16[128,768]{1,0:T(8,128)(2,1)S(1)}, f32[64,256]{1,0:T(8,128)S(1)}) custom-call(f32[64,384]{1,0:T(8,128)S(1)} %collective-permute-done.7.one_ref, f32[64,768]{1,0:T(8,128)S(1)} %flux.5.local_ref, f32[64,384]{1,0:T(8,128)S(1)} %get-tuple-element.90.rest_0_.target_ref, f32[16,1664]{1,0:T(8,128)S(1)} %get-tuple-element.72.place_ref, ...), custom_call_target="tpu_custom_call" | custom-call | flops 16777216 | bytes 1048576 | tf_op jit(solution)/shard_map/update/pallas_call | solution.py:707
  22.0 0.4 collective-permute-start.8
  22.4 0.4 own.6.own_ref
  22.8 0.5 collective-permute-done.8.sent_ref
  23.3 0.1 carry.6
  23.4 1.8 %collective-permute-start.9 = (f32[64,256]{1,0:T(8,128)S(1)}, f32[64,256]{1,0:T(8,128)S(1)}, u32[]{:S(2)}, u32[]{:S(2)}) collective-permute-start(f32[64,256]{1,0:T(8,128)S(1)} %get-tuple-element.100), channel_id=1, source_target_pairs={{0,2},{1,0},{2,1},{3,5},{4,6},{5,3},{6,4},{7,9},{8,10},{9,7},{10,8... | collective-permute-start | bytes 196616 | tf_op jit(solution)/shard_map/ppermute | solution.py:730
  25.3 2.5 %collective-permute-start.10 = (f32[64,128]{1,0:T(8,128)S(1)}, f32[64,128]{1,0:T(8,128)S(1)}, u32[]{:S(2)}, u32[]{:S(2)}) collective-permute-start(f32[64,128]{1,0:T(8,128)S(1)} %get-tuple-element.101), channel_id=1, source_target_pairs={{0,4},{1,3},{2,6},{3,1},{4,0},{5,9},{6,2},{7,11},{8,12},{9,5},{10,... | collective-permute-start | bytes 98312 | tf_op jit(solution)/shard_map/ppermute | solution.py:730
  27.8 1.2 %sides.6 = (f32[64,1280]{1,0:T(8,128)S(1)}, f32[64,1024]{1,0:T(8,128)S(1)}, f32[64,384]{1,0:T(8,128)S(1)}) custom-call(bf16[128,768]{1,0:T(8,128)(2,1)S(1)} %get-tuple-element.99.stack_ref, bf16[768,1280]{1,0:T(8,128)(2,1)S(1)} %get-tuple-element.85.rest_0_.own_hot_ref, bf16[768,1024]{1,0:T(8,128)(2,1)S(1)} %get-tuple-element.88.partner_hot_ref, ...), custom_call_target="tpu_custom_call" | custom-call | flops 16777216 | bytes 1048576 | tf_op jit(solution)/shard_map/sides/pallas_call | solution.py:707
  28.9 0.7 %collective-permute-done.10.two_ref = f32[64,128]{1,0:T(8,128)S(1)} collective-permute-done((f32[64,128]{1,0:T(8,128)S(1)}, f32[64,128]{1,0:T(8,128)S(1)}, u32[]{:S(2)}, u32[]{:S(2)}) %collective-permute-start.10) | collective-permute-done | bytes 32800 | tf_op jit(solution)/shard_map/ppermute | solution.py:730
  29.6 0.0 collective-permute-done.9.one_ref
  29.7 0.1 relay.6
  29.7 0.1 collective-permute-start.11
  29.8 0.9 %flux.6.local_ref = f32[64,768]{1,0:T(8,128)S(1)} custom-call(f32[64,256]{1,0:T(8,128)S(1)} %collective-permute-done.9.one_ref, f32[64,128]{1,0:T(8,128)S(1)} %collective-permute-done.10.two_ref, f32[64,1280]{1,0:T(8,128)S(1)} %get-tuple-element.103.mine_ref, f32[64,1024]{1,0:T(8,128)S(1)} %get-tuple-element.104.other_ref, ...), custom_call_target="tpu_custom_call" | custom-call | flops 16777216 | bytes 1048576 | tf_op jit(solution)/shard_map/flux/pallas_call | solution.py:707
  30.7 0.4 collective-permute-done.11.one_ref
  31.1 1.4 %update.6 = (f32[128,128]{1,0:T(8,128)S(1)}, bf16[64,768]{1,0:T(8,128)(2,1)S(1)}, f32[32,256]{1,0:T(8,128)S(1)}) custom-call(f32[64,384]{1,0:T(8,128)S(1)} %collective-permute-done.11.one_ref, f32[64,768]{1,0:T(8,128)S(1)} %flux.6.local_ref, f32[64,384]{1,0:T(8,128)S(1)} %get-tuple-element.102.rest_0_.target_ref, ...), custom_call_target="tpu_custom_call" | custom-call | flops 16777216 | bytes 1048576 | tf_op jit(solution)/shard_map/update/pallas_call | solution.py:707
  32.5 0.2 collective-permute-start.12
  32.7 0.3 own.7.own_ref
  33.0 0.7 %collective-permute-done.12.sent_ref = f32[32,256]{1,0:T(8,128)S(1)} collective-permute-done((f32[32,256]{1,0:T(8,128)S(1)}, f32[32,256]{1,0:T(8,128)S(1)}, u32[]{:S(2)}, u32[]{:S(2)}) %collective-permute-start.12) | collective-permute-done | bytes 32800 | tf_op jit(solution)/shard_map/ppermute | solution.py:730
  33.8 0.1 carry.7
  33.9 0.5 collective-permute-start.13
  34.3 2.7 %collective-permute-start.14 = (f32[32,128]{1,0:T(8,128)S(1)}, f32[32,128]{1,0:T(8,128)S(1)}, u32[]{:S(2)}, u32[]{:S(2)}) collective-permute-start(f32[32,128]{1,0:T(8,128)S(1)} %get-tuple-element.109), channel_id=1, source_target_pairs={{0,4},{1,3},{2,6},{3,1},{4,0},{5,9},{6,2},{7,11},{8,12},{9,5},{10,... | collective-permute-start | bytes 49160 | tf_op jit(solution)/shard_map/ppermute | solution.py:730
  37.0 1.0 %sides.7 = (f32[32,1280]{1,0:T(8,128)S(1)}, f32[32,1024]{1,0:T(8,128)S(1)}, f32[32,384]{1,0:T(8,128)S(1)}) custom-call(bf16[64,768]{1,0:T(8,128)(2,1)S(1)} %get-tuple-element.107.stack_ref, bf16[768,1280]{1,0:T(8,128)(2,1)S(1)} %get-tuple-element.85.rest_0_.own_hot_ref, bf16[768,1024]{1,0:T(8,128)(2,1)S(1)} %get-tuple-element.88.partner_hot_ref, ...), custom_call_target="tpu_custom_call" | custom-call | flops 16777216 | bytes 1048576 | tf_op jit(solution)/shard_map/sides/pallas_call | solution.py:707
  38.0 0.7 %collective-permute-done.14.two_ref = f32[32,128]{1,0:T(8,128)S(1)} collective-permute-done((f32[32,128]{1,0:T(8,128)S(1)}, f32[32,128]{1,0:T(8,128)S(1)}, u32[]{:S(2)}, u32[]{:S(2)}) %collective-permute-start.14) | collective-permute-done | bytes 16416 | tf_op jit(solution)/shard_map/ppermute | solution.py:730
  38.7 0.0 collective-permute-done.13.one_ref
  38.7 0.1 relay.7
  38.8 0.1 collective-permute-start.15
  39.0 0.6 %flux.7.local_ref = f32[32,768]{1,0:T(8,128)S(1)} custom-call(f32[32,256]{1,0:T(8,128)S(1)} %collective-permute-done.13.one_ref, f32[32,128]{1,0:T(8,128)S(1)} %collective-permute-done.14.two_ref, f32[32,1280]{1,0:T(8,128)S(1)} %get-tuple-element.111.mine_ref, f32[32,1024]{1,0:T(8,128)S(1)} %get-tuple-element.112.other_ref, ...), custom_call_target="tpu_custom_call" | custom-call | flops 16777216 | bytes 1048576 | tf_op jit(solution)/shard_map/flux/pallas_call | solution.py:707
  39.6 0.5 collective-permute-done.15.one_ref
  40.1 0.8 %update.7 = f32[32,128]{1,0:T(8,128)S(1)} custom-call(f32[32,384]{1,0:T(8,128)S(1)} %collective-permute-done.15.one_ref, f32[32,768]{1,0:T(8,128)S(1)} %flux.7.local_ref, f32[32,384]{1,0:T(8,128)S(1)} %get-tuple-element.110.rest_0_.target_ref, f32[16,1664]{1,0:T(8,128)S(1)} %get-tuple-element.72.place_ref, f32[8,640]{1,0:T(8,128)S(1)} %get-tuple-element.74.arrival_ref, ...), custom_call_target="tpu_custom_call" | custom-call | flops 16777216 | bytes 1048576 | tf_op jit(solution)/shard_map/update/pallas_call | solution.py:707
  40.9 12.1 %all_to_all.5 = f32[32,1,128]{2,1,0:T(1,128)S(1)} all-to-all(f32[32,1,128]{2,1,0:T(1,128)S(1)} %bitcast.13), channel_id=1, replica_groups=mesh['dom'=32] {'dom'}, dimensions={0} | all-to-all | bytes 32768 | tf_op jit(solution)/shard_map/all_to_all | solution.py:865
  53.0 0.7 %finish.1 = (f32[64,128]{1,0:T(8,128)}, f32[1,128]{1,0:T(1,128)}) custom-call(f32[32,128]{1,0:T(8,128)S(1)} %bitcast.14, f32[64,128]{1,0:T(8,128)S(1)} %get-tuple-element.79.rest_0_.guess_ref, f32[128,128]{1,0:T(8,128)S(1)} %get-tuple-element.105.field_ref.first_ref, f32[128,128]{1,0:T(8,128)S(1)} %get-tuple-element.113.second_ref), custom_call_target="tpu_custom_call" | custom-call | flops 16777216 | bytes 1048576 | tf_op jit(solution)/shard_map/finish/pallas_call | solution.py:707
  (10 shorter events, 0.0 us)
Async XLA Ops:
  0.6 10.0 %copy-start.2 = (f32[32,128]{1,0:T(8,128)S(1)}, f32[32,128]{1,0:T(8,128)}, u32[]{:S(2)}) copy-start(f32[32,128]{1,0:T(8,128)} %constant.8.clone.weight_ref) | copy-start | bytes 49156
  0.6 11.2 %copy-start.1 = (bf16[64,768]{1,0:T(8,128)(2,1)S(1)}, bf16[64,768]{1,0:T(8,128)(2,1)}, u32[]{:S(2)}) copy-start(bf16[64,768]{1,0:T(8,128)(2,1)} %constant.7.clone.lift_ref) | copy-start | bytes 294916
  0.7 11.2 %copy-start.3 = (f32[64,128]{1,0:T(8,128)S(1)}, f32[64,128]{1,0:T(8,128)}, u32[]{:S(2)}) copy-start(f32[64,128]{1,0:T(8,128)} %field_ref.1) | copy-start | bytes 98308
  0.7 11.2 %copy-start = (bf16[64,64,128]{2,1,0:T(8,128)(2,1)S(1)}, bf16[64,64,128]{2,1,0:T(8,128)(2,1)}, u32[]{:S(2)}) copy-start(bf16[64,64,128]{2,1,0:T(8,128)(2,1)} %inverse_ref.7) | copy-start | bytes 3145732
  2.4 1.4 %collective-permute-start = (f32[40,256]{1,0:T(8,128)S(1)}, f32[40,256]{1,0:T(8,128)S(1)}, u32[]{:S(2)}, u32[]{:S(2)}) collective-permute-start(f32[40,256]{1,0:T(8,128)S(1)} %get-tuple-element.59), channel_id=1, source_target_pairs={{0,1},{1,0},{2,3},{3,2},{4,5},{5,4},{6,7},{7,6},{8,9},{9,8},{10,11... | collective-permute-start | bytes 122888 | tf_op jit(solution)/shard_map/ppermute | solution.py:730
  3.9 6.6 %collective-permute-start.1 = (f32[40,256]{1,0:T(8,128)S(1)}, f32[40,256]{1,0:T(8,128)S(1)}, u32[]{:S(2)}, u32[]{:S(2)}) collective-permute-start(f32[40,256]{1,0:T(8,128)S(1)} %get-tuple-element.65), channel_id=1, source_target_pairs={{0,2},{1,0},{2,1},{3,5},{4,6},{5,3},{6,4},{7,9},{8,10},{9,7},{10,8... | collective-permute-start | bytes 122888 | tf_op jit(solution)/shard_map/ppermute | solution.py:730
  6.7 3.8 %collective-permute-start.2 = (f32[40,128]{1,0:T(8,128)S(1)}, f32[40,128]{1,0:T(8,128)S(1)}, u32[]{:S(2)}, u32[]{:S(2)}) collective-permute-start(f32[40,128]{1,0:T(8,128)S(1)} %get-tuple-element.66), channel_id=1, source_target_pairs={{0,4},{1,3},{2,6},{3,1},{4,0},{5,9},{6,2},{7,11},{8,12},{9,5},{10,... | collective-permute-start | bytes 61448 | tf_op jit(solution)/shard_map/ppermute | solution.py:730
  10.6 1.3 %collective-permute-start.3 = (f32[40,384]{1,0:T(8,128)S(1)}, f32[40,384]{1,0:T(8,128)S(1)}, u32[]{:S(2)}, u32[]{:S(2)}) collective-permute-start(f32[40,384]{1,0:T(8,128)S(1)} %relay.4), channel_id=1, source_target_pairs={{0,1},{1,0},{2,3},{3,2},{4,5},{5,4},{6,7},{7,6},{8,9},{9,8},{10,11... | collective-permute-start | bytes 184328 | tf_op jit(solution)/shard_map/ppermute | solution.py:730
  13.0 1.3 %collective-permute-start.4 = (f32[64,256]{1,0:T(8,128)S(1)}, f32[64,256]{1,0:T(8,128)S(1)}, u32[]{:S(2)}, u32[]{:S(2)}) collective-permute-start(f32[64,256]{1,0:T(8,128)S(1)} %get-tuple-element.83), channel_id=1, source_target_pairs={{0,1},{1,0},{2,3},{3,2},{4,5},{5,4},{6,7},{7,6},{8,9},{9,8},{10,11... | collective-permute-start | bytes 196616 | tf_op jit(solution)/shard_map/ppermute | solution.py:730
  14.4 4.5 %collective-permute-start.5 = (f32[64,256]{1,0:T(8,128)S(1)}, f32[64,256]{1,0:T(8,128)S(1)}, u32[]{:S(2)}, u32[]{:S(2)}) collective-permute-start(f32[64,256]{1,0:T(8,128)S(1)} %get-tuple-element.86), channel_id=1, source_target_pairs={{0,2},{1,0},{2,1},{3,5},{4,6},{5,3},{6,4},{7,9},{8,10},{9,7},{10,8... | collective-permute-start | bytes 196616 | tf_op jit(solution)/shard_map/ppermute | solution.py:730
  15.0 3.9 %collective-permute-start.6 = (f32[64,128]{1,0:T(8,128)S(1)}, f32[64,128]{1,0:T(8,128)S(1)}, u32[]{:S(2)}, u32[]{:S(2)}) collective-permute-start(f32[64,128]{1,0:T(8,128)S(1)} %get-tuple-element.87), channel_id=1, source_target_pairs={{0,4},{1,3},{2,6},{3,1},{4,0},{5,9},{6,2},{7,11},{8,12},{9,5},{10,... | collective-permute-start | bytes 98312 | tf_op jit(solution)/shard_map/ppermute | solution.py:730
  19.0 1.5 %copy-start.4 = (f32[64,128]{1,0:T(8,128)S(1)}, f32[64,128]{1,0:T(8,128)}, u32[]{:S(2)}) copy-start(f32[64,128]{1,0:T(8,128)} %rest_1_.1) | copy-start | bytes 98308
  19.0 1.5 %collective-permute-start.7 = (f32[64,384]{1,0:T(8,128)S(1)}, f32[64,384]{1,0:T(8,128)S(1)}, u32[]{:S(2)}, u32[]{:S(2)}) collective-permute-start(f32[64,384]{1,0:T(8,128)S(1)} %relay.5), channel_id=1, source_target_pairs={{0,1},{1,0},{2,3},{3,2},{4,5},{5,4},{6,7},{7,6},{8,9},{9,8},{10,11... | collective-permute-start | bytes 294920 | tf_op jit(solution)/shard_map/ppermute | solution.py:730
  22.0 1.3 %collective-permute-start.8 = (f32[64,256]{1,0:T(8,128)S(1)}, f32[64,256]{1,0:T(8,128)S(1)}, u32[]{:S(2)}, u32[]{:S(2)}) collective-permute-start(f32[64,256]{1,0:T(8,128)S(1)} %get-tuple-element.98), channel_id=1, source_target_pairs={{0,1},{1,0},{2,3},{3,2},{4,5},{5,4},{6,7},{7,6},{8,9},{9,8},{10,11... | collective-permute-start | bytes 196616 | tf_op jit(solution)/shard_map/ppermute | solution.py:730
  23.4 6.2 %collective-permute-start.9 = (f32[64,256]{1,0:T(8,128)S(1)}, f32[64,256]{1,0:T(8,128)S(1)}, u32[]{:S(2)}, u32[]{:S(2)}) collective-permute-start(f32[64,256]{1,0:T(8,128)S(1)} %get-tuple-element.100), channel_id=1, source_target_pairs={{0,2},{1,0},{2,1},{3,5},{4,6},{5,3},{6,4},{7,9},{8,10},{9,7},{10,8... | collective-permute-start | bytes 196616 | tf_op jit(solution)/shard_map/ppermute | solution.py:730
  25.3 4.4 %collective-permute-start.10 = (f32[64,128]{1,0:T(8,128)S(1)}, f32[64,128]{1,0:T(8,128)S(1)}, u32[]{:S(2)}, u32[]{:S(2)}) collective-permute-start(f32[64,128]{1,0:T(8,128)S(1)} %get-tuple-element.101), channel_id=1, source_target_pairs={{0,4},{1,3},{2,6},{3,1},{4,0},{5,9},{6,2},{7,11},{8,12},{9,5},{10,... | collective-permute-start | bytes 98312 | tf_op jit(solution)/shard_map/ppermute | solution.py:730
  29.7 1.3 %collective-permute-start.11 = (f32[64,384]{1,0:T(8,128)S(1)}, f32[64,384]{1,0:T(8,128)S(1)}, u32[]{:S(2)}, u32[]{:S(2)}) collective-permute-start(f32[64,384]{1,0:T(8,128)S(1)} %relay.6), channel_id=1, source_target_pairs={{0,1},{1,0},{2,3},{3,2},{4,5},{5,4},{6,7},{7,6},{8,9},{9,8},{10,11... | collective-permute-start | bytes 294920 | tf_op jit(solution)/shard_map/ppermute | solution.py:730
  32.5 1.3 %collective-permute-start.12 = (f32[32,256]{1,0:T(8,128)S(1)}, f32[32,256]{1,0:T(8,128)S(1)}, u32[]{:S(2)}, u32[]{:S(2)}) collective-permute-start(f32[32,256]{1,0:T(8,128)S(1)} %get-tuple-element.106), channel_id=1, source_target_pairs={{0,1},{1,0},{2,3},{3,2},{4,5},{5,4},{6,7},{7,6},{8,9},{9,8},{10,11... | collective-permute-start | bytes 98312 | tf_op jit(solution)/shard_map/ppermute | solution.py:730
  33.9 4.9 %collective-permute-start.13 = (f32[32,256]{1,0:T(8,128)S(1)}, f32[32,256]{1,0:T(8,128)S(1)}, u32[]{:S(2)}, u32[]{:S(2)}) collective-permute-start(f32[32,256]{1,0:T(8,128)S(1)} %get-tuple-element.108), channel_id=1, source_target_pairs={{0,2},{1,0},{2,1},{3,5},{4,6},{5,3},{6,4},{7,9},{8,10},{9,7},{10,8... | collective-permute-start | bytes 98312 | tf_op jit(solution)/shard_map/ppermute | solution.py:730
  34.3 4.4 %collective-permute-start.14 = (f32[32,128]{1,0:T(8,128)S(1)}, f32[32,128]{1,0:T(8,128)S(1)}, u32[]{:S(2)}, u32[]{:S(2)}) collective-permute-start(f32[32,128]{1,0:T(8,128)S(1)} %get-tuple-element.109), channel_id=1, source_target_pairs={{0,4},{1,3},{2,6},{3,1},{4,0},{5,9},{6,2},{7,11},{8,12},{9,5},{10,... | collective-permute-start | bytes 49160 | tf_op jit(solution)/shard_map/ppermute | solution.py:730
  38.8 1.2 %collective-permute-start.15 = (f32[32,384]{1,0:T(8,128)S(1)}, f32[32,384]{1,0:T(8,128)S(1)}, u32[]{:S(2)}, u32[]{:S(2)}) collective-permute-start(f32[32,384]{1,0:T(8,128)S(1)} %relay.7), channel_id=1, source_target_pairs={{0,1},{1,0},{2,3},{3,2},{4,5},{5,4},{6,7},{7,6},{8,9},{9,8},{10,11... | collective-permute-start | bytes 147464 | tf_op jit(solution)/shard_map/ppermute | solution.py:730

commit v6 on v5

--- a/solution.py
+++ b/solution.py
@@ -44,38 +44,21 @@
     return weights, derivative, halves
 
 
-def basis_tables():
+def stiffness_table():
     weights, derivative, halves = lagrange_tables()
     mass = np.diag(weights)
     line = derivative.T @ mass @ derivative
-    stiffness = (
+    return (
         np.kron(np.kron(line, mass), mass)
         + np.kron(np.kron(mass, line), mass)
         + np.kron(np.kron(mass, mass), line)
     )
-    trace = np.zeros((6, 32, 64))
-    for dim in range(3):
-        others = [d for d in range(3) if d != dim]
-        for lower in range(2):
-            face = 2 * dim + lower
-            fixed = 0 if lower else 3
-            sign = -1.0 if lower else 1.0
-            for first in range(4):
-                for second in range(4):
-                    node = first * 4 + second
-                    for along in range(4):
-                        place = [0, 0, 0]
-                        place[others[0]] = first
-                        place[others[1]] = second
-                        place[dim] = along
-                        nodal = place[0] * 16 + place[1] * 4 + place[2]
-                        if along == fixed:
-                            trace[face, node, nodal] = 1.0
-                        trace[face, 16 + node, nodal] = sign * derivative[fixed, along]
-    face_weight = np.kron(weights, weights)
-    order = [16 * part + 4 * first + second for first in range(4) for part in range(2) for second in range(4)]
-    weight = np.concatenate([face_weight, face_weight])[order]
-    return stiffness, trace[:, order].reshape(192, 64), weight
+
+
+def weight_table():
+    weights = lagrange_tables()[0]
+    rows = [weights[first] * weights[second] for first in range(4) for part in range(2) for second in range(4)]
+    return np.broadcast_to(np.array(rows, np.float32)[:, None], (32, lanes))
 
 
 def stacked(table):
@@ -86,10 +69,7 @@
 
 
 def const_tables():
-    stiffness, trace, face_weight = basis_tables()
-    lift = np.concatenate([stacked(trace.T), stacked(stiffness)], axis=1)
-    weight = np.broadcast_to(face_weight[:, None], (32, lanes))
-    return stacked(trace), lift, np.asarray(weight, np.float32)
+    return stacked(stiffness_table()), np.ascontiguousarray(weight_table())
 
 
 def two(x):
@@ -221,15 +201,102 @@
     return coef, size, coef * size, coef * inverse
 
 
-def face_stack(trace_ref, u, normal_scale, nf):
-    faces = table_dot(trace_ref[...], cat(u, 1))
+def by_place(values):
+    place = lax.broadcasted_iota(i32, (8, lanes), 0) & (len(values) - 1)
+    tile = jnp.full((8, lanes), float(values[0]), f32)
+    for p in range(1, len(values)):
+        tile = jnp.where(place == p, float(values[p]), tile)
+    return tile
+
+
+def face_ends():
+    derivative = lagrange_tables()[1]
+    for dim in range(3):
+        for lower in range(2):
+            node = 0 if lower else 3
+            yield dim, 2 * dim + lower, node, (-1.0 if lower else 1.0) * derivative[node]
+
+
+def face_traces(u):
+    sub = lax.broadcasted_iota(i32, (8, lanes), 0)
+    low = sub < 4
+    v = [[u[16 * i + 8 * m : 16 * i + 8 * m + 8] for m in range(2)] for i in range(4)]
+    out = {}
+    for dim, face, node, slope in face_ends():
+        rows = []
+        if dim == 0:
+            for m in range(2):
+                normal = sum(float(slope[i]) * v[i][m] for i in range(4))
+                rows.append(jnp.where(low, v[node][m], pltpu.roll(normal, 4, 0)))
+                rows.append(jnp.where(low, pltpu.roll(v[node][m], 4, 0), normal))
+        elif dim == 1:
+            scale = [by_place([slope[2 * m]] * 4 + [slope[2 * m + 1]] * 4) for m in range(2)]
+            for i in range(4):
+                normal = scale[0] * v[i][0] + scale[1] * v[i][1]
+                normal = normal + pltpu.roll(normal, 4, 0)
+                rows.append(jnp.where(low, pltpu.roll(v[i][1], 4, 0) if node else v[i][0], normal))
+        else:
+            scale = by_place(slope)
+            for i in range(4):
+                row = None
+                for m in range(2):
+                    normal = scale * v[i][m]
+                    normal = normal + pltpu.roll(normal, 7, 0)
+                    normal = normal + pltpu.roll(normal, 6, 0)
+                    for half in range(2):
+                        to = 2 * m + half
+                        value = pltpu.roll(v[i][m], (to - 4 * half - node) % 8, 0)
+                        shift = (to + 4 - 4 * half) % 8
+                        moved = pltpu.roll(normal, shift, 0) if shift else normal
+                        row = value if row is None else jnp.where(sub == to, value, row)
+                        row = jnp.where(sub == to + 4, moved, row)
+                rows.append(row)
+        out[face] = jnp.concatenate(rows, axis=0)
+    return [out[f] for f in range(6)]
+
+
+def lift_traces(total, faces):
+    sub = lax.broadcasted_iota(i32, (8, lanes), 0)
+    low = sub < 4
+    r = [[total[16 * i + 8 * m : 16 * i + 8 * m + 8] for m in range(2)] for i in range(4)]
+    for dim, face, node, slope in face_ends():
+        b = [faces[face][8 * i : 8 * i + 8] for i in range(4)]
+        if dim == 0:
+            for m in range(2):
+                even, odd = b[2 * m], b[2 * m + 1]
+                normal = jnp.where(low, pltpu.roll(even, 4, 0), odd)
+                for i in range(4):
+                    r[i][m] = r[i][m] + float(slope[i]) * normal
+                r[node][m] = r[node][m] + jnp.where(low, even, pltpu.roll(odd, 4, 0))
+        elif dim == 1:
+            scale = [by_place([slope[2 * m]] * 4 + [slope[2 * m + 1]] * 4) for m in range(2)]
+            for i in range(4):
+                turned = pltpu.roll(b[i], 4, 0)
+                normal = jnp.where(low, turned, b[i])
+                for m in range(2):
+                    r[i][m] = r[i][m] + scale[m] * normal
+                value = jnp.where(low, 0.0, turned) if node else jnp.where(low, b[i], 0.0)
+                r[i][node // 2] = r[i][node // 2] + value
+        else:
+            scale = by_place(slope)
+            here = by_place([1.0 if p == node else 0.0 for p in range(4)])
+            for i in range(4):
+                for m in range(2):
+                    spread = [
+                        jnp.where(
+                            low,
+                            jnp.broadcast_to(b[i][at : at + 1], (8, lanes)),
+                            jnp.broadcast_to(b[i][at + 1 : at + 2], (8, lanes)),
+                        )
+                        for at in (2 * m, 4 + 2 * m)
+                    ]
+                    r[i][m] = r[i][m] + (here * spread[0] + scale * spread[1])
+    return jnp.concatenate([r[i][m] for i in range(4) for m in range(2)], axis=0)
+
+
+def face_stack(u, normal_scale):
     scale = jnp.where(slope_rows((32, lanes)), jnp.broadcast_to(normal_scale, (32, lanes)), 1.0)
-    fields = []
-    for k in range(nf):
-        part = faces[:, lanes * k : lanes * k + lanes]
-        fields.append(
-            jnp.concatenate([part[32 * f : 32 * f + 32] * scale for f in range(6)], axis=1)
-        )
+    fields = [jnp.concatenate([part * scale for part in face_traces(x)], axis=1) for x in u]
     high, low = two(cat(fields, 0))
     return jnp.concatenate([high, low], axis=0)
 
@@ -313,10 +380,10 @@
 
 
 def send_setup_kernel(chips, *refs):
-    sources, refs = refs[:11], refs[11:]
+    sources, refs = refs[:10], refs[10:]
     hot_ref, case_ref, stack_ref, side_ref, rolled_ref = refs[:5]
-    sent_ref, landed = refs[5], (*refs[11:18], *refs[6:10])
-    slot_ref, arrived = refs[10], refs[18]
+    sent_ref, landed = refs[5], (*refs[10:17], *refs[6:9])
+    slot_ref, arrived = refs[9], refs[17]
     copies = [
         pltpu.make_async_copy(source, target, arrived.at[k])
         for k, (source, target) in enumerate(zip(sources, landed))
@@ -324,7 +391,7 @@
     for copy in copies:
         copy.start()
     elem_ref, dir_ref, sidecase_ref, kind_ref, partner_ref, list_ref = landed[:6]
-    start_ref, coef_ref, level_ref, trace_ref = landed[6:10]
+    start_ref, coef_ref, level_ref = landed[6:9]
     for copy in copies:
         copy.wait()
     side_ref[...] = jnp.full((8, side_pad), -1, i32)
@@ -354,7 +421,7 @@
     fill_one_hot(hot_ref, elem, face)
 
     coef, size, volume_scale, normal_scale = element_rows(coef_ref, level_ref)
-    stack = face_stack(trace_ref, [start_ref[...]], normal_scale, 1)
+    stack = face_stack([start_ref[...]], normal_scale)
     scalars = rows_of([x.astype(f32) for x in three(coef)] + [size], 16, lanes).astype(bf16)
     stack = jnp.concatenate([stack, jnp.concatenate([scalars] * 6, axis=1)], axis=0)
     stack_ref[...] = stack
@@ -567,7 +634,7 @@
 
 def flux_kernel(
     nf, chips, one_ref, two_ref, mine_ref, other_ref, place_ref, info_ref, arrival_ref, weight_ref,
-    own_hot_ref, *rest,
+    own_hot_ref, field_ref, coef_ref, level_ref, stiffness_ref, *rest,
 ):
     h = 32 * nf
     core, near, far, end, near_there, far_there = where_am_i(chips)
@@ -579,13 +646,13 @@
         [jnp.where(inside, kept, one_ref[:, 0:128]), one_ref[:, 128:256]], axis=1
     )
     if got.shape[0] > h:
-        sum_ref, halo_ref = rest
+        sum_ref, volume_ref, halo_ref = rest
         halo = halo_coefs(
             arrival_ref[1:2, 0:256], arrival_ref[2:3, 0:256], got[h : h + 1], got[h + 1 : h + 2]
         )
         halo_ref[...] = rows_of(halo, 8, 256)
     else:
-        halo_ref, sum_ref = rest
+        halo_ref, sum_ref, volume_ref = rest
         halo = halo_ref[0:1], halo_ref[1:2]
     coefs = [
         jnp.concatenate([info_ref[k : k + 1, 0:side_pad], halo[k // 2]], axis=1) for k in range(4)
@@ -595,6 +662,11 @@
         nf, mine_ref, outer, coefs, info_ref[4:5], place_ref[1:2, 0 : side_pad + 256], weight_ref,
         own_hot_ref[...],
     )
+    volume_scale = element_rows(coef_ref, level_ref)[2]
+    fields = [field_ref[64 * k : 64 * k + 64] * volume_scale for k in range(nf)]
+    volume = table_dot(stiffness_ref[...], cat(fields, 1))
+    for k in range(nf):
+        volume_ref[64 * k : 64 * k + 64, :] = volume[:, lanes * k : lanes * k + lanes]
 
 
 def solve_blocks(inverse_ref, hold_ref, nf):
@@ -608,7 +680,7 @@
 
 def update_kernel(
     turn, nf, nf_next,
-    one_ref, local_ref, target_ref, place_ref, arrival_ref, far_hot_ref, weight_ref, lift_ref,
+    one_ref, local_ref, volume_ref, target_ref, place_ref, arrival_ref, far_hot_ref, weight_ref,
     field_ref, coef_ref, level_ref, inverse_ref, *rest,
 ):
     if turn == 0:
@@ -618,7 +690,7 @@
     if turn == 1:
         rhs_ref, *rest = rest
     if nf_next:
-        trace_ref, hot_ref, case_ref, new_ref, stack_ref, sent_ref, *rest = rest
+        hot_ref, case_ref, new_ref, stack_ref, sent_ref, *rest = rest
     else:
         part_ref, *rest = rest
     hold_ref = rest[-1]
@@ -637,20 +709,10 @@
     )
     coef, size, volume_scale, normal_scale = element_rows(coef_ref, level_ref)
     scale = jnp.where(slope_rows((32, lanes)), jnp.broadcast_to(normal_scale, (32, lanes)), 1.0)
-    operands = []
     for k in range(nf):
         mine = total[32 * k : 32 * k + 32]
-        faces = jnp.concatenate(
-            [mine[:, lanes * f : lanes * f + lanes] * scale for f in range(6)], axis=0
-        )
-        high, low = two(faces)
-        field_high, field_low = two(field_ref[64 * k : 64 * k + 64] * volume_scale)
-        operands.append(
-            jnp.concatenate([high, low, high, field_high, field_low, field_high], axis=0)
-        )
-    image = dot(lift_ref[...], cat(operands, 1))
-    for k in range(nf):
-        part = image[:, lanes * k : lanes * k + lanes]
+        faces = [mine[:, lanes * f : lanes * f + lanes] * scale for f in range(6)]
+        part = lift_traces(volume_ref[64 * k : 64 * k + 64], faces)
         if turn == 1 and k == 1:
             part = rhs_ref[...] - part
         hold_ref[64 * k : 64 * k + 64, :] = part
@@ -660,7 +722,7 @@
     if nf_next:
         for k, x in enumerate(new):
             new_ref[64 * k : 64 * k + 64, :] = x
-        stack = face_stack(trace_ref, new[:nf_next], normal_scale, nf_next)
+        stack = face_stack(new[:nf_next], normal_scale)
         stack_ref[...] = stack
         sent = gather_message(stack, hot_ref[...], case_ref[0:1], nf_next)
         sent_ref[...] = sent
@@ -722,7 +784,7 @@
 ):
     devices = lax.axis_size("dom")
     chips = devices // 2
-    trace, lift, weight = (jnp.asarray(t) for t in const_tables())
+    stiffness, weight = (jnp.asarray(t) for t in const_tables())
     coef = coefficient.reshape(1, lanes)
     level = refine_level.reshape(1, lanes)
 
@@ -758,8 +820,8 @@
         return arrivals, permute(last, swapped), made
 
     sides = [x.reshape(1, -1) for x in (side_elem, side_dir, side_case, side_kind, partner)]
-    first = [*sides, send_list, start_vector, coef, level, trace, initial_guess]
-    hot, case, stack, sides, rolled, sent, coef, level, trace, guess = run(
+    first = [*sides, send_list, start_vector, coef, level, initial_guess]
+    hot, case, stack, sides, rolled, sent, coef, level, guess = run(
         functools.partial(send_setup_kernel, chips),
         [((768, 256), bf16), ((8, 256), i32), ((80, 768), bf16), ((8, side_pad), i32), ((32, lanes), i32),
          ((40, 256), f32), *((x.shape, x.dtype) for x in first[7:])],
@@ -826,23 +888,23 @@
             *((hots[0], own_scatter) if turn == 1 else ()),
         )
         mine, others, targets = made
-        sums, *made = run(
+        sums, volume, *made = run(
             functools.partial(flux_kernel, nf, chips),
-            [((h, 768), f32)] + ([] if turn else [((8, 256), f32)]),
-            [*arrivals, mine, others, *places, weight, own_scatter]
+            [((h, 768), f32), ((64 * nf, lanes), f32)] + ([] if turn else [((8, 256), f32)]),
+            [*arrivals, mine, others, *places, weight, own_scatter, fields, coef, level, stiffness]
             + ([near_halo] if turn else []),
             "flux",
         )
         if turn == 0:
             near_halo = made[0]
         ins = [
-            last, sums, targets, place, arrival, far_scatter, weight, lift,
+            last, sums, volume, targets, place, arrival, far_scatter, weight,
             fields, coef, level, block_inverse,
         ]
         ins += [far_halo] if turn else [guess]
         ins += [rhs_field] if turn == 1 else []
         if nf_next:
-            ins += [trace, hot, case]
+            ins += [hot, case]
             outs = [
                 ((64 * max(nf, nf_next), lanes), f32), ((64 * nf_next, 768), bf16), ((32 * nf_next, 256), f32)
             ]

time: 53.9 us -> 52.7 us (0.978)
  Pallas kernels: 18.6 us -> 17.5 us
    pallas_call x30, Pallas kernels: 18.6 us -> 17.5 us  [run(): pl.pallas_call(body, out_shape=[(pltpu.VMEM if kept else jax.ShapeDtypeSt...]
  transfers between devices with their start and end apart: 16 -> 16, of which waited for: 12 -> 11; matrix products, arithmetic and copies ran while one was open for 0% -> 0% of each run, Pallas kernels for 20% -> 20%
where the time goes in v6:
time: 52.7 us; the launch traced here: 52.5 us
  Pallas kernels  17.5 us (33%)
  starting transfers between devices  16.5 us (31%)
  blocking collectives  12.1 us (23%)
  waiting for transfers between devices  5.5 us (10%)
  between operations  0.87 us (2%)
    pallas_call x30, Pallas kernels, run(): pl.pallas_call(body, out_shape=[(pltpu.VMEM if kept else jax.ShapeDtypeSt...  17.5 us
    ppermute x16, starting transfers between devices, permute(): return lax.ppermute(x, 'dom', sorted(to.items()))  16.5 us
    all_to_all x1, blocking collectives, local(): lax.all_to_all(parts.reshape(devices, 1, lanes), 'dom', 0, 0)  12.1 us
    ppermute x16, waiting for transfers between devices, permute(): return lax.ppermute(x, 'dom', sorted(to.items()))  5.5 us
  transfers between devices with their start and end apart: 16, of which 11 were waited for; matrix products, arithmetic and copies ran while one was open for 0% of the time, Pallas kernels for 20%

profile of v6, /device:TPU:0, one launch (start us, length us, event | category | flops | bytes accessed | tf_op | source)
XLA Modules:
  0.0 52.5 jit_solution(5977636152579095446)
XLA Ops:
  0.6 0.0 copy-start.1
  0.6 0.0 copy-start.2
  0.7 1.6 %send_setup.1 = (bf16[768,256]{1,0:T(8,128)(2,1)S(1)}, s32[8,256]{1,0:T(8,128)S(1)}, bf16[80,768]{1,0:T(8,128)(2,1)S(1)}, s32[8,1024]{1,0:T(8,128)S(1)}, s32[32,...) custom-call(s32[1,930]{1,0:T(1,128)} %bitcast.15, ...), custom_call_target="tpu_custom_call" | custom-call | flops 16777216 | bytes 1048576 | tf_op jit(solution)/shard_map/send_setup/pallas_call | solution.py:769
  2.3 0.5 collective-permute-start
  2.8 0.3 own_setup.1
  3.1 0.3 own.4.own_ref
  3.4 0.2 collective-permute-done.sent_ref
  3.7 0.1 carry.4
  3.7 2.8 %collective-permute-start.1 = (f32[40,256]{1,0:T(8,128)S(1)}, f32[40,256]{1,0:T(8,128)S(1)}, u32[]{:S(2)}, u32[]{:S(2)}) collective-permute-start(f32[40,256]{1,0:T(8,128)S(1)} %get-tuple-element.71), channel_id=1, source_target_pairs={{0,2},{1,0},{2,1},{3,5},{4,6},{5,3},{6,4},{7,9},{8,10},{9,7},{10,8... | collective-permute-start | bytes 122888 | tf_op jit(solution)/shard_map/ppermute | solution.py:792
  6.6 1.5 %collective-permute-start.2 = (f32[40,128]{1,0:T(8,128)S(1)}, f32[40,128]{1,0:T(8,128)S(1)}, u32[]{:S(2)}, u32[]{:S(2)}) collective-permute-start(f32[40,128]{1,0:T(8,128)S(1)} %get-tuple-element.72), channel_id=1, source_target_pairs={{0,4},{1,3},{2,6},{3,1},{4,0},{5,9},{6,2},{7,11},{8,12},{9,5},{10,... | collective-permute-start | bytes 61448 | tf_op jit(solution)/shard_map/ppermute | solution.py:792
  8.1 0.7 %setup.1 = (bf16[128,1280]{1,0:T(8,128)(2,1)S(1)}, bf16[128,1024]{1,0:T(8,128)(2,1)S(1)}, bf16[128,384]{1,0:T(8,128)(2,1)S(1)}, f32[16,1664]{1,0:T(8,128)S(1)}, ...) custom-call(f32[1,128]{1,0:T(1,128)S(1)} %get-tuple-element.73.coef_ref, s32[1,128]{1,0:T(1,128)S(1)} %get-tuple-element.74.level_ref, ...), custom_call_target="tpu_custom_call" | custom-call | flops 16777216 | bytes 1048576 | tf_op jit(solution)/shard_map/setup/pallas_call | solution.py:769
  8.8 0.8 %sides.4 = (f32[32,1280]{1,0:T(8,128)S(1)}, f32[32,1024]{1,0:T(8,128)S(1)}, f32[32,384]{1,0:T(8,128)S(1)}) custom-call(bf16[80,768]{1,0:T(8,128)(2,1)S(1)} %get-tuple-element.66.stack_ref, bf16[128,1280]{1,0:T(8,128)(2,1)S(1)} %get-tuple-element.75.own_hot_ref.own_elem_ref, bf16[128,1024]{1,0:T(8,128)(2,1)S(1)} %get-tuple-element.76.partner_hot_ref.partner_elem_ref, ...), custom_call_target="tpu_custom_call" | custom-call | flops 16777216 | bytes 1048576 | tf_op jit(solution)/shard_map/sides/pallas_call | solution.py:769
  9.6 0.8 %collective-permute-done.2.two_ref = f32[40,128]{1,0:T(8,128)S(1)} collective-permute-done((f32[40,128]{1,0:T(8,128)S(1)}, f32[40,128]{1,0:T(8,128)S(1)}, u32[]{:S(2)}, u32[]{:S(2)}) %collective-permute-start.2) | collective-permute-done | bytes 20512 | tf_op jit(solution)/shard_map/ppermute | solution.py:792
  10.4 0.0 collective-permute-done.1.one_ref
  10.4 0.1 relay.4
  10.4 0.0 collective-permute-start.3
  10.5 0.6 %flux.4 = (f32[32,768]{1,0:T(8,128)S(1)}, f32[64,128]{1,0:T(8,128)S(1)}, f32[8,256]{1,0:T(8,128)S(1)}) custom-call(f32[40,256]{1,0:T(8,128)S(1)} %collective-permute-done.1.one_ref, f32[40,128]{1,0:T(8,128)S(1)} %collective-permute-done.2.two_ref, f32[32,1280]{1,0:T(8,128)S(1)} %get-tuple-element.82.mine_ref, f32[32,1024]{1,0:T(8,128)S(1)} %get-tuple-element.83.other_ref, ...), custom_call_target="tpu_custom_call" | custom-call | flops 16777216 | bytes 1048576 | tf_op jit(solution)/shard_map/flux/pallas_call | solution.py:769
  11.1 0.6 %collective-permute-done.3.one_ref = f32[40,384]{1,0:T(8,128)S(1)} collective-permute-done((f32[40,384]{1,0:T(8,128)S(1)}, f32[40,384]{1,0:T(8,128)S(1)}, u32[]{:S(2)}, u32[]{:S(2)}) %collective-permute-start.3) | collective-permute-done | bytes 61472 | tf_op jit(solution)/shard_map/ppermute | solution.py:792
  11.7 0.9 %update.4 = (f32[128,128]{1,0:T(8,128)S(1)}, bf16[128,768]{1,0:T(8,128)(2,1)S(1)}, f32[64,256]{1,0:T(8,128)S(1)}, f32[8,384]{1,0:T(8,128)S(1)}) custom-call(f32[40,384]{1,0:T(8,128)S(1)} %collective-permute-done.3.one_ref, f32[32,768]{1,0:T(8,128)S(1)} %get-tuple-element.84.local_ref, f32[64,128]{1,0:T(8,128)S(1)} %get-tuple-element.85.volume_ref, ...), custom_call_target="tpu_custom_call" | custom-call | flops 16777216 | bytes 1048576 | tf_op jit(solution)/shard_map/update/pallas_call | solution.py:769
  12.6 0.2 collective-permute-start.4
  12.8 0.4 whole.1
  13.2 0.4 own.5.own_ref
  13.6 0.3 collective-permute-done.4.sent_ref
  13.9 0.1 carry.5
  14.0 0.6 %collective-permute-start.5 = (f32[64,256]{1,0:T(8,128)S(1)}, f32[64,256]{1,0:T(8,128)S(1)}, u32[]{:S(2)}, u32[]{:S(2)}) collective-permute-start(f32[64,256]{1,0:T(8,128)S(1)} %get-tuple-element.92), channel_id=1, source_target_pairs={{0,2},{1,0},{2,1},{3,5},{4,6},{5,3},{6,4},{7,9},{8,10},{9,7},{10,8... | collective-permute-start | bytes 196616 | tf_op jit(solution)/shard_map/ppermute | solution.py:792
  14.6 1.9 %collective-permute-start.6 = (f32[64,128]{1,0:T(8,128)S(1)}, f32[64,128]{1,0:T(8,128)S(1)}, u32[]{:S(2)}, u32[]{:S(2)}) collective-permute-start(f32[64,128]{1,0:T(8,128)S(1)} %get-tuple-element.93), channel_id=1, source_target_pairs={{0,4},{1,3},{2,6},{3,1},{4,0},{5,9},{6,2},{7,11},{8,12},{9,5},{10,... | collective-permute-start | bytes 98312 | tf_op jit(solution)/shard_map/ppermute | solution.py:792
  16.5 0.7 %turn.1 = (bf16[1280,768]{1,0:T(8,128)(2,1)S(1)}, bf16[384,768]{1,0:T(8,128)(2,1)S(1)}) custom-call(f32[16,1664]{1,0:T(8,128)S(1)} %get-tuple-element.78.place_ref), custom_call_target="tpu_custom_call" | custom-call | flops 16777216 | bytes 1048576 | tf_op jit(solution)/shard_map/turn/pallas_call | solution.py:769
  17.2 1.2 %sides.5 = (f32[64,1280]{1,0:T(8,128)S(1)}, f32[64,1024]{1,0:T(8,128)S(1)}, f32[64,384]{1,0:T(8,128)S(1)}) custom-call(bf16[128,768]{1,0:T(8,128)(2,1)S(1)} %get-tuple-element.90.stack_ref, bf16[768,1280]{1,0:T(8,128)(2,1)S(1)} %get-tuple-element.91.rest_0_.own_hot_ref, bf16[768,1024]{1,0:T(8,128)(2,1)S(1)} %get-tuple-element.94.partner_hot_ref, ...), custom_call_target="tpu_custom_call" | custom-call | flops 16777216 | bytes 1048576 | tf_op jit(solution)/shard_map/sides/pallas_call | solution.py:769
  18.4 0.1 collective-permute-done.6.two_ref
  18.5 0.0 collective-permute-done.5.one_ref
  18.5 0.1 relay.5
  18.6 0.5 %collective-permute-start.7 = (f32[64,384]{1,0:T(8,128)S(1)}, f32[64,384]{1,0:T(8,128)S(1)}, u32[]{:S(2)}, u32[]{:S(2)}) collective-permute-start(f32[64,384]{1,0:T(8,128)S(1)} %relay.5), channel_id=1, source_target_pairs={{0,1},{1,0},{2,3},{3,2},{4,5},{5,4},{6,7},{7,6},{8,9},{9,8},{10,11... | collective-permute-start | bytes 294920 | tf_op jit(solution)/shard_map/ppermute | solution.py:792
  19.1 0.9 %flux.5 = (f32[64,768]{1,0:T(8,128)S(1)}, f32[128,128]{1,0:T(8,128)S(1)}) custom-call(f32[64,256]{1,0:T(8,128)S(1)} %collective-permute-done.5.one_ref, f32[64,128]{1,0:T(8,128)S(1)} %collective-permute-done.6.two_ref, f32[64,1280]{1,0:T(8,128)S(1)} %get-tuple-element.98.mine_ref, f32[64,1024]{1,0:T(8,128)S(1)} %get-tuple-element.99.other_ref, ...), custom_call_target="tpu_custom_call" | custom-call | flops 16777216 | bytes 1048576 | tf_op jit(solution)/shard_map/flux/pallas_call | solution.py:769
  20.0 0.0 collective-permute-done.7.one_ref
  20.1 1.2 %update.5 = (f32[128,128]{1,0:T(8,128)S(1)}, bf16[128,768]{1,0:T(8,128)(2,1)S(1)}, f32[64,256]{1,0:T(8,128)S(1)}) custom-call(f32[64,384]{1,0:T(8,128)S(1)} %collective-permute-done.7.one_ref, f32[64,768]{1,0:T(8,128)S(1)} %get-tuple-element.102.local_ref, f32[128,128]{1,0:T(8,128)S(1)} %get-tuple-element.103.volume_ref, ...), custom_call_target="tpu_custom_call" | custom-call | flops 16777216 | bytes 1048576 | tf_op jit(solution)/shard_map/update/pallas_call | solution.py:769
  21.3 0.4 collective-permute-start.8
  21.7 0.4 own.6.own_ref
  22.1 0.5 collective-permute-done.8.sent_ref
  22.6 0.1 carry.6
  22.7 1.8 %collective-permute-start.9 = (f32[64,256]{1,0:T(8,128)S(1)}, f32[64,256]{1,0:T(8,128)S(1)}, u32[]{:S(2)}, u32[]{:S(2)}) collective-permute-start(f32[64,256]{1,0:T(8,128)S(1)} %get-tuple-element.108), channel_id=1, source_target_pairs={{0,2},{1,0},{2,1},{3,5},{4,6},{5,3},{6,4},{7,9},{8,10},{9,7},{10,8... | collective-permute-start | bytes 196616 | tf_op jit(solution)/shard_map/ppermute | solution.py:792
  24.5 2.5 %collective-permute-start.10 = (f32[64,128]{1,0:T(8,128)S(1)}, f32[64,128]{1,0:T(8,128)S(1)}, u32[]{:S(2)}, u32[]{:S(2)}) collective-permute-start(f32[64,128]{1,0:T(8,128)S(1)} %get-tuple-element.109), channel_id=1, source_target_pairs={{0,4},{1,3},{2,6},{3,1},{4,0},{5,9},{6,2},{7,11},{8,12},{9,5},{10,... | collective-permute-start | bytes 98312 | tf_op jit(solution)/shard_map/ppermute | solution.py:792
  27.0 1.2 %sides.6 = (f32[64,1280]{1,0:T(8,128)S(1)}, f32[64,1024]{1,0:T(8,128)S(1)}, f32[64,384]{1,0:T(8,128)S(1)}) custom-call(bf16[128,768]{1,0:T(8,128)(2,1)S(1)} %get-tuple-element.107.stack_ref, bf16[768,1280]{1,0:T(8,128)(2,1)S(1)} %get-tuple-element.91.rest_0_.own_hot_ref, bf16[768,1024]{1,0:T(8,128)(2,1)S(1)} %get-tuple-element.94.partner_hot_ref, ...), custom_call_target="tpu_custom_call" | custom-call | flops 16777216 | bytes 1048576 | tf_op jit(solution)/shard_map/sides/pallas_call | solution.py:769
  28.3 0.7 %collective-permute-done.10.two_ref = f32[64,128]{1,0:T(8,128)S(1)} collective-permute-done((f32[64,128]{1,0:T(8,128)S(1)}, f32[64,128]{1,0:T(8,128)S(1)}, u32[]{:S(2)}, u32[]{:S(2)}) %collective-permute-start.10) | collective-permute-done | bytes 32800 | tf_op jit(solution)/shard_map/ppermute | solution.py:792
  28.9 0.0 collective-permute-done.9.one_ref
  28.9 0.1 relay.6
  29.0 0.1 collective-permute-start.11
  29.1 0.9 %flux.6 = (f32[64,768]{1,0:T(8,128)S(1)}, f32[128,128]{1,0:T(8,128)S(1)}) custom-call(f32[64,256]{1,0:T(8,128)S(1)} %collective-permute-done.9.one_ref, f32[64,128]{1,0:T(8,128)S(1)} %collective-permute-done.10.two_ref, f32[64,1280]{1,0:T(8,128)S(1)} %get-tuple-element.111.mine_ref, f32[64,1024]{1,0:T(8,128)S(1)} %get-tuple-element.112.other_ref, ...), custom_call_target="tpu_custom_call" | custom-call | flops 16777216 | bytes 1048576 | tf_op jit(solution)/shard_map/flux/pallas_call | solution.py:769
  30.0 0.4 collective-permute-done.11.one_ref
  30.4 1.1 %update.6 = (f32[128,128]{1,0:T(8,128)S(1)}, bf16[64,768]{1,0:T(8,128)(2,1)S(1)}, f32[32,256]{1,0:T(8,128)S(1)}) custom-call(f32[64,384]{1,0:T(8,128)S(1)} %collective-permute-done.11.one_ref, f32[64,768]{1,0:T(8,128)S(1)} %get-tuple-element.114.local_ref, f32[128,128]{1,0:T(8,128)S(1)} %get-tuple-element.115.volume_ref, ...), custom_call_target="tpu_custom_call" | custom-call | flops 16777216 | bytes 1048576 | tf_op jit(solution)/shard_map/update/pallas_call | solution.py:769
  31.5 0.2 collective-permute-start.12
  31.7 0.3 own.7.own_ref
  32.0 0.7 %collective-permute-done.12.sent_ref = f32[32,256]{1,0:T(8,128)S(1)} collective-permute-done((f32[32,256]{1,0:T(8,128)S(1)}, f32[32,256]{1,0:T(8,128)S(1)}, u32[]{:S(2)}, u32[]{:S(2)}) %collective-permute-start.12) | collective-permute-done | bytes 32800 | tf_op jit(solution)/shard_map/ppermute | solution.py:792
  32.7 0.1 carry.7
  32.8 0.5 collective-permute-start.13
  33.3 2.7 %collective-permute-start.14 = (f32[32,128]{1,0:T(8,128)S(1)}, f32[32,128]{1,0:T(8,128)S(1)}, u32[]{:S(2)}, u32[]{:S(2)}) collective-permute-start(f32[32,128]{1,0:T(8,128)S(1)} %get-tuple-element.119), channel_id=1, source_target_pairs={{0,4},{1,3},{2,6},{3,1},{4,0},{5,9},{6,2},{7,11},{8,12},{9,5},{10,... | collective-permute-start | bytes 49160 | tf_op jit(solution)/shard_map/ppermute | solution.py:792
  36.0 1.0 %sides.7 = (f32[32,1280]{1,0:T(8,128)S(1)}, f32[32,1024]{1,0:T(8,128)S(1)}, f32[32,384]{1,0:T(8,128)S(1)}) custom-call(bf16[64,768]{1,0:T(8,128)(2,1)S(1)} %get-tuple-element.117.stack_ref, bf16[768,1280]{1,0:T(8,128)(2,1)S(1)} %get-tuple-element.91.rest_0_.own_hot_ref, bf16[768,1024]{1,0:T(8,128)(2,1)S(1)} %get-tuple-element.94.partner_hot_ref, ...), custom_call_target="tpu_custom_call" | custom-call | flops 16777216 | bytes 1048576 | tf_op jit(solution)/shard_map/sides/pallas_call | solution.py:769
  37.0 0.7 %collective-permute-done.14.two_ref = f32[32,128]{1,0:T(8,128)S(1)} collective-permute-done((f32[32,128]{1,0:T(8,128)S(1)}, f32[32,128]{1,0:T(8,128)S(1)}, u32[]{:S(2)}, u32[]{:S(2)}) %collective-permute-start.14) | collective-permute-done | bytes 16416 | tf_op jit(solution)/shard_map/ppermute | solution.py:792
  37.7 0.1 relay.7
  37.8 0.1 collective-permute-start.15
  37.9 0.6 %flux.7 = (f32[32,768]{1,0:T(8,128)S(1)}, f32[64,128]{1,0:T(8,128)S(1)}) custom-call(f32[32,256]{1,0:T(8,128)S(1)} %collective-permute-done.13.one_ref, f32[32,128]{1,0:T(8,128)S(1)} %collective-permute-done.14.two_ref, f32[32,1280]{1,0:T(8,128)S(1)} %get-tuple-element.121.mine_ref, f32[32,1024]{1,0:T(8,128)S(1)} %get-tuple-element.122.other_ref, ...), custom_call_target="tpu_custom_call" | custom-call | flops 16777216 | bytes 1048576 | tf_op jit(solution)/shard_map/flux/pallas_call | solution.py:769
  38.6 0.5 collective-permute-done.15.one_ref
  39.0 0.6 %update.7 = f32[32,128]{1,0:T(8,128)S(1)} custom-call(f32[32,384]{1,0:T(8,128)S(1)} %collective-permute-done.15.one_ref, f32[32,768]{1,0:T(8,128)S(1)} %get-tuple-element.124.local_ref, f32[64,128]{1,0:T(8,128)S(1)} %get-tuple-element.125.volume_ref, f32[32,384]{1,0:T(8,128)S(1)} %get-tuple-element.120.rest_0_.target_ref, ...), custom_call_target="tpu_custom_call" | custom-call | flops 16777216 | bytes 1048576 | tf_op jit(solution)/shard_map/update/pallas_call | solution.py:769
  39.7 12.1 %all_to_all.5 = f32[32,1,128]{2,1,0:T(1,128)S(1)} all-to-all(f32[32,1,128]{2,1,0:T(1,128)S(1)} %bitcast.13), channel_id=1, replica_groups=mesh['dom'=32] {'dom'}, dimensions={0} | all-to-all | bytes 32768 | tf_op jit(solution)/shard_map/all_to_all | solution.py:927
  51.8 0.7 %finish.1 = (f32[64,128]{1,0:T(8,128)}, f32[1,128]{1,0:T(1,128)}) custom-call(f32[32,128]{1,0:T(8,128)S(1)} %bitcast.14, f32[64,128]{1,0:T(8,128)S(1)} %get-tuple-element.86.rest_0_.guess_ref, f32[128,128]{1,0:T(8,128)S(1)} %get-tuple-element.113.field_ref.first_ref, f32[128,128]{1,0:T(8,128)S(1)} %get-tuple-element.123.second_ref), custom_call_target="tpu_custom_call" | custom-call | flops 16777216 | bytes 1048576 | tf_op jit(solution)/shard_map/finish/pallas_call | solution.py:769
  (10 shorter events, 0.0 us)
Async XLA Ops:
  0.6 9.8 %copy-start.1 = (f32[32,128]{1,0:T(8,128)S(1)}, f32[32,128]{1,0:T(8,128)}, u32[]{:S(2)}) copy-start(f32[32,128]{1,0:T(8,128)} %constant.5.clone.weight_ref) | copy-start | bytes 49156
  0.6 9.8 %copy-start.2 = (bf16[64,192]{1,0:T(8,128)(2,1)S(1)}, bf16[64,192]{1,0:T(8,128)(2,1)}, u32[]{:S(2)}) copy-start(bf16[64,192]{1,0:T(8,128)(2,1)} %constant.4.clone.stiffness_ref) | copy-start | bytes 73732
  0.7 9.8 %copy-start.3 = (f32[64,128]{1,0:T(8,128)S(1)}, f32[64,128]{1,0:T(8,128)}, u32[]{:S(2)}) copy-start(f32[64,128]{1,0:T(8,128)} %field_ref.3) | copy-start | bytes 98308
  0.7 11.0 %copy-start = (bf16[64,64,128]{2,1,0:T(8,128)(2,1)S(1)}, bf16[64,64,128]{2,1,0:T(8,128)(2,1)}, u32[]{:S(2)}) copy-start(bf16[64,64,128]{2,1,0:T(8,128)(2,1)} %inverse_ref.7) | copy-start | bytes 3145732
  2.3 1.4 %collective-permute-start = (f32[40,256]{1,0:T(8,128)S(1)}, f32[40,256]{1,0:T(8,128)S(1)}, u32[]{:S(2)}, u32[]{:S(2)}) collective-permute-start(f32[40,256]{1,0:T(8,128)S(1)} %get-tuple-element.65), channel_id=1, source_target_pairs={{0,1},{1,0},{2,3},{3,2},{4,5},{5,4},{6,7},{7,6},{8,9},{9,8},{10,11... | collective-permute-start | bytes 122888 | tf_op jit(solution)/shard_map/ppermute | solution.py:792
  3.7 6.6 %collective-permute-start.1 = (f32[40,256]{1,0:T(8,128)S(1)}, f32[40,256]{1,0:T(8,128)S(1)}, u32[]{:S(2)}, u32[]{:S(2)}) collective-permute-start(f32[40,256]{1,0:T(8,128)S(1)} %get-tuple-element.71), channel_id=1, source_target_pairs={{0,2},{1,0},{2,1},{3,5},{4,6},{5,3},{6,4},{7,9},{8,10},{9,7},{10,8... | collective-permute-start | bytes 122888 | tf_op jit(solution)/shard_map/ppermute | solution.py:792
  6.6 3.8 %collective-permute-start.2 = (f32[40,128]{1,0:T(8,128)S(1)}, f32[40,128]{1,0:T(8,128)S(1)}, u32[]{:S(2)}, u32[]{:S(2)}) collective-permute-start(f32[40,128]{1,0:T(8,128)S(1)} %get-tuple-element.72), channel_id=1, source_target_pairs={{0,4},{1,3},{2,6},{3,1},{4,0},{5,9},{6,2},{7,11},{8,12},{9,5},{10,... | collective-permute-start | bytes 61448 | tf_op jit(solution)/shard_map/ppermute | solution.py:792
  10.4 1.3 %collective-permute-start.3 = (f32[40,384]{1,0:T(8,128)S(1)}, f32[40,384]{1,0:T(8,128)S(1)}, u32[]{:S(2)}, u32[]{:S(2)}) collective-permute-start(f32[40,384]{1,0:T(8,128)S(1)} %relay.4), channel_id=1, source_target_pairs={{0,1},{1,0},{2,3},{3,2},{4,5},{5,4},{6,7},{7,6},{8,9},{9,8},{10,11... | collective-permute-start | bytes 184328 | tf_op jit(solution)/shard_map/ppermute | solution.py:792
  12.6 1.3 %collective-permute-start.4 = (f32[64,256]{1,0:T(8,128)S(1)}, f32[64,256]{1,0:T(8,128)S(1)}, u32[]{:S(2)}, u32[]{:S(2)}) collective-permute-start(f32[64,256]{1,0:T(8,128)S(1)} %get-tuple-element.89), channel_id=1, source_target_pairs={{0,1},{1,0},{2,3},{3,2},{4,5},{5,4},{6,7},{7,6},{8,9},{9,8},{10,11... | collective-permute-start | bytes 196616 | tf_op jit(solution)/shard_map/ppermute | solution.py:792
  14.0 4.5 %collective-permute-start.5 = (f32[64,256]{1,0:T(8,128)S(1)}, f32[64,256]{1,0:T(8,128)S(1)}, u32[]{:S(2)}, u32[]{:S(2)}) collective-permute-start(f32[64,256]{1,0:T(8,128)S(1)} %get-tuple-element.92), channel_id=1, source_target_pairs={{0,2},{1,0},{2,1},{3,5},{4,6},{5,3},{6,4},{7,9},{8,10},{9,7},{10,8... | collective-permute-start | bytes 196616 | tf_op jit(solution)/shard_map/ppermute | solution.py:792
  14.6 3.9 %collective-permute-start.6 = (f32[64,128]{1,0:T(8,128)S(1)}, f32[64,128]{1,0:T(8,128)S(1)}, u32[]{:S(2)}, u32[]{:S(2)}) collective-permute-start(f32[64,128]{1,0:T(8,128)S(1)} %get-tuple-element.93), channel_id=1, source_target_pairs={{0,4},{1,3},{2,6},{3,1},{4,0},{5,9},{6,2},{7,11},{8,12},{9,5},{10,... | collective-permute-start | bytes 98312 | tf_op jit(solution)/shard_map/ppermute | solution.py:792
  18.6 1.5 %copy-start.4 = (f32[64,128]{1,0:T(8,128)S(1)}, f32[64,128]{1,0:T(8,128)}, u32[]{:S(2)}) copy-start(f32[64,128]{1,0:T(8,128)} %rest_1_.1) | copy-start | bytes 98308
  18.6 1.5 %collective-permute-start.7 = (f32[64,384]{1,0:T(8,128)S(1)}, f32[64,384]{1,0:T(8,128)S(1)}, u32[]{:S(2)}, u32[]{:S(2)}) collective-permute-start(f32[64,384]{1,0:T(8,128)S(1)} %relay.5), channel_id=1, source_target_pairs={{0,1},{1,0},{2,3},{3,2},{4,5},{5,4},{6,7},{7,6},{8,9},{9,8},{10,11... | collective-permute-start | bytes 294920 | tf_op jit(solution)/shard_map/ppermute | solution.py:792
  21.3 1.3 %collective-permute-start.8 = (f32[64,256]{1,0:T(8,128)S(1)}, f32[64,256]{1,0:T(8,128)S(1)}, u32[]{:S(2)}, u32[]{:S(2)}) collective-permute-start(f32[64,256]{1,0:T(8,128)S(1)} %get-tuple-element.106), channel_id=1, source_target_pairs={{0,1},{1,0},{2,3},{3,2},{4,5},{5,4},{6,7},{7,6},{8,9},{9,8},{10,11... | collective-permute-start | bytes 196616 | tf_op jit(solution)/shard_map/ppermute | solution.py:792
  22.7 6.2 %collective-permute-start.9 = (f32[64,256]{1,0:T(8,128)S(1)}, f32[64,256]{1,0:T(8,128)S(1)}, u32[]{:S(2)}, u32[]{:S(2)}) collective-permute-start(f32[64,256]{1,0:T(8,128)S(1)} %get-tuple-element.108), channel_id=1, source_target_pairs={{0,2},{1,0},{2,1},{3,5},{4,6},{5,3},{6,4},{7,9},{8,10},{9,7},{10,8... | collective-permute-start | bytes 196616 | tf_op jit(solution)/shard_map/ppermute | solution.py:792
  24.5 4.4 %collective-permute-start.10 = (f32[64,128]{1,0:T(8,128)S(1)}, f32[64,128]{1,0:T(8,128)S(1)}, u32[]{:S(2)}, u32[]{:S(2)}) collective-permute-start(f32[64,128]{1,0:T(8,128)S(1)} %get-tuple-element.109), channel_id=1, source_target_pairs={{0,4},{1,3},{2,6},{3,1},{4,0},{5,9},{6,2},{7,11},{8,12},{9,5},{10,... | collective-permute-start | bytes 98312 | tf_op jit(solution)/shard_map/ppermute | solution.py:792
  29.0 1.3 %collective-permute-start.11 = (f32[64,384]{1,0:T(8,128)S(1)}, f32[64,384]{1,0:T(8,128)S(1)}, u32[]{:S(2)}, u32[]{:S(2)}) collective-permute-start(f32[64,384]{1,0:T(8,128)S(1)} %relay.6), channel_id=1, source_target_pairs={{0,1},{1,0},{2,3},{3,2},{4,5},{5,4},{6,7},{7,6},{8,9},{9,8},{10,11... | collective-permute-start | bytes 294920 | tf_op jit(solution)/shard_map/ppermute | solution.py:792
  31.5 1.3 %collective-permute-start.12 = (f32[32,256]{1,0:T(8,128)S(1)}, f32[32,256]{1,0:T(8,128)S(1)}, u32[]{:S(2)}, u32[]{:S(2)}) collective-permute-start(f32[32,256]{1,0:T(8,128)S(1)} %get-tuple-element.116), channel_id=1, source_target_pairs={{0,1},{1,0},{2,3},{3,2},{4,5},{5,4},{6,7},{7,6},{8,9},{9,8},{10,11... | collective-permute-start | bytes 98312 | tf_op jit(solution)/shard_map/ppermute | solution.py:792
  32.8 4.9 %collective-permute-start.13 = (f32[32,256]{1,0:T(8,128)S(1)}, f32[32,256]{1,0:T(8,128)S(1)}, u32[]{:S(2)}, u32[]{:S(2)}) collective-permute-start(f32[32,256]{1,0:T(8,128)S(1)} %get-tuple-element.118), channel_id=1, source_target_pairs={{0,2},{1,0},{2,1},{3,5},{4,6},{5,3},{6,4},{7,9},{8,10},{9,7},{10,8... | collective-permute-start | bytes 98312 | tf_op jit(solution)/shard_map/ppermute | solution.py:792
  33.3 4.4 %collective-permute-start.14 = (f32[32,128]{1,0:T(8,128)S(1)}, f32[32,128]{1,0:T(8,128)S(1)}, u32[]{:S(2)}, u32[]{:S(2)}) collective-permute-start(f32[32,128]{1,0:T(8,128)S(1)} %get-tuple-element.119), channel_id=1, source_target_pairs={{0,4},{1,3},{2,6},{3,1},{4,0},{5,9},{6,2},{7,11},{8,12},{9,5},{10,... | collective-permute-start | bytes 49160 | tf_op jit(solution)/shard_map/ppermute | solution.py:792
  37.8 1.2 %collective-permute-start.15 = (f32[32,384]{1,0:T(8,128)S(1)}, f32[32,384]{1,0:T(8,128)S(1)}, u32[]{:S(2)}, u32[]{:S(2)}) collective-permute-start(f32[32,384]{1,0:T(8,128)S(1)} %relay.7), channel_id=1, source_target_pairs={{0,1},{1,0},{2,3},{3,2},{4,5},{5,4},{6,7},{7,6},{8,9},{9,8},{10,11... | collective-permute-start | bytes 147464 | tf_op jit(solution)/shard_map/ppermute | solution.py:792

commit v7 on v6

--- a/solution.py
+++ b/solution.py
@@ -633,10 +633,11 @@
 
 
 def flux_kernel(
-    nf, chips, one_ref, two_ref, mine_ref, other_ref, place_ref, info_ref, arrival_ref, weight_ref,
+    turn, nf, skip, chips, one_ref, two_ref, mine_ref, other_ref, place_ref, info_ref, arrival_ref, weight_ref,
     own_hot_ref, field_ref, coef_ref, level_ref, stiffness_ref, *rest,
 ):
     h = 32 * nf
+    rows = slice(32 * skip, 32 * skip + h)
     core, near, far, end, near_there, far_there = where_am_i(chips)
     lane = lax.broadcasted_iota(i32, (1, lanes), 1)
     two_away = two_ref[...]
@@ -645,7 +646,7 @@
     got = jnp.concatenate(
         [jnp.where(inside, kept, one_ref[:, 0:128]), one_ref[:, 128:256]], axis=1
     )
-    if got.shape[0] > h:
+    if turn == 0:
         sum_ref, volume_ref, halo_ref = rest
         halo = halo_coefs(
             arrival_ref[1:2, 0:256], arrival_ref[2:3, 0:256], got[h : h + 1], got[h + 1 : h + 2]
@@ -657,13 +658,14 @@
     coefs = [
         jnp.concatenate([info_ref[k : k + 1, 0:side_pad], halo[k // 2]], axis=1) for k in range(4)
     ]
-    outer = jnp.concatenate([other_ref[...], got[0:h]], axis=1)
+    outer = jnp.concatenate([other_ref[rows], got[rows]], axis=1)
     sum_ref[...] = side_flux(
-        nf, mine_ref, outer, coefs, info_ref[4:5], place_ref[1:2, 0 : side_pad + 256], weight_ref,
+        nf, mine_ref[rows], outer, coefs, info_ref[4:5], place_ref[1:2, 0 : side_pad + 256], weight_ref,
         own_hot_ref[...],
     )
     volume_scale = element_rows(coef_ref, level_ref)[2]
-    fields = [field_ref[64 * k : 64 * k + 64] * volume_scale for k in range(nf)]
+    low = 64 * skip
+    fields = [field_ref[low + 64 * k : low + 64 * k + 64] * volume_scale for k in range(nf)]
     volume = table_dot(stiffness_ref[...], cat(fields, 1))
     for k in range(nf):
         volume_ref[64 * k : 64 * k + 64, :] = volume[:, lanes * k : lanes * k + lanes]
@@ -679,7 +681,7 @@
 
 
 def update_kernel(
-    turn, nf, nf_next,
+    turn, nf, skip, nf_next,
     one_ref, local_ref, volume_ref, target_ref, place_ref, arrival_ref, far_hot_ref, weight_ref,
     field_ref, coef_ref, level_ref, inverse_ref, *rest,
 ):
@@ -691,10 +693,13 @@
         rhs_ref, *rest = rest
     if nf_next:
         hot_ref, case_ref, new_ref, stack_ref, sent_ref, *rest = rest
+    elif turn == 3:
+        part_ref, *rest = rest
     else:
-        part_ref, *rest = rest
+        new_ref, *rest = rest
     hold_ref = rest[-1]
     h = 32 * nf
+    rows = slice(32 * skip, 32 * skip + h)
     if turn == 0:
         halo = halo_coefs(
             arrival_ref[1:2, 256:640], arrival_ref[2:3, 256:640],
@@ -704,7 +709,7 @@
     else:
         halo = (halo_ref[0:1], halo_ref[1:2])
     total = local_ref[...] + side_flux(
-        nf, target_ref, one_ref, (halo[0], halo[0], halo[1], halo[1]), arrival_ref[0:1, 256:640],
+        nf, target_ref[rows], one_ref[rows], (halo[0], halo[0], halo[1], halo[1]), arrival_ref[0:1, 256:640],
         place_ref[1:2, side_pad + 256 :], weight_ref, far_hot_ref[...],
     )
     coef, size, volume_scale, normal_scale = element_rows(coef_ref, level_ref)
@@ -719,14 +724,15 @@
     new = solve_blocks(inverse_ref, hold_ref, nf)
     if turn == 0:
         new.append(guess_ref[...])
-    if nf_next:
+    if turn < 3:
         for k, x in enumerate(new):
             new_ref[64 * k : 64 * k + 64, :] = x
+    if nf_next:
         stack = face_stack(new[:nf_next], normal_scale)
         stack_ref[...] = stack
         sent = gather_message(stack, hot_ref[...], case_ref[0:1], nf_next)
         sent_ref[...] = sent
-    else:
+    if turn == 3:
         lane = lax.broadcasted_iota(i32, (1, lanes), 1)
         sums = []
         for x in (field_ref[...], new[0]):
@@ -749,7 +755,7 @@
     damping = 1.0 / ratio
     damping_next = 1.0 / (2.0 * ratio - damping)
     first = first_ref[64:128] / center
-    second = first_ref[64:128] - second_ref[64:128] / center
+    second = first_ref[64:128] - second_ref[...] / center
     out_ref[...] = (
         guess_ref[...] + first + (damping_next * damping * first + 2.0 * damping_next / half * second)
     )
@@ -840,8 +846,7 @@
         "own_setup",
         scratch=[pltpu.VMEM((8, 512), i32)],
     )
-    fields = start_vector
-    history = []
+    fields, halo, late = start_vector, [], []
     for turn, (nf, nf_next) in enumerate(((1, 2), (2, 2), (2, 1), (1, 0))):
         h = 32 * nf
         def own_work():
@@ -883,52 +888,57 @@
                 [place],
                 "turn",
             )
+        beside = (hots[0], own_scatter) if turn == 1 else late if turn == 3 else ()
         arrivals, last, made = exchange(
-            sent, nf, own_work, functools.partial(side_work, hots),
-            *((hots[0], own_scatter) if turn == 1 else ()),
+            sent, nf, own_work, functools.partial(side_work, hots), *beside
         )
         mine, others, targets = made
-        sums, volume, *made = run(
-            functools.partial(flux_kernel, nf, chips),
-            [((h, 768), f32), ((64 * nf, lanes), f32)] + ([] if turn else [((8, 256), f32)]),
-            [*arrivals, mine, others, *places, weight, own_scatter, fields, coef, level, stiffness]
-            + ([near_halo] if turn else []),
-            "flux",
-        )
+
+        def apply(count, skip, count_next):
+            rows = 32 * count
+            sums, volume, *near = run(
+                functools.partial(flux_kernel, turn, count, skip, chips),
+                [((rows, 768), f32), ((64 * count, lanes), f32)] + ([] if turn else [((8, 256), f32)]),
+                [*arrivals, mine, others, *places, weight, own_scatter, fields, coef, level, stiffness]
+                + halo[:1],
+                "flux",
+            )
+            ins = [
+                last, sums, volume, targets, place, arrival, far_scatter, weight, fields, coef, level,
+                block_inverse, *(halo[1:] if turn else [guess]), *([rhs_field] if turn == 1 else []),
+            ]
+            outs = [((devices, lanes) if turn == 3 else (64 * max(count, count_next), lanes), f32)]
+            if count_next:
+                ins += [hot, case]
+                outs += [((64 * count_next, 768), bf16), ((32 * count_next, 256), f32)]
+            outs += [] if turn else [((8, 384), f32)]
+            late.append(sums)
+            made = run(
+                functools.partial(update_kernel, turn, count, skip, count_next),
+                outs, ins, "update",
+                scratch=[pltpu.VMEM((64 * count, lanes), f32)],
+            )
+            return [*made, *near]
+
         if turn == 0:
-            near_halo = made[0]
-        ins = [
-            last, sums, volume, targets, place, arrival, far_scatter, weight,
-            fields, coef, level, block_inverse,
-        ]
-        ins += [far_halo] if turn else [guess]
-        ins += [rhs_field] if turn == 1 else []
-        if nf_next:
-            ins += [hot, case]
-            outs = [
-                ((64 * max(nf, nf_next), lanes), f32), ((64 * nf_next, 768), bf16), ((32 * nf_next, 256), f32)
-            ]
+            new, stack, sent, far_halo, near_halo = apply(nf, 0, nf_next)
+            halo = [near_halo, far_halo]
+        elif turn == 1:
+            new, stack, sent = apply(nf, 0, nf_next)
+            first = new
+        elif turn == 2:
+            new, stack, sent = apply(1, 0, 1)
+            late.clear()
+            late += apply(1, 1, 0)
+            second = late[1]
         else:
-            outs = [((devices, lanes), f32)]
-        made = run(
-            functools.partial(update_kernel, turn, nf, nf_next),
-            outs + ([] if turn else [((8, 384), f32)]), ins, "update",
-            scratch=[pltpu.VMEM((64 * nf, lanes), f32)],
-        )
-        if turn == 0:
-            far_halo = made[-1]
-        if nf_next:
-            fields, stack, sent = made[:3]
-            history.append(fields)
-            if nf_next < nf:
-                fields = fields[:64]
-        else:
-            (parts,) = made
+            (parts,) = apply(1, 0, 0)
+        fields = new
     parts = lax.all_to_all(parts.reshape(devices, 1, lanes), "dom", 0, 0).reshape(devices, lanes)
     smoothed, bound = run(
         finish_kernel,
         [((64, lanes), f32), ((1, lanes), f32)],
-        [parts, guess, history[1], history[2]],
+        [parts, guess, first, second],
         "finish",
         kept=False,
     )

time: 52.7 us -> 52.4 us (level)
  waiting for transfers between devices: 5.5 us -> 4.56 us
  Pallas kernels: 17.5 us -> 18.2 us
    ppermute x16, waiting for transfers between devices: 5.5 us -> 4.56 us  [permute(): return lax.ppermute(x, 'dom', sorted(to.items()))]
    pallas_call x30 -> x32, Pallas kernels: 17.5 us -> 18.2 us  [run(): pl.pallas_call(body, out_shape=[(pltpu.VMEM if kept else jax.ShapeDtypeSt...]
  transfers between devices with their start and end apart: 16 -> 16, of which waited for: 11 -> 11; matrix products, arithmetic and copies ran while one was open for 0% -> 0% of each run, Pallas kernels for 20% -> 22%
where the time goes in v7:
time: 52.4 us; the launch traced here: 52.2 us
  Pallas kernels  18.2 us (35%)
  starting transfers between devices  16.6 us (32%)
  blocking collectives  12 us (23%)
  waiting for transfers between devices  4.56 us (9%)
  between operations  0.87 us (2%)
    pallas_call x32, Pallas kernels, run(): pl.pallas_call(body, out_shape=[(pltpu.VMEM if kept else jax.ShapeDtypeSt...  18.2 us
    ppermute x16, starting transfers between devices, permute(): return lax.ppermute(x, 'dom', sorted(to.items()))  16.6 us
    all_to_all x1, blocking collectives, local(): lax.all_to_all(parts.reshape(devices, 1, lanes), 'dom', 0, 0)  12 us
    ppermute x16, waiting for transfers between devices, permute(): return lax.ppermute(x, 'dom', sorted(to.items()))  4.56 us
  transfers between devices with their start and end apart: 16, of which 11 were waited for; matrix products, arithmetic and copies ran while one was open for 0% of the time, Pallas kernels for 22%

profile of v7, /device:TPU:0, one launch (start us, length us, event | category | flops | bytes accessed | tf_op | source)
XLA Modules:
  0.0 52.2 jit_solution(15891495574255299917)
XLA Ops:
  0.6 0.0 copy-start.1
  0.6 0.0 copy-start.2
  0.7 1.6 %send_setup.1 = (bf16[768,256]{1,0:T(8,128)(2,1)S(1)}, s32[8,256]{1,0:T(8,128)S(1)}, bf16[80,768]{1,0:T(8,128)(2,1)S(1)}, s32[8,1024]{1,0:T(8,128)S(1)}, s32[32,...) custom-call(s32[1,930]{1,0:T(1,128)} %bitcast.15, ...), custom_call_target="tpu_custom_call" | custom-call | flops 16777216 | bytes 1048576 | tf_op jit(solution)/shard_map/send_setup/pallas_call | solution.py:775
  2.3 0.5 collective-permute-start
  2.8 0.3 own_setup.1
  3.1 0.3 own.4.own_ref
  3.4 0.2 collective-permute-done.sent_ref
  3.7 0.1 carry.4
  3.7 2.8 %collective-permute-start.1 = (f32[40,256]{1,0:T(8,128)S(1)}, f32[40,256]{1,0:T(8,128)S(1)}, u32[]{:S(2)}, u32[]{:S(2)}) collective-permute-start(f32[40,256]{1,0:T(8,128)S(1)} %get-tuple-element.73), channel_id=1, source_target_pairs={{0,2},{1,0},{2,1},{3,5},{4,6},{5,3},{6,4},{7,9},{8,10},{9,7},{10,8... | collective-permute-start | bytes 122888 | tf_op jit(solution)/shard_map/ppermute | solution.py:798
  6.6 1.5 %collective-permute-start.2 = (f32[40,128]{1,0:T(8,128)S(1)}, f32[40,128]{1,0:T(8,128)S(1)}, u32[]{:S(2)}, u32[]{:S(2)}) collective-permute-start(f32[40,128]{1,0:T(8,128)S(1)} %get-tuple-element.74), channel_id=1, source_target_pairs={{0,4},{1,3},{2,6},{3,1},{4,0},{5,9},{6,2},{7,11},{8,12},{9,5},{10,... | collective-permute-start | bytes 61448 | tf_op jit(solution)/shard_map/ppermute | solution.py:798
  8.1 0.7 %setup.1 = (bf16[128,1280]{1,0:T(8,128)(2,1)S(1)}, bf16[128,1024]{1,0:T(8,128)(2,1)S(1)}, bf16[128,384]{1,0:T(8,128)(2,1)S(1)}, f32[16,1664]{1,0:T(8,128)S(1)}, ...) custom-call(f32[1,128]{1,0:T(1,128)S(1)} %get-tuple-element.75.coef_ref, s32[1,128]{1,0:T(1,128)S(1)} %get-tuple-element.76.level_ref, ...), custom_call_target="tpu_custom_call" | custom-call | flops 16777216 | bytes 1048576 | tf_op jit(solution)/shard_map/setup/pallas_call | solution.py:775
  8.8 0.8 %sides.4 = (f32[32,1280]{1,0:T(8,128)S(1)}, f32[32,1024]{1,0:T(8,128)S(1)}, f32[32,384]{1,0:T(8,128)S(1)}) custom-call(bf16[80,768]{1,0:T(8,128)(2,1)S(1)} %get-tuple-element.68.stack_ref, bf16[128,1280]{1,0:T(8,128)(2,1)S(1)} %get-tuple-element.77.own_hot_ref.own_elem_ref, bf16[128,1024]{1,0:T(8,128)(2,1)S(1)} %get-tuple-element.78.partner_hot_ref.partner_elem_ref, ...), custom_call_target="tpu_custom_call" | custom-call | flops 16777216 | bytes 1048576 | tf_op jit(solution)/shard_map/sides/pallas_call | solution.py:775
  9.6 0.8 %collective-permute-done.2.two_ref = f32[40,128]{1,0:T(8,128)S(1)} collective-permute-done((f32[40,128]{1,0:T(8,128)S(1)}, f32[40,128]{1,0:T(8,128)S(1)}, u32[]{:S(2)}, u32[]{:S(2)}) %collective-permute-start.2) | collective-permute-done | bytes 20512 | tf_op jit(solution)/shard_map/ppermute | solution.py:798
  10.4 0.0 collective-permute-done.1.one_ref
  10.4 0.1 relay.4
  10.4 0.0 collective-permute-start.3
  10.5 0.6 %flux.5 = (f32[32,768]{1,0:T(8,128)S(1)}, f32[64,128]{1,0:T(8,128)S(1)}, f32[8,256]{1,0:T(8,128)S(1)}) custom-call(f32[40,256]{1,0:T(8,128)S(1)} %collective-permute-done.1.one_ref, f32[40,128]{1,0:T(8,128)S(1)} %collective-permute-done.2.two_ref, f32[32,1280]{1,0:T(8,128)S(1)} %get-tuple-element.84.mine_ref, f32[32,1024]{1,0:T(8,128)S(1)} %get-tuple-element.85.other_ref, ...), custom_call_target="tpu_custom_call" | custom-call | flops 16777216 | bytes 1048576 | tf_op jit(solution)/shard_map/flux/pallas_call | solution.py:775
  11.2 0.5 %collective-permute-done.3.one_ref = f32[40,384]{1,0:T(8,128)S(1)} collective-permute-done((f32[40,384]{1,0:T(8,128)S(1)}, f32[40,384]{1,0:T(8,128)S(1)}, u32[]{:S(2)}, u32[]{:S(2)}) %collective-permute-start.3) | collective-permute-done | bytes 61472 | tf_op jit(solution)/shard_map/ppermute | solution.py:798
  11.7 0.9 %update.5 = (f32[128,128]{1,0:T(8,128)S(1)}, bf16[128,768]{1,0:T(8,128)(2,1)S(1)}, f32[64,256]{1,0:T(8,128)S(1)}, f32[8,384]{1,0:T(8,128)S(1)}) custom-call(f32[40,384]{1,0:T(8,128)S(1)} %collective-permute-done.3.one_ref, f32[32,768]{1,0:T(8,128)S(1)} %get-tuple-element.86.local_ref, f32[64,128]{1,0:T(8,128)S(1)} %get-tuple-element.87.volume_ref, ...), custom_call_target="tpu_custom_call" | custom-call | flops 16777216 | bytes 1048576 | tf_op jit(solution)/shard_map/update/pallas_call | solution.py:775
  12.6 0.2 collective-permute-start.4
  12.8 0.4 whole.1
  13.2 0.4 own.5.own_ref
  13.6 0.3 collective-permute-done.4.sent_ref
  13.9 0.1 carry.5
  14.0 0.6 %collective-permute-start.5 = (f32[64,256]{1,0:T(8,128)S(1)}, f32[64,256]{1,0:T(8,128)S(1)}, u32[]{:S(2)}, u32[]{:S(2)}) collective-permute-start(f32[64,256]{1,0:T(8,128)S(1)} %get-tuple-element.94), channel_id=1, source_target_pairs={{0,2},{1,0},{2,1},{3,5},{4,6},{5,3},{6,4},{7,9},{8,10},{9,7},{10,8... | collective-permute-start | bytes 196616 | tf_op jit(solution)/shard_map/ppermute | solution.py:798
  14.6 1.9 %collective-permute-start.6 = (f32[64,128]{1,0:T(8,128)S(1)}, f32[64,128]{1,0:T(8,128)S(1)}, u32[]{:S(2)}, u32[]{:S(2)}) collective-permute-start(f32[64,128]{1,0:T(8,128)S(1)} %get-tuple-element.95), channel_id=1, source_target_pairs={{0,4},{1,3},{2,6},{3,1},{4,0},{5,9},{6,2},{7,11},{8,12},{9,5},{10,... | collective-permute-start | bytes 98312 | tf_op jit(solution)/shard_map/ppermute | solution.py:798
  16.5 0.7 %turn.1 = (bf16[1280,768]{1,0:T(8,128)(2,1)S(1)}, bf16[384,768]{1,0:T(8,128)(2,1)S(1)}) custom-call(f32[16,1664]{1,0:T(8,128)S(1)} %get-tuple-element.80.place_ref), custom_call_target="tpu_custom_call" | custom-call | flops 16777216 | bytes 1048576 | tf_op jit(solution)/shard_map/turn/pallas_call | solution.py:775
  17.2 1.2 %sides.5 = (f32[64,1280]{1,0:T(8,128)S(1)}, f32[64,1024]{1,0:T(8,128)S(1)}, f32[64,384]{1,0:T(8,128)S(1)}) custom-call(bf16[128,768]{1,0:T(8,128)(2,1)S(1)} %get-tuple-element.92.stack_ref, bf16[768,1280]{1,0:T(8,128)(2,1)S(1)} %get-tuple-element.93.rest_0_.own_hot_ref, bf16[768,1024]{1,0:T(8,128)(2,1)S(1)} %get-tuple-element.96.partner_hot_ref, ...), custom_call_target="tpu_custom_call" | custom-call | flops 16777216 | bytes 1048576 | tf_op jit(solution)/shard_map/sides/pallas_call | solution.py:775
  18.4 0.1 collective-permute-done.6.two_ref
  18.5 0.1 relay.5
  18.6 0.5 %collective-permute-start.7 = (f32[64,384]{1,0:T(8,128)S(1)}, f32[64,384]{1,0:T(8,128)S(1)}, u32[]{:S(2)}, u32[]{:S(2)}) collective-permute-start(f32[64,384]{1,0:T(8,128)S(1)} %relay.5), channel_id=1, source_target_pairs={{0,1},{1,0},{2,3},{3,2},{4,5},{5,4},{6,7},{7,6},{8,9},{9,8},{10,11... | collective-permute-start | bytes 294920 | tf_op jit(solution)/shard_map/ppermute | solution.py:798
  19.1 0.9 %flux.6 = (f32[64,768]{1,0:T(8,128)S(1)}, f32[128,128]{1,0:T(8,128)S(1)}) custom-call(f32[64,256]{1,0:T(8,128)S(1)} %collective-permute-done.5.one_ref, f32[64,128]{1,0:T(8,128)S(1)} %collective-permute-done.6.two_ref, f32[64,1280]{1,0:T(8,128)S(1)} %get-tuple-element.100.mine_ref, f32[64,1024]{1,0:T(8,128)S(1)} %get-tuple-element.101.other_ref, ...), custom_call_target="tpu_custom_call" | custom-call | flops 16777216 | bytes 1048576 | tf_op jit(solution)/shard_map/flux/pallas_call | solution.py:775
  20.0 0.0 collective-permute-done.7.one_ref
  20.1 1.2 %update.6 = (f32[128,128]{1,0:T(8,128)S(1)}, bf16[128,768]{1,0:T(8,128)(2,1)S(1)}, f32[64,256]{1,0:T(8,128)S(1)}) custom-call(f32[64,384]{1,0:T(8,128)S(1)} %collective-permute-done.7.one_ref, f32[64,768]{1,0:T(8,128)S(1)} %get-tuple-element.104.local_ref, f32[128,128]{1,0:T(8,128)S(1)} %get-tuple-element.105.volume_ref, ...), custom_call_target="tpu_custom_call" | custom-call | flops 16777216 | bytes 1048576 | tf_op jit(solution)/shard_map/update/pallas_call | solution.py:775
  21.3 0.4 collective-permute-start.8
  21.7 0.4 own.6.own_ref
  22.1 0.5 collective-permute-done.8.sent_ref
  22.6 0.1 carry.6
  22.7 1.8 %collective-permute-start.9 = (f32[64,256]{1,0:T(8,128)S(1)}, f32[64,256]{1,0:T(8,128)S(1)}, u32[]{:S(2)}, u32[]{:S(2)}) collective-permute-start(f32[64,256]{1,0:T(8,128)S(1)} %get-tuple-element.110), channel_id=1, source_target_pairs={{0,2},{1,0},{2,1},{3,5},{4,6},{5,3},{6,4},{7,9},{8,10},{9,7},{10,8... | collective-permute-start | bytes 196616 | tf_op jit(solution)/shard_map/ppermute | solution.py:798
  24.5 2.5 %collective-permute-start.10 = (f32[64,128]{1,0:T(8,128)S(1)}, f32[64,128]{1,0:T(8,128)S(1)}, u32[]{:S(2)}, u32[]{:S(2)}) collective-permute-start(f32[64,128]{1,0:T(8,128)S(1)} %get-tuple-element.111), channel_id=1, source_target_pairs={{0,4},{1,3},{2,6},{3,1},{4,0},{5,9},{6,2},{7,11},{8,12},{9,5},{10,... | collective-permute-start | bytes 98312 | tf_op jit(solution)/shard_map/ppermute | solution.py:798
  27.0 1.2 %sides.6 = (f32[64,1280]{1,0:T(8,128)S(1)}, f32[64,1024]{1,0:T(8,128)S(1)}, f32[64,384]{1,0:T(8,128)S(1)}) custom-call(bf16[128,768]{1,0:T(8,128)(2,1)S(1)} %get-tuple-element.109.stack_ref, bf16[768,1280]{1,0:T(8,128)(2,1)S(1)} %get-tuple-element.93.rest_0_.own_hot_ref, bf16[768,1024]{1,0:T(8,128)(2,1)S(1)} %get-tuple-element.96.partner_hot_ref, ...), custom_call_target="tpu_custom_call" | custom-call | flops 16777216 | bytes 1048576 | tf_op jit(solution)/shard_map/sides/pallas_call | solution.py:775
  28.2 0.7 %collective-permute-done.10.two_ref = f32[64,128]{1,0:T(8,128)S(1)} collective-permute-done((f32[64,128]{1,0:T(8,128)S(1)}, f32[64,128]{1,0:T(8,128)S(1)}, u32[]{:S(2)}, u32[]{:S(2)}) %collective-permute-start.10) | collective-permute-done | bytes 32800 | tf_op jit(solution)/shard_map/ppermute | solution.py:798
  28.9 0.1 relay.6
  29.0 0.1 collective-permute-start.11
  29.1 0.6 %flux.7 = (f32[32,768]{1,0:T(8,128)S(1)}, f32[64,128]{1,0:T(8,128)S(1)}) custom-call(f32[64,256]{1,0:T(8,128)S(1)} %collective-permute-done.9.one_ref, f32[64,128]{1,0:T(8,128)S(1)} %collective-permute-done.10.two_ref, f32[64,1280]{1,0:T(8,128)S(1)} %get-tuple-element.113.mine_ref, f32[64,1024]{1,0:T(8,128)S(1)} %get-tuple-element.114.other_ref, ...), custom_call_target="tpu_custom_call" | custom-call | flops 16777216 | bytes 1048576 | tf_op jit(solution)/shard_map/flux/pallas_call | solution.py:775
  29.7 0.6 %collective-permute-done.11.one_ref = f32[64,384]{1,0:T(8,128)S(1)} collective-permute-done((f32[64,384]{1,0:T(8,128)S(1)}, f32[64,384]{1,0:T(8,128)S(1)}, u32[]{:S(2)}, u32[]{:S(2)}) %collective-permute-start.11) | collective-permute-done | bytes 98336 | tf_op jit(solution)/shard_map/ppermute | solution.py:798
  30.4 0.8 %update.7 = (f32[64,128]{1,0:T(8,128)S(1)}, bf16[64,768]{1,0:T(8,128)(2,1)S(1)}, f32[32,256]{1,0:T(8,128)S(1)}) custom-call(f32[64,384]{1,0:T(8,128)S(1)} %collective-permute-done.11.one_ref, f32[32,768]{1,0:T(8,128)S(1)} %get-tuple-element.116.local_ref, f32[64,128]{1,0:T(8,128)S(1)} %get-tuple-element.117.volume_ref, ...), custom_call_target="tpu_custom_call" | custom-call | flops 16777216 | bytes 1048576 | tf_op jit(solution)/shard_map/update/pallas_call | solution.py:775
  31.2 0.2 collective-permute-start.12
  31.4 0.6 %flux.8 = (f32[32,768]{1,0:T(8,128)S(1)}, f32[64,128]{1,0:T(8,128)S(1)}) custom-call(f32[64,256]{1,0:T(8,128)S(1)} %collective-permute-done.9.one_ref, f32[64,128]{1,0:T(8,128)S(1)} %collective-permute-done.10.two_ref, f32[64,1280]{1,0:T(8,128)S(1)} %get-tuple-element.113.mine_ref, f32[64,1024]{1,0:T(8,128)S(1)} %get-tuple-element.114.other_ref, ...), custom_call_target="tpu_custom_call" | custom-call | flops 16777216 | bytes 1048576 | tf_op jit(solution)/shard_map/flux/pallas_call | solution.py:775
  32.1 0.3 own.7.own_ref
  32.4 0.1 collective-permute-done.12.sent_ref
  32.5 0.1 carry.7
  32.5 0.5 collective-permute-start.13
  33.1 2.8 %collective-permute-start.14 = (f32[32,128]{1,0:T(8,128)S(1)}, f32[32,128]{1,0:T(8,128)S(1)}, u32[]{:S(2)}, u32[]{:S(2)}) collective-permute-start(f32[32,128]{1,0:T(8,128)S(1)} %get-tuple-element.122), channel_id=1, source_target_pairs={{0,4},{1,3},{2,6},{3,1},{4,0},{5,9},{6,2},{7,11},{8,12},{9,5},{10,... | collective-permute-start | bytes 49160 | tf_op jit(solution)/shard_map/ppermute | solution.py:798
  35.9 1.0 %sides.7 = (f32[32,1280]{1,0:T(8,128)S(1)}, f32[32,1024]{1,0:T(8,128)S(1)}, f32[32,384]{1,0:T(8,128)S(1)}) custom-call(bf16[64,768]{1,0:T(8,128)(2,1)S(1)} %get-tuple-element.119.stack_ref, bf16[768,1280]{1,0:T(8,128)(2,1)S(1)} %get-tuple-element.93.rest_0_.own_hot_ref, bf16[768,1024]{1,0:T(8,128)(2,1)S(1)} %get-tuple-element.96.partner_hot_ref, ...), custom_call_target="tpu_custom_call" | custom-call | flops 16777216 | bytes 1048576 | tf_op jit(solution)/shard_map/sides/pallas_call | solution.py:775
  36.9 0.5 %update.8.rest_1_.second_ref = f32[64,128]{1,0:T(8,128)S(1)} custom-call(f32[64,384]{1,0:T(8,128)S(1)} %collective-permute-done.11.one_ref, f32[32,768]{1,0:T(8,128)S(1)} %get-tuple-element.120.rest_0_.local_ref, f32[64,128]{1,0:T(8,128)S(1)} %get-tuple-element.124.volume_ref, f32[64,384]{1,0:T(8,128)S(1)} %get-tuple-element.112.rest_0_.target_ref, ...), custom_call_target="tpu_custom_call" | custom-call | flops 16777216 | bytes 1048576 | tf_op jit(solution)/shard_map/update/pallas_call | solution.py:775
  37.4 0.2 collective-permute-done.14.two_ref
  37.6 0.1 relay.7
  37.7 0.1 collective-permute-start.15
  37.8 0.6 %flux.9 = (f32[32,768]{1,0:T(8,128)S(1)}, f32[64,128]{1,0:T(8,128)S(1)}) custom-call(f32[32,256]{1,0:T(8,128)S(1)} %collective-permute-done.13.one_ref, f32[32,128]{1,0:T(8,128)S(1)} %collective-permute-done.14.two_ref, f32[32,1280]{1,0:T(8,128)S(1)} %get-tuple-element.125.mine_ref, f32[32,1024]{1,0:T(8,128)S(1)} %get-tuple-element.126.other_ref, ...), custom_call_target="tpu_custom_call" | custom-call | flops 16777216 | bytes 1048576 | tf_op jit(solution)/shard_map/flux/pallas_call | solution.py:775
  38.4 0.5 collective-permute-done.15.one_ref
  38.9 0.6 %update.9 = f32[32,128]{1,0:T(8,128)S(1)} custom-call(f32[32,384]{1,0:T(8,128)S(1)} %collective-permute-done.15.one_ref, f32[32,768]{1,0:T(8,128)S(1)} %get-tuple-element.128.local_ref, f32[64,128]{1,0:T(8,128)S(1)} %get-tuple-element.129.volume_ref, f32[32,384]{1,0:T(8,128)S(1)} %get-tuple-element.123.rest_0_.target_ref, ...), custom_call_target="tpu_custom_call" | custom-call | flops 16777216 | bytes 1048576 | tf_op jit(solution)/shard_map/update/pallas_call | solution.py:775
  39.5 12.0 %all_to_all.5 = f32[32,1,128]{2,1,0:T(1,128)S(1)} all-to-all(f32[32,1,128]{2,1,0:T(1,128)S(1)} %bitcast.13), channel_id=1, replica_groups=mesh['dom'=32] {'dom'}, dimensions={0} | all-to-all | bytes 32768 | tf_op jit(solution)/shard_map/all_to_all | solution.py:937
  51.5 0.7 %finish.1 = (f32[64,128]{1,0:T(8,128)}, f32[1,128]{1,0:T(1,128)}) custom-call(f32[32,128]{1,0:T(8,128)S(1)} %bitcast.14, f32[64,128]{1,0:T(8,128)S(1)} %get-tuple-element.88.rest_0_.guess_ref, f32[128,128]{1,0:T(8,128)S(1)} %get-tuple-element.115.field_ref.first_ref, f32[64,128]{1,0:T(8,128)S(1)} %update.8.rest_1_.second_ref), custom_call_target="tpu_custom_call" | custom-call | flops 16777216 | bytes 1048576 | tf_op jit(solution)/shard_map/finish/pallas_call | solution.py:775
  (11 shorter events, 0.0 us)
Async XLA Ops:
  0.6 9.8 %copy-start.1 = (f32[32,128]{1,0:T(8,128)S(1)}, f32[32,128]{1,0:T(8,128)}, u32[]{:S(2)}) copy-start(f32[32,128]{1,0:T(8,128)} %constant.5.clone.weight_ref) | copy-start | bytes 49156
  0.6 9.8 %copy-start.2 = (bf16[64,192]{1,0:T(8,128)(2,1)S(1)}, bf16[64,192]{1,0:T(8,128)(2,1)}, u32[]{:S(2)}) copy-start(bf16[64,192]{1,0:T(8,128)(2,1)} %constant.4.clone.stiffness_ref) | copy-start | bytes 73732
  0.7 9.8 %copy-start.3 = (f32[64,128]{1,0:T(8,128)S(1)}, f32[64,128]{1,0:T(8,128)}, u32[]{:S(2)}) copy-start(f32[64,128]{1,0:T(8,128)} %field_ref.3) | copy-start | bytes 98308
  0.7 11.0 %copy-start = (bf16[64,64,128]{2,1,0:T(8,128)(2,1)S(1)}, bf16[64,64,128]{2,1,0:T(8,128)(2,1)}, u32[]{:S(2)}) copy-start(bf16[64,64,128]{2,1,0:T(8,128)(2,1)} %inverse_ref.9) | copy-start | bytes 3145732
  2.3 1.4 %collective-permute-start = (f32[40,256]{1,0:T(8,128)S(1)}, f32[40,256]{1,0:T(8,128)S(1)}, u32[]{:S(2)}, u32[]{:S(2)}) collective-permute-start(f32[40,256]{1,0:T(8,128)S(1)} %get-tuple-element.67), channel_id=1, source_target_pairs={{0,1},{1,0},{2,3},{3,2},{4,5},{5,4},{6,7},{7,6},{8,9},{9,8},{10,11... | collective-permute-start | bytes 122888 | tf_op jit(solution)/shard_map/ppermute | solution.py:798
  3.7 6.6 %collective-permute-start.1 = (f32[40,256]{1,0:T(8,128)S(1)}, f32[40,256]{1,0:T(8,128)S(1)}, u32[]{:S(2)}, u32[]{:S(2)}) collective-permute-start(f32[40,256]{1,0:T(8,128)S(1)} %get-tuple-element.73), channel_id=1, source_target_pairs={{0,2},{1,0},{2,1},{3,5},{4,6},{5,3},{6,4},{7,9},{8,10},{9,7},{10,8... | collective-permute-start | bytes 122888 | tf_op jit(solution)/shard_map/ppermute | solution.py:798
  6.6 3.8 %collective-permute-start.2 = (f32[40,128]{1,0:T(8,128)S(1)}, f32[40,128]{1,0:T(8,128)S(1)}, u32[]{:S(2)}, u32[]{:S(2)}) collective-permute-start(f32[40,128]{1,0:T(8,128)S(1)} %get-tuple-element.74), channel_id=1, source_target_pairs={{0,4},{1,3},{2,6},{3,1},{4,0},{5,9},{6,2},{7,11},{8,12},{9,5},{10,... | collective-permute-start | bytes 61448 | tf_op jit(solution)/shard_map/ppermute | solution.py:798
  10.4 1.3 %collective-permute-start.3 = (f32[40,384]{1,0:T(8,128)S(1)}, f32[40,384]{1,0:T(8,128)S(1)}, u32[]{:S(2)}, u32[]{:S(2)}) collective-permute-start(f32[40,384]{1,0:T(8,128)S(1)} %relay.4), channel_id=1, source_target_pairs={{0,1},{1,0},{2,3},{3,2},{4,5},{5,4},{6,7},{7,6},{8,9},{9,8},{10,11... | collective-permute-start | bytes 184328 | tf_op jit(solution)/shard_map/ppermute | solution.py:798
  12.6 1.3 %collective-permute-start.4 = (f32[64,256]{1,0:T(8,128)S(1)}, f32[64,256]{1,0:T(8,128)S(1)}, u32[]{:S(2)}, u32[]{:S(2)}) collective-permute-start(f32[64,256]{1,0:T(8,128)S(1)} %get-tuple-element.91), channel_id=1, source_target_pairs={{0,1},{1,0},{2,3},{3,2},{4,5},{5,4},{6,7},{7,6},{8,9},{9,8},{10,11... | collective-permute-start | bytes 196616 | tf_op jit(solution)/shard_map/ppermute | solution.py:798
  14.0 4.5 %collective-permute-start.5 = (f32[64,256]{1,0:T(8,128)S(1)}, f32[64,256]{1,0:T(8,128)S(1)}, u32[]{:S(2)}, u32[]{:S(2)}) collective-permute-start(f32[64,256]{1,0:T(8,128)S(1)} %get-tuple-element.94), channel_id=1, source_target_pairs={{0,2},{1,0},{2,1},{3,5},{4,6},{5,3},{6,4},{7,9},{8,10},{9,7},{10,8... | collective-permute-start | bytes 196616 | tf_op jit(solution)/shard_map/ppermute | solution.py:798
  14.6 3.9 %collective-permute-start.6 = (f32[64,128]{1,0:T(8,128)S(1)}, f32[64,128]{1,0:T(8,128)S(1)}, u32[]{:S(2)}, u32[]{:S(2)}) collective-permute-start(f32[64,128]{1,0:T(8,128)S(1)} %get-tuple-element.95), channel_id=1, source_target_pairs={{0,4},{1,3},{2,6},{3,1},{4,0},{5,9},{6,2},{7,11},{8,12},{9,5},{10,... | collective-permute-start | bytes 98312 | tf_op jit(solution)/shard_map/ppermute | solution.py:798
  18.6 1.5 %copy-start.4 = (f32[64,128]{1,0:T(8,128)S(1)}, f32[64,128]{1,0:T(8,128)}, u32[]{:S(2)}) copy-start(f32[64,128]{1,0:T(8,128)} %rest_1_.1) | copy-start | bytes 98308
  18.6 1.5 %collective-permute-start.7 = (f32[64,384]{1,0:T(8,128)S(1)}, f32[64,384]{1,0:T(8,128)S(1)}, u32[]{:S(2)}, u32[]{:S(2)}) collective-permute-start(f32[64,384]{1,0:T(8,128)S(1)} %relay.5), channel_id=1, source_target_pairs={{0,1},{1,0},{2,3},{3,2},{4,5},{5,4},{6,7},{7,6},{8,9},{9,8},{10,11... | collective-permute-start | bytes 294920 | tf_op jit(solution)/shard_map/ppermute | solution.py:798
  21.3 1.3 %collective-permute-start.8 = (f32[64,256]{1,0:T(8,128)S(1)}, f32[64,256]{1,0:T(8,128)S(1)}, u32[]{:S(2)}, u32[]{:S(2)}) collective-permute-start(f32[64,256]{1,0:T(8,128)S(1)} %get-tuple-element.108), channel_id=1, source_target_pairs={{0,1},{1,0},{2,3},{3,2},{4,5},{5,4},{6,7},{7,6},{8,9},{9,8},{10,11... | collective-permute-start | bytes 196616 | tf_op jit(solution)/shard_map/ppermute | solution.py:798
  22.7 6.2 %collective-permute-start.9 = (f32[64,256]{1,0:T(8,128)S(1)}, f32[64,256]{1,0:T(8,128)S(1)}, u32[]{:S(2)}, u32[]{:S(2)}) collective-permute-start(f32[64,256]{1,0:T(8,128)S(1)} %get-tuple-element.110), channel_id=1, source_target_pairs={{0,2},{1,0},{2,1},{3,5},{4,6},{5,3},{6,4},{7,9},{8,10},{9,7},{10,8... | collective-permute-start | bytes 196616 | tf_op jit(solution)/shard_map/ppermute | solution.py:798
  24.5 4.4 %collective-permute-start.10 = (f32[64,128]{1,0:T(8,128)S(1)}, f32[64,128]{1,0:T(8,128)S(1)}, u32[]{:S(2)}, u32[]{:S(2)}) collective-permute-start(f32[64,128]{1,0:T(8,128)S(1)} %get-tuple-element.111), channel_id=1, source_target_pairs={{0,4},{1,3},{2,6},{3,1},{4,0},{5,9},{6,2},{7,11},{8,12},{9,5},{10,... | collective-permute-start | bytes 98312 | tf_op jit(solution)/shard_map/ppermute | solution.py:798
  29.0 1.3 %collective-permute-start.11 = (f32[64,384]{1,0:T(8,128)S(1)}, f32[64,384]{1,0:T(8,128)S(1)}, u32[]{:S(2)}, u32[]{:S(2)}) collective-permute-start(f32[64,384]{1,0:T(8,128)S(1)} %relay.6), channel_id=1, source_target_pairs={{0,1},{1,0},{2,3},{3,2},{4,5},{5,4},{6,7},{7,6},{8,9},{9,8},{10,11... | collective-permute-start | bytes 294920 | tf_op jit(solution)/shard_map/ppermute | solution.py:798
  31.2 1.3 %collective-permute-start.12 = (f32[32,256]{1,0:T(8,128)S(1)}, f32[32,256]{1,0:T(8,128)S(1)}, u32[]{:S(2)}, u32[]{:S(2)}) collective-permute-start(f32[32,256]{1,0:T(8,128)S(1)} %get-tuple-element.118), channel_id=1, source_target_pairs={{0,1},{1,0},{2,3},{3,2},{4,5},{5,4},{6,7},{7,6},{8,9},{9,8},{10,11... | collective-permute-start | bytes 98312 | tf_op jit(solution)/shard_map/ppermute | solution.py:798
  32.5 5.0 %collective-permute-start.13 = (f32[32,256]{1,0:T(8,128)S(1)}, f32[32,256]{1,0:T(8,128)S(1)}, u32[]{:S(2)}, u32[]{:S(2)}) collective-permute-start(f32[32,256]{1,0:T(8,128)S(1)} %get-tuple-element.121), channel_id=1, source_target_pairs={{0,2},{1,0},{2,1},{3,5},{4,6},{5,3},{6,4},{7,9},{8,10},{9,7},{10,8... | collective-permute-start | bytes 98312 | tf_op jit(solution)/shard_map/ppermute | solution.py:798
  33.1 4.5 %collective-permute-start.14 = (f32[32,128]{1,0:T(8,128)S(1)}, f32[32,128]{1,0:T(8,128)S(1)}, u32[]{:S(2)}, u32[]{:S(2)}) collective-permute-start(f32[32,128]{1,0:T(8,128)S(1)} %get-tuple-element.122), channel_id=1, source_target_pairs={{0,4},{1,3},{2,6},{3,1},{4,0},{5,9},{6,2},{7,11},{8,12},{9,5},{10,... | collective-permute-start | bytes 49160 | tf_op jit(solution)/shard_map/ppermute | solution.py:798
  37.7 1.2 %collective-permute-start.15 = (f32[32,384]{1,0:T(8,128)S(1)}, f32[32,384]{1,0:T(8,128)S(1)}, u32[]{:S(2)}, u32[]{:S(2)}) collective-permute-start(f32[32,384]{1,0:T(8,128)S(1)} %relay.7), channel_id=1, source_target_pairs={{0,1},{1,0},{2,3},{3,2},{4,5},{5,4},{6,7},{7,6},{8,9},{9,8},{10,11... | collective-permute-start | bytes 147464 | tf_op jit(solution)/shard_map/ppermute | solution.py:798

commit v8 on v7

--- a/solution.py
+++ b/solution.py
@@ -17,6 +17,7 @@
 lanes = 128
 shifts = (0, 24, 48, 96)
 side_pad = 1024
+terms = 2
 
 
 def lagrange_tables():
@@ -62,19 +63,17 @@
 
 
 def stacked(table):
-    table = np.asarray(table, np.float32)
-    high = table.astype(jnp.bfloat16)
-    low = (table - high.astype(np.float32)).astype(jnp.bfloat16)
-    return np.concatenate([high, high, low], axis=1)
+    rest = np.asarray(table, np.float32)
+    parts = []
+    for _ in range(3):
+        parts.append(rest.astype(jnp.bfloat16))
+        rest = rest - parts[-1].astype(np.float32)
+    high, mid, low = parts
+    return np.concatenate([high, high, mid, mid, high, low], axis=1)
 
 
 def const_tables():
     return stacked(stiffness_table()), np.ascontiguousarray(weight_table())
-
-
-def two(x):
-    high = x.astype(bf16)
-    return high, (x - high.astype(f32)).astype(bf16)
 
 
 def three(x):
@@ -84,6 +83,12 @@
     return high, mid, (rest - mid.astype(f32)).astype(bf16)
 
 
+def added(got, first, rows):
+    return sum(got[first + rows * t : first + rows * t + rows] for t in range(1, terms)) + got[
+        first : first + rows
+    ]
+
+
 def dot(a, b):
     return jnp.dot(a, b, preferred_element_type=f32)
 
@@ -97,8 +102,8 @@
 
 
 def table_dot(table, x):
-    high, low = two(x)
-    return dot(table, jnp.concatenate([high, low, high], axis=0))
+    high, mid, low = three(x)
+    return dot(table, jnp.concatenate([high, mid, high, mid, low, high], axis=0))
 
 
 def interpolate(x, case, nf, transposed=False):
@@ -167,30 +172,23 @@
 def gather_columns(stack, hot, face, nf):
     h = 32 * nf
     if hot.shape[0] == 768:
-        got = dot(stack, hot)
-        return got[:h] + got[h:]
+        return added(dot(stack, hot), 0, h)
     parts = [stack[:, lanes * f : lanes * f + lanes] for f in range(6)]
     got = dot(jnp.concatenate(parts, axis=0), hot)
-    out = got[:h] + got[h : 2 * h]
+    out = added(got, 0, h)
     for f in range(1, 6):
-        low = 2 * h * f
-        out = jnp.where(face == f, got[low : low + h] + got[low + h : low + 2 * h], out)
+        out = jnp.where(face == f, added(got, terms * h * f, h), out)
     return out
 
 
 def scatter_columns(x, hot, face, nf):
     h = 32 * nf
-    high, low = two(x)
-    both = jnp.concatenate([high, low], axis=0)
+    stack = jnp.concatenate(three(x)[:terms], axis=0)
     if hot.shape[1] == 768:
-        got = dot(both, hot)
-        return got[:h] + got[h:]
-    parts = [both * jnp.where(face == f, 1.0, 0.0).astype(bf16) for f in range(6)]
+        return added(dot(stack, hot), 0, h)
+    parts = [stack * jnp.where(face == f, 1.0, 0.0).astype(bf16) for f in range(6)]
     got = dot_t(jnp.concatenate(parts, axis=0), hot)
-    return jnp.concatenate(
-        [got[2 * h * f : 2 * h * f + h] + got[2 * h * f + h : 2 * h * f + 2 * h] for f in range(6)],
-        axis=1,
-    )
+    return jnp.concatenate([added(got, terms * h * f, h) for f in range(6)], axis=1)
 
 
 def element_rows(coef_ref, level_ref):
@@ -297,18 +295,18 @@
 def face_stack(u, normal_scale):
     scale = jnp.where(slope_rows((32, lanes)), jnp.broadcast_to(normal_scale, (32, lanes)), 1.0)
     fields = [jnp.concatenate([part * scale for part in face_traces(x)], axis=1) for x in u]
-    high, low = two(cat(fields, 0))
-    return jnp.concatenate([high, low], axis=0)
+    return jnp.concatenate(three(cat(fields, 0))[:terms], axis=0)
 
 
 def gather_message(stack, hot, case, nf):
     got = dot(stack, hot)
     h = 32 * nf
-    out = interpolate(got[:h] + got[h : 2 * h], case, nf)
-    if stack.shape[0] == 2 * h:
+    out = interpolate(added(got, 0, h), case, nf)
+    low = terms * h
+    if stack.shape[0] == low:
         return out
-    coef = got[2 * h : 2 * h + 1] + got[2 * h + 1 : 2 * h + 2] + got[2 * h + 2 : 2 * h + 3]
-    size = got[2 * h + 3 : 2 * h + 4] * jnp.where((case >= 0) & (case < 4), 0.5, 1.0)
+    coef = got[low : low + 1] + got[low + 1 : low + 2] + got[low + 2 : low + 3]
+    size = got[low + 3 : low + 4] * jnp.where((case >= 0) & (case < 4), 0.5, 1.0)
     row = lax.broadcasted_iota(i32, (8, out.shape[1]), 0)
     scalars = jnp.where(row == 0, coef, jnp.where(row == 1, size, 0.0))
     return jnp.concatenate([out, scalars], axis=0)
@@ -388,16 +386,13 @@
         pltpu.make_async_copy(source, target, arrived.at[k])
         for k, (source, target) in enumerate(zip(sources, landed))
     ]
-    for copy in copies:
-        copy.start()
-    elem_ref, dir_ref, sidecase_ref, kind_ref, partner_ref, list_ref = landed[:6]
+    for k in (5, 0, 1, 2, 6, 7, 8, 3, 4, 9):
+        copies[k].start()
+    list_ref = landed[5]
     start_ref, coef_ref, level_ref = landed[6:9]
-    for copy in copies:
-        copy.wait()
     side_ref[...] = jnp.full((8, side_pad), -1, i32)
-    sides = elem_ref.shape[1]
-    for k, ref in enumerate((elem_ref, dir_ref, sidecase_ref, kind_ref, partner_ref)):
-        side_ref[k : k + 1, 0:sides] = ref[...]
+    sides = landed[0].shape[1]
+    copies[5].wait()
     core, near, far, end, near_there, far_there = where_am_i(chips)
     listed = jnp.concatenate([list_ref[...], jnp.full((8, 32), -1, i32)], axis=1)
     for place, shift in enumerate(shifts):
@@ -416,10 +411,15 @@
     )
     slot_ref[0:1, 0:128] = functools.reduce(jnp.maximum, first)
     slot_ref[0:1, 128:256] = part(0, cross, 0, 96, there & ~narrow(cross))
+    for k in range(3):
+        copies[k].wait()
+        side_ref[k : k + 1, 0:sides] = landed[k][...]
     elem, face, slot_case = place_of(look_up(side_attributes(side_ref), slot_ref[0:1, :]))
     case_ref[0:1, :] = slot_case
     fill_one_hot(hot_ref, elem, face)
 
+    for k in (6, 7, 8):
+        copies[k].wait()
     coef, size, volume_scale, normal_scale = element_rows(coef_ref, level_ref)
     stack = face_stack([start_ref[...]], normal_scale)
     scalars = rows_of([x.astype(f32) for x in three(coef)] + [size], 16, lanes).astype(bf16)
@@ -427,6 +427,10 @@
     stack_ref[...] = stack
     sent = gather_message(stack, hot_ref[...], slot_case, 1)
     sent_ref[...] = sent
+    for k in (3, 4):
+        copies[k].wait()
+        side_ref[k : k + 1, 0:sides] = landed[k][...]
+    copies[9].wait()
 
 
 def own_setup_kernel(chips, side_ref, rolled_ref, hot_ref, case_ref, slot_ref):
@@ -455,25 +459,63 @@
     )
 
 
-def carry_kernel(sent_ref, own_ref, *rest):
+def pack(x, nf):
+    lane = lax.broadcasted_iota(i32, (1, lanes), 1)
+    out = []
+    for k in range(nf):
+        last = x[32 * k + 24 : 32 * k + 32]
+        for g in range(3):
+            part = x[32 * k + 8 * g : 32 * k + 8 * g + 8]
+            out.append(jnp.where(lane < 96, part, pltpu.roll(last, 96 - 32 * g, 1)))
+    return jnp.concatenate(out, axis=0)
+
+
+def unpack(x, nf):
+    lane = lax.broadcasted_iota(i32, (1, lanes), 1)
+    out = []
+    for k in range(nf):
+        part = [x[24 * k + 8 * g : 24 * k + 8 * g + 8] for g in range(3)]
+        moved = [pltpu.roll(p, 32 * g + 32, 1) for g, p in enumerate(part)]
+        out += part
+        out.append(jnp.where(lane < 32, moved[0], jnp.where(lane < 64, moved[1], moved[2])))
+    return jnp.concatenate(out, axis=0)
+
+
+def carry_kernel(nf, sent_ref, own_ref, *rest):
     two_ref, one_ref = rest[-2:]
+    h = 32 * nf
     lane = lax.broadcasted_iota(i32, (1, lanes), 1)
     sent = sent_ref[:, 0:128]
     handed = jnp.where((lane >= 48) & (lane < 96), pltpu.roll(sent, 48, 1), 0.0)
-    two_ref[...] = own_ref[:, 0:128] + handed
-    one_ref[:, 0:128] = own_ref[:, 128:256] + jnp.where(lane >= 48, sent, 0.0)
-    one_ref[:, 128:256] = own_ref[:, 256:384] + sent_ref[:, 128:256]
-
-
-def relay_kernel(chips, one_ref, two_ref, own_ref, *rest):
+    two_away = own_ref[:, 0:128] + handed
+    first = own_ref[:, 128:256] + jnp.where(lane >= 48, sent, 0.0)
+    second = own_ref[:, 256:384] + sent_ref[:, 128:256]
+    if nf == 1:
+        two_ref[...] = two_away
+        one_ref[:, 0:128] = first
+        one_ref[:, 128:256] = second
+    else:
+        two_ref[...] = pack(two_away, nf)
+        one_ref[0:h] = first
+        one_ref[h:] = pack(second, nf)
+
+
+def received(nf, one_ref, two_ref):
+    if nf == 1:
+        return two_ref[...], one_ref[:, 0:128], one_ref[:, 128:256]
+    h = 32 * nf
+    return unpack(two_ref[...], nf), one_ref[0:h], unpack(one_ref[h:], nf)
+
+
+def relay_kernel(nf, chips, one_ref, two_ref, own_ref, *rest):
     out_ref = rest[-1]
     core, near, far, end, near_there, far_there = where_am_i(chips)
     lane = lax.broadcasted_iota(i32, (1, lanes), 1)
-    one, two_away = one_ref[:, 0:128], two_ref[...]
+    two_away, one, second = received(nf, one_ref, two_ref)
     out_ref[:, 0:128] = own_ref[:, 384:512]
     passed = jnp.where(lane < 24, pltpu.roll(two_away, 56, 1), two_away)
     out_ref[:, 128:256] = jnp.where((lane < 48) & ~(end & (core == 1)), passed, one)
-    out_ref[:, 256:384] = one_ref[:, 128:256]
+    out_ref[:, 256:384] = second
 
 
 def setup_kernel(
@@ -604,7 +646,7 @@
     nf, stack_ref, own_hot_ref, partner_hot_ref, far_hot_ref, place_ref, info_ref,
     arrival_ref, mine_ref, other_ref, target_ref,
 ):
-    stack = stack_ref[0 : 64 * nf]
+    stack = stack_ref[0 : 32 * terms * nf]
     near = side_pad + 256
     for hot_ref, face, case, out_ref in (
         (own_hot_ref, place_ref[1:2, 0:near], info_ref[4:5], mine_ref),
@@ -633,18 +675,18 @@
 
 
 def flux_kernel(
-    turn, nf, skip, chips, one_ref, two_ref, mine_ref, other_ref, place_ref, info_ref, arrival_ref, weight_ref,
+    turn, nf, skip, both, chips, one_ref, two_ref, mine_ref, other_ref, place_ref, info_ref, arrival_ref, weight_ref,
     own_hot_ref, field_ref, coef_ref, level_ref, stiffness_ref, *rest,
 ):
     h = 32 * nf
     rows = slice(32 * skip, 32 * skip + h)
     core, near, far, end, near_there, far_there = where_am_i(chips)
     lane = lax.broadcasted_iota(i32, (1, lanes), 1)
-    two_away = two_ref[...]
+    two_away, first, second = received(both, one_ref, two_ref)
     kept = jnp.where(lane < 72, two_away, pltpu.roll(two_away, 72, 1))
     inside = (lane >= 48) & (lane < 96) & ~(end & (core == 1))
     got = jnp.concatenate(
-        [jnp.where(inside, kept, one_ref[:, 0:128]), one_ref[:, 128:256]], axis=1
+        [jnp.where(inside, kept, first), second], axis=1
     )
     if turn == 0:
         sum_ref, volume_ref, halo_ref = rest
@@ -814,13 +856,15 @@
         rows = sent.shape[0]
         (own,) = own_work()
         two_out, one_out = run(
-            carry_kernel, [((rows, lanes), f32), ((rows, 256), f32)],
+            functools.partial(carry_kernel, nf),
+            [((rows, lanes), f32), ((rows, 256), f32)] if nf == 1
+            else [((24 * nf, lanes), f32), ((56 * nf, lanes), f32)],
             [permute(sent, swapped), own, *beside[:1]], "carry",
         )
         arrivals = permute(one_out, one_away), permute(two_out, two_away)
         made = work()
         (last,) = run(
-            functools.partial(relay_kernel, chips), [((rows, 384), f32)],
+            functools.partial(relay_kernel, nf, chips), [((rows, 384), f32)],
             [*arrivals, own, made[2], *beside[1:]], "relay",
         )
         return arrivals, permute(last, swapped), made
@@ -829,7 +873,7 @@
     first = [*sides, send_list, start_vector, coef, level, initial_guess]
     hot, case, stack, sides, rolled, sent, coef, level, guess = run(
         functools.partial(send_setup_kernel, chips),
-        [((768, 256), bf16), ((8, 256), i32), ((80, 768), bf16), ((8, side_pad), i32), ((32, lanes), i32),
+        [((768, 256), bf16), ((8, 256), i32), ((32 * terms + 16, 768), bf16), ((8, side_pad), i32), ((32, lanes), i32),
          ((40, 256), f32), *((x.shape, x.dtype) for x in first[7:])],
         first,
         "send_setup",
@@ -897,7 +941,7 @@
         def apply(count, skip, count_next):
             rows = 32 * count
             sums, volume, *near = run(
-                functools.partial(flux_kernel, turn, count, skip, chips),
+                functools.partial(flux_kernel, turn, count, skip, nf, chips),
                 [((rows, 768), f32), ((64 * count, lanes), f32)] + ([] if turn else [((8, 256), f32)]),
                 [*arrivals, mine, others, *places, weight, own_scatter, fields, coef, level, stiffness]
                 + halo[:1],
@@ -910,7 +954,7 @@
             outs = [((devices, lanes) if turn == 3 else (64 * max(count, count_next), lanes), f32)]
             if count_next:
                 ins += [hot, case]
-                outs += [((64 * count_next, 768), bf16), ((32 * count_next, 256), f32)]
+                outs += [((32 * terms * count_next, 768), bf16), ((32 * count_next, 256), f32)]
             outs += [] if turn else [((8, 384), f32)]
             late.append(sums)
             made = run(

time: 52.4 us -> 51.8 us (0.989)
  starting transfers between devices: 16.6 us -> 16 us
    ppermute x16, starting transfers between devices: 16.6 us -> 16 us  [permute(): return lax.ppermute(x, 'dom', sorted(to.items()))]
  transfers between devices with their start and end apart: 16 -> 16, of which waited for: 11 -> 9; matrix products, arithmetic and copies ran while one was open for 0% -> 0% of each run, Pallas kernels for 22% -> 23%
where the time goes in v8:
time: 51.8 us; the launch traced here: 51.7 us
  Pallas kernels  18.4 us (36%)
  starting transfers between devices  16 us (31%)
  blocking collectives  12 us (23%)
  waiting for transfers between devices  4.34 us (8%)
  between operations  0.86 us (2%)
    pallas_call x32, Pallas kernels, run(): pl.pallas_call(body, out_shape=[(pltpu.VMEM if kept else jax.ShapeDtypeSt...  18.4 us
    ppermute x16, starting transfers between devices, permute(): return lax.ppermute(x, 'dom', sorted(to.items()))  16 us
    all_to_all x1, blocking collectives, local(): lax.all_to_all(parts.reshape(devices, 1, lanes), 'dom', 0, 0)  12 us
    ppermute x16, waiting for transfers between devices, permute(): return lax.ppermute(x, 'dom', sorted(to.items()))  4.34 us
  transfers between devices with their start and end apart: 16, of which 9 were waited for; matrix products, arithmetic and copies ran while one was open for 0% of the time, Pallas kernels for 23%

profile of v8, /device:TPU:0, one launch (start us, length us, event | category | flops | bytes accessed | tf_op | source)
XLA Modules:
  0.0 51.7 jit_solution(949987104937723333)
XLA Ops:
  0.6 0.0 copy-start.1
  0.6 0.0 copy-start.2
  0.7 1.4 %send_setup.1 = (bf16[768,256]{1,0:T(8,128)(2,1)S(1)}, s32[8,256]{1,0:T(8,128)S(1)}, bf16[80,768]{1,0:T(8,128)(2,1)S(1)}, s32[8,1024]{1,0:T(8,128)S(1)}, s32[32,...) custom-call(s32[1,930]{1,0:T(1,128)} %bitcast.15, ...), custom_call_target="tpu_custom_call" | custom-call | flops 16777216 | bytes 1048576 | tf_op jit(solution)/shard_map/send_setup/pallas_call | solution.py:817
  2.1 0.5 %collective-permute-start = (f32[40,256]{1,0:T(8,128)S(1)}, f32[40,256]{1,0:T(8,128)S(1)}, u32[]{:S(2)}, u32[]{:S(2)}) collective-permute-start(f32[40,256]{1,0:T(8,128)S(1)} %get-tuple-element.67), channel_id=1, source_target_pairs={{0,1},{1,0},{2,3},{3,2},{4,5},{5,4},{6,7},{7,6},{8,9},{9,8},{10,11... | collective-permute-start | bytes 122888 | tf_op jit(solution)/shard_map/ppermute | solution.py:840
  2.6 0.3 own_setup.1
  3.0 0.3 own.4.own_ref
  3.3 0.2 collective-permute-done.sent_ref
  3.5 0.1 carry.4
  3.6 2.8 %collective-permute-start.1 = (f32[40,256]{1,0:T(8,128)S(1)}, f32[40,256]{1,0:T(8,128)S(1)}, u32[]{:S(2)}, u32[]{:S(2)}) collective-permute-start(f32[40,256]{1,0:T(8,128)S(1)} %get-tuple-element.73), channel_id=1, source_target_pairs={{0,2},{1,0},{2,1},{3,5},{4,6},{5,3},{6,4},{7,9},{8,10},{9,7},{10,8... | collective-permute-start | bytes 122888 | tf_op jit(solution)/shard_map/ppermute | solution.py:840
  6.4 1.5 %collective-permute-start.2 = (f32[40,128]{1,0:T(8,128)S(1)}, f32[40,128]{1,0:T(8,128)S(1)}, u32[]{:S(2)}, u32[]{:S(2)}) collective-permute-start(f32[40,128]{1,0:T(8,128)S(1)} %get-tuple-element.74), channel_id=1, source_target_pairs={{0,4},{1,3},{2,6},{3,1},{4,0},{5,9},{6,2},{7,11},{8,12},{9,5},{10,... | collective-permute-start | bytes 61448 | tf_op jit(solution)/shard_map/ppermute | solution.py:840
  8.0 0.7 %setup.1 = (bf16[128,1280]{1,0:T(8,128)(2,1)S(1)}, bf16[128,1024]{1,0:T(8,128)(2,1)S(1)}, bf16[128,384]{1,0:T(8,128)(2,1)S(1)}, f32[16,1664]{1,0:T(8,128)S(1)}, ...) custom-call(f32[1,128]{1,0:T(1,128)S(1)} %get-tuple-element.75.coef_ref, s32[1,128]{1,0:T(1,128)S(1)} %get-tuple-element.76.level_ref, ...), custom_call_target="tpu_custom_call" | custom-call | flops 16777216 | bytes 1048576 | tf_op jit(solution)/shard_map/setup/pallas_call | solution.py:817
  8.6 0.8 %sides.4 = (f32[32,1280]{1,0:T(8,128)S(1)}, f32[32,1024]{1,0:T(8,128)S(1)}, f32[32,384]{1,0:T(8,128)S(1)}) custom-call(bf16[80,768]{1,0:T(8,128)(2,1)S(1)} %get-tuple-element.68.stack_ref, bf16[128,1280]{1,0:T(8,128)(2,1)S(1)} %get-tuple-element.77.own_hot_ref.own_elem_ref, bf16[128,1024]{1,0:T(8,128)(2,1)S(1)} %get-tuple-element.78.partner_hot_ref.partner_elem_ref, ...), custom_call_target="tpu_custom_call" | custom-call | flops 16777216 | bytes 1048576 | tf_op jit(solution)/shard_map/sides/pallas_call | solution.py:817
  9.5 0.8 %collective-permute-done.2.two_ref = f32[40,128]{1,0:T(8,128)S(1)} collective-permute-done((f32[40,128]{1,0:T(8,128)S(1)}, f32[40,128]{1,0:T(8,128)S(1)}, u32[]{:S(2)}, u32[]{:S(2)}) %collective-permute-start.2) | collective-permute-done | bytes 20512 | tf_op jit(solution)/shard_map/ppermute | solution.py:840
  10.2 0.0 collective-permute-done.1.one_ref
  10.2 0.1 relay.4
  10.3 0.0 collective-permute-start.3
  10.4 0.7 %flux.5 = (f32[32,768]{1,0:T(8,128)S(1)}, f32[64,128]{1,0:T(8,128)S(1)}, f32[8,256]{1,0:T(8,128)S(1)}) custom-call(f32[40,256]{1,0:T(8,128)S(1)} %collective-permute-done.1.one_ref, f32[40,128]{1,0:T(8,128)S(1)} %collective-permute-done.2.two_ref, f32[32,1280]{1,0:T(8,128)S(1)} %get-tuple-element.84.mine_ref, f32[32,1024]{1,0:T(8,128)S(1)} %get-tuple-element.85.other_ref, ...), custom_call_target="tpu_custom_call" | custom-call | flops 16777216 | bytes 1048576 | tf_op jit(solution)/shard_map/flux/pallas_call | solution.py:817
  11.0 0.5 %collective-permute-done.3.one_ref = f32[40,384]{1,0:T(8,128)S(1)} collective-permute-done((f32[40,384]{1,0:T(8,128)S(1)}, f32[40,384]{1,0:T(8,128)S(1)}, u32[]{:S(2)}, u32[]{:S(2)}) %collective-permute-start.3) | collective-permute-done | bytes 61472 | tf_op jit(solution)/shard_map/ppermute | solution.py:840
  11.6 0.9 %update.5 = (f32[128,128]{1,0:T(8,128)S(1)}, bf16[128,768]{1,0:T(8,128)(2,1)S(1)}, f32[64,256]{1,0:T(8,128)S(1)}, f32[8,384]{1,0:T(8,128)S(1)}) custom-call(f32[40,384]{1,0:T(8,128)S(1)} %collective-permute-done.3.one_ref, f32[32,768]{1,0:T(8,128)S(1)} %get-tuple-element.86.local_ref, f32[64,128]{1,0:T(8,128)S(1)} %get-tuple-element.87.volume_ref, ...), custom_call_target="tpu_custom_call" | custom-call | flops 16777216 | bytes 1048576 | tf_op jit(solution)/shard_map/update/pallas_call | solution.py:817
  12.5 0.2 collective-permute-start.4
  12.7 0.4 whole.1
  13.1 0.4 own.5.own_ref
  13.4 0.3 collective-permute-done.4.sent_ref
  13.8 0.1 carry.5
  13.9 0.5 collective-permute-start.5
  14.4 1.9 %collective-permute-start.6 = (f32[48,128]{1,0:T(8,128)S(1)}, f32[48,128]{1,0:T(8,128)S(1)}, u32[]{:S(2)}, u32[]{:S(2)}) collective-permute-start(f32[48,128]{1,0:T(8,128)S(1)} %get-tuple-element.95), channel_id=1, source_target_pairs={{0,4},{1,3},{2,6},{3,1},{4,0},{5,9},{6,2},{7,11},{8,12},{9,5},{10,... | collective-permute-start | bytes 73736 | tf_op jit(solution)/shard_map/ppermute | solution.py:840
  16.3 0.7 %turn.1 = (bf16[1280,768]{1,0:T(8,128)(2,1)S(1)}, bf16[384,768]{1,0:T(8,128)(2,1)S(1)}) custom-call(f32[16,1664]{1,0:T(8,128)S(1)} %get-tuple-element.80.place_ref), custom_call_target="tpu_custom_call" | custom-call | flops 16777216 | bytes 1048576 | tf_op jit(solution)/shard_map/turn/pallas_call | solution.py:817
  17.1 1.2 %sides.5 = (f32[64,1280]{1,0:T(8,128)S(1)}, f32[64,1024]{1,0:T(8,128)S(1)}, f32[64,384]{1,0:T(8,128)S(1)}) custom-call(bf16[128,768]{1,0:T(8,128)(2,1)S(1)} %get-tuple-element.92.stack_ref, bf16[768,1280]{1,0:T(8,128)(2,1)S(1)} %get-tuple-element.93.rest_0_.own_hot_ref, bf16[768,1024]{1,0:T(8,128)(2,1)S(1)} %get-tuple-element.96.partner_hot_ref, ...), custom_call_target="tpu_custom_call" | custom-call | flops 16777216 | bytes 1048576 | tf_op jit(solution)/shard_map/sides/pallas_call | solution.py:817
  18.3 0.0 collective-permute-done.6.two_ref
  18.3 0.1 relay.5
  18.4 0.4 collective-permute-start.7
  18.8 0.9 %flux.6 = (f32[64,768]{1,0:T(8,128)S(1)}, f32[128,128]{1,0:T(8,128)S(1)}) custom-call(f32[112,128]{1,0:T(8,128)S(1)} %collective-permute-done.5.one_ref, f32[48,128]{1,0:T(8,128)S(1)} %collective-permute-done.6.two_ref, f32[64,1280]{1,0:T(8,128)S(1)} %get-tuple-element.100.mine_ref, f32[64,1024]{1,0:T(8,128)S(1)} %get-tuple-element.101.other_ref, ...), custom_call_target="tpu_custom_call" | custom-call | flops 16777216 | bytes 1048576 | tf_op jit(solution)/shard_map/flux/pallas_call | solution.py:817
  19.7 0.0 collective-permute-done.7.one_ref
  19.8 1.2 %update.6 = (f32[128,128]{1,0:T(8,128)S(1)}, bf16[128,768]{1,0:T(8,128)(2,1)S(1)}, f32[64,256]{1,0:T(8,128)S(1)}) custom-call(f32[64,384]{1,0:T(8,128)S(1)} %collective-permute-done.7.one_ref, f32[64,768]{1,0:T(8,128)S(1)} %get-tuple-element.104.local_ref, f32[128,128]{1,0:T(8,128)S(1)} %get-tuple-element.105.volume_ref, ...), custom_call_target="tpu_custom_call" | custom-call | flops 16777216 | bytes 1048576 | tf_op jit(solution)/shard_map/update/pallas_call | solution.py:817
  21.0 0.4 collective-permute-start.8
  21.4 0.4 own.6.own_ref
  21.8 0.5 %collective-permute-done.8.sent_ref = f32[64,256]{1,0:T(8,128)S(1)} collective-permute-done((f32[64,256]{1,0:T(8,128)S(1)}, f32[64,256]{1,0:T(8,128)S(1)}, u32[]{:S(2)}, u32[]{:S(2)}) %collective-permute-start.8) | collective-permute-done | bytes 65568 | tf_op jit(solution)/shard_map/ppermute | solution.py:840
  22.3 0.1 carry.6
  22.4 1.8 %collective-permute-start.9 = (f32[112,128]{1,0:T(8,128)S(1)}, f32[112,128]{1,0:T(8,128)S(1)}, u32[]{:S(2)}, u32[]{:S(2)}) collective-permute-start(f32[112,128]{1,0:T(8,128)S(1)} %get-tuple-element.110), channel_id=1, source_target_pairs={{0,2},{1,0},{2,1},{3,5},{4,6},{5,3},{6,4},{7,9},{8,10},{9,7},{10,8... | collective-permute-start | bytes 172040 | tf_op jit(solution)/shard_map/ppermute | solution.py:840
  24.3 2.2 %collective-permute-start.10 = (f32[48,128]{1,0:T(8,128)S(1)}, f32[48,128]{1,0:T(8,128)S(1)}, u32[]{:S(2)}, u32[]{:S(2)}) collective-permute-start(f32[48,128]{1,0:T(8,128)S(1)} %get-tuple-element.111), channel_id=1, source_target_pairs={{0,4},{1,3},{2,6},{3,1},{4,0},{5,9},{6,2},{7,11},{8,12},{9,5},{10,... | collective-permute-start | bytes 73736 | tf_op jit(solution)/shard_map/ppermute | solution.py:840
  26.4 1.2 %sides.6 = (f32[64,1280]{1,0:T(8,128)S(1)}, f32[64,1024]{1,0:T(8,128)S(1)}, f32[64,384]{1,0:T(8,128)S(1)}) custom-call(bf16[128,768]{1,0:T(8,128)(2,1)S(1)} %get-tuple-element.109.stack_ref, bf16[768,1280]{1,0:T(8,128)(2,1)S(1)} %get-tuple-element.93.rest_0_.own_hot_ref, bf16[768,1024]{1,0:T(8,128)(2,1)S(1)} %get-tuple-element.96.partner_hot_ref, ...), custom_call_target="tpu_custom_call" | custom-call | flops 16777216 | bytes 1048576 | tf_op jit(solution)/shard_map/sides/pallas_call | solution.py:817
  27.6 0.6 %collective-permute-done.10.two_ref = f32[48,128]{1,0:T(8,128)S(1)} collective-permute-done((f32[48,128]{1,0:T(8,128)S(1)}, f32[48,128]{1,0:T(8,128)S(1)}, u32[]{:S(2)}, u32[]{:S(2)}) %collective-permute-start.10) | collective-permute-done | bytes 24608 | tf_op jit(solution)/shard_map/ppermute | solution.py:840
  28.2 0.1 relay.6
  28.4 0.0 collective-permute-start.11
  28.4 0.7 %flux.7 = (f32[32,768]{1,0:T(8,128)S(1)}, f32[64,128]{1,0:T(8,128)S(1)}) custom-call(f32[112,128]{1,0:T(8,128)S(1)} %collective-permute-done.9.one_ref, f32[48,128]{1,0:T(8,128)S(1)} %collective-permute-done.10.two_ref, f32[64,1280]{1,0:T(8,128)S(1)} %get-tuple-element.113.mine_ref, f32[64,1024]{1,0:T(8,128)S(1)} %get-tuple-element.114.other_ref, ...), custom_call_target="tpu_custom_call" | custom-call | flops 16777216 | bytes 1048576 | tf_op jit(solution)/shard_map/flux/pallas_call | solution.py:817
  29.1 0.6 %collective-permute-done.11.one_ref = f32[64,384]{1,0:T(8,128)S(1)} collective-permute-done((f32[64,384]{1,0:T(8,128)S(1)}, f32[64,384]{1,0:T(8,128)S(1)}, u32[]{:S(2)}, u32[]{:S(2)}) %collective-permute-start.11) | collective-permute-done | bytes 98336 | tf_op jit(solution)/shard_map/ppermute | solution.py:840
  29.7 0.8 %update.7 = (f32[64,128]{1,0:T(8,128)S(1)}, bf16[64,768]{1,0:T(8,128)(2,1)S(1)}, f32[32,256]{1,0:T(8,128)S(1)}) custom-call(f32[64,384]{1,0:T(8,128)S(1)} %collective-permute-done.11.one_ref, f32[32,768]{1,0:T(8,128)S(1)} %get-tuple-element.116.local_ref, f32[64,128]{1,0:T(8,128)S(1)} %get-tuple-element.117.volume_ref, ...), custom_call_target="tpu_custom_call" | custom-call | flops 16777216 | bytes 1048576 | tf_op jit(solution)/shard_map/update/pallas_call | solution.py:817
  30.5 0.2 collective-permute-start.12
  30.7 0.7 %flux.8 = (f32[32,768]{1,0:T(8,128)S(1)}, f32[64,128]{1,0:T(8,128)S(1)}) custom-call(f32[112,128]{1,0:T(8,128)S(1)} %collective-permute-done.9.one_ref, f32[48,128]{1,0:T(8,128)S(1)} %collective-permute-done.10.two_ref, f32[64,1280]{1,0:T(8,128)S(1)} %get-tuple-element.113.mine_ref, f32[64,1024]{1,0:T(8,128)S(1)} %get-tuple-element.114.other_ref, ...), custom_call_target="tpu_custom_call" | custom-call | flops 16777216 | bytes 1048576 | tf_op jit(solution)/shard_map/flux/pallas_call | solution.py:817
  31.4 0.3 own.7.own_ref
  31.8 0.0 collective-permute-done.12.sent_ref
  31.8 0.1 carry.7
  31.9 0.8 %collective-permute-start.13 = (f32[32,256]{1,0:T(8,128)S(1)}, f32[32,256]{1,0:T(8,128)S(1)}, u32[]{:S(2)}, u32[]{:S(2)}) collective-permute-start(f32[32,256]{1,0:T(8,128)S(1)} %get-tuple-element.121), channel_id=1, source_target_pairs={{0,2},{1,0},{2,1},{3,5},{4,6},{5,3},{6,4},{7,9},{8,10},{9,7},{10,8... | collective-permute-start | bytes 98312 | tf_op jit(solution)/shard_map/ppermute | solution.py:840
  32.6 2.6 %collective-permute-start.14 = (f32[32,128]{1,0:T(8,128)S(1)}, f32[32,128]{1,0:T(8,128)S(1)}, u32[]{:S(2)}, u32[]{:S(2)}) collective-permute-start(f32[32,128]{1,0:T(8,128)S(1)} %get-tuple-element.122), channel_id=1, source_target_pairs={{0,4},{1,3},{2,6},{3,1},{4,0},{5,9},{6,2},{7,11},{8,12},{9,5},{10,... | collective-permute-start | bytes 49160 | tf_op jit(solution)/shard_map/ppermute | solution.py:840
  35.2 1.0 %sides.7 = (f32[32,1280]{1,0:T(8,128)S(1)}, f32[32,1024]{1,0:T(8,128)S(1)}, f32[32,384]{1,0:T(8,128)S(1)}) custom-call(bf16[64,768]{1,0:T(8,128)(2,1)S(1)} %get-tuple-element.119.stack_ref, bf16[768,1280]{1,0:T(8,128)(2,1)S(1)} %get-tuple-element.93.rest_0_.own_hot_ref, bf16[768,1024]{1,0:T(8,128)(2,1)S(1)} %get-tuple-element.96.partner_hot_ref, ...), custom_call_target="tpu_custom_call" | custom-call | flops 16777216 | bytes 1048576 | tf_op jit(solution)/shard_map/sides/pallas_call | solution.py:817
  36.2 0.5 %update.8.rest_1_.second_ref = f32[64,128]{1,0:T(8,128)S(1)} custom-call(f32[64,384]{1,0:T(8,128)S(1)} %collective-permute-done.11.one_ref, f32[32,768]{1,0:T(8,128)S(1)} %get-tuple-element.120.rest_0_.local_ref, f32[64,128]{1,0:T(8,128)S(1)} %get-tuple-element.124.volume_ref, f32[64,384]{1,0:T(8,128)S(1)} %get-tuple-element.112.rest_0_.target_ref, ...), custom_call_target="tpu_custom_call" | custom-call | flops 16777216 | bytes 1048576 | tf_op jit(solution)/shard_map/update/pallas_call | solution.py:817
  36.8 0.2 collective-permute-done.14.two_ref
  36.9 0.1 relay.7
  37.0 0.1 collective-permute-start.15
  37.1 0.7 %flux.9 = (f32[32,768]{1,0:T(8,128)S(1)}, f32[64,128]{1,0:T(8,128)S(1)}) custom-call(f32[32,256]{1,0:T(8,128)S(1)} %collective-permute-done.13.one_ref, f32[32,128]{1,0:T(8,128)S(1)} %collective-permute-done.14.two_ref, f32[32,1280]{1,0:T(8,128)S(1)} %get-tuple-element.125.mine_ref, f32[32,1024]{1,0:T(8,128)S(1)} %get-tuple-element.126.other_ref, ...), custom_call_target="tpu_custom_call" | custom-call | flops 16777216 | bytes 1048576 | tf_op jit(solution)/shard_map/flux/pallas_call | solution.py:817
  37.8 0.4 collective-permute-done.15.one_ref
  38.3 0.6 %update.9 = f32[32,128]{1,0:T(8,128)S(1)} custom-call(f32[32,384]{1,0:T(8,128)S(1)} %collective-permute-done.15.one_ref, f32[32,768]{1,0:T(8,128)S(1)} %get-tuple-element.128.local_ref, f32[64,128]{1,0:T(8,128)S(1)} %get-tuple-element.129.volume_ref, f32[32,384]{1,0:T(8,128)S(1)} %get-tuple-element.123.rest_0_.target_ref, ...), custom_call_target="tpu_custom_call" | custom-call | flops 16777216 | bytes 1048576 | tf_op jit(solution)/shard_map/update/pallas_call | solution.py:817
  38.9 12.0 %all_to_all.5 = f32[32,1,128]{2,1,0:T(1,128)S(1)} all-to-all(f32[32,1,128]{2,1,0:T(1,128)S(1)} %bitcast.13), channel_id=1, replica_groups=mesh['dom'=32] {'dom'}, dimensions={0} | all-to-all | bytes 32768 | tf_op jit(solution)/shard_map/all_to_all | solution.py:981
  50.9 0.7 %finish.1 = (f32[64,128]{1,0:T(8,128)}, f32[1,128]{1,0:T(1,128)}) custom-call(f32[32,128]{1,0:T(8,128)S(1)} %bitcast.14, f32[64,128]{1,0:T(8,128)S(1)} %get-tuple-element.88.rest_0_.guess_ref, f32[128,128]{1,0:T(8,128)S(1)} %get-tuple-element.115.field_ref.first_ref, f32[64,128]{1,0:T(8,128)S(1)} %update.8.rest_1_.second_ref), custom_call_target="tpu_custom_call" | custom-call | flops 16777216 | bytes 1048576 | tf_op jit(solution)/shard_map/finish/pallas_call | solution.py:817
  (11 shorter events, 0.0 us)
Async XLA Ops:
  0.6 9.7 %copy-start.1 = (f32[32,128]{1,0:T(8,128)S(1)}, f32[32,128]{1,0:T(8,128)}, u32[]{:S(2)}) copy-start(f32[32,128]{1,0:T(8,128)} %constant.5.clone.weight_ref) | copy-start | bytes 49156
  0.6 9.7 %copy-start.2 = (bf16[64,384]{1,0:T(8,128)(2,1)S(1)}, bf16[64,384]{1,0:T(8,128)(2,1)}, u32[]{:S(2)}) copy-start(bf16[64,384]{1,0:T(8,128)(2,1)} %constant.4.clone.stiffness_ref) | copy-start | bytes 147460
  0.7 9.7 %copy-start.3 = (f32[64,128]{1,0:T(8,128)S(1)}, f32[64,128]{1,0:T(8,128)}, u32[]{:S(2)}) copy-start(f32[64,128]{1,0:T(8,128)} %field_ref.3) | copy-start | bytes 98308
  0.7 10.9 %copy-start = (bf16[64,64,128]{2,1,0:T(8,128)(2,1)S(1)}, bf16[64,64,128]{2,1,0:T(8,128)(2,1)}, u32[]{:S(2)}) copy-start(bf16[64,64,128]{2,1,0:T(8,128)(2,1)} %inverse_ref.9) | copy-start | bytes 3145732
  2.1 1.4 %collective-permute-start = (f32[40,256]{1,0:T(8,128)S(1)}, f32[40,256]{1,0:T(8,128)S(1)}, u32[]{:S(2)}, u32[]{:S(2)}) collective-permute-start(f32[40,256]{1,0:T(8,128)S(1)} %get-tuple-element.67), channel_id=1, source_target_pairs={{0,1},{1,0},{2,3},{3,2},{4,5},{5,4},{6,7},{7,6},{8,9},{9,8},{10,11... | collective-permute-start | bytes 122888 | tf_op jit(solution)/shard_map/ppermute | solution.py:840
  3.6 6.6 %collective-permute-start.1 = (f32[40,256]{1,0:T(8,128)S(1)}, f32[40,256]{1,0:T(8,128)S(1)}, u32[]{:S(2)}, u32[]{:S(2)}) collective-permute-start(f32[40,256]{1,0:T(8,128)S(1)} %get-tuple-element.73), channel_id=1, source_target_pairs={{0,2},{1,0},{2,1},{3,5},{4,6},{5,3},{6,4},{7,9},{8,10},{9,7},{10,8... | collective-permute-start | bytes 122888 | tf_op jit(solution)/shard_map/ppermute | solution.py:840
  6.4 3.8 %collective-permute-start.2 = (f32[40,128]{1,0:T(8,128)S(1)}, f32[40,128]{1,0:T(8,128)S(1)}, u32[]{:S(2)}, u32[]{:S(2)}) collective-permute-start(f32[40,128]{1,0:T(8,128)S(1)} %get-tuple-element.74), channel_id=1, source_target_pairs={{0,4},{1,3},{2,6},{3,1},{4,0},{5,9},{6,2},{7,11},{8,12},{9,5},{10,... | collective-permute-start | bytes 61448 | tf_op jit(solution)/shard_map/ppermute | solution.py:840
  10.3 1.3 %collective-permute-start.3 = (f32[40,384]{1,0:T(8,128)S(1)}, f32[40,384]{1,0:T(8,128)S(1)}, u32[]{:S(2)}, u32[]{:S(2)}) collective-permute-start(f32[40,384]{1,0:T(8,128)S(1)} %relay.4), channel_id=1, source_target_pairs={{0,1},{1,0},{2,3},{3,2},{4,5},{5,4},{6,7},{7,6},{8,9},{9,8},{10,11... | collective-permute-start | bytes 184328 | tf_op jit(solution)/shard_map/ppermute | solution.py:840
  12.5 1.3 %collective-permute-start.4 = (f32[64,256]{1,0:T(8,128)S(1)}, f32[64,256]{1,0:T(8,128)S(1)}, u32[]{:S(2)}, u32[]{:S(2)}) collective-permute-start(f32[64,256]{1,0:T(8,128)S(1)} %get-tuple-element.91), channel_id=1, source_target_pairs={{0,1},{1,0},{2,3},{3,2},{4,5},{5,4},{6,7},{7,6},{8,9},{9,8},{10,11... | collective-permute-start | bytes 196616 | tf_op jit(solution)/shard_map/ppermute | solution.py:840
  13.9 4.3 %collective-permute-start.5 = (f32[112,128]{1,0:T(8,128)S(1)}, f32[112,128]{1,0:T(8,128)S(1)}, u32[]{:S(2)}, u32[]{:S(2)}) collective-permute-start(f32[112,128]{1,0:T(8,128)S(1)} %get-tuple-element.94), channel_id=1, source_target_pairs={{0,2},{1,0},{2,1},{3,5},{4,6},{5,3},{6,4},{7,9},{8,10},{9,7},{10,8... | collective-permute-start | bytes 172040 | tf_op jit(solution)/shard_map/ppermute | solution.py:840
  14.4 3.8 %collective-permute-start.6 = (f32[48,128]{1,0:T(8,128)S(1)}, f32[48,128]{1,0:T(8,128)S(1)}, u32[]{:S(2)}, u32[]{:S(2)}) collective-permute-start(f32[48,128]{1,0:T(8,128)S(1)} %get-tuple-element.95), channel_id=1, source_target_pairs={{0,4},{1,3},{2,6},{3,1},{4,0},{5,9},{6,2},{7,11},{8,12},{9,5},{10,... | collective-permute-start | bytes 73736 | tf_op jit(solution)/shard_map/ppermute | solution.py:840
  18.4 1.3 %copy-start.4 = (f32[64,128]{1,0:T(8,128)S(1)}, f32[64,128]{1,0:T(8,128)}, u32[]{:S(2)}) copy-start(f32[64,128]{1,0:T(8,128)} %rest_1_.1) | copy-start | bytes 98308
  18.4 1.3 %collective-permute-start.7 = (f32[64,384]{1,0:T(8,128)S(1)}, f32[64,384]{1,0:T(8,128)S(1)}, u32[]{:S(2)}, u32[]{:S(2)}) collective-permute-start(f32[64,384]{1,0:T(8,128)S(1)} %relay.5), channel_id=1, source_target_pairs={{0,1},{1,0},{2,3},{3,2},{4,5},{5,4},{6,7},{7,6},{8,9},{9,8},{10,11... | collective-permute-start | bytes 294920 | tf_op jit(solution)/shard_map/ppermute | solution.py:840
  21.0 1.3 %collective-permute-start.8 = (f32[64,256]{1,0:T(8,128)S(1)}, f32[64,256]{1,0:T(8,128)S(1)}, u32[]{:S(2)}, u32[]{:S(2)}) collective-permute-start(f32[64,256]{1,0:T(8,128)S(1)} %get-tuple-element.108), channel_id=1, source_target_pairs={{0,1},{1,0},{2,3},{3,2},{4,5},{5,4},{6,7},{7,6},{8,9},{9,8},{10,11... | collective-permute-start | bytes 196616 | tf_op jit(solution)/shard_map/ppermute | solution.py:840
  22.4 5.8 %collective-permute-start.9 = (f32[112,128]{1,0:T(8,128)S(1)}, f32[112,128]{1,0:T(8,128)S(1)}, u32[]{:S(2)}, u32[]{:S(2)}) collective-permute-start(f32[112,128]{1,0:T(8,128)S(1)} %get-tuple-element.110), channel_id=1, source_target_pairs={{0,2},{1,0},{2,1},{3,5},{4,6},{5,3},{6,4},{7,9},{8,10},{9,7},{10,8... | collective-permute-start | bytes 172040 | tf_op jit(solution)/shard_map/ppermute | solution.py:840
  24.3 4.0 %collective-permute-start.10 = (f32[48,128]{1,0:T(8,128)S(1)}, f32[48,128]{1,0:T(8,128)S(1)}, u32[]{:S(2)}, u32[]{:S(2)}) collective-permute-start(f32[48,128]{1,0:T(8,128)S(1)} %get-tuple-element.111), channel_id=1, source_target_pairs={{0,4},{1,3},{2,6},{3,1},{4,0},{5,9},{6,2},{7,11},{8,12},{9,5},{10,... | collective-permute-start | bytes 73736 | tf_op jit(solution)/shard_map/ppermute | solution.py:840
  28.4 1.3 %collective-permute-start.11 = (f32[64,384]{1,0:T(8,128)S(1)}, f32[64,384]{1,0:T(8,128)S(1)}, u32[]{:S(2)}, u32[]{:S(2)}) collective-permute-start(f32[64,384]{1,0:T(8,128)S(1)} %relay.6), channel_id=1, source_target_pairs={{0,1},{1,0},{2,3},{3,2},{4,5},{5,4},{6,7},{7,6},{8,9},{9,8},{10,11... | collective-permute-start | bytes 294920 | tf_op jit(solution)/shard_map/ppermute | solution.py:840
  30.5 1.3 %collective-permute-start.12 = (f32[32,256]{1,0:T(8,128)S(1)}, f32[32,256]{1,0:T(8,128)S(1)}, u32[]{:S(2)}, u32[]{:S(2)}) collective-permute-start(f32[32,256]{1,0:T(8,128)S(1)} %get-tuple-element.118), channel_id=1, source_target_pairs={{0,1},{1,0},{2,3},{3,2},{4,5},{5,4},{6,7},{7,6},{8,9},{9,8},{10,11... | collective-permute-start | bytes 98312 | tf_op jit(solution)/shard_map/ppermute | solution.py:840
  31.9 5.0 %collective-permute-start.13 = (f32[32,256]{1,0:T(8,128)S(1)}, f32[32,256]{1,0:T(8,128)S(1)}, u32[]{:S(2)}, u32[]{:S(2)}) collective-permute-start(f32[32,256]{1,0:T(8,128)S(1)} %get-tuple-element.121), channel_id=1, source_target_pairs={{0,2},{1,0},{2,1},{3,5},{4,6},{5,3},{6,4},{7,9},{8,10},{9,7},{10,8... | collective-permute-start | bytes 98312 | tf_op jit(solution)/shard_map/ppermute | solution.py:840
  32.6 4.3 %collective-permute-start.14 = (f32[32,128]{1,0:T(8,128)S(1)}, f32[32,128]{1,0:T(8,128)S(1)}, u32[]{:S(2)}, u32[]{:S(2)}) collective-permute-start(f32[32,128]{1,0:T(8,128)S(1)} %get-tuple-element.122), channel_id=1, source_target_pairs={{0,4},{1,3},{2,6},{3,1},{4,0},{5,9},{6,2},{7,11},{8,12},{9,5},{10,... | collective-permute-start | bytes 49160 | tf_op jit(solution)/shard_map/ppermute | solution.py:840
  37.0 1.2 %collective-permute-start.15 = (f32[32,384]{1,0:T(8,128)S(1)}, f32[32,384]{1,0:T(8,128)S(1)}, u32[]{:S(2)}, u32[]{:S(2)}) collective-permute-start(f32[32,384]{1,0:T(8,128)S(1)} %relay.7), channel_id=1, source_target_pairs={{0,1},{1,0},{2,3},{3,2},{4,5},{5,4},{6,7},{7,6},{8,9},{9,8},{10,11... | collective-permute-start | bytes 147464 | tf_op jit(solution)/shard_map/ppermute | solution.py:840

commit v9 on v8

--- a/solution.py
+++ b/solution.py
@@ -17,6 +17,7 @@
 lanes = 128
 shifts = (0, 24, 48, 96)
 side_pad = 1024
+near_lanes, far_lanes = 384, 256
 terms = 2
 
 
@@ -411,6 +412,7 @@
     )
     slot_ref[0:1, 0:128] = functools.reduce(jnp.maximum, first)
     slot_ref[0:1, 128:256] = part(0, cross, 0, 96, there & ~narrow(cross))
+    slot_ref[0:1, 256:384] = part(0, 1 - 2 * core, 0, 96, core >= 0)
     for k in range(3):
         copies[k].wait()
         side_ref[k : k + 1, 0:sides] = landed[k][...]
@@ -447,16 +449,13 @@
         part(0, 2 * step, 0, 48, there), part(96, cross, 96, 120, there & narrow(cross))
     )
     slot_ref[0:1, 256:384] = part(0, cross, 0, 96, there & ~narrow(cross))
-    slot_ref[0:1, 384:512] = part(0, flip, 0, 96, core >= 0)
     elem, face, slot_case = place_of(look_up(side_attributes(side_ref), slot_ref[0:1, :]))
     case_ref[0:1, :] = slot_case
     fill_one_hot(hot_ref, elem, face)
 
 
 def own_kernel(nf, stack_ref, hot_ref, case_ref, own_ref):
-    own_ref[...] = gather_message(
-        stack_ref[...], hot_ref[...], case_ref[0:1], nf
-    )
+    own_ref[...] = gather_message(stack_ref[...], hot_ref[...], case_ref[0:1], nf)
 
 
 def pack(x, nf):
@@ -507,15 +506,14 @@
     return unpack(two_ref[...], nf), one_ref[0:h], unpack(one_ref[h:], nf)
 
 
-def relay_kernel(nf, chips, one_ref, two_ref, own_ref, *rest):
+def relay_kernel(nf, chips, one_ref, two_ref, *rest):
     out_ref = rest[-1]
     core, near, far, end, near_there, far_there = where_am_i(chips)
     lane = lax.broadcasted_iota(i32, (1, lanes), 1)
     two_away, one, second = received(nf, one_ref, two_ref)
-    out_ref[:, 0:128] = own_ref[:, 384:512]
     passed = jnp.where(lane < 24, pltpu.roll(two_away, 56, 1), two_away)
-    out_ref[:, 128:256] = jnp.where((lane < 48) & ~(end & (core == 1)), passed, one)
-    out_ref[:, 256:384] = second
+    out_ref[:, 0:128] = jnp.where((lane < 48) & ~(end & (core == 1)), passed, one)
+    out_ref[:, 128:256] = second
 
 
 def setup_kernel(
@@ -572,7 +570,6 @@
             two_parts = ((*span(48, 72, there_two & narrow(cross_two)), cross_two),
                          (*span(72, 96, there_two), straight_two))
         else:
-            segments.append(((0, 96, 2 * core - 1),))
             two_parts = ((*span(0, 24, there_two), straight_two),
                          (*span(24, 48, there_two & narrow(cross_two)), cross_two))
         segments.append((
@@ -580,6 +577,8 @@
             (*span(96, 120, slim), cross), *two_parts,
         ))
         segments.append(((*span(0, 96, wide), cross),))
+        if mine:
+            segments.append(((0, 96, 2 * core - 1),))
     entry = partner - 930
     peer = (entry * 683) >> 16
     entry = entry - 96 * peer
@@ -600,7 +599,7 @@
     target_elem, target_face, target_case = place_of(target)
     elems = jnp.concatenate([elem, target_elem], axis=1)
     faces = jnp.concatenate([direction, target_face], axis=1)
-    near = side_pad + 256
+    near = side_pad + near_lanes
     own_hot_ref[...] = one_hot(elems[:, :near], lanes)
     far_hot_ref[...] = one_hot(elems[:, near:], lanes)
     other_face = jnp.concatenate([other_face, jnp.full((1, 640), -1, i32)], axis=1)
@@ -608,7 +607,7 @@
         [elems.astype(f32), faces.astype(f32), other_face.astype(f32)], 16, elems.shape[1]
     )
     info_ref[:, side_pad:] = rows_of(
-        [jnp.zeros((1, 256), f32)] * 4 + [target_case[:, 0:256].astype(f32)], 8, 256
+        [jnp.zeros((1, near_lanes), f32)] * 4 + [target_case[:, 0:near_lanes].astype(f32)], 8, near_lanes
     )
     arrival_ref[...] = rows_of(
         [target_case.astype(f32), target[4:5] + target[5:6] + target[6:7], target[7:8]],
@@ -617,11 +616,11 @@
 
 
 def whole_kernel(own_elem_ref, partner_elem_ref, far_elem_ref, place_ref, own_ref, partner_ref, far_ref):
-    near = side_pad + 256
+    near = side_pad + near_lanes
     for source, row, low, high, target in (
         (own_elem_ref, 1, 0, near, own_ref),
         (partner_elem_ref, 2, 0, side_pad, partner_ref),
-        (far_elem_ref, 1, near, near + 384, far_ref),
+        (far_elem_ref, 1, near, near + far_lanes, far_ref),
     ):
         hot, face = source[...], place_ref[row : row + 1, low:high]
         for f in range(6):
@@ -647,11 +646,11 @@
     arrival_ref, mine_ref, other_ref, target_ref,
 ):
     stack = stack_ref[0 : 32 * terms * nf]
-    near = side_pad + 256
+    near = side_pad + near_lanes
     for hot_ref, face, case, out_ref in (
         (own_hot_ref, place_ref[1:2, 0:near], info_ref[4:5], mine_ref),
         (partner_hot_ref, place_ref[2:3, 0:side_pad], info_ref[5:6, 0:side_pad], other_ref),
-        (far_hot_ref, place_ref[1:2, near:], arrival_ref[0:1, 256:640], target_ref),
+        (far_hot_ref, place_ref[1:2, near:], arrival_ref[0:1, near_lanes:640], target_ref),
     ):
         got = gather_columns(stack, hot_ref[...], face, nf)
         out_ref[...] = interpolate(got, case.astype(i32), nf)
@@ -675,8 +674,8 @@
 
 
 def flux_kernel(
-    turn, nf, skip, both, chips, one_ref, two_ref, mine_ref, other_ref, place_ref, info_ref, arrival_ref, weight_ref,
-    own_hot_ref, field_ref, coef_ref, level_ref, stiffness_ref, *rest,
+    turn, nf, skip, both, chips, handed_ref, one_ref, two_ref, mine_ref, other_ref, place_ref,
+    info_ref, arrival_ref, weight_ref, own_hot_ref, field_ref, coef_ref, level_ref, stiffness_ref, *rest,
 ):
     h = 32 * nf
     rows = slice(32 * skip, 32 * skip + h)
@@ -686,14 +685,15 @@
     kept = jnp.where(lane < 72, two_away, pltpu.roll(two_away, 72, 1))
     inside = (lane >= 48) & (lane < 96) & ~(end & (core == 1))
     got = jnp.concatenate(
-        [jnp.where(inside, kept, first), second], axis=1
+        [jnp.where(inside, kept, first), second, handed_ref[:, 256:384]], axis=1
     )
     if turn == 0:
         sum_ref, volume_ref, halo_ref = rest
         halo = halo_coefs(
-            arrival_ref[1:2, 0:256], arrival_ref[2:3, 0:256], got[h : h + 1], got[h + 1 : h + 2]
+            arrival_ref[1:2, 0:near_lanes], arrival_ref[2:3, 0:near_lanes],
+            got[h : h + 1], got[h + 1 : h + 2],
         )
-        halo_ref[...] = rows_of(halo, 8, 256)
+        halo_ref[...] = rows_of(halo, 8, near_lanes)
     else:
         halo_ref, sum_ref, volume_ref = rest
         halo = halo_ref[0:1], halo_ref[1:2]
@@ -702,7 +702,7 @@
     ]
     outer = jnp.concatenate([other_ref[rows], got[rows]], axis=1)
     sum_ref[...] = side_flux(
-        nf, mine_ref[rows], outer, coefs, info_ref[4:5], place_ref[1:2, 0 : side_pad + 256], weight_ref,
+        nf, mine_ref[rows], outer, coefs, info_ref[4:5], place_ref[1:2, 0 : side_pad + near_lanes], weight_ref,
         own_hot_ref[...],
     )
     volume_scale = element_rows(coef_ref, level_ref)[2]
@@ -744,15 +744,15 @@
     rows = slice(32 * skip, 32 * skip + h)
     if turn == 0:
         halo = halo_coefs(
-            arrival_ref[1:2, 256:640], arrival_ref[2:3, 256:640],
+            arrival_ref[1:2, near_lanes:640], arrival_ref[2:3, near_lanes:640],
             one_ref[h : h + 1], one_ref[h + 1 : h + 2],
         )
-        rest[0][...] = rows_of(halo, 8, 384)
+        rest[0][...] = rows_of(halo, 8, far_lanes)
     else:
         halo = (halo_ref[0:1], halo_ref[1:2])
     total = local_ref[...] + side_flux(
-        nf, target_ref[rows], one_ref[rows], (halo[0], halo[0], halo[1], halo[1]), arrival_ref[0:1, 256:640],
-        place_ref[1:2, side_pad + 256 :], weight_ref, far_hot_ref[...],
+        nf, target_ref[rows], one_ref[rows], (halo[0], halo[0], halo[1], halo[1]), arrival_ref[0:1, near_lanes:640],
+        place_ref[1:2, side_pad + near_lanes :], weight_ref, far_hot_ref[...],
     )
     coef, size, volume_scale, normal_scale = element_rows(coef_ref, level_ref)
     scale = jnp.where(slope_rows((32, lanes)), jnp.broadcast_to(normal_scale, (32, lanes)), 1.0)
@@ -855,40 +855,41 @@
     def exchange(sent, nf, own_work, work, *beside):
         rows = sent.shape[0]
         (own,) = own_work()
+        handed = permute(sent, swapped)
         two_out, one_out = run(
             functools.partial(carry_kernel, nf),
             [((rows, lanes), f32), ((rows, 256), f32)] if nf == 1
             else [((24 * nf, lanes), f32), ((56 * nf, lanes), f32)],
-            [permute(sent, swapped), own, *beside[:1]], "carry",
+            [handed, own, *beside[:1]], "carry",
         )
         arrivals = permute(one_out, one_away), permute(two_out, two_away)
         made = work()
         (last,) = run(
-            functools.partial(relay_kernel, nf, chips), [((rows, 384), f32)],
-            [*arrivals, own, made[2], *beside[1:]], "relay",
+            functools.partial(relay_kernel, nf, chips), [((rows, 256), f32)],
+            [*arrivals, made[2], *beside[1:]], "relay",
         )
-        return arrivals, permute(last, swapped), made
+        return (handed, *arrivals), permute(last, swapped), made
 
     sides = [x.reshape(1, -1) for x in (side_elem, side_dir, side_case, side_kind, partner)]
     first = [*sides, send_list, start_vector, coef, level, initial_guess]
     hot, case, stack, sides, rolled, sent, coef, level, guess = run(
         functools.partial(send_setup_kernel, chips),
-        [((768, 256), bf16), ((8, 256), i32), ((32 * terms + 16, 768), bf16), ((8, side_pad), i32), ((32, lanes), i32),
-         ((40, 256), f32), *((x.shape, x.dtype) for x in first[7:])],
+        [((768, 384), bf16), ((8, 384), i32), ((32 * terms + 16, 768), bf16), ((8, side_pad), i32), ((32, lanes), i32),
+         ((40, 384), f32), *((x.shape, x.dtype) for x in first[7:])],
         first,
         "send_setup",
         scratch=[
-            pltpu.VMEM((8, 256), i32),
+            pltpu.VMEM((8, 384), i32),
             *(pltpu.VMEM(x.shape, x.dtype) for x in first[:7]), pltpu.SemaphoreType.DMA((len(first),)),
         ],
         placed=False,
     )
     own_slots = run(
         functools.partial(own_setup_kernel, chips),
-        [((768, 512), bf16), ((8, 512), i32)],
+        [((768, 384), bf16), ((8, 384), i32)],
         [sides, rolled],
         "own_setup",
-        scratch=[pltpu.VMEM((8, 512), i32)],
+        scratch=[pltpu.VMEM((8, 384), i32)],
     )
     fields, halo, late = start_vector, [], []
     for turn, (nf, nf_next) in enumerate(((1, 2), (2, 2), (2, 1), (1, 0))):
@@ -896,7 +897,7 @@
         def own_work():
             return run(
                 functools.partial(own_kernel, nf),
-                [((sent.shape[0], 512), f32)],
+                [((sent.shape[0], 384), f32)],
                 [stack, *own_slots],
                 "own",
             )
@@ -904,7 +905,7 @@
         def side_work(hots):
             return run(
                 functools.partial(sides_kernel, nf),
-                [((h, side_pad + 256), f32), ((h, side_pad), f32), ((h, 384), f32)],
+                [((h, side_pad + near_lanes), f32), ((h, side_pad), f32), ((h, far_lanes), f32)],
                 [stack, *hots, *places],
                 "sides",
             )
@@ -912,8 +913,8 @@
         if turn == 0:
             *hots, place, info, arrival = run(
                 functools.partial(setup_kernel, chips),
-                [((lanes, side_pad + 256), bf16), ((lanes, side_pad), bf16), ((lanes, 384), bf16),
-                 ((16, side_pad + 640), f32), ((8, side_pad + 256), f32), ((8, 640), f32)],
+                [((lanes, side_pad + near_lanes), bf16), ((lanes, side_pad), bf16), ((lanes, far_lanes), bf16),
+                 ((16, side_pad + 640), f32), ((8, side_pad + near_lanes), f32), ((8, 640), f32)],
                 [coef, level, sides],
                 "setup",
             )
@@ -922,13 +923,13 @@
         elif turn == 1:
             hots = run(
                 whole_kernel,
-                [((768, side_pad + 256), bf16), ((768, side_pad), bf16), ((768, 384), bf16)],
+                [((768, side_pad + near_lanes), bf16), ((768, side_pad), bf16), ((768, far_lanes), bf16)],
                 [*hots, place],
                 "whole",
             )
             own_scatter, far_scatter = run(
                 turn_kernel,
-                [((side_pad + 256, 768), bf16), ((384, 768), bf16)],
+                [((side_pad + near_lanes, 768), bf16), ((far_lanes, 768), bf16)],
                 [place],
                 "turn",
             )
@@ -942,7 +943,7 @@
             rows = 32 * count
             sums, volume, *near = run(
                 functools.partial(flux_kernel, turn, count, skip, nf, chips),
-                [((rows, 768), f32), ((64 * count, lanes), f32)] + ([] if turn else [((8, 256), f32)]),
+                [((rows, 768), f32), ((64 * count, lanes), f32)] + ([] if turn else [((8, near_lanes), f32)]),
                 [*arrivals, mine, others, *places, weight, own_scatter, fields, coef, level, stiffness]
                 + halo[:1],
                 "flux",
@@ -954,8 +955,8 @@
             outs = [((devices, lanes) if turn == 3 else (64 * max(count, count_next), lanes), f32)]
             if count_next:
                 ins += [hot, case]
-                outs += [((32 * terms * count_next, 768), bf16), ((32 * count_next, 256), f32)]
-            outs += [] if turn else [((8, 384), f32)]
+                outs += [((32 * terms * count_next, 768), bf16), ((32 * count_next, 384), f32)]
+            outs += [] if turn else [((8, far_lanes), f32)]
             late.append(sums)
             made = run(
                 functools.partial(update_kernel, turn, count, skip, count_next),

time: 51.8 us -> 51.9 us (level)
  transfers between devices with their start and end apart: 16 -> 16, of which waited for: 9 -> 10; matrix products, arithmetic and copies ran while one was open for 0% -> 0% of each run, Pallas kernels for 23% -> 23%
where the time goes in v9:
time: 51.9 us; the launch traced here: 51.7 us
  Pallas kernels  18.4 us (35%)
  starting transfers between devices  15.6 us (30%)
  blocking collectives  12.1 us (23%)
  waiting for transfers between devices  4.62 us (9%)
  between operations  0.91 us (2%)
    pallas_call x32, Pallas kernels, run(): pl.pallas_call(body, out_shape=[(pltpu.VMEM if kept else jax.ShapeDtypeSt...  18.4 us
    ppermute x16, starting transfers between devices, permute(): return lax.ppermute(x, 'dom', sorted(to.items()))  15.6 us
    all_to_all x1, blocking collectives, local(): lax.all_to_all(parts.reshape(devices, 1, lanes), 'dom', 0, 0)  12.1 us
    ppermute x16, waiting for transfers between devices, permute(): return lax.ppermute(x, 'dom', sorted(to.items()))  4.62 us
  transfers between devices with their start and end apart: 16, of which 10 were waited for; matrix products, arithmetic and copies ran while one was open for 0% of the time, Pallas kernels for 23%

profile of v9, /device:TPU:0, one launch (start us, length us, event | category | flops | bytes accessed | tf_op | source)
XLA Modules:
  0.0 51.7 jit_solution(15087159396596667283)
XLA Ops:
  0.6 0.0 copy-start.1
  0.6 0.0 copy-start.2
  0.7 1.5 %send_setup.1 = (bf16[768,384]{1,0:T(8,128)(2,1)S(1)}, s32[8,384]{1,0:T(8,128)S(1)}, bf16[80,768]{1,0:T(8,128)(2,1)S(1)}, s32[8,1024]{1,0:T(8,128)S(1)}, s32[32,...) custom-call(s32[1,930]{1,0:T(1,128)} %bitcast.15, ...), custom_call_target="tpu_custom_call" | custom-call | flops 16777216 | bytes 1048576 | tf_op jit(solution)/shard_map/send_setup/pallas_call | solution.py:817
  2.2 0.5 %collective-permute-start = (f32[40,384]{1,0:T(8,128)S(1)}, f32[40,384]{1,0:T(8,128)S(1)}, u32[]{:S(2)}, u32[]{:S(2)}) collective-permute-start(f32[40,384]{1,0:T(8,128)S(1)} %get-tuple-element.67), channel_id=1, source_target_pairs={{0,1},{1,0},{2,3},{3,2},{4,5},{5,4},{6,7},{7,6},{8,9},{9,8},{10,11... | collective-permute-start | bytes 184328 | tf_op jit(solution)/shard_map/ppermute | solution.py:840
  2.7 0.3 own_setup.1
  3.1 0.3 own.4.own_ref
  3.3 0.3 collective-permute-done.sent_ref.handed_ref
  3.6 0.1 carry.4
  3.7 2.8 %collective-permute-start.1 = (f32[40,256]{1,0:T(8,128)S(1)}, f32[40,256]{1,0:T(8,128)S(1)}, u32[]{:S(2)}, u32[]{:S(2)}) collective-permute-start(f32[40,256]{1,0:T(8,128)S(1)} %get-tuple-element.73), channel_id=1, source_target_pairs={{0,2},{1,0},{2,1},{3,5},{4,6},{5,3},{6,4},{7,9},{8,10},{9,7},{10,8... | collective-permute-start | bytes 122888 | tf_op jit(solution)/shard_map/ppermute | solution.py:840
  6.6 1.5 %collective-permute-start.2 = (f32[40,128]{1,0:T(8,128)S(1)}, f32[40,128]{1,0:T(8,128)S(1)}, u32[]{:S(2)}, u32[]{:S(2)}) collective-permute-start(f32[40,128]{1,0:T(8,128)S(1)} %get-tuple-element.74), channel_id=1, source_target_pairs={{0,4},{1,3},{2,6},{3,1},{4,0},{5,9},{6,2},{7,11},{8,12},{9,5},{10,... | collective-permute-start | bytes 61448 | tf_op jit(solution)/shard_map/ppermute | solution.py:840
  8.1 0.7 %setup.1 = (bf16[128,1408]{1,0:T(8,128)(2,1)S(1)}, bf16[128,1024]{1,0:T(8,128)(2,1)S(1)}, bf16[128,256]{1,0:T(8,128)(2,1)S(1)}, f32[16,1664]{1,0:T(8,128)S(1)}, ...) custom-call(f32[1,128]{1,0:T(1,128)S(1)} %get-tuple-element.75.coef_ref, s32[1,128]{1,0:T(1,128)S(1)} %get-tuple-element.76.level_ref, ...), custom_call_target="tpu_custom_call" | custom-call | flops 16777216 | bytes 1048576 | tf_op jit(solution)/shard_map/setup/pallas_call | solution.py:817
  8.8 0.8 %sides.4 = (f32[32,1408]{1,0:T(8,128)S(1)}, f32[32,1024]{1,0:T(8,128)S(1)}, f32[32,256]{1,0:T(8,128)S(1)}) custom-call(bf16[80,768]{1,0:T(8,128)(2,1)S(1)} %get-tuple-element.68.stack_ref, bf16[128,1408]{1,0:T(8,128)(2,1)S(1)} %get-tuple-element.77.own_hot_ref.own_elem_ref, bf16[128,1024]{1,0:T(8,128)(2,1)S(1)} %get-tuple-element.78.partner_hot_ref.partner_elem_ref, ...), custom_call_target="tpu_custom_call" | custom-call | flops 16777216 | bytes 1048576 | tf_op jit(solution)/shard_map/sides/pallas_call | solution.py:817
  9.6 0.8 %collective-permute-done.2.two_ref = f32[40,128]{1,0:T(8,128)S(1)} collective-permute-done((f32[40,128]{1,0:T(8,128)S(1)}, f32[40,128]{1,0:T(8,128)S(1)}, u32[]{:S(2)}, u32[]{:S(2)}) %collective-permute-start.2) | collective-permute-done | bytes 20512 | tf_op jit(solution)/shard_map/ppermute | solution.py:840
  10.3 0.0 collective-permute-done.1.one_ref
  10.3 0.1 relay.4
  10.4 0.0 collective-permute-start.3
  10.5 0.7 %flux.5 = (f32[32,768]{1,0:T(8,128)S(1)}, f32[64,128]{1,0:T(8,128)S(1)}, f32[8,384]{1,0:T(8,128)S(1)}) custom-call(f32[40,384]{1,0:T(8,128)S(1)} %collective-permute-done.sent_ref.handed_ref, f32[40,256]{1,0:T(8,128)S(1)} %collective-permute-done.1.one_ref, f32[40,128]{1,0:T(8,128)S(1)} %collective-permute-done.2.two_ref, ...), custom_call_target="tpu_custom_call" | custom-call | flops 16777216 | bytes 1048576 | tf_op jit(solution)/shard_map/flux/pallas_call | solution.py:817
  11.2 0.4 collective-permute-done.3.one_ref
  11.7 0.9 %update.5 = (f32[128,128]{1,0:T(8,128)S(1)}, bf16[128,768]{1,0:T(8,128)(2,1)S(1)}, f32[64,384]{1,0:T(8,128)S(1)}, f32[8,256]{1,0:T(8,128)S(1)}) custom-call(f32[40,256]{1,0:T(8,128)S(1)} %collective-permute-done.3.one_ref, f32[32,768]{1,0:T(8,128)S(1)} %get-tuple-element.86.local_ref, f32[64,128]{1,0:T(8,128)S(1)} %get-tuple-element.87.volume_ref, ...), custom_call_target="tpu_custom_call" | custom-call | flops 16777216 | bytes 1048576 | tf_op jit(solution)/shard_map/update/pallas_call | solution.py:817
  12.6 0.2 collective-permute-start.4
  12.8 0.4 whole.1
  13.2 0.3 own.5.own_ref
  13.5 0.4 collective-permute-done.4.sent_ref.handed_ref
  14.0 0.1 carry.5
  14.1 0.5 collective-permute-start.5
  14.6 1.9 %collective-permute-start.6 = (f32[48,128]{1,0:T(8,128)S(1)}, f32[48,128]{1,0:T(8,128)S(1)}, u32[]{:S(2)}, u32[]{:S(2)}) collective-permute-start(f32[48,128]{1,0:T(8,128)S(1)} %get-tuple-element.95), channel_id=1, source_target_pairs={{0,4},{1,3},{2,6},{3,1},{4,0},{5,9},{6,2},{7,11},{8,12},{9,5},{10,... | collective-permute-start | bytes 73736 | tf_op jit(solution)/shard_map/ppermute | solution.py:840
  16.5 0.7 %turn.1 = (bf16[1408,768]{1,0:T(8,128)(2,1)S(1)}, bf16[256,768]{1,0:T(8,128)(2,1)S(1)}) custom-call(f32[16,1664]{1,0:T(8,128)S(1)} %get-tuple-element.80.place_ref), custom_call_target="tpu_custom_call" | custom-call | flops 16777216 | bytes 1048576 | tf_op jit(solution)/shard_map/turn/pallas_call | solution.py:817
  17.2 1.2 %sides.5 = (f32[64,1408]{1,0:T(8,128)S(1)}, f32[64,1024]{1,0:T(8,128)S(1)}, f32[64,256]{1,0:T(8,128)S(1)}) custom-call(bf16[128,768]{1,0:T(8,128)(2,1)S(1)} %get-tuple-element.92.stack_ref, bf16[768,1408]{1,0:T(8,128)(2,1)S(1)} %get-tuple-element.93.rest_0_.own_hot_ref, bf16[768,1024]{1,0:T(8,128)(2,1)S(1)} %get-tuple-element.96.partner_hot_ref, ...), custom_call_target="tpu_custom_call" | custom-call | flops 16777216 | bytes 1048576 | tf_op jit(solution)/shard_map/sides/pallas_call | solution.py:817
  18.4 0.0 collective-permute-done.6.two_ref
  18.5 0.1 relay.5
  18.6 0.4 collective-permute-start.7
  19.0 1.0 %flux.6 = (f32[64,768]{1,0:T(8,128)S(1)}, f32[128,128]{1,0:T(8,128)S(1)}) custom-call(f32[64,384]{1,0:T(8,128)S(1)} %collective-permute-done.4.sent_ref.handed_ref, f32[112,128]{1,0:T(8,128)S(1)} %collective-permute-done.5.one_ref, f32[48,128]{1,0:T(8,128)S(1)} %collective-permute-done.6.two_ref, f32[64,1408]{1,0:T(8,128)S(1)} %get-tuple-element.100.mine_ref, ...), custom_call_target="tpu_custom_call" | custom-call | flops 16777216 | bytes 1048576 | tf_op jit(solution)/shard_map/flux/pallas_call | solution.py:817
  20.0 1.1 %update.6 = (f32[128,128]{1,0:T(8,128)S(1)}, bf16[128,768]{1,0:T(8,128)(2,1)S(1)}, f32[64,384]{1,0:T(8,128)S(1)}) custom-call(f32[64,256]{1,0:T(8,128)S(1)} %collective-permute-done.7.one_ref, f32[64,768]{1,0:T(8,128)S(1)} %get-tuple-element.104.local_ref, f32[128,128]{1,0:T(8,128)S(1)} %get-tuple-element.105.volume_ref, ...), custom_call_target="tpu_custom_call" | custom-call | flops 16777216 | bytes 1048576 | tf_op jit(solution)/shard_map/update/pallas_call | solution.py:817
  21.2 0.3 collective-permute-start.8
  21.5 0.3 own.6.own_ref
  21.8 0.7 %collective-permute-done.8.sent_ref.handed_ref = f32[64,384]{1,0:T(8,128)S(1)} collective-permute-done((f32[64,384]{1,0:T(8,128)S(1)}, f32[64,384]{1,0:T(8,128)S(1)}, u32[]{:S(2)}, u32[]{:S(2)}) %collective-permute-start.8) | collective-permute-done | bytes 98336 | tf_op jit(solution)/shard_map/ppermute | solution.py:840
  22.5 0.1 carry.6
  22.7 1.8 %collective-permute-start.9 = (f32[112,128]{1,0:T(8,128)S(1)}, f32[112,128]{1,0:T(8,128)S(1)}, u32[]{:S(2)}, u32[]{:S(2)}) collective-permute-start(f32[112,128]{1,0:T(8,128)S(1)} %get-tuple-element.110), channel_id=1, source_target_pairs={{0,2},{1,0},{2,1},{3,5},{4,6},{5,3},{6,4},{7,9},{8,10},{9,7},{10,8... | collective-permute-start | bytes 172040 | tf_op jit(solution)/shard_map/ppermute | solution.py:840
  24.5 2.0 %collective-permute-start.10 = (f32[48,128]{1,0:T(8,128)S(1)}, f32[48,128]{1,0:T(8,128)S(1)}, u32[]{:S(2)}, u32[]{:S(2)}) collective-permute-start(f32[48,128]{1,0:T(8,128)S(1)} %get-tuple-element.111), channel_id=1, source_target_pairs={{0,4},{1,3},{2,6},{3,1},{4,0},{5,9},{6,2},{7,11},{8,12},{9,5},{10,... | collective-permute-start | bytes 73736 | tf_op jit(solution)/shard_map/ppermute | solution.py:840
  26.5 1.2 %sides.6 = (f32[64,1408]{1,0:T(8,128)S(1)}, f32[64,1024]{1,0:T(8,128)S(1)}, f32[64,256]{1,0:T(8,128)S(1)}) custom-call(bf16[128,768]{1,0:T(8,128)(2,1)S(1)} %get-tuple-element.109.stack_ref, bf16[768,1408]{1,0:T(8,128)(2,1)S(1)} %get-tuple-element.93.rest_0_.own_hot_ref, bf16[768,1024]{1,0:T(8,128)(2,1)S(1)} %get-tuple-element.96.partner_hot_ref, ...), custom_call_target="tpu_custom_call" | custom-call | flops 16777216 | bytes 1048576 | tf_op jit(solution)/shard_map/sides/pallas_call | solution.py:817
  27.7 0.6 %collective-permute-done.10.two_ref = f32[48,128]{1,0:T(8,128)S(1)} collective-permute-done((f32[48,128]{1,0:T(8,128)S(1)}, f32[48,128]{1,0:T(8,128)S(1)}, u32[]{:S(2)}, u32[]{:S(2)}) %collective-permute-start.10) | collective-permute-done | bytes 24608 | tf_op jit(solution)/shard_map/ppermute | solution.py:840
  28.3 0.1 relay.6
  28.5 0.0 collective-permute-start.11
  28.5 0.7 %flux.7 = (f32[32,768]{1,0:T(8,128)S(1)}, f32[64,128]{1,0:T(8,128)S(1)}) custom-call(f32[64,384]{1,0:T(8,128)S(1)} %collective-permute-done.8.sent_ref.handed_ref, f32[112,128]{1,0:T(8,128)S(1)} %collective-permute-done.9.one_ref, f32[48,128]{1,0:T(8,128)S(1)} %collective-permute-done.10.two_ref, f32[64,1408]{1,0:T(8,128)S(1)} %get-tuple-element.113.mine_ref, ...), custom_call_target="tpu_custom_call" | custom-call | flops 16777216 | bytes 1048576 | tf_op jit(solution)/shard_map/flux/pallas_call | solution.py:817
  29.2 0.5 collective-permute-done.11.one_ref
  29.8 0.8 %update.7 = (f32[64,128]{1,0:T(8,128)S(1)}, bf16[64,768]{1,0:T(8,128)(2,1)S(1)}, f32[32,384]{1,0:T(8,128)S(1)}) custom-call(f32[64,256]{1,0:T(8,128)S(1)} %collective-permute-done.11.one_ref, f32[32,768]{1,0:T(8,128)S(1)} %get-tuple-element.116.local_ref, f32[64,128]{1,0:T(8,128)S(1)} %get-tuple-element.117.volume_ref, ...), custom_call_target="tpu_custom_call" | custom-call | flops 16777216 | bytes 1048576 | tf_op jit(solution)/shard_map/update/pallas_call | solution.py:817
  30.5 0.2 collective-permute-start.12
  30.7 0.7 %flux.8 = (f32[32,768]{1,0:T(8,128)S(1)}, f32[64,128]{1,0:T(8,128)S(1)}) custom-call(f32[64,384]{1,0:T(8,128)S(1)} %collective-permute-done.8.sent_ref.handed_ref, f32[112,128]{1,0:T(8,128)S(1)} %collective-permute-done.9.one_ref, f32[48,128]{1,0:T(8,128)S(1)} %collective-permute-done.10.two_ref, f32[64,1408]{1,0:T(8,128)S(1)} %get-tuple-element.113.mine_ref, ...), custom_call_target="tpu_custom_call" | custom-call | flops 16777216 | bytes 1048576 | tf_op jit(solution)/shard_map/flux/pallas_call | solution.py:817
  31.5 0.3 own.7.own_ref
  31.7 0.1 collective-permute-done.12.sent_ref.handed_ref
  31.8 0.1 carry.7
  31.9 0.8 %collective-permute-start.13 = (f32[32,256]{1,0:T(8,128)S(1)}, f32[32,256]{1,0:T(8,128)S(1)}, u32[]{:S(2)}, u32[]{:S(2)}) collective-permute-start(f32[32,256]{1,0:T(8,128)S(1)} %get-tuple-element.121), channel_id=1, source_target_pairs={{0,2},{1,0},{2,1},{3,5},{4,6},{5,3},{6,4},{7,9},{8,10},{9,7},{10,8... | collective-permute-start | bytes 98312 | tf_op jit(solution)/shard_map/ppermute | solution.py:840
  32.7 2.6 %collective-permute-start.14 = (f32[32,128]{1,0:T(8,128)S(1)}, f32[32,128]{1,0:T(8,128)S(1)}, u32[]{:S(2)}, u32[]{:S(2)}) collective-permute-start(f32[32,128]{1,0:T(8,128)S(1)} %get-tuple-element.122), channel_id=1, source_target_pairs={{0,4},{1,3},{2,6},{3,1},{4,0},{5,9},{6,2},{7,11},{8,12},{9,5},{10,... | collective-permute-start | bytes 49160 | tf_op jit(solution)/shard_map/ppermute | solution.py:840
  35.2 0.9 %sides.7 = (f32[32,1408]{1,0:T(8,128)S(1)}, f32[32,1024]{1,0:T(8,128)S(1)}, f32[32,256]{1,0:T(8,128)S(1)}) custom-call(bf16[64,768]{1,0:T(8,128)(2,1)S(1)} %get-tuple-element.119.stack_ref, bf16[768,1408]{1,0:T(8,128)(2,1)S(1)} %get-tuple-element.93.rest_0_.own_hot_ref, bf16[768,1024]{1,0:T(8,128)(2,1)S(1)} %get-tuple-element.96.partner_hot_ref, ...), custom_call_target="tpu_custom_call" | custom-call | flops 16777216 | bytes 1048576 | tf_op jit(solution)/shard_map/sides/pallas_call | solution.py:817
  36.2 0.5 update.8.rest_1_.second_ref
  36.7 0.3 collective-permute-done.14.two_ref
  37.0 0.0 collective-permute-done.13.one_ref
  37.0 0.1 relay.7
  37.0 0.0 collective-permute-start.15
  37.1 0.7 %flux.9 = (f32[32,768]{1,0:T(8,128)S(1)}, f32[64,128]{1,0:T(8,128)S(1)}) custom-call(f32[32,384]{1,0:T(8,128)S(1)} %collective-permute-done.12.sent_ref.handed_ref, f32[32,256]{1,0:T(8,128)S(1)} %collective-permute-done.13.one_ref, f32[32,128]{1,0:T(8,128)S(1)} %collective-permute-done.14.two_ref, f32[32,1408]{1,0:T(8,128)S(1)} %get-tuple-element.125.mine_ref, ...), custom_call_target="tpu_custom_call" | custom-call | flops 16777216 | bytes 1048576 | tf_op jit(solution)/shard_map/flux/pallas_call | solution.py:817
  37.8 0.5 collective-permute-done.15.one_ref
  38.3 0.6 %update.9 = f32[32,128]{1,0:T(8,128)S(1)} custom-call(f32[32,256]{1,0:T(8,128)S(1)} %collective-permute-done.15.one_ref, f32[32,768]{1,0:T(8,128)S(1)} %get-tuple-element.128.local_ref, f32[64,128]{1,0:T(8,128)S(1)} %get-tuple-element.129.volume_ref, f32[32,256]{1,0:T(8,128)S(1)} %get-tuple-element.123.rest_0_.target_ref, ...), custom_call_target="tpu_custom_call" | custom-call | flops 16777216 | bytes 1048576 | tf_op jit(solution)/shard_map/update/pallas_call | solution.py:817
  38.8 12.1 %all_to_all.5 = f32[32,1,128]{2,1,0:T(1,128)S(1)} all-to-all(f32[32,1,128]{2,1,0:T(1,128)S(1)} %bitcast.13), channel_id=1, replica_groups=mesh['dom'=32] {'dom'}, dimensions={0} | all-to-all | bytes 32768 | tf_op jit(solution)/shard_map/all_to_all | solution.py:982
  50.9 0.7 %finish.1 = (f32[64,128]{1,0:T(8,128)}, f32[1,128]{1,0:T(1,128)}) custom-call(f32[32,128]{1,0:T(8,128)S(1)} %bitcast.14, f32[64,128]{1,0:T(8,128)S(1)} %get-tuple-element.88.rest_0_.guess_ref, f32[128,128]{1,0:T(8,128)S(1)} %get-tuple-element.115.field_ref.first_ref, f32[64,128]{1,0:T(8,128)S(1)} %update.8.rest_1_.second_ref), custom_call_target="tpu_custom_call" | custom-call | flops 16777216 | bytes 1048576 | tf_op jit(solution)/shard_map/finish/pallas_call | solution.py:817
  (11 shorter events, 0.0 us)
Async XLA Ops:
  0.6 9.8 %copy-start.1 = (f32[32,128]{1,0:T(8,128)S(1)}, f32[32,128]{1,0:T(8,128)}, u32[]{:S(2)}) copy-start(f32[32,128]{1,0:T(8,128)} %constant.5.clone.weight_ref) | copy-start | bytes 49156
  0.6 9.8 %copy-start.2 = (bf16[64,384]{1,0:T(8,128)(2,1)S(1)}, bf16[64,384]{1,0:T(8,128)(2,1)}, u32[]{:S(2)}) copy-start(bf16[64,384]{1,0:T(8,128)(2,1)} %constant.4.clone.stiffness_ref) | copy-start | bytes 147460
  0.7 9.8 %copy-start.3 = (f32[64,128]{1,0:T(8,128)S(1)}, f32[64,128]{1,0:T(8,128)}, u32[]{:S(2)}) copy-start(f32[64,128]{1,0:T(8,128)} %field_ref.3) | copy-start | bytes 98308
  0.7 11.0 %copy-start = (bf16[64,64,128]{2,1,0:T(8,128)(2,1)S(1)}, bf16[64,64,128]{2,1,0:T(8,128)(2,1)}, u32[]{:S(2)}) copy-start(bf16[64,64,128]{2,1,0:T(8,128)(2,1)} %inverse_ref.9) | copy-start | bytes 3145732
  2.2 1.4 %collective-permute-start = (f32[40,384]{1,0:T(8,128)S(1)}, f32[40,384]{1,0:T(8,128)S(1)}, u32[]{:S(2)}, u32[]{:S(2)}) collective-permute-start(f32[40,384]{1,0:T(8,128)S(1)} %get-tuple-element.67), channel_id=1, source_target_pairs={{0,1},{1,0},{2,3},{3,2},{4,5},{5,4},{6,7},{7,6},{8,9},{9,8},{10,11... | collective-permute-start | bytes 184328 | tf_op jit(solution)/shard_map/ppermute | solution.py:840
  3.7 6.6 %collective-permute-start.1 = (f32[40,256]{1,0:T(8,128)S(1)}, f32[40,256]{1,0:T(8,128)S(1)}, u32[]{:S(2)}, u32[]{:S(2)}) collective-permute-start(f32[40,256]{1,0:T(8,128)S(1)} %get-tuple-element.73), channel_id=1, source_target_pairs={{0,2},{1,0},{2,1},{3,5},{4,6},{5,3},{6,4},{7,9},{8,10},{9,7},{10,8... | collective-permute-start | bytes 122888 | tf_op jit(solution)/shard_map/ppermute | solution.py:840
  6.6 3.8 %collective-permute-start.2 = (f32[40,128]{1,0:T(8,128)S(1)}, f32[40,128]{1,0:T(8,128)S(1)}, u32[]{:S(2)}, u32[]{:S(2)}) collective-permute-start(f32[40,128]{1,0:T(8,128)S(1)} %get-tuple-element.74), channel_id=1, source_target_pairs={{0,4},{1,3},{2,6},{3,1},{4,0},{5,9},{6,2},{7,11},{8,12},{9,5},{10,... | collective-permute-start | bytes 61448 | tf_op jit(solution)/shard_map/ppermute | solution.py:840
  10.4 1.2 %collective-permute-start.3 = (f32[40,256]{1,0:T(8,128)S(1)}, f32[40,256]{1,0:T(8,128)S(1)}, u32[]{:S(2)}, u32[]{:S(2)}) collective-permute-start(f32[40,256]{1,0:T(8,128)S(1)} %relay.4), channel_id=1, source_target_pairs={{0,1},{1,0},{2,3},{3,2},{4,5},{5,4},{6,7},{7,6},{8,9},{9,8},{10,11... | collective-permute-start | bytes 122888 | tf_op jit(solution)/shard_map/ppermute | solution.py:840
  12.6 1.4 %collective-permute-start.4 = (f32[64,384]{1,0:T(8,128)S(1)}, f32[64,384]{1,0:T(8,128)S(1)}, u32[]{:S(2)}, u32[]{:S(2)}) collective-permute-start(f32[64,384]{1,0:T(8,128)S(1)} %get-tuple-element.91), channel_id=1, source_target_pairs={{0,1},{1,0},{2,3},{3,2},{4,5},{5,4},{6,7},{7,6},{8,9},{9,8},{10,11... | collective-permute-start | bytes 294920 | tf_op jit(solution)/shard_map/ppermute | solution.py:840
  14.1 4.3 %collective-permute-start.5 = (f32[112,128]{1,0:T(8,128)S(1)}, f32[112,128]{1,0:T(8,128)S(1)}, u32[]{:S(2)}, u32[]{:S(2)}) collective-permute-start(f32[112,128]{1,0:T(8,128)S(1)} %get-tuple-element.94), channel_id=1, source_target_pairs={{0,2},{1,0},{2,1},{3,5},{4,6},{5,3},{6,4},{7,9},{8,10},{9,7},{10,8... | collective-permute-start | bytes 172040 | tf_op jit(solution)/shard_map/ppermute | solution.py:840
  14.6 3.8 %collective-permute-start.6 = (f32[48,128]{1,0:T(8,128)S(1)}, f32[48,128]{1,0:T(8,128)S(1)}, u32[]{:S(2)}, u32[]{:S(2)}) collective-permute-start(f32[48,128]{1,0:T(8,128)S(1)} %get-tuple-element.95), channel_id=1, source_target_pairs={{0,4},{1,3},{2,6},{3,1},{4,0},{5,9},{6,2},{7,11},{8,12},{9,5},{10,... | collective-permute-start | bytes 73736 | tf_op jit(solution)/shard_map/ppermute | solution.py:840
  18.6 1.4 %copy-start.4 = (f32[64,128]{1,0:T(8,128)S(1)}, f32[64,128]{1,0:T(8,128)}, u32[]{:S(2)}) copy-start(f32[64,128]{1,0:T(8,128)} %rest_1_.1) | copy-start | bytes 98308
  18.6 1.4 %collective-permute-start.7 = (f32[64,256]{1,0:T(8,128)S(1)}, f32[64,256]{1,0:T(8,128)S(1)}, u32[]{:S(2)}, u32[]{:S(2)}) collective-permute-start(f32[64,256]{1,0:T(8,128)S(1)} %relay.5), channel_id=1, source_target_pairs={{0,1},{1,0},{2,3},{3,2},{4,5},{5,4},{6,7},{7,6},{8,9},{9,8},{10,11... | collective-permute-start | bytes 196616 | tf_op jit(solution)/shard_map/ppermute | solution.py:840
  21.2 1.4 %collective-permute-start.8 = (f32[64,384]{1,0:T(8,128)S(1)}, f32[64,384]{1,0:T(8,128)S(1)}, u32[]{:S(2)}, u32[]{:S(2)}) collective-permute-start(f32[64,384]{1,0:T(8,128)S(1)} %get-tuple-element.108), channel_id=1, source_target_pairs={{0,1},{1,0},{2,3},{3,2},{4,5},{5,4},{6,7},{7,6},{8,9},{9,8},{10,11... | collective-permute-start | bytes 294920 | tf_op jit(solution)/shard_map/ppermute | solution.py:840
  22.7 5.6 %collective-permute-start.9 = (f32[112,128]{1,0:T(8,128)S(1)}, f32[112,128]{1,0:T(8,128)S(1)}, u32[]{:S(2)}, u32[]{:S(2)}) collective-permute-start(f32[112,128]{1,0:T(8,128)S(1)} %get-tuple-element.110), channel_id=1, source_target_pairs={{0,2},{1,0},{2,1},{3,5},{4,6},{5,3},{6,4},{7,9},{8,10},{9,7},{10,8... | collective-permute-start | bytes 172040 | tf_op jit(solution)/shard_map/ppermute | solution.py:840
  24.5 3.8 %collective-permute-start.10 = (f32[48,128]{1,0:T(8,128)S(1)}, f32[48,128]{1,0:T(8,128)S(1)}, u32[]{:S(2)}, u32[]{:S(2)}) collective-permute-start(f32[48,128]{1,0:T(8,128)S(1)} %get-tuple-element.111), channel_id=1, source_target_pairs={{0,4},{1,3},{2,6},{3,1},{4,0},{5,9},{6,2},{7,11},{8,12},{9,5},{10,... | collective-permute-start | bytes 73736 | tf_op jit(solution)/shard_map/ppermute | solution.py:840
  28.5 1.3 %collective-permute-start.11 = (f32[64,256]{1,0:T(8,128)S(1)}, f32[64,256]{1,0:T(8,128)S(1)}, u32[]{:S(2)}, u32[]{:S(2)}) collective-permute-start(f32[64,256]{1,0:T(8,128)S(1)} %relay.6), channel_id=1, source_target_pairs={{0,1},{1,0},{2,3},{3,2},{4,5},{5,4},{6,7},{7,6},{8,9},{9,8},{10,11... | collective-permute-start | bytes 196616 | tf_op jit(solution)/shard_map/ppermute | solution.py:840
  30.5 1.3 %collective-permute-start.12 = (f32[32,384]{1,0:T(8,128)S(1)}, f32[32,384]{1,0:T(8,128)S(1)}, u32[]{:S(2)}, u32[]{:S(2)}) collective-permute-start(f32[32,384]{1,0:T(8,128)S(1)} %get-tuple-element.118), channel_id=1, source_target_pairs={{0,1},{1,0},{2,3},{3,2},{4,5},{5,4},{6,7},{7,6},{8,9},{9,8},{10,11... | collective-permute-start | bytes 147464 | tf_op jit(solution)/shard_map/ppermute | solution.py:840
  31.9 5.1 %collective-permute-start.13 = (f32[32,256]{1,0:T(8,128)S(1)}, f32[32,256]{1,0:T(8,128)S(1)}, u32[]{:S(2)}, u32[]{:S(2)}) collective-permute-start(f32[32,256]{1,0:T(8,128)S(1)} %get-tuple-element.121), channel_id=1, source_target_pairs={{0,2},{1,0},{2,1},{3,5},{4,6},{5,3},{6,4},{7,9},{8,10},{9,7},{10,8... | collective-permute-start | bytes 98312 | tf_op jit(solution)/shard_map/ppermute | solution.py:840
  32.7 4.3 %collective-permute-start.14 = (f32[32,128]{1,0:T(8,128)S(1)}, f32[32,128]{1,0:T(8,128)S(1)}, u32[]{:S(2)}, u32[]{:S(2)}) collective-permute-start(f32[32,128]{1,0:T(8,128)S(1)} %get-tuple-element.122), channel_id=1, source_target_pairs={{0,4},{1,3},{2,6},{3,1},{4,0},{5,9},{6,2},{7,11},{8,12},{9,5},{10,... | collective-permute-start | bytes 49160 | tf_op jit(solution)/shard_map/ppermute | solution.py:840
  37.0 1.2 %collective-permute-start.15 = (f32[32,256]{1,0:T(8,128)S(1)}, f32[32,256]{1,0:T(8,128)S(1)}, u32[]{:S(2)}, u32[]{:S(2)}) collective-permute-start(f32[32,256]{1,0:T(8,128)S(1)} %relay.7), channel_id=1, source_target_pairs={{0,1},{1,0},{2,3},{3,2},{4,5},{5,4},{6,7},{7,6},{8,9},{9,8},{10,11... | collective-permute-start | bytes 98312 | tf_op jit(solution)/shard_map/ppermute | solution.py:840

commit v10 on v9

--- a/solution.py
+++ b/solution.py
@@ -713,6 +713,11 @@
         volume_ref[64 * k : 64 * k + 64, :] = volume[:, lanes * k : lanes * k + lanes]
 
 
+def widen_kernel(inverse_ref, wide_ref):
+    for col in range(64):
+        wide_ref[col] = inverse_ref[col].astype(f32)
+
+
 def solve_blocks(inverse_ref, hold_ref, nf):
     sums = [jnp.zeros((64, lanes), f32) for _ in range(nf)]
     for col in range(64):
@@ -892,6 +897,7 @@
         scratch=[pltpu.VMEM((8, 384), i32)],
     )
     fields, halo, late = start_vector, [], []
+    (inverse,) = run(widen_kernel, [(block_inverse.shape, f32)], [block_inverse], "widen")
     for turn, (nf, nf_next) in enumerate(((1, 2), (2, 2), (2, 1), (1, 0))):
         h = 32 * nf
         def own_work():
@@ -950,7 +956,7 @@
             )
             ins = [
                 last, sums, volume, targets, place, arrival, far_scatter, weight, fields, coef, level,
-                block_inverse, *(halo[1:] if turn else [guess]), *([rhs_field] if turn == 1 else []),
+                inverse, *(halo[1:] if turn else [guess]), *([rhs_field] if turn == 1 else []),
             ]
             outs = [((devices, lanes) if turn == 3 else (64 * max(count, count_next), lanes), f32)]
             if count_next:

time: 51.9 us -> 51.5 us (level)
    pallas_call x32 -> x33, Pallas kernels: 18.4 us -> 18.1 us  [run(): pl.pallas_call(body, out_shape=[(pltpu.VMEM if kept else jax.ShapeDtypeSt...]
where the time goes in v10:
time: 51.5 us; the launch traced here: 51.3 us
  Pallas kernels  18.1 us (35%)
  starting transfers between devices  15.6 us (30%)
  blocking collectives  12.1 us (23%)
  waiting for transfers between devices  4.53 us (9%)
  between operations  0.9 us (2%)
    pallas_call x33, Pallas kernels, run(): pl.pallas_call(body, out_shape=[(pltpu.VMEM if kept else jax.ShapeDtypeSt...  18.1 us
    ppermute x16, starting transfers between devices, permute(): return lax.ppermute(x, 'dom', sorted(to.items()))  15.6 us
    all_to_all x1, blocking collectives, local(): lax.all_to_all(parts.reshape(devices, 1, lanes), 'dom', 0, 0)  12.1 us
    ppermute x16, waiting for transfers between devices, permute(): return lax.ppermute(x, 'dom', sorted(to.items()))  4.53 us
  transfers between devices with their start and end apart: 16, of which 10 were waited for; matrix products, arithmetic and copies ran while one was open for 0% of the time, Pallas kernels for 23%

profile of v10, /device:TPU:0, one launch (start us, length us, event | category | flops | bytes accessed | tf_op | source)
XLA Modules:
  0.0 51.3 jit_solution(1112360417060303687)
XLA Ops:
  0.6 1.5 %send_setup.1 = (bf16[768,384]{1,0:T(8,128)(2,1)S(1)}, s32[8,384]{1,0:T(8,128)S(1)}, bf16[80,768]{1,0:T(8,128)(2,1)S(1)}, s32[8,1024]{1,0:T(8,128)S(1)}, s32[32,...) custom-call(s32[1,930]{1,0:T(1,128)} %bitcast.15, ...), custom_call_target="tpu_custom_call" | custom-call | flops 16777216 | bytes 1048576 | tf_op jit(solution)/shard_map/send_setup/pallas_call | solution.py:822
  2.2 0.5 %collective-permute-start = (f32[40,384]{1,0:T(8,128)S(1)}, f32[40,384]{1,0:T(8,128)S(1)}, u32[]{:S(2)}, u32[]{:S(2)}) collective-permute-start(f32[40,384]{1,0:T(8,128)S(1)} %get-tuple-element.67), channel_id=1, source_target_pairs={{0,1},{1,0},{2,3},{3,2},{4,5},{5,4},{6,7},{7,6},{8,9},{9,8},{10,11... | collective-permute-start | bytes 184328 | tf_op jit(solution)/shard_map/ppermute | solution.py:845
  2.7 0.3 own_setup.1
  3.0 0.3 own.4.own_ref
  3.3 0.3 collective-permute-done.sent_ref.handed_ref
  3.6 0.1 carry.4
  3.7 2.8 %collective-permute-start.1 = (f32[40,256]{1,0:T(8,128)S(1)}, f32[40,256]{1,0:T(8,128)S(1)}, u32[]{:S(2)}, u32[]{:S(2)}) collective-permute-start(f32[40,256]{1,0:T(8,128)S(1)} %get-tuple-element.73), channel_id=1, source_target_pairs={{0,2},{1,0},{2,1},{3,5},{4,6},{5,3},{6,4},{7,9},{8,10},{9,7},{10,8... | collective-permute-start | bytes 122888 | tf_op jit(solution)/shard_map/ppermute | solution.py:845
  6.5 1.5 %collective-permute-start.2 = (f32[40,128]{1,0:T(8,128)S(1)}, f32[40,128]{1,0:T(8,128)S(1)}, u32[]{:S(2)}, u32[]{:S(2)}) collective-permute-start(f32[40,128]{1,0:T(8,128)S(1)} %get-tuple-element.74), channel_id=1, source_target_pairs={{0,4},{1,3},{2,6},{3,1},{4,0},{5,9},{6,2},{7,11},{8,12},{9,5},{10,... | collective-permute-start | bytes 61448 | tf_op jit(solution)/shard_map/ppermute | solution.py:845
  8.0 0.7 %setup.1 = (bf16[128,1408]{1,0:T(8,128)(2,1)S(1)}, bf16[128,1024]{1,0:T(8,128)(2,1)S(1)}, bf16[128,256]{1,0:T(8,128)(2,1)S(1)}, f32[16,1664]{1,0:T(8,128)S(1)}, ...) custom-call(f32[1,128]{1,0:T(1,128)S(1)} %get-tuple-element.75.coef_ref, s32[1,128]{1,0:T(1,128)S(1)} %get-tuple-element.76.level_ref, ...), custom_call_target="tpu_custom_call" | custom-call | flops 16777216 | bytes 1048576 | tf_op jit(solution)/shard_map/setup/pallas_call | solution.py:822
  8.7 0.8 %sides.4 = (f32[32,1408]{1,0:T(8,128)S(1)}, f32[32,1024]{1,0:T(8,128)S(1)}, f32[32,256]{1,0:T(8,128)S(1)}) custom-call(bf16[80,768]{1,0:T(8,128)(2,1)S(1)} %get-tuple-element.68.stack_ref, bf16[128,1408]{1,0:T(8,128)(2,1)S(1)} %get-tuple-element.77.own_hot_ref.own_elem_ref, bf16[128,1024]{1,0:T(8,128)(2,1)S(1)} %get-tuple-element.78.partner_hot_ref.partner_elem_ref, ...), custom_call_target="tpu_custom_call" | custom-call | flops 16777216 | bytes 1048576 | tf_op jit(solution)/shard_map/sides/pallas_call | solution.py:822
  9.5 0.8 %collective-permute-done.2.two_ref = f32[40,128]{1,0:T(8,128)S(1)} collective-permute-done((f32[40,128]{1,0:T(8,128)S(1)}, f32[40,128]{1,0:T(8,128)S(1)}, u32[]{:S(2)}, u32[]{:S(2)}) %collective-permute-start.2) | collective-permute-done | bytes 20512 | tf_op jit(solution)/shard_map/ppermute | solution.py:845
  10.3 0.0 collective-permute-done.1.one_ref
  10.3 0.1 relay.4
  10.4 0.0 collective-permute-start.3
  10.4 0.1 widen.1.inverse_ref
  10.6 0.7 %flux.5 = (f32[32,768]{1,0:T(8,128)S(1)}, f32[64,128]{1,0:T(8,128)S(1)}, f32[8,384]{1,0:T(8,128)S(1)}) custom-call(f32[40,384]{1,0:T(8,128)S(1)} %collective-permute-done.sent_ref.handed_ref, f32[40,256]{1,0:T(8,128)S(1)} %collective-permute-done.1.one_ref, f32[40,128]{1,0:T(8,128)S(1)} %collective-permute-done.2.two_ref, ...), custom_call_target="tpu_custom_call" | custom-call | flops 16777216 | bytes 1048576 | tf_op jit(solution)/shard_map/flux/pallas_call | solution.py:822
  11.3 0.3 collective-permute-done.3.one_ref
  11.6 0.9 %update.5 = (f32[128,128]{1,0:T(8,128)S(1)}, bf16[128,768]{1,0:T(8,128)(2,1)S(1)}, f32[64,384]{1,0:T(8,128)S(1)}, f32[8,256]{1,0:T(8,128)S(1)}) custom-call(f32[40,256]{1,0:T(8,128)S(1)} %collective-permute-done.3.one_ref, f32[32,768]{1,0:T(8,128)S(1)} %get-tuple-element.86.local_ref, f32[64,128]{1,0:T(8,128)S(1)} %get-tuple-element.87.volume_ref, ...), custom_call_target="tpu_custom_call" | custom-call | flops 16777216 | bytes 1048576 | tf_op jit(solution)/shard_map/update/pallas_call | solution.py:822
  12.5 0.3 collective-permute-start.4
  12.8 0.4 whole.1
  13.1 0.3 own.5.own_ref
  13.5 0.4 collective-permute-done.4.sent_ref.handed_ref
  13.8 0.1 carry.5
  14.0 0.5 collective-permute-start.5
  14.5 2.0 %collective-permute-start.6 = (f32[48,128]{1,0:T(8,128)S(1)}, f32[48,128]{1,0:T(8,128)S(1)}, u32[]{:S(2)}, u32[]{:S(2)}) collective-permute-start(f32[48,128]{1,0:T(8,128)S(1)} %get-tuple-element.95), channel_id=1, source_target_pairs={{0,4},{1,3},{2,6},{3,1},{4,0},{5,9},{6,2},{7,11},{8,12},{9,5},{10,... | collective-permute-start | bytes 73736 | tf_op jit(solution)/shard_map/ppermute | solution.py:845
  16.5 0.7 %turn.1 = (bf16[1408,768]{1,0:T(8,128)(2,1)S(1)}, bf16[256,768]{1,0:T(8,128)(2,1)S(1)}) custom-call(f32[16,1664]{1,0:T(8,128)S(1)} %get-tuple-element.80.place_ref), custom_call_target="tpu_custom_call" | custom-call | flops 16777216 | bytes 1048576 | tf_op jit(solution)/shard_map/turn/pallas_call | solution.py:822
  17.2 1.2 %sides.5 = (f32[64,1408]{1,0:T(8,128)S(1)}, f32[64,1024]{1,0:T(8,128)S(1)}, f32[64,256]{1,0:T(8,128)S(1)}) custom-call(bf16[128,768]{1,0:T(8,128)(2,1)S(1)} %get-tuple-element.92.stack_ref, bf16[768,1408]{1,0:T(8,128)(2,1)S(1)} %get-tuple-element.93.rest_0_.own_hot_ref, bf16[768,1024]{1,0:T(8,128)(2,1)S(1)} %get-tuple-element.96.partner_hot_ref, ...), custom_call_target="tpu_custom_call" | custom-call | flops 16777216 | bytes 1048576 | tf_op jit(solution)/shard_map/sides/pallas_call | solution.py:822
  18.4 0.0 collective-permute-done.6.two_ref
  18.4 0.0 collective-permute-done.5.one_ref
  18.4 0.1 relay.5
  18.6 0.4 collective-permute-start.7
  18.9 1.0 %flux.6 = (f32[64,768]{1,0:T(8,128)S(1)}, f32[128,128]{1,0:T(8,128)S(1)}) custom-call(f32[64,384]{1,0:T(8,128)S(1)} %collective-permute-done.4.sent_ref.handed_ref, f32[112,128]{1,0:T(8,128)S(1)} %collective-permute-done.5.one_ref, f32[48,128]{1,0:T(8,128)S(1)} %collective-permute-done.6.two_ref, f32[64,1408]{1,0:T(8,128)S(1)} %get-tuple-element.100.mine_ref, ...), custom_call_target="tpu_custom_call" | custom-call | flops 16777216 | bytes 1048576 | tf_op jit(solution)/shard_map/flux/pallas_call | solution.py:822
  20.0 0.0 collective-permute-done.7.one_ref
  20.0 1.0 %update.6 = (f32[128,128]{1,0:T(8,128)S(1)}, bf16[128,768]{1,0:T(8,128)(2,1)S(1)}, f32[64,384]{1,0:T(8,128)S(1)}) custom-call(f32[64,256]{1,0:T(8,128)S(1)} %collective-permute-done.7.one_ref, f32[64,768]{1,0:T(8,128)S(1)} %get-tuple-element.104.local_ref, f32[128,128]{1,0:T(8,128)S(1)} %get-tuple-element.105.volume_ref, ...), custom_call_target="tpu_custom_call" | custom-call | flops 16777216 | bytes 1048576 | tf_op jit(solution)/shard_map/update/pallas_call | solution.py:822
  21.0 0.3 collective-permute-start.8
  21.3 0.3 own.6.own_ref
  21.6 0.7 %collective-permute-done.8.sent_ref.handed_ref = f32[64,384]{1,0:T(8,128)S(1)} collective-permute-done((f32[64,384]{1,0:T(8,128)S(1)}, f32[64,384]{1,0:T(8,128)S(1)}, u32[]{:S(2)}, u32[]{:S(2)}) %collective-permute-start.8) | collective-permute-done | bytes 98336 | tf_op jit(solution)/shard_map/ppermute | solution.py:845
  22.4 0.1 carry.6
  22.5 1.8 %collective-permute-start.9 = (f32[112,128]{1,0:T(8,128)S(1)}, f32[112,128]{1,0:T(8,128)S(1)}, u32[]{:S(2)}, u32[]{:S(2)}) collective-permute-start(f32[112,128]{1,0:T(8,128)S(1)} %get-tuple-element.110), channel_id=1, source_target_pairs={{0,2},{1,0},{2,1},{3,5},{4,6},{5,3},{6,4},{7,9},{8,10},{9,7},{10,8... | collective-permute-start | bytes 172040 | tf_op jit(solution)/shard_map/ppermute | solution.py:845
  24.3 2.0 %collective-permute-start.10 = (f32[48,128]{1,0:T(8,128)S(1)}, f32[48,128]{1,0:T(8,128)S(1)}, u32[]{:S(2)}, u32[]{:S(2)}) collective-permute-start(f32[48,128]{1,0:T(8,128)S(1)} %get-tuple-element.111), channel_id=1, source_target_pairs={{0,4},{1,3},{2,6},{3,1},{4,0},{5,9},{6,2},{7,11},{8,12},{9,5},{10,... | collective-permute-start | bytes 73736 | tf_op jit(solution)/shard_map/ppermute | solution.py:845
  26.3 1.2 %sides.6 = (f32[64,1408]{1,0:T(8,128)S(1)}, f32[64,1024]{1,0:T(8,128)S(1)}, f32[64,256]{1,0:T(8,128)S(1)}) custom-call(bf16[128,768]{1,0:T(8,128)(2,1)S(1)} %get-tuple-element.109.stack_ref, bf16[768,1408]{1,0:T(8,128)(2,1)S(1)} %get-tuple-element.93.rest_0_.own_hot_ref, bf16[768,1024]{1,0:T(8,128)(2,1)S(1)} %get-tuple-element.96.partner_hot_ref, ...), custom_call_target="tpu_custom_call" | custom-call | flops 16777216 | bytes 1048576 | tf_op jit(solution)/shard_map/sides/pallas_call | solution.py:822
  27.5 0.6 %collective-permute-done.10.two_ref = f32[48,128]{1,0:T(8,128)S(1)} collective-permute-done((f32[48,128]{1,0:T(8,128)S(1)}, f32[48,128]{1,0:T(8,128)S(1)}, u32[]{:S(2)}, u32[]{:S(2)}) %collective-permute-start.10) | collective-permute-done | bytes 24608 | tf_op jit(solution)/shard_map/ppermute | solution.py:845
  28.2 0.1 relay.6
  28.3 0.0 collective-permute-start.11
  28.3 0.7 %flux.7 = (f32[32,768]{1,0:T(8,128)S(1)}, f32[64,128]{1,0:T(8,128)S(1)}) custom-call(f32[64,384]{1,0:T(8,128)S(1)} %collective-permute-done.8.sent_ref.handed_ref, f32[112,128]{1,0:T(8,128)S(1)} %collective-permute-done.9.one_ref, f32[48,128]{1,0:T(8,128)S(1)} %collective-permute-done.10.two_ref, f32[64,1408]{1,0:T(8,128)S(1)} %get-tuple-element.113.mine_ref, ...), custom_call_target="tpu_custom_call" | custom-call | flops 16777216 | bytes 1048576 | tf_op jit(solution)/shard_map/flux/pallas_call | solution.py:822
  29.1 0.5 collective-permute-done.11.one_ref
  29.6 0.7 %update.7 = (f32[64,128]{1,0:T(8,128)S(1)}, bf16[64,768]{1,0:T(8,128)(2,1)S(1)}, f32[32,384]{1,0:T(8,128)S(1)}) custom-call(f32[64,256]{1,0:T(8,128)S(1)} %collective-permute-done.11.one_ref, f32[32,768]{1,0:T(8,128)S(1)} %get-tuple-element.116.local_ref, f32[64,128]{1,0:T(8,128)S(1)} %get-tuple-element.117.volume_ref, ...), custom_call_target="tpu_custom_call" | custom-call | flops 16777216 | bytes 1048576 | tf_op jit(solution)/shard_map/update/pallas_call | solution.py:822
  30.3 0.2 collective-permute-start.12
  30.5 0.7 %flux.8 = (f32[32,768]{1,0:T(8,128)S(1)}, f32[64,128]{1,0:T(8,128)S(1)}) custom-call(f32[64,384]{1,0:T(8,128)S(1)} %collective-permute-done.8.sent_ref.handed_ref, f32[112,128]{1,0:T(8,128)S(1)} %collective-permute-done.9.one_ref, f32[48,128]{1,0:T(8,128)S(1)} %collective-permute-done.10.two_ref, f32[64,1408]{1,0:T(8,128)S(1)} %get-tuple-element.113.mine_ref, ...), custom_call_target="tpu_custom_call" | custom-call | flops 16777216 | bytes 1048576 | tf_op jit(solution)/shard_map/flux/pallas_call | solution.py:822
  31.2 0.3 own.7.own_ref
  31.5 0.1 collective-permute-done.12.sent_ref.handed_ref
  31.6 0.1 carry.7
  31.6 0.8 %collective-permute-start.13 = (f32[32,256]{1,0:T(8,128)S(1)}, f32[32,256]{1,0:T(8,128)S(1)}, u32[]{:S(2)}, u32[]{:S(2)}) collective-permute-start(f32[32,256]{1,0:T(8,128)S(1)} %get-tuple-element.121), channel_id=1, source_target_pairs={{0,2},{1,0},{2,1},{3,5},{4,6},{5,3},{6,4},{7,9},{8,10},{9,7},{10,8... | collective-permute-start | bytes 98312 | tf_op jit(solution)/shard_map/ppermute | solution.py:845
  32.4 2.5 %collective-permute-start.14 = (f32[32,128]{1,0:T(8,128)S(1)}, f32[32,128]{1,0:T(8,128)S(1)}, u32[]{:S(2)}, u32[]{:S(2)}) collective-permute-start(f32[32,128]{1,0:T(8,128)S(1)} %get-tuple-element.122), channel_id=1, source_target_pairs={{0,4},{1,3},{2,6},{3,1},{4,0},{5,9},{6,2},{7,11},{8,12},{9,5},{10,... | collective-permute-start | bytes 49160 | tf_op jit(solution)/shard_map/ppermute | solution.py:845
  34.9 0.9 %sides.7 = (f32[32,1408]{1,0:T(8,128)S(1)}, f32[32,1024]{1,0:T(8,128)S(1)}, f32[32,256]{1,0:T(8,128)S(1)}) custom-call(bf16[64,768]{1,0:T(8,128)(2,1)S(1)} %get-tuple-element.119.stack_ref, bf16[768,1408]{1,0:T(8,128)(2,1)S(1)} %get-tuple-element.93.rest_0_.own_hot_ref, bf16[768,1024]{1,0:T(8,128)(2,1)S(1)} %get-tuple-element.96.partner_hot_ref, ...), custom_call_target="tpu_custom_call" | custom-call | flops 16777216 | bytes 1048576 | tf_op jit(solution)/shard_map/sides/pallas_call | solution.py:822
  35.9 0.4 update.8.rest_1_.second_ref
  36.3 0.3 collective-permute-done.14.two_ref
  36.6 0.1 relay.7
  36.7 0.0 collective-permute-start.15
  36.7 0.7 %flux.9 = (f32[32,768]{1,0:T(8,128)S(1)}, f32[64,128]{1,0:T(8,128)S(1)}) custom-call(f32[32,384]{1,0:T(8,128)S(1)} %collective-permute-done.12.sent_ref.handed_ref, f32[32,256]{1,0:T(8,128)S(1)} %collective-permute-done.13.one_ref, f32[32,128]{1,0:T(8,128)S(1)} %collective-permute-done.14.two_ref, f32[32,1408]{1,0:T(8,128)S(1)} %get-tuple-element.125.mine_ref, ...), custom_call_target="tpu_custom_call" | custom-call | flops 16777216 | bytes 1048576 | tf_op jit(solution)/shard_map/flux/pallas_call | solution.py:822
  37.5 0.5 collective-permute-done.15.one_ref
  37.9 0.5 update.9
  38.4 12.1 %all_to_all.5 = f32[32,1,128]{2,1,0:T(1,128)S(1)} all-to-all(f32[32,1,128]{2,1,0:T(1,128)S(1)} %bitcast.13), channel_id=1, replica_groups=mesh['dom'=32] {'dom'}, dimensions={0} | all-to-all | bytes 32768 | tf_op jit(solution)/shard_map/all_to_all | solution.py:988
  50.6 0.7 %finish.1 = (f32[64,128]{1,0:T(8,128)}, f32[1,128]{1,0:T(1,128)}) custom-call(f32[32,128]{1,0:T(8,128)S(1)} %bitcast.14, f32[64,128]{1,0:T(8,128)S(1)} %get-tuple-element.88.rest_0_.guess_ref, f32[128,128]{1,0:T(8,128)S(1)} %get-tuple-element.115.field_ref.first_ref, f32[64,128]{1,0:T(8,128)S(1)} %update.8.rest_1_.second_ref), custom_call_target="tpu_custom_call" | custom-call | flops 16777216 | bytes 1048576 | tf_op jit(solution)/shard_map/finish/pallas_call | solution.py:822
  (12 shorter events, 0.0 us)
Async XLA Ops:
  0.6 9.8 %copy-start.2 = (bf16[64,64,128]{2,1,0:T(8,128)(2,1)S(1)}, bf16[64,64,128]{2,1,0:T(8,128)(2,1)}, u32[]{:S(2)}) copy-start(bf16[64,64,128]{2,1,0:T(8,128)(2,1)} %inverse_ref.1) | copy-start | bytes 3145732
  2.2 1.4 %collective-permute-start = (f32[40,384]{1,0:T(8,128)S(1)}, f32[40,384]{1,0:T(8,128)S(1)}, u32[]{:S(2)}, u32[]{:S(2)}) collective-permute-start(f32[40,384]{1,0:T(8,128)S(1)} %get-tuple-element.67), channel_id=1, source_target_pairs={{0,1},{1,0},{2,3},{3,2},{4,5},{5,4},{6,7},{7,6},{8,9},{9,8},{10,11... | collective-permute-start | bytes 184328 | tf_op jit(solution)/shard_map/ppermute | solution.py:845
  3.7 6.6 %collective-permute-start.1 = (f32[40,256]{1,0:T(8,128)S(1)}, f32[40,256]{1,0:T(8,128)S(1)}, u32[]{:S(2)}, u32[]{:S(2)}) collective-permute-start(f32[40,256]{1,0:T(8,128)S(1)} %get-tuple-element.73), channel_id=1, source_target_pairs={{0,2},{1,0},{2,1},{3,5},{4,6},{5,3},{6,4},{7,9},{8,10},{9,7},{10,8... | collective-permute-start | bytes 122888 | tf_op jit(solution)/shard_map/ppermute | solution.py:845
  6.5 3.8 %collective-permute-start.2 = (f32[40,128]{1,0:T(8,128)S(1)}, f32[40,128]{1,0:T(8,128)S(1)}, u32[]{:S(2)}, u32[]{:S(2)}) collective-permute-start(f32[40,128]{1,0:T(8,128)S(1)} %get-tuple-element.74), channel_id=1, source_target_pairs={{0,4},{1,3},{2,6},{3,1},{4,0},{5,9},{6,2},{7,11},{8,12},{9,5},{10,... | collective-permute-start | bytes 61448 | tf_op jit(solution)/shard_map/ppermute | solution.py:845
  8.0 2.5 %copy-start = (f32[32,128]{1,0:T(8,128)S(1)}, f32[32,128]{1,0:T(8,128)}, u32[]{:S(2)}) copy-start(f32[32,128]{1,0:T(8,128)} %constant.5.clone.weight_ref) | copy-start | bytes 49156
  8.0 2.5 %copy-start.1 = (bf16[64,384]{1,0:T(8,128)(2,1)S(1)}, bf16[64,384]{1,0:T(8,128)(2,1)}, u32[]{:S(2)}) copy-start(bf16[64,384]{1,0:T(8,128)(2,1)} %constant.4.clone.stiffness_ref) | copy-start | bytes 147460
  8.0 2.5 %copy-start.3 = (f32[64,128]{1,0:T(8,128)S(1)}, f32[64,128]{1,0:T(8,128)}, u32[]{:S(2)}) copy-start(f32[64,128]{1,0:T(8,128)} %field_ref.3) | copy-start | bytes 98308
  10.4 1.2 %collective-permute-start.3 = (f32[40,256]{1,0:T(8,128)S(1)}, f32[40,256]{1,0:T(8,128)S(1)}, u32[]{:S(2)}, u32[]{:S(2)}) collective-permute-start(f32[40,256]{1,0:T(8,128)S(1)} %relay.4), channel_id=1, source_target_pairs={{0,1},{1,0},{2,3},{3,2},{4,5},{5,4},{6,7},{7,6},{8,9},{9,8},{10,11... | collective-permute-start | bytes 122888 | tf_op jit(solution)/shard_map/ppermute | solution.py:845
  12.5 1.4 %collective-permute-start.4 = (f32[64,384]{1,0:T(8,128)S(1)}, f32[64,384]{1,0:T(8,128)S(1)}, u32[]{:S(2)}, u32[]{:S(2)}) collective-permute-start(f32[64,384]{1,0:T(8,128)S(1)} %get-tuple-element.91), channel_id=1, source_target_pairs={{0,1},{1,0},{2,3},{3,2},{4,5},{5,4},{6,7},{7,6},{8,9},{9,8},{10,11... | collective-permute-start | bytes 294920 | tf_op jit(solution)/shard_map/ppermute | solution.py:845
  14.0 4.4 %collective-permute-start.5 = (f32[112,128]{1,0:T(8,128)S(1)}, f32[112,128]{1,0:T(8,128)S(1)}, u32[]{:S(2)}, u32[]{:S(2)}) collective-permute-start(f32[112,128]{1,0:T(8,128)S(1)} %get-tuple-element.94), channel_id=1, source_target_pairs={{0,2},{1,0},{2,1},{3,5},{4,6},{5,3},{6,4},{7,9},{8,10},{9,7},{10,8... | collective-permute-start | bytes 172040 | tf_op jit(solution)/shard_map/ppermute | solution.py:845
  14.5 3.9 %collective-permute-start.6 = (f32[48,128]{1,0:T(8,128)S(1)}, f32[48,128]{1,0:T(8,128)S(1)}, u32[]{:S(2)}, u32[]{:S(2)}) collective-permute-start(f32[48,128]{1,0:T(8,128)S(1)} %get-tuple-element.95), channel_id=1, source_target_pairs={{0,4},{1,3},{2,6},{3,1},{4,0},{5,9},{6,2},{7,11},{8,12},{9,5},{10,... | collective-permute-start | bytes 73736 | tf_op jit(solution)/shard_map/ppermute | solution.py:845
  18.6 1.4 %copy-start.4 = (f32[64,128]{1,0:T(8,128)S(1)}, f32[64,128]{1,0:T(8,128)}, u32[]{:S(2)}) copy-start(f32[64,128]{1,0:T(8,128)} %rest_1_.1) | copy-start | bytes 98308
  18.6 1.4 %collective-permute-start.7 = (f32[64,256]{1,0:T(8,128)S(1)}, f32[64,256]{1,0:T(8,128)S(1)}, u32[]{:S(2)}, u32[]{:S(2)}) collective-permute-start(f32[64,256]{1,0:T(8,128)S(1)} %relay.5), channel_id=1, source_target_pairs={{0,1},{1,0},{2,3},{3,2},{4,5},{5,4},{6,7},{7,6},{8,9},{9,8},{10,11... | collective-permute-start | bytes 196616 | tf_op jit(solution)/shard_map/ppermute | solution.py:845
  21.0 1.4 %collective-permute-start.8 = (f32[64,384]{1,0:T(8,128)S(1)}, f32[64,384]{1,0:T(8,128)S(1)}, u32[]{:S(2)}, u32[]{:S(2)}) collective-permute-start(f32[64,384]{1,0:T(8,128)S(1)} %get-tuple-element.108), channel_id=1, source_target_pairs={{0,1},{1,0},{2,3},{3,2},{4,5},{5,4},{6,7},{7,6},{8,9},{9,8},{10,11... | collective-permute-start | bytes 294920 | tf_op jit(solution)/shard_map/ppermute | solution.py:845
  22.5 5.6 %collective-permute-start.9 = (f32[112,128]{1,0:T(8,128)S(1)}, f32[112,128]{1,0:T(8,128)S(1)}, u32[]{:S(2)}, u32[]{:S(2)}) collective-permute-start(f32[112,128]{1,0:T(8,128)S(1)} %get-tuple-element.110), channel_id=1, source_target_pairs={{0,2},{1,0},{2,1},{3,5},{4,6},{5,3},{6,4},{7,9},{8,10},{9,7},{10,8... | collective-permute-start | bytes 172040 | tf_op jit(solution)/shard_map/ppermute | solution.py:845
  24.3 3.8 %collective-permute-start.10 = (f32[48,128]{1,0:T(8,128)S(1)}, f32[48,128]{1,0:T(8,128)S(1)}, u32[]{:S(2)}, u32[]{:S(2)}) collective-permute-start(f32[48,128]{1,0:T(8,128)S(1)} %get-tuple-element.111), channel_id=1, source_target_pairs={{0,4},{1,3},{2,6},{3,1},{4,0},{5,9},{6,2},{7,11},{8,12},{9,5},{10,... | collective-permute-start | bytes 73736 | tf_op jit(solution)/shard_map/ppermute | solution.py:845
  28.3 1.3 %collective-permute-start.11 = (f32[64,256]{1,0:T(8,128)S(1)}, f32[64,256]{1,0:T(8,128)S(1)}, u32[]{:S(2)}, u32[]{:S(2)}) collective-permute-start(f32[64,256]{1,0:T(8,128)S(1)} %relay.6), channel_id=1, source_target_pairs={{0,1},{1,0},{2,3},{3,2},{4,5},{5,4},{6,7},{7,6},{8,9},{9,8},{10,11... | collective-permute-start | bytes 196616 | tf_op jit(solution)/shard_map/ppermute | solution.py:845
  30.3 1.3 %collective-permute-start.12 = (f32[32,384]{1,0:T(8,128)S(1)}, f32[32,384]{1,0:T(8,128)S(1)}, u32[]{:S(2)}, u32[]{:S(2)}) collective-permute-start(f32[32,384]{1,0:T(8,128)S(1)} %get-tuple-element.118), channel_id=1, source_target_pairs={{0,1},{1,0},{2,3},{3,2},{4,5},{5,4},{6,7},{7,6},{8,9},{9,8},{10,11... | collective-permute-start | bytes 147464 | tf_op jit(solution)/shard_map/ppermute | solution.py:845
  31.6 5.0 %collective-permute-start.13 = (f32[32,256]{1,0:T(8,128)S(1)}, f32[32,256]{1,0:T(8,128)S(1)}, u32[]{:S(2)}, u32[]{:S(2)}) collective-permute-start(f32[32,256]{1,0:T(8,128)S(1)} %get-tuple-element.121), channel_id=1, source_target_pairs={{0,2},{1,0},{2,1},{3,5},{4,6},{5,3},{6,4},{7,9},{8,10},{9,7},{10,8... | collective-permute-start | bytes 98312 | tf_op jit(solution)/shard_map/ppermute | solution.py:845
  32.4 4.2 %collective-permute-start.14 = (f32[32,128]{1,0:T(8,128)S(1)}, f32[32,128]{1,0:T(8,128)S(1)}, u32[]{:S(2)}, u32[]{:S(2)}) collective-permute-start(f32[32,128]{1,0:T(8,128)S(1)} %get-tuple-element.122), channel_id=1, source_target_pairs={{0,4},{1,3},{2,6},{3,1},{4,0},{5,9},{6,2},{7,11},{8,12},{9,5},{10,... | collective-permute-start | bytes 49160 | tf_op jit(solution)/shard_map/ppermute | solution.py:845
  36.7 1.2 %collective-permute-start.15 = (f32[32,256]{1,0:T(8,128)S(1)}, f32[32,256]{1,0:T(8,128)S(1)}, u32[]{:S(2)}, u32[]{:S(2)}) collective-permute-start(f32[32,256]{1,0:T(8,128)S(1)} %relay.7), channel_id=1, source_target_pairs={{0,1},{1,0},{2,3},{3,2},{4,5},{5,4},{6,7},{7,6},{8,9},{9,8},{10,11... | collective-permute-start | bytes 98312 | tf_op jit(solution)/shard_map/ppermute | solution.py:845

commit v11 on v8

--- a/solution.py
+++ b/solution.py
@@ -713,6 +713,11 @@
         volume_ref[64 * k : 64 * k + 64, :] = volume[:, lanes * k : lanes * k + lanes]
 
 
+def widen_kernel(inverse_ref, wide_ref):
+    for col in range(64):
+        wide_ref[col] = inverse_ref[col].astype(f32)
+
+
 def solve_blocks(inverse_ref, hold_ref, nf):
     sums = [jnp.zeros((64, lanes), f32) for _ in range(nf)]
     for col in range(64):
@@ -891,6 +896,7 @@
         scratch=[pltpu.VMEM((8, 512), i32)],
     )
     fields, halo, late = start_vector, [], []
+    (inverse,) = run(widen_kernel, [(block_inverse.shape, f32)], [block_inverse], "widen")
     for turn, (nf, nf_next) in enumerate(((1, 2), (2, 2), (2, 1), (1, 0))):
         h = 32 * nf
         def own_work():
@@ -949,7 +955,7 @@
             )
             ins = [
                 last, sums, volume, targets, place, arrival, far_scatter, weight, fields, coef, level,
-                block_inverse, *(halo[1:] if turn else [guess]), *([rhs_field] if turn == 1 else []),
+                inverse, *(halo[1:] if turn else [guess]), *([rhs_field] if turn == 1 else []),
             ]
             outs = [((devices, lanes) if turn == 3 else (64 * max(count, count_next), lanes), f32)]
             if count_next:

time: 51.8 us -> 51.5 us (level)
    pallas_call x32 -> x33, Pallas kernels: 18.4 us -> 18.1 us  [run(): pl.pallas_call(body, out_shape=[(pltpu.VMEM if kept else jax.ShapeDtypeSt...]
where the time goes in v11:
time: 51.5 us; the launch traced here: 51.3 us
  Pallas kernels  18.1 us (35%)
  starting transfers between devices  16 us (31%)
  blocking collectives  12 us (23%)
  waiting for transfers between devices  4.22 us (8%)
  between operations  0.88 us (2%)
    pallas_call x33, Pallas kernels, run(): pl.pallas_call(body, out_shape=[(pltpu.VMEM if kept else jax.ShapeDtypeSt...  18.1 us
    ppermute x16, starting transfers between devices, permute(): return lax.ppermute(x, 'dom', sorted(to.items()))  16 us
    all_to_all x1, blocking collectives, local(): lax.all_to_all(parts.reshape(devices, 1, lanes), 'dom', 0, 0)  12 us
    ppermute x16, waiting for transfers between devices, permute(): return lax.ppermute(x, 'dom', sorted(to.items()))  4.22 us
  transfers between devices with their start and end apart: 16, of which 9 were waited for; matrix products, arithmetic and copies ran while one was open for 0% of the time, Pallas kernels for 23%

profile of v11, /device:TPU:0, one launch (start us, length us, event | category | flops | bytes accessed | tf_op | source)
XLA Modules:
  0.0 51.3 jit_solution(17371269907593209729)
XLA Ops:
  0.6 1.4 %send_setup.1 = (bf16[768,256]{1,0:T(8,128)(2,1)S(1)}, s32[8,256]{1,0:T(8,128)S(1)}, bf16[80,768]{1,0:T(8,128)(2,1)S(1)}, s32[8,1024]{1,0:T(8,128)S(1)}, s32[32,...) custom-call(s32[1,930]{1,0:T(1,128)} %bitcast.15, ...), custom_call_target="tpu_custom_call" | custom-call | flops 16777216 | bytes 1048576 | tf_op jit(solution)/shard_map/send_setup/pallas_call | solution.py:822
  2.1 0.5 %collective-permute-start = (f32[40,256]{1,0:T(8,128)S(1)}, f32[40,256]{1,0:T(8,128)S(1)}, u32[]{:S(2)}, u32[]{:S(2)}) collective-permute-start(f32[40,256]{1,0:T(8,128)S(1)} %get-tuple-element.67), channel_id=1, source_target_pairs={{0,1},{1,0},{2,3},{3,2},{4,5},{5,4},{6,7},{7,6},{8,9},{9,8},{10,11... | collective-permute-start | bytes 122888 | tf_op jit(solution)/shard_map/ppermute | solution.py:845
  2.6 0.3 own_setup.1
  2.9 0.3 own.4.own_ref
  3.3 0.2 collective-permute-done.sent_ref
  3.5 0.1 carry.4
  3.6 2.8 %collective-permute-start.1 = (f32[40,256]{1,0:T(8,128)S(1)}, f32[40,256]{1,0:T(8,128)S(1)}, u32[]{:S(2)}, u32[]{:S(2)}) collective-permute-start(f32[40,256]{1,0:T(8,128)S(1)} %get-tuple-element.73), channel_id=1, source_target_pairs={{0,2},{1,0},{2,1},{3,5},{4,6},{5,3},{6,4},{7,9},{8,10},{9,7},{10,8... | collective-permute-start | bytes 122888 | tf_op jit(solution)/shard_map/ppermute | solution.py:845
  6.4 1.5 %collective-permute-start.2 = (f32[40,128]{1,0:T(8,128)S(1)}, f32[40,128]{1,0:T(8,128)S(1)}, u32[]{:S(2)}, u32[]{:S(2)}) collective-permute-start(f32[40,128]{1,0:T(8,128)S(1)} %get-tuple-element.74), channel_id=1, source_target_pairs={{0,4},{1,3},{2,6},{3,1},{4,0},{5,9},{6,2},{7,11},{8,12},{9,5},{10,... | collective-permute-start | bytes 61448 | tf_op jit(solution)/shard_map/ppermute | solution.py:845
  7.9 0.7 %setup.1 = (bf16[128,1280]{1,0:T(8,128)(2,1)S(1)}, bf16[128,1024]{1,0:T(8,128)(2,1)S(1)}, bf16[128,384]{1,0:T(8,128)(2,1)S(1)}, f32[16,1664]{1,0:T(8,128)S(1)}, ...) custom-call(f32[1,128]{1,0:T(1,128)S(1)} %get-tuple-element.75.coef_ref, s32[1,128]{1,0:T(1,128)S(1)} %get-tuple-element.76.level_ref, ...), custom_call_target="tpu_custom_call" | custom-call | flops 16777216 | bytes 1048576 | tf_op jit(solution)/shard_map/setup/pallas_call | solution.py:822
  8.6 0.0 copy-start
  8.6 0.0 copy-start.1
  8.6 0.0 copy-start.3
  8.6 0.8 %sides.4 = (f32[32,1280]{1,0:T(8,128)S(1)}, f32[32,1024]{1,0:T(8,128)S(1)}, f32[32,384]{1,0:T(8,128)S(1)}) custom-call(bf16[80,768]{1,0:T(8,128)(2,1)S(1)} %get-tuple-element.68.stack_ref, bf16[128,1280]{1,0:T(8,128)(2,1)S(1)} %get-tuple-element.77.own_hot_ref.own_elem_ref, bf16[128,1024]{1,0:T(8,128)(2,1)S(1)} %get-tuple-element.78.partner_hot_ref.partner_elem_ref, ...), custom_call_target="tpu_custom_call" | custom-call | flops 16777216 | bytes 1048576 | tf_op jit(solution)/shard_map/sides/pallas_call | solution.py:822
  9.4 0.7 %collective-permute-done.2.two_ref = f32[40,128]{1,0:T(8,128)S(1)} collective-permute-done((f32[40,128]{1,0:T(8,128)S(1)}, f32[40,128]{1,0:T(8,128)S(1)}, u32[]{:S(2)}, u32[]{:S(2)}) %collective-permute-start.2) | collective-permute-done | bytes 20512 | tf_op jit(solution)/shard_map/ppermute | solution.py:845
  10.2 0.1 relay.4
  10.3 0.0 collective-permute-start.3
  10.3 0.1 widen.1.inverse_ref
  10.5 0.7 %flux.5 = (f32[32,768]{1,0:T(8,128)S(1)}, f32[64,128]{1,0:T(8,128)S(1)}, f32[8,256]{1,0:T(8,128)S(1)}) custom-call(f32[40,256]{1,0:T(8,128)S(1)} %collective-permute-done.1.one_ref, f32[40,128]{1,0:T(8,128)S(1)} %collective-permute-done.2.two_ref, f32[32,1280]{1,0:T(8,128)S(1)} %get-tuple-element.84.mine_ref, f32[32,1024]{1,0:T(8,128)S(1)} %get-tuple-element.85.other_ref, ...), custom_call_target="tpu_custom_call" | custom-call | flops 16777216 | bytes 1048576 | tf_op jit(solution)/shard_map/flux/pallas_call | solution.py:822
  11.1 0.4 collective-permute-done.3.one_ref
  11.5 0.8 %update.5 = (f32[128,128]{1,0:T(8,128)S(1)}, bf16[128,768]{1,0:T(8,128)(2,1)S(1)}, f32[64,256]{1,0:T(8,128)S(1)}, f32[8,384]{1,0:T(8,128)S(1)}) custom-call(f32[40,384]{1,0:T(8,128)S(1)} %collective-permute-done.3.one_ref, f32[32,768]{1,0:T(8,128)S(1)} %get-tuple-element.86.local_ref, f32[64,128]{1,0:T(8,128)S(1)} %get-tuple-element.87.volume_ref, ...), custom_call_target="tpu_custom_call" | custom-call | flops 16777216 | bytes 1048576 | tf_op jit(solution)/shard_map/update/pallas_call | solution.py:822
  12.3 0.2 collective-permute-start.4
  12.6 0.4 whole.1
  12.9 0.4 own.5.own_ref
  13.3 0.3 collective-permute-done.4.sent_ref
  13.7 0.1 carry.5
  13.8 0.5 collective-permute-start.5
  14.3 1.9 %collective-permute-start.6 = (f32[48,128]{1,0:T(8,128)S(1)}, f32[48,128]{1,0:T(8,128)S(1)}, u32[]{:S(2)}, u32[]{:S(2)}) collective-permute-start(f32[48,128]{1,0:T(8,128)S(1)} %get-tuple-element.95), channel_id=1, source_target_pairs={{0,4},{1,3},{2,6},{3,1},{4,0},{5,9},{6,2},{7,11},{8,12},{9,5},{10,... | collective-permute-start | bytes 73736 | tf_op jit(solution)/shard_map/ppermute | solution.py:845
  16.2 0.7 %turn.1 = (bf16[1280,768]{1,0:T(8,128)(2,1)S(1)}, bf16[384,768]{1,0:T(8,128)(2,1)S(1)}) custom-call(f32[16,1664]{1,0:T(8,128)S(1)} %get-tuple-element.80.place_ref), custom_call_target="tpu_custom_call" | custom-call | flops 16777216 | bytes 1048576 | tf_op jit(solution)/shard_map/turn/pallas_call | solution.py:822
  16.9 1.2 %sides.5 = (f32[64,1280]{1,0:T(8,128)S(1)}, f32[64,1024]{1,0:T(8,128)S(1)}, f32[64,384]{1,0:T(8,128)S(1)}) custom-call(bf16[128,768]{1,0:T(8,128)(2,1)S(1)} %get-tuple-element.92.stack_ref, bf16[768,1280]{1,0:T(8,128)(2,1)S(1)} %get-tuple-element.93.rest_0_.own_hot_ref, bf16[768,1024]{1,0:T(8,128)(2,1)S(1)} %get-tuple-element.96.partner_hot_ref, ...), custom_call_target="tpu_custom_call" | custom-call | flops 16777216 | bytes 1048576 | tf_op jit(solution)/shard_map/sides/pallas_call | solution.py:822
  18.2 0.1 relay.5
  18.3 0.4 collective-permute-start.7
  18.7 0.9 %flux.6 = (f32[64,768]{1,0:T(8,128)S(1)}, f32[128,128]{1,0:T(8,128)S(1)}) custom-call(f32[112,128]{1,0:T(8,128)S(1)} %collective-permute-done.5.one_ref, f32[48,128]{1,0:T(8,128)S(1)} %collective-permute-done.6.two_ref, f32[64,1280]{1,0:T(8,128)S(1)} %get-tuple-element.100.mine_ref, f32[64,1024]{1,0:T(8,128)S(1)} %get-tuple-element.101.other_ref, ...), custom_call_target="tpu_custom_call" | custom-call | flops 16777216 | bytes 1048576 | tf_op jit(solution)/shard_map/flux/pallas_call | solution.py:822
  19.6 0.0 collective-permute-done.7.one_ref
  19.7 1.1 %update.6 = (f32[128,128]{1,0:T(8,128)S(1)}, bf16[128,768]{1,0:T(8,128)(2,1)S(1)}, f32[64,256]{1,0:T(8,128)S(1)}) custom-call(f32[64,384]{1,0:T(8,128)S(1)} %collective-permute-done.7.one_ref, f32[64,768]{1,0:T(8,128)S(1)} %get-tuple-element.104.local_ref, f32[128,128]{1,0:T(8,128)S(1)} %get-tuple-element.105.volume_ref, ...), custom_call_target="tpu_custom_call" | custom-call | flops 16777216 | bytes 1048576 | tf_op jit(solution)/shard_map/update/pallas_call | solution.py:822
  20.8 0.4 collective-permute-start.8
  21.2 0.4 own.6.own_ref
  21.6 0.5 %collective-permute-done.8.sent_ref = f32[64,256]{1,0:T(8,128)S(1)} collective-permute-done((f32[64,256]{1,0:T(8,128)S(1)}, f32[64,256]{1,0:T(8,128)S(1)}, u32[]{:S(2)}, u32[]{:S(2)}) %collective-permute-start.8) | collective-permute-done | bytes 65568 | tf_op jit(solution)/shard_map/ppermute | solution.py:845
  22.1 0.1 carry.6
  22.2 1.8 %collective-permute-start.9 = (f32[112,128]{1,0:T(8,128)S(1)}, f32[112,128]{1,0:T(8,128)S(1)}, u32[]{:S(2)}, u32[]{:S(2)}) collective-permute-start(f32[112,128]{1,0:T(8,128)S(1)} %get-tuple-element.110), channel_id=1, source_target_pairs={{0,2},{1,0},{2,1},{3,5},{4,6},{5,3},{6,4},{7,9},{8,10},{9,7},{10,8... | collective-permute-start | bytes 172040 | tf_op jit(solution)/shard_map/ppermute | solution.py:845
  24.0 2.2 %collective-permute-start.10 = (f32[48,128]{1,0:T(8,128)S(1)}, f32[48,128]{1,0:T(8,128)S(1)}, u32[]{:S(2)}, u32[]{:S(2)}) collective-permute-start(f32[48,128]{1,0:T(8,128)S(1)} %get-tuple-element.111), channel_id=1, source_target_pairs={{0,4},{1,3},{2,6},{3,1},{4,0},{5,9},{6,2},{7,11},{8,12},{9,5},{10,... | collective-permute-start | bytes 73736 | tf_op jit(solution)/shard_map/ppermute | solution.py:845
  26.2 1.2 %sides.6 = (f32[64,1280]{1,0:T(8,128)S(1)}, f32[64,1024]{1,0:T(8,128)S(1)}, f32[64,384]{1,0:T(8,128)S(1)}) custom-call(bf16[128,768]{1,0:T(8,128)(2,1)S(1)} %get-tuple-element.109.stack_ref, bf16[768,1280]{1,0:T(8,128)(2,1)S(1)} %get-tuple-element.93.rest_0_.own_hot_ref, bf16[768,1024]{1,0:T(8,128)(2,1)S(1)} %get-tuple-element.96.partner_hot_ref, ...), custom_call_target="tpu_custom_call" | custom-call | flops 16777216 | bytes 1048576 | tf_op jit(solution)/shard_map/sides/pallas_call | solution.py:822
  27.4 0.6 %collective-permute-done.10.two_ref = f32[48,128]{1,0:T(8,128)S(1)} collective-permute-done((f32[48,128]{1,0:T(8,128)S(1)}, f32[48,128]{1,0:T(8,128)S(1)}, u32[]{:S(2)}, u32[]{:S(2)}) %collective-permute-start.10) | collective-permute-done | bytes 24608 | tf_op jit(solution)/shard_map/ppermute | solution.py:845
  28.0 0.1 relay.6
  28.1 0.0 collective-permute-start.11
  28.2 0.7 %flux.7 = (f32[32,768]{1,0:T(8,128)S(1)}, f32[64,128]{1,0:T(8,128)S(1)}) custom-call(f32[112,128]{1,0:T(8,128)S(1)} %collective-permute-done.9.one_ref, f32[48,128]{1,0:T(8,128)S(1)} %collective-permute-done.10.two_ref, f32[64,1280]{1,0:T(8,128)S(1)} %get-tuple-element.113.mine_ref, f32[64,1024]{1,0:T(8,128)S(1)} %get-tuple-element.114.other_ref, ...), custom_call_target="tpu_custom_call" | custom-call | flops 16777216 | bytes 1048576 | tf_op jit(solution)/shard_map/flux/pallas_call | solution.py:822
  28.8 0.6 %collective-permute-done.11.one_ref = f32[64,384]{1,0:T(8,128)S(1)} collective-permute-done((f32[64,384]{1,0:T(8,128)S(1)}, f32[64,384]{1,0:T(8,128)S(1)}, u32[]{:S(2)}, u32[]{:S(2)}) %collective-permute-start.11) | collective-permute-done | bytes 98336 | tf_op jit(solution)/shard_map/ppermute | solution.py:845
  29.4 0.8 %update.7 = (f32[64,128]{1,0:T(8,128)S(1)}, bf16[64,768]{1,0:T(8,128)(2,1)S(1)}, f32[32,256]{1,0:T(8,128)S(1)}) custom-call(f32[64,384]{1,0:T(8,128)S(1)} %collective-permute-done.11.one_ref, f32[32,768]{1,0:T(8,128)S(1)} %get-tuple-element.116.local_ref, f32[64,128]{1,0:T(8,128)S(1)} %get-tuple-element.117.volume_ref, ...), custom_call_target="tpu_custom_call" | custom-call | flops 16777216 | bytes 1048576 | tf_op jit(solution)/shard_map/update/pallas_call | solution.py:822
  30.2 0.2 collective-permute-start.12
  30.4 0.7 %flux.8 = (f32[32,768]{1,0:T(8,128)S(1)}, f32[64,128]{1,0:T(8,128)S(1)}) custom-call(f32[112,128]{1,0:T(8,128)S(1)} %collective-permute-done.9.one_ref, f32[48,128]{1,0:T(8,128)S(1)} %collective-permute-done.10.two_ref, f32[64,1280]{1,0:T(8,128)S(1)} %get-tuple-element.113.mine_ref, f32[64,1024]{1,0:T(8,128)S(1)} %get-tuple-element.114.other_ref, ...), custom_call_target="tpu_custom_call" | custom-call | flops 16777216 | bytes 1048576 | tf_op jit(solution)/shard_map/flux/pallas_call | solution.py:822
  31.1 0.3 own.7.own_ref
  31.4 0.0 collective-permute-done.12.sent_ref
  31.5 0.1 carry.7
  31.6 0.8 %collective-permute-start.13 = (f32[32,256]{1,0:T(8,128)S(1)}, f32[32,256]{1,0:T(8,128)S(1)}, u32[]{:S(2)}, u32[]{:S(2)}) collective-permute-start(f32[32,256]{1,0:T(8,128)S(1)} %get-tuple-element.121), channel_id=1, source_target_pairs={{0,2},{1,0},{2,1},{3,5},{4,6},{5,3},{6,4},{7,9},{8,10},{9,7},{10,8... | collective-permute-start | bytes 98312 | tf_op jit(solution)/shard_map/ppermute | solution.py:845
  32.3 2.6 %collective-permute-start.14 = (f32[32,128]{1,0:T(8,128)S(1)}, f32[32,128]{1,0:T(8,128)S(1)}, u32[]{:S(2)}, u32[]{:S(2)}) collective-permute-start(f32[32,128]{1,0:T(8,128)S(1)} %get-tuple-element.122), channel_id=1, source_target_pairs={{0,4},{1,3},{2,6},{3,1},{4,0},{5,9},{6,2},{7,11},{8,12},{9,5},{10,... | collective-permute-start | bytes 49160 | tf_op jit(solution)/shard_map/ppermute | solution.py:845
  34.9 1.0 %sides.7 = (f32[32,1280]{1,0:T(8,128)S(1)}, f32[32,1024]{1,0:T(8,128)S(1)}, f32[32,384]{1,0:T(8,128)S(1)}) custom-call(bf16[64,768]{1,0:T(8,128)(2,1)S(1)} %get-tuple-element.119.stack_ref, bf16[768,1280]{1,0:T(8,128)(2,1)S(1)} %get-tuple-element.93.rest_0_.own_hot_ref, bf16[768,1024]{1,0:T(8,128)(2,1)S(1)} %get-tuple-element.96.partner_hot_ref, ...), custom_call_target="tpu_custom_call" | custom-call | flops 16777216 | bytes 1048576 | tf_op jit(solution)/shard_map/sides/pallas_call | solution.py:822
  35.9 0.5 update.8.rest_1_.second_ref
  36.4 0.2 collective-permute-done.14.two_ref
  36.6 0.1 relay.7
  36.7 0.1 collective-permute-start.15
  36.8 0.7 %flux.9 = (f32[32,768]{1,0:T(8,128)S(1)}, f32[64,128]{1,0:T(8,128)S(1)}) custom-call(f32[32,256]{1,0:T(8,128)S(1)} %collective-permute-done.13.one_ref, f32[32,128]{1,0:T(8,128)S(1)} %collective-permute-done.14.two_ref, f32[32,1280]{1,0:T(8,128)S(1)} %get-tuple-element.125.mine_ref, f32[32,1024]{1,0:T(8,128)S(1)} %get-tuple-element.126.other_ref, ...), custom_call_target="tpu_custom_call" | custom-call | flops 16777216 | bytes 1048576 | tf_op jit(solution)/shard_map/flux/pallas_call | solution.py:822
  37.5 0.5 collective-permute-done.15.one_ref
  37.9 0.6 %update.9 = f32[32,128]{1,0:T(8,128)S(1)} custom-call(f32[32,384]{1,0:T(8,128)S(1)} %collective-permute-done.15.one_ref, f32[32,768]{1,0:T(8,128)S(1)} %get-tuple-element.128.local_ref, f32[64,128]{1,0:T(8,128)S(1)} %get-tuple-element.129.volume_ref, f32[32,384]{1,0:T(8,128)S(1)} %get-tuple-element.123.rest_0_.target_ref, ...), custom_call_target="tpu_custom_call" | custom-call | flops 16777216 | bytes 1048576 | tf_op jit(solution)/shard_map/update/pallas_call | solution.py:822
  38.5 12.0 %all_to_all.5 = f32[32,1,128]{2,1,0:T(1,128)S(1)} all-to-all(f32[32,1,128]{2,1,0:T(1,128)S(1)} %bitcast.13), channel_id=1, replica_groups=mesh['dom'=32] {'dom'}, dimensions={0} | all-to-all | bytes 32768 | tf_op jit(solution)/shard_map/all_to_all | solution.py:987
  50.5 0.7 %finish.1 = (f32[64,128]{1,0:T(8,128)}, f32[1,128]{1,0:T(1,128)}) custom-call(f32[32,128]{1,0:T(8,128)S(1)} %bitcast.14, f32[64,128]{1,0:T(8,128)S(1)} %get-tuple-element.88.rest_0_.guess_ref, f32[128,128]{1,0:T(8,128)S(1)} %get-tuple-element.115.field_ref.first_ref, f32[64,128]{1,0:T(8,128)S(1)} %update.8.rest_1_.second_ref), custom_call_target="tpu_custom_call" | custom-call | flops 16777216 | bytes 1048576 | tf_op jit(solution)/shard_map/finish/pallas_call | solution.py:822
  (12 shorter events, 0.0 us)
Async XLA Ops:
  0.6 9.7 %copy-start.2 = (bf16[64,64,128]{2,1,0:T(8,128)(2,1)S(1)}, bf16[64,64,128]{2,1,0:T(8,128)(2,1)}, u32[]{:S(2)}) copy-start(bf16[64,64,128]{2,1,0:T(8,128)(2,1)} %inverse_ref.1) | copy-start | bytes 3145732
  2.1 1.4 %collective-permute-start = (f32[40,256]{1,0:T(8,128)S(1)}, f32[40,256]{1,0:T(8,128)S(1)}, u32[]{:S(2)}, u32[]{:S(2)}) collective-permute-start(f32[40,256]{1,0:T(8,128)S(1)} %get-tuple-element.67), channel_id=1, source_target_pairs={{0,1},{1,0},{2,3},{3,2},{4,5},{5,4},{6,7},{7,6},{8,9},{9,8},{10,11... | collective-permute-start | bytes 122888 | tf_op jit(solution)/shard_map/ppermute | solution.py:845
  3.6 6.6 %collective-permute-start.1 = (f32[40,256]{1,0:T(8,128)S(1)}, f32[40,256]{1,0:T(8,128)S(1)}, u32[]{:S(2)}, u32[]{:S(2)}) collective-permute-start(f32[40,256]{1,0:T(8,128)S(1)} %get-tuple-element.73), channel_id=1, source_target_pairs={{0,2},{1,0},{2,1},{3,5},{4,6},{5,3},{6,4},{7,9},{8,10},{9,7},{10,8... | collective-permute-start | bytes 122888 | tf_op jit(solution)/shard_map/ppermute | solution.py:845
  6.4 3.8 %collective-permute-start.2 = (f32[40,128]{1,0:T(8,128)S(1)}, f32[40,128]{1,0:T(8,128)S(1)}, u32[]{:S(2)}, u32[]{:S(2)}) collective-permute-start(f32[40,128]{1,0:T(8,128)S(1)} %get-tuple-element.74), channel_id=1, source_target_pairs={{0,4},{1,3},{2,6},{3,1},{4,0},{5,9},{6,2},{7,11},{8,12},{9,5},{10,... | collective-permute-start | bytes 61448 | tf_op jit(solution)/shard_map/ppermute | solution.py:845
  8.6 1.9 %copy-start = (f32[32,128]{1,0:T(8,128)S(1)}, f32[32,128]{1,0:T(8,128)}, u32[]{:S(2)}) copy-start(f32[32,128]{1,0:T(8,128)} %constant.5.clone.weight_ref) | copy-start | bytes 49156
  8.6 1.9 %copy-start.1 = (bf16[64,384]{1,0:T(8,128)(2,1)S(1)}, bf16[64,384]{1,0:T(8,128)(2,1)}, u32[]{:S(2)}) copy-start(bf16[64,384]{1,0:T(8,128)(2,1)} %constant.4.clone.stiffness_ref) | copy-start | bytes 147460
  8.6 1.8 %copy-start.3 = (f32[64,128]{1,0:T(8,128)S(1)}, f32[64,128]{1,0:T(8,128)}, u32[]{:S(2)}) copy-start(f32[64,128]{1,0:T(8,128)} %field_ref.3) | copy-start | bytes 98308
  10.3 1.3 %collective-permute-start.3 = (f32[40,384]{1,0:T(8,128)S(1)}, f32[40,384]{1,0:T(8,128)S(1)}, u32[]{:S(2)}, u32[]{:S(2)}) collective-permute-start(f32[40,384]{1,0:T(8,128)S(1)} %relay.4), channel_id=1, source_target_pairs={{0,1},{1,0},{2,3},{3,2},{4,5},{5,4},{6,7},{7,6},{8,9},{9,8},{10,11... | collective-permute-start | bytes 184328 | tf_op jit(solution)/shard_map/ppermute | solution.py:845
  12.3 1.3 %collective-permute-start.4 = (f32[64,256]{1,0:T(8,128)S(1)}, f32[64,256]{1,0:T(8,128)S(1)}, u32[]{:S(2)}, u32[]{:S(2)}) collective-permute-start(f32[64,256]{1,0:T(8,128)S(1)} %get-tuple-element.91), channel_id=1, source_target_pairs={{0,1},{1,0},{2,3},{3,2},{4,5},{5,4},{6,7},{7,6},{8,9},{9,8},{10,11... | collective-permute-start | bytes 196616 | tf_op jit(solution)/shard_map/ppermute | solution.py:845
  13.8 4.4 %collective-permute-start.5 = (f32[112,128]{1,0:T(8,128)S(1)}, f32[112,128]{1,0:T(8,128)S(1)}, u32[]{:S(2)}, u32[]{:S(2)}) collective-permute-start(f32[112,128]{1,0:T(8,128)S(1)} %get-tuple-element.94), channel_id=1, source_target_pairs={{0,2},{1,0},{2,1},{3,5},{4,6},{5,3},{6,4},{7,9},{8,10},{9,7},{10,8... | collective-permute-start | bytes 172040 | tf_op jit(solution)/shard_map/ppermute | solution.py:845
  14.3 3.8 %collective-permute-start.6 = (f32[48,128]{1,0:T(8,128)S(1)}, f32[48,128]{1,0:T(8,128)S(1)}, u32[]{:S(2)}, u32[]{:S(2)}) collective-permute-start(f32[48,128]{1,0:T(8,128)S(1)} %get-tuple-element.95), channel_id=1, source_target_pairs={{0,4},{1,3},{2,6},{3,1},{4,0},{5,9},{6,2},{7,11},{8,12},{9,5},{10,... | collective-permute-start | bytes 73736 | tf_op jit(solution)/shard_map/ppermute | solution.py:845
  18.3 1.3 %copy-start.4 = (f32[64,128]{1,0:T(8,128)S(1)}, f32[64,128]{1,0:T(8,128)}, u32[]{:S(2)}) copy-start(f32[64,128]{1,0:T(8,128)} %rest_1_.1) | copy-start | bytes 98308
  18.3 1.3 %collective-permute-start.7 = (f32[64,384]{1,0:T(8,128)S(1)}, f32[64,384]{1,0:T(8,128)S(1)}, u32[]{:S(2)}, u32[]{:S(2)}) collective-permute-start(f32[64,384]{1,0:T(8,128)S(1)} %relay.5), channel_id=1, source_target_pairs={{0,1},{1,0},{2,3},{3,2},{4,5},{5,4},{6,7},{7,6},{8,9},{9,8},{10,11... | collective-permute-start | bytes 294920 | tf_op jit(solution)/shard_map/ppermute | solution.py:845
  20.8 1.3 %collective-permute-start.8 = (f32[64,256]{1,0:T(8,128)S(1)}, f32[64,256]{1,0:T(8,128)S(1)}, u32[]{:S(2)}, u32[]{:S(2)}) collective-permute-start(f32[64,256]{1,0:T(8,128)S(1)} %get-tuple-element.108), channel_id=1, source_target_pairs={{0,1},{1,0},{2,3},{3,2},{4,5},{5,4},{6,7},{7,6},{8,9},{9,8},{10,11... | collective-permute-start | bytes 196616 | tf_op jit(solution)/shard_map/ppermute | solution.py:845
  22.2 5.8 %collective-permute-start.9 = (f32[112,128]{1,0:T(8,128)S(1)}, f32[112,128]{1,0:T(8,128)S(1)}, u32[]{:S(2)}, u32[]{:S(2)}) collective-permute-start(f32[112,128]{1,0:T(8,128)S(1)} %get-tuple-element.110), channel_id=1, source_target_pairs={{0,2},{1,0},{2,1},{3,5},{4,6},{5,3},{6,4},{7,9},{8,10},{9,7},{10,8... | collective-permute-start | bytes 172040 | tf_op jit(solution)/shard_map/ppermute | solution.py:845
  24.0 4.0 %collective-permute-start.10 = (f32[48,128]{1,0:T(8,128)S(1)}, f32[48,128]{1,0:T(8,128)S(1)}, u32[]{:S(2)}, u32[]{:S(2)}) collective-permute-start(f32[48,128]{1,0:T(8,128)S(1)} %get-tuple-element.111), channel_id=1, source_target_pairs={{0,4},{1,3},{2,6},{3,1},{4,0},{5,9},{6,2},{7,11},{8,12},{9,5},{10,... | collective-permute-start | bytes 73736 | tf_op jit(solution)/shard_map/ppermute | solution.py:845
  28.1 1.3 %collective-permute-start.11 = (f32[64,384]{1,0:T(8,128)S(1)}, f32[64,384]{1,0:T(8,128)S(1)}, u32[]{:S(2)}, u32[]{:S(2)}) collective-permute-start(f32[64,384]{1,0:T(8,128)S(1)} %relay.6), channel_id=1, source_target_pairs={{0,1},{1,0},{2,3},{3,2},{4,5},{5,4},{6,7},{7,6},{8,9},{9,8},{10,11... | collective-permute-start | bytes 294920 | tf_op jit(solution)/shard_map/ppermute | solution.py:845
  30.2 1.3 %collective-permute-start.12 = (f32[32,256]{1,0:T(8,128)S(1)}, f32[32,256]{1,0:T(8,128)S(1)}, u32[]{:S(2)}, u32[]{:S(2)}) collective-permute-start(f32[32,256]{1,0:T(8,128)S(1)} %get-tuple-element.118), channel_id=1, source_target_pairs={{0,1},{1,0},{2,3},{3,2},{4,5},{5,4},{6,7},{7,6},{8,9},{9,8},{10,11... | collective-permute-start | bytes 98312 | tf_op jit(solution)/shard_map/ppermute | solution.py:845
  31.6 5.1 %collective-permute-start.13 = (f32[32,256]{1,0:T(8,128)S(1)}, f32[32,256]{1,0:T(8,128)S(1)}, u32[]{:S(2)}, u32[]{:S(2)}) collective-permute-start(f32[32,256]{1,0:T(8,128)S(1)} %get-tuple-element.121), channel_id=1, source_target_pairs={{0,2},{1,0},{2,1},{3,5},{4,6},{5,3},{6,4},{7,9},{8,10},{9,7},{10,8... | collective-permute-start | bytes 98312 | tf_op jit(solution)/shard_map/ppermute | solution.py:845
  32.3 4.3 %collective-permute-start.14 = (f32[32,128]{1,0:T(8,128)S(1)}, f32[32,128]{1,0:T(8,128)S(1)}, u32[]{:S(2)}, u32[]{:S(2)}) collective-permute-start(f32[32,128]{1,0:T(8,128)S(1)} %get-tuple-element.122), channel_id=1, source_target_pairs={{0,4},{1,3},{2,6},{3,1},{4,0},{5,9},{6,2},{7,11},{8,12},{9,5},{10,... | collective-permute-start | bytes 49160 | tf_op jit(solution)/shard_map/ppermute | solution.py:845
  36.7 1.2 %collective-permute-start.15 = (f32[32,384]{1,0:T(8,128)S(1)}, f32[32,384]{1,0:T(8,128)S(1)}, u32[]{:S(2)}, u32[]{:S(2)}) collective-permute-start(f32[32,384]{1,0:T(8,128)S(1)} %relay.7), channel_id=1, source_target_pairs={{0,1},{1,0},{2,3},{3,2},{4,5},{5,4},{6,7},{7,6},{8,9},{9,8},{10,11... | collective-permute-start | bytes 147464 | tf_op jit(solution)/shard_map/ppermute | solution.py:845
